TPU v7x, 32 devices: a whole 2x2x4 slice. The times are simulated.
32 devices in a mesh: ta: 2 (over x), gx: 4 (over z), gy: 4 (over y, core).
Axes of the slice: x: 2, y: 2, z: 4, core: 2. Of those that a mesh axis runs over, the one named last changes fastest.
Arguments:
- eigvecs: bfloat16 [2, 4, 8, 24, 3, 2, 128], P('ta', 'gx', 'gy'), may hold values from -6 to 6
- links: bfloat16 [2, 4, 8, 24, 3, 2, 3, 3], P('ta', 'gx', 'gy'), may hold values from -4 to 4
- op_dirs: int32 [8], replicated, may hold values from 0 to 6, as said below
- op_moms: int32 [8], replicated, may hold values from 0 to 2
- perams: bfloat16 [8, 2, 512, 512], P(('ta', 'gx')), may hold values from -0.25 to 0.25
- pair_times: int32 [8, 2], P(('ta', 'gx')), may hold values from 0 to 1
- slot_counts: int32 [8], P(('ta', 'gx')), may hold values from 1 to 1, as said below
Outputs:
- margins: float32 [2, 8, 2, 128, 128], P('ta', 'gy')
- correlators: float32 [8, 8, 2], P(('ta', 'gx'), 'gy')
Inputs may be any that keep to these rules, and one draw needn't show every extreme that they name: Owner k holds slot k of the slot dimension; slot_counts[k] is 1 in every draw. `op_dirs`: codes 0, 1, 2 step forward along the first, second, third dimension, codes 3, 4, 5 step backward along them, code 6 is no displacement. Every code is used by some operator. `op_moms`: momentum in units of 2 pi / 24.
All inputs are finite; a program needn't handle non-finite values.
Results may differ from a plain program's by a relative error of at most 0.0061.
Values may be sent and summed in bfloat16 or wider, within the bound.
No kernel may reach another device: no remote copies, remote signals or barrier semaphores. Data moves between devices by JAX's collectives and lax.ppermute only.
A program may use at most 64 MiB of HBM per device.

v0:
```python
import math

import jax
import jax.numpy as jnp
from jax import lax
from jax.sharding import PartitionSpec as P


def padded(block, sides, width):
    for axis, dim in sides:
        count = lax.axis_size(axis)
        forward = [(i, i + 1) for i in range(count - 1)]
        forward.append((count - 1, 0))
        backward = [(target, source) for source, target in forward]
        low = lax.ppermute(
            lax.slice_in_dim(block, block.shape[dim] - width, None, axis=dim), axis, forward
        )
        high = lax.ppermute(lax.slice_in_dim(block, 0, width, axis=dim), axis, backward)
        block = jnp.concatenate([low, block, high], axis=dim)
    return block


def color_apply(link_dir, vec_field):
    link_real = link_dir[..., 0, :, :]
    link_imag = link_dir[..., 1, :, :]
    field_real = vec_field[..., :, 0, :]
    field_imag = vec_field[..., :, 1, :]
    real_part = jnp.einsum(
        "...ab,...bn->...an", link_real, field_real, preferred_element_type=jnp.float32
    ) - jnp.einsum("...ab,...bn->...an", link_imag, field_imag, preferred_element_type=jnp.float32)
    imag_part = jnp.einsum(
        "...ab,...bn->...an", link_real, field_imag, preferred_element_type=jnp.float32
    ) + jnp.einsum("...ab,...bn->...an", link_imag, field_real, preferred_element_type=jnp.float32)
    return jnp.stack([real_part, imag_part], axis=-2)


def color_adjoint(link_dir, vec_field):
    link_real = link_dir[..., 0, :, :]
    link_imag = link_dir[..., 1, :, :]
    field_real = vec_field[..., :, 0, :]
    field_imag = vec_field[..., :, 1, :]
    real_part = jnp.einsum(
        "...ba,...bn->...an", link_real, field_real, preferred_element_type=jnp.float32
    ) + jnp.einsum("...ba,...bn->...an", link_imag, field_imag, preferred_element_type=jnp.float32)
    imag_part = jnp.einsum(
        "...ba,...bn->...an", link_real, field_imag, preferred_element_type=jnp.float32
    ) - jnp.einsum("...ba,...bn->...an", link_imag, field_real, preferred_element_type=jnp.float32)
    return jnp.stack([real_part, imag_part], axis=-2)


def phase_turn(values, momentum, z_coord):
    angle = 2.0 * math.pi * momentum.astype(jnp.float32) * z_coord / z_coord.shape[0]
    cosine = jnp.cos(angle)[:, None, None]
    sine = jnp.sin(angle)[:, None, None]
    values_real = values[..., 0, :]
    values_imag = values[..., 1, :]
    return jnp.stack(
        [cosine * values_real - sine * values_imag, sine * values_real + cosine * values_imag],
        axis=-2,
    )


def margin_block(left_matrix, displaced):
    vectors = displaced.shape[-1]
    rotated = jnp.stack([displaced[..., 1, :], -displaced[..., 0, :]], axis=-2)
    right_matrix = jnp.concatenate(
        [displaced.reshape(-1, vectors), rotated.reshape(-1, vectors)], axis=1
    )
    product = jnp.dot(left_matrix.T, right_matrix, preferred_element_type=jnp.float32)
    return product.reshape(vectors, 2, vectors).transpose(1, 0, 2)


def contract(tau_matrix, sink_margin, source_margin):
    order = tau_matrix.shape[-1]
    vectors = sink_margin.shape[-1]
    spins = order // vectors
    count_ops = sink_margin.shape[0]
    sink_real = sink_margin[:, 0]
    sink_imag = sink_margin[:, 1]
    source_real = source_margin[:, 0]
    source_imag = source_margin[:, 1]
    rows_real = tau_matrix[0].reshape(spins, vectors, order)
    rows_imag = tau_matrix[1].reshape(spins, vectors, order)
    left_real = jnp.einsum(
        "oab,sbc->osac", sink_real, rows_real, preferred_element_type=jnp.float32
    ) - jnp.einsum("oab,sbc->osac", sink_imag, rows_imag, preferred_element_type=jnp.float32)
    left_imag = jnp.einsum(
        "oab,sbc->osac", sink_real, rows_imag, preferred_element_type=jnp.float32
    ) + jnp.einsum("oab,sbc->osac", sink_imag, rows_real, preferred_element_type=jnp.float32)
    cols_real = tau_matrix[0].reshape(order, spins, vectors)
    cols_imag = tau_matrix[1].reshape(order, spins, vectors)
    right_real = jnp.einsum(
        "isd,ocd->oisc", cols_real, source_real, preferred_element_type=jnp.float32
    ) + jnp.einsum("isd,ocd->oisc", cols_imag, source_imag, preferred_element_type=jnp.float32)
    right_imag = jnp.einsum(
        "isd,ocd->oisc", cols_imag, source_real, preferred_element_type=jnp.float32
    ) - jnp.einsum("isd,ocd->oisc", cols_real, source_imag, preferred_element_type=jnp.float32)
    left_real = left_real.reshape(count_ops, order, order)
    left_imag = left_imag.reshape(count_ops, order, order)
    right_real = right_real.reshape(count_ops, order, order)
    right_imag = right_imag.reshape(count_ops, order, order)
    trace_real = jnp.sum(left_real * right_real + left_imag * right_imag, axis=(1, 2))
    trace_imag = jnp.sum(left_imag * right_real - left_real * right_imag, axis=(1, 2))
    return jnp.stack([trace_real, trace_imag], axis=-1) / vectors


def per_device(eigvecs, links, op_dirs, op_moms, perams, pair_times, slot_counts):
    eigen_field = eigvecs[0]
    link_field = links[0]
    cells_x = eigen_field.shape[0]
    cells_y = eigen_field.shape[1]
    cells_z = eigen_field.shape[2]
    vectors = eigen_field.shape[-1]
    carried = [
        color_adjoint(link_field[..., d, :, :, :], eigen_field).astype(jnp.bfloat16)
        for d in range(3)
    ]
    padded_first = padded(jnp.stack([eigen_field, carried[0]]), (("gx", 1),), 1)
    padded_second = padded(jnp.stack([eigen_field, carried[1]]), (("gy", 2),), 1)
    forward = [
        padded_first[0, 2 : cells_x + 2],
        padded_second[0, :, 2 : cells_y + 2],
        jnp.roll(eigen_field, -1, axis=2),
    ]
    behind = [
        padded_first[1, 0:cells_x],
        padded_second[1, :, 0:cells_y],
        jnp.roll(carried[2], 1, axis=2),
    ]
    shifted = [color_apply(link_field[..., d, :, :, :], forward[d]) for d in range(3)]
    shifted = (
        shifted
        + [piece.astype(jnp.float32) for piece in behind]
        + [eigen_field.astype(jnp.float32)]
    )
    stacked = jnp.stack(shifted)
    z_coord = jnp.arange(cells_z, dtype=jnp.float32)
    left_matrix = eigen_field.reshape(-1, vectors)
    norm_factor = 1.0 / math.sqrt(
        3.0 * cells_x * lax.axis_size("gx") * cells_y * lax.axis_size("gy") * cells_z
    )
    op_rows = []
    for o in range(op_dirs.shape[0]):
        chosen = lax.dynamic_index_in_dim(stacked, op_dirs[o], 0, keepdims=False)
        displaced = phase_turn(chosen, op_moms[o], z_coord).astype(jnp.bfloat16)
        op_rows.append(margin_block(left_matrix, displaced))
    partial_sums = jnp.stack(op_rows) * norm_factor
    shared = lax.psum_scatter(partial_sums, "gy", scatter_dimension=0, tiled=True)
    own_ops = lax.psum(shared, "gx")
    margin_out = own_ops[None]
    every_time = lax.all_gather(own_ops.astype(jnp.bfloat16)[None], "ta", axis=0, tiled=True)
    live_count = slot_counts[0]
    tau_matrix = lax.dynamic_index_in_dim(perams, 0, 0, keepdims=False)
    pair_row = lax.dynamic_index_in_dim(pair_times, 0, 0, keepdims=False)
    sink_margin = lax.dynamic_index_in_dim(every_time, pair_row[0], 0, keepdims=False)
    source_margin = lax.dynamic_index_in_dim(every_time, pair_row[1], 0, keepdims=False)
    value_here = contract(tau_matrix, sink_margin, source_margin)
    results = [jnp.where(0 < live_count, value_here, jnp.zeros_like(value_here))]
    correlators = jnp.stack(results)
    return (margin_out, correlators)


def solution(mesh):
    placed = (
        P("ta", "gx", "gy", None, None, None, None),
        P("ta", "gx", "gy", None, None, None, None, None),
        P(),
        P(),
        P(("ta", "gx"), None, None, None),
        P(("ta", "gx"), None),
        P(("ta", "gx")),
    )
    return jax.shard_map(
        per_device,
        mesh=mesh,
        in_specs=placed,
        out_specs=(P("ta", "gy", None, None, None), P(("ta", "gx"), "gy", None)),
        check_vma=False,
    )
```

profile of v0, /device:TPU:0, one launch (start us, length us, event | category | flops | bytes accessed | tf_op | source)
XLA Modules:
  0.0 155.2 jit_solution(9204379298824826071)
XLA Ops:
  7.2 0.9 copy.503
  8.2 1.1 copy.292
  11.0 5.1 %collective-permute-start = (bf16[2,1,2,24,3,2,128]{6,3,5,4,2,1,0:T(8,128)(2,1)S(1)}, bf16[2,1,2,24,3,2,128]{6,3,5,4,2,1,0:T(8,128)(2,1)S(1)}, u32[]{:S(2)}, u32[]{:S(2)}) collective-permute-start(bf16[2,1,2,24,3,2,128]{6,3,5,4,2,1,0:T(8,128)(2,1)S(1)} %get-tuple-element.68), channel_id=1, source_target_pairs={{4,0},{8,4},{12,8},{0,12},{5,1},{9,5},{13,9},{1,13},{6,2},{10,6},{... | collective-permute-start | bytes 442376 | tf_op jit(solution)/shard_map/ppermute | solution.py:18
  16.1 0.7 collective-permute-start.1
  17.1 0.3 fusion.93
  17.4 0.3 fusion.96
  17.6 0.3 fusion.97
  18.7 0.7 fusion.139
  29.4 0.7 fusion.138
  40.6 0.2 fusion.62
  40.8 0.3 fusion.60
  41.1 0.3 fusion.66
  41.4 0.3 fusion.64
  41.7 0.2 fusion.70
  41.9 0.3 fusion.68
  42.2 0.3 fusion.74
  42.5 0.3 fusion.72
  44.7 0.3 fusion.35
  45.2 0.3 fusion.31
  45.6 0.3 fusion.27
  46.1 0.3 fusion.23
  46.5 0.3 fusion.19
  47.0 0.3 fusion.15
  47.4 0.3 fusion.11
  47.9 0.3 fusion.7
  48.4 1.1 broadcast_multiply_fusion
  49.6 0.6 fusion.137
  52.8 23.3 %reduce-scatter.2.cloned.1.call-done = f32[2,2,128,128]{3,2,1,0:T(8,128)} async-done(((f32[8,2,128,128]{3,2,1,0:T(8,128)}), f32[2,2,128,128]{3,2,1,0:T(8,128)}) %reduce-scatter.2.cloned.1.call-update) | async-done | bytes 262160 | tf_op jit(solution)/shard_map/reduce_scatter | solution.py:148
  76.2 1.0 copy.406
  77.2 1.0 copy.407
  80.2 33.7 %all-reduce.2.cloned.1.call-done = f32[2,2,128,128]{3,2,1,0:T(8,128)} async-done(((f32[2,2,128,128]{3,2,1,0:T(8,128)}), f32[2,2,128,128]{3,2,1,0:T(8,128)}) %all-reduce.2.cloned.1.call-update) | async-done | bytes 262160 | tf_op jit(solution)/shard_map/psum | solution.py:149
  113.9 1.0 convert_element_type.242
  114.8 5.8 %all-gather = bf16[4,2,128,128]{3,2,1,0:T(8,128)(2,1)S(1)} all-gather(bf16[2,2,128,128]{3,2,1,0:T(8,128)(2,1)S(1)} %convert_element_type.242), channel_id=2, replica_groups=mesh['ta'=2,'gx'=4,'gy'=4] {'ta'}, dimensions={0}, use_global_device_ids=true | all-gather | bytes 393216 | tf_op jit(solution)/shard_map/all_gather | solution.py:151
  120.7 0.4 fusion.54
  121.1 1.8 %fusion.53 = f32[2,128,4,512]{3,1,2,0:T(8,128)} fusion(bf16[4,128,512,1]{2,1,0,3:T(8,128)(2,1)S(1)} %bitcast.352, bf16[2,2,128,128]{3,2,0,1:T(8,128)(2,1)S(1)} %bitcast.359), kind=kOutput, calls=%fused_computation.151 | convolution fusion | flops 134217728 | bytes 2686976 | tf_op jit(solution)/shard_map/oab,sbc->osac/dot_general | solution.py:87
  122.9 0.4 convolution_subtract_fusion
  123.3 0.6 copy-done.1
  123.9 0.4 fusion.56
  124.4 1.8 %fusion.55 = f32[2,128,512,4]{2,1,3,0:T(8,128)} fusion(bf16[512,4,128,1]{0,2,1,3:T(8,128)(2,1)S(1)} %bitcast.356, bf16[2,2,128,128]{3,2,0,1:T(8,128)(2,1)S(1)} %bitcast.363), kind=kOutput, calls=%fused_computation.153 | convolution fusion | flops 134217728 | bytes 2686976 | tf_op jit(solution)/shard_map/isd,ocd->oisc/dot_general | solution.py:95
  126.2 1.8 %add_bitcast_fusion = f32[2,512,4,128]{1,3,2,0:T(8,128)} fusion(f32[2,128,512,4]{2,1,3,0:T(8,128)S(1)} %fusion.56, bf16[512,4,128,1]{0,2,1,3:T(8,128)(2,1)S(1)} %bitcast.357, bf16[2,2,128,128]{3,2,0,1:T(8,128)(2,1)S(1)} %bitcast.364), kind=kOutput, calls=%fused_computation.9 | convolution fusion | flops 134742016 | bytes 4784128 | tf_op jit(solution)/shard_map/isd,ocd->oisc/dot_general | solution.py:94
  127.9 3.0 %reshape.1006 = f32[2,4,128,512]{2,1,3,0:T(4,128)} reshape(f32[2,512,4,128]{1,3,2,0:T(8,128)} %add_bitcast_fusion) | data formatting | bytes 4194304 | tf_op jit(solution)/shard_map/reshape | solution.py:100
  130.9 3.0 %copy.401 = f32[2,4,128,512]{3,2,1,0:T(8,128)} copy(f32[2,4,128,512]{2,1,3,0:T(4,128)} %reshape.1006) | data formatting | bytes 4194304 | tf_op jit(solution)/shard_map/reshape | solution.py:100
  133.9 3.4 %subtract_bitcast_fusion = f32[2,512,4,128]{1,3,2,0:T(8,128)} fusion(f32[2,128,512,4]{2,1,3,0:T(8,128)} %fusion.55, bf16[512,4,128,1]{0,2,1,3:T(8,128)(2,1)S(1)} %bitcast.355, bf16[2,2,128,128]{3,2,0,1:T(8,128)(2,1)S(1)} %bitcast.365), kind=kOutput, calls=%fused_computation.8 | convolution fusion | flops 134742016 | bytes 4784128 | tf_op jit(solution)/shard_map/isd,ocd->oisc/dot_general | solution.py:97
  137.2 3.0 %reshape.1007 = f32[2,4,128,512]{2,1,3,0:T(4,128)} reshape(f32[2,512,4,128]{1,3,2,0:T(8,128)} %subtract_bitcast_fusion) | data formatting | bytes 4194304 | tf_op jit(solution)/shard_map/reshape | solution.py:101
  140.2 2.9 %copy.404 = f32[2,4,128,512]{3,2,1,0:T(8,128)} copy(f32[2,4,128,512]{2,1,3,0:T(4,128)} %reshape.1007) | data formatting | bytes 4194304 | tf_op jit(solution)/shard_map/reshape | solution.py:101
  143.1 3.8 %fusion.1 = (f32[2]{0:T(128)S(1)}, f32[2]{0:T(128)S(1)}) fusion(f32[2,4,128,512]{3,2,1,0:T(8,128)} %copy.404, f32[2,4,128,512]{3,2,1,0:T(8,128)} %copy.401, f32[2,128,4,512]{3,1,2,0:T(8,128)S(1)} %convolution_subtract_fusion, f32[2,128,4,512]{3,1,2,0:T(8,128)} %fusion.53, bf16[4,128,512,1]{2,1,0,3:T(8,128)(2,1)S(1)} %bitcast.351, ...), kind=kOutput, calls=%fused_computation.3 | convolution fusion | flops 138936320 | bytes 8978448 | tf_op jit(solution)/shard_map/oab,sbc->osac/dot_general | solution.py:89
  147.0 0.7 copy.378
  147.6 0.7 copy.519
  (145 shorter events, 6.6 us)
Async XLA Ops:
  7.2 3.7 %copy-start = (bf16[1,1,2,24,3,2,128]{6,5,4,3,2,1,0:T(2,128)(2,1)S(1)}, bf16[1,1,2,24,3,2,128]{6,5,4,3,2,1,0:T(2,128)(2,1)}, u32[]{:S(2)}) copy-start(bf16[1,1,2,24,3,2,128]{6,5,4,3,2,1,0:T(2,128)(2,1)} %param.7) | copy-start | bytes 221188
  7.2 68.9 %reduce-scatter.2.cloned.1.call-start = ((), (), s32[]{:S(2)}) async-start(), calls=%async_computation.1 | async-start | bytes 1310720 | tf_op jit(solution)/shard_map/reduce_scatter | solution.py:148
  10.9 7.8 %copy-start.6 = (s32[8]{0:T(128)S(1)}, s32[8]{0:T(128)}, u32[]{:S(2)}) copy-start(s32[8]{0:T(128)} %param.9) | copy-start | bytes 100
  10.9 18.5 %copy-start.7 = (s32[8]{0:T(128)S(1)}, s32[8]{0:T(128)}, u32[]{:S(2)}) copy-start(s32[8]{0:T(128)} %param.10) | copy-start | bytes 100
  11.0 30.7 %collective-permute-start = (bf16[2,1,2,24,3,2,128]{6,3,5,4,2,1,0:T(8,128)(2,1)S(1)}, bf16[2,1,2,24,3,2,128]{6,3,5,4,2,1,0:T(8,128)(2,1)S(1)}, u32[]{:S(2)}, u32[]{:S(2)}) collective-permute-start(bf16[2,1,2,24,3,2,128]{6,3,5,4,2,1,0:T(8,128)(2,1)S(1)} %get-tuple-element.68), channel_id=1, source_target_pairs={{4,0},{8,4},{12,8},{0,12},{5,1},{9,5},{13,9},{1,13},{6,2},{10,6},{... | collective-permute-start | bytes 442376 | tf_op jit(solution)/shard_map/ppermute | solution.py:18
  16.1 26.7 %collective-permute-start.2 = (bf16[2,1,2,24,3,2,128]{6,3,5,4,2,1,0:T(8,128)(2,1)S(1)}, bf16[2,1,2,24,3,2,128]{6,3,5,4,2,1,0:T(8,128)(2,1)S(1)}, u32[]{:S(2)}, u32[]{:S(2)}) collective-permute-start(bf16[2,1,2,24,3,2,128]{6,3,5,4,2,1,0:T(8,128)(2,1)S(1)} %get-tuple-element.68), channel_id=1, source_target_pairs={{0,4},{4,8},{8,12},{12,0},{1,5},{5,9},{9,13},{13,1},{2,6},{6,10},{... | collective-permute-start | bytes 442376 | tf_op jit(solution)/shard_map/ppermute | solution.py:15
  16.1 24.5 %collective-permute-start.1 = (bf16[2,1,1,24,3,2,128]{6,3,5,4,2,1,0:T(8,128)(2,1)S(1)}, bf16[2,1,1,24,3,2,128]{6,3,5,4,2,1,0:T(8,128)(2,1)S(1)}, u32[]{:S(2)}, u32[]{:S(2)}) collective-permute-start(bf16[2,1,1,24,3,2,128]{6,3,5,4,2,1,0:T(8,128)(2,1)S(1)} %get-tuple-element.48), channel_id=1, source_target_pairs={{1,0},{2,1},{3,2},{0,3},{5,4},{6,5},{7,6},{4,7},{9,8},{10,9},{11,1... | collective-permute-start | bytes 221192 | tf_op jit(solution)/shard_map/ppermute | solution.py:18
  16.8 26.0 %collective-permute-start.3 = (bf16[2,1,1,24,3,2,128]{6,3,5,4,2,1,0:T(8,128)(2,1)S(1)}, bf16[2,1,1,24,3,2,128]{6,3,5,4,2,1,0:T(8,128)(2,1)S(1)}, u32[]{:S(2)}, u32[]{:S(2)}) collective-permute-start(bf16[2,1,1,24,3,2,128]{6,3,5,4,2,1,0:T(8,128)(2,1)S(1)} %get-tuple-element.47), channel_id=1, source_target_pairs={{0,1},{1,2},{2,3},{3,0},{4,5},{5,6},{6,7},{7,4},{8,9},{9,10},{10,1... | collective-permute-start | bytes 221192 | tf_op jit(solution)/shard_map/ppermute | solution.py:15
  48.3 1.3 copy-start.8
  48.4 27.7 %copy-start.4 = (bf16[1,2,512,512]{3,2,1,0:T(8,128)(2,1)S(1)}, bf16[1,2,512,512]{3,2,1,0:T(8,128)(2,1)}, u32[]{:S(2)}) copy-start(bf16[1,2,512,512]{3,2,1,0:T(8,128)(2,1)} %param.11) | copy-start | bytes 3145732
  49.6 64.3 %all-reduce.2.cloned.1.call-start = ((), (), s32[]{:S(2)}) async-start(), calls=%async_computation.2 | async-start | bytes 524288 | tf_op jit(solution)/shard_map/psum | solution.py:149
  122.9 1.0 copy-start.1
  123.3 1.1 copy-start.3
  130.9 3.0 %copy-start.2 = (bf16[1,1,512,512]{2,3,1,0:T(8,128)(2,1)S(1)}, bf16[1,1,512,512]{2,3,1,0:T(8,128)(2,1)}, u32[]{:S(2)}) copy-start(bf16[1,1,512,512]{2,3,1,0:T(8,128)(2,1)} %copy.406) | copy-start | bytes 1572868
  143.1 4.5 %copy-start.5 = (f32[2,2,128,128]{3,2,1,0:T(8,128)S(1)}, f32[2,2,128,128]{3,2,1,0:T(8,128)}, u32[]{:S(2)}) copy-start(f32[2,2,128,128]{3,2,1,0:T(8,128)} %all-reduce.2.cloned.1.call-done) | copy-start | bytes 786436
Sparse Core Ops, SparseCore 0:
  49.7 26.3 reduce-scatter.1
  78.5 35.3 all-reduce.1
where the time goes:
time: 156 us; the launch traced here: 155 us
  waiting for transfers between devices  57 us (37%)
  between operations  39.6 us (25%)
  local copies, waits for them, and re-layouts  22.1 us (14%)
  matrix products  21 us (13%)
  starting transfers between devices  5.92 us (4%)
  blocking collectives  5.83 us (4%)
  other arithmetic  3.83 us (2%)
    psum x1, waiting for transfers between devices, per_device(): own_ops = lax.psum(shared, 'gx')  33.7 us
    reduce_scatter x1, waiting for transfers between devices, per_device(): lax.psum_scatter(partial_sums, 'gy', scatter_dimension=0, tiled=True)  23.3 us
    unnamed x34, local copies, waits for them, and re-layouts  6.21 us
    reshape x2, local copies, waits for them, and re-layouts, contract(): right_real = right_real.reshape(count_ops, order, order)  5.93 us
    reshape x2, local copies, waits for them, and re-layouts, contract(): right_imag = right_imag.reshape(count_ops, order, order)  5.9 us
    ppermute x2, starting transfers between devices, padded(): lax.ppermute(lax.slice_in_dim(block, 0, width, axis=dim), axis, backward)  5.84 us
    all_gather x1, blocking collectives, per_device(): lax.all_gather(own_ops.astype(jnp.bfloat16)[None], 'ta', axis=0, tiled=True)  5.83 us
    dot_general x1, matrix products, contract(): jnp.einsum('oab,sbc->osac', sink_imag, rows_real, preferred_element_type=...  3.84 us
  transfers between devices with their start and end apart: 6, of which 2 were waited for; matrix products, arithmetic and copies ran while one was open for 5% of the time, Pallas kernels for 0%

commit v1 on v0

v1 whole, which is shorter than its diff:
```python
import functools
import math

import jax
import jax.numpy as jnp
import numpy as np
from jax import lax
from jax.experimental import pallas as pl
from jax.experimental.pallas import tpu as pltpu
from jax.sharding import PartitionSpec as P

VMEM_LIMIT = 24 * 1024 * 1024
MOMENTA = 3
LINK_COLS = 54
DIRECT_LIMIT = 8


def line_constants(cells_z):
    order = 6 * cells_z
    rows = np.arange(2 * order)
    turned = rows // order
    row = rows % order
    z_row, a_row, r_row = row // 6, (row % 6) // 2, row % 2
    spread = (z_row[:, None] == np.arange(cells_z)[None, :]).astype(np.float32)
    cols = np.arange(128)
    live = cols < 2 * LINK_COLS
    copy, dir_col = cols // LINK_COLS, (cols % LINK_COLS) // 18
    a_col, b_col, part_col = (cols % 18) // 6, (cols % 6) // 2, cols % 2
    source_part = np.where(turned == 0, r_row, 1 - r_row)
    sign = np.where((turned == 1) & (r_row == 0), -1.0, 1.0)
    pick = (a_row[:, None] == a_col[None, :]) & (source_part[:, None] == copy[None, :])
    pick = (pick & live[None, :]) * sign[:, None]
    out = np.arange(order)
    z_out, b_out, s_out = out // 6, (out % 6) // 2, out % 2
    needed = np.where(copy[:, None] == 0, s_out[None, :], 1 - s_out[None, :])
    value = np.where((copy[:, None] == 0) & (s_out[None, :] == 1), -1.0, 1.0)
    expand = []
    for d in range(3):
        hit = (dir_col[:, None] == d) & (b_col[:, None] == b_out[None, :]) & live[:, None]
        expand.append(np.where(hit & (part_col[:, None] == needed), value, 0.0))
    same = (z_row[:, None] == z_out[None, :]).astype(np.float32)
    plain = np.zeros((2 * order, order), np.float32)
    plain[np.arange(order), np.arange(order)] = 1.0
    partner = np.where(r_row == 0, row + 1, row - 1)
    plain[rows[order:], partner[order:]] = sign[order:]
    as_b = lambda x: jnp.asarray(np.asarray(x, np.float32), jnp.bfloat16)
    return (
        as_b(spread),
        as_b(pick),
        as_b(np.stack(expand)),
        as_b(same),
        as_b(plain),
        as_b(wave_constants(cells_z)),
    )


def wave_constants(cells_z):
    z_row = np.arange(6 * cells_z) // 6
    columns = []
    for ahead in range(2):
        for momentum in range(MOMENTA):
            angle = 2.0 * math.pi * momentum * ((z_row + ahead) % cells_z) / cells_z
            columns.append(np.cos(angle))
            columns.append(np.sin(angle))
    left = np.stack(columns, axis=1).astype(np.float32)
    terms = []
    for _ in range(3):
        term = left.astype(jnp.bfloat16).astype(np.float32)
        terms.append(term)
        left = left - term
    return np.concatenate(terms, axis=1)


def halo_fields(cells_x, cells_y):
    pairs = [(0, (cells_x - 1) * cells_y + y) for y in range(cells_y)]
    return pairs + [(1, x * cells_y + cells_y - 1) for x in range(cells_x)]


def local_fields(cells_x, cells_y):
    lines = cells_x * cells_y
    outside = halo_fields(cells_x, cells_y)
    every = [(code, line) for code in range(7) for line in range(lines)]
    return [pair for pair in every if pair not in outside]


def prepare_kernel(cells_x, cells_y, *refs):
    inputs, refs = refs[:10], refs[10:]
    matrix_ref, local_ref, left_ref, phase_ref = refs[:4]
    held, link_rows_ref, sems = refs[4:14], refs[14], refs[15]
    copies = [
        pltpu.make_async_copy(src, dst, sems.at[k])
        for k, (src, dst) in enumerate(zip(inputs, held))
    ]
    for copy in copies:
        copy.start()
    v_ref, link_ref, dirs_ref, moms_ref, spread_ref, pick_ref, expand_ref, near_ref = held[:8]
    plain_ref, waves_ref = held[8:]
    f32, bf16 = jnp.float32, jnp.bfloat16
    order, vectors = v_ref.shape[2], v_ref.shape[3]
    lines = cells_x * cells_y
    link_rows_ref[...] = jnp.zeros_like(link_rows_ref)
    for copy in copies:
        copy.wait()
    for line in range(lines):
        for k in range(LINK_COLS // 2):
            pair = link_ref[line, k].astype(f32)
            link_rows_ref[line, 2 * k : 2 * k + 2] = pair
            link_rows_ref[line, LINK_COLS + 2 * k : LINK_COLS + 2 * k + 2] = pair
    outside = halo_fields(cells_x, cells_y)
    inside = local_fields(cells_x, cells_y)
    for line in range(lines):
        x, y = line // cells_y, line % cells_y
        seen = lax.dot_general(
            spread_ref[...],
            link_rows_ref[line].astype(bf16),
            (((1,), (1,)), ((), ())),
            preferred_element_type=f32,
        )
        seen = (seen * pick_ref[...].astype(f32)).astype(bf16)
        for d in range(3):
            matrix = jnp.dot(seen, expand_ref[d], preferred_element_type=f32)
            matrix = (matrix * near_ref[...].astype(f32)).astype(bf16)
            carried = lax.dot_general(
                matrix[:order],
                v_ref[x, y],
                (((0,), (0,)), ((), ())),
                preferred_element_type=f32,
            ).astype(bf16)
            local_ref[inside.index((3 + d, line))] = jnp.dot(
                plain_ref[...], carried, preferred_element_type=f32
            )
            if (d, line) in outside:
                matrix_ref[outside.index((d, line))] = matrix
                continue
            if d == 2:
                ahead = jnp.concatenate([v_ref[x, y, 6:], v_ref[x, y, :6]], axis=0)
            else:
                ahead = v_ref[x + 1, y] if d == 0 else v_ref[x, y + 1]
            local_ref[inside.index((d, line))] = jnp.dot(
                matrix, ahead, preferred_element_type=f32
            )
        local_ref[inside.index((6, line))] = jnp.dot(
            plain_ref[...], v_ref[x, y], preferred_element_type=f32
        )
        here = v_ref[x, y].astype(f32).T
        columns = slice(line * order, (line + 1) * order)
        left_ref[0, :, columns] = here.astype(bf16)
        left_ref[1, :, columns] = jnp.concatenate([here[:, 6:], here[:, :6]], axis=1).astype(bf16)
    wave_cols = waves_ref.shape[1]
    per_term = wave_cols // 3
    wave_row = lax.broadcasted_iota(jnp.int32, (wave_cols, 2 * vectors), 0) % per_term
    wave_half = lax.broadcasted_iota(jnp.int32, (wave_cols, 2 * vectors), 1) // vectors
    wave_at = wave_row - wave_half
    for o in range(phase_ref.shape[0]):
        code = dirs_ref[o]
        column = 2 * (jnp.where(code == 5, MOMENTA, 0) + moms_ref[o])
        chosen = (wave_at == column).astype(f32).astype(bf16)
        phase_ref[o] = jnp.dot(waves_ref[...], chosen, preferred_element_type=f32)


def low_bit(j):
    return (j & -j).bit_length() - 1


def margin_kernel(cells_x, cells_y, groups, *refs):
    matrix_ref, local_ref, left_ref, phase_ref, halo_x_ref, halo_y_ref, dirs_hbm = refs[:7]
    levels = groups.bit_length() - 1
    out_refs = refs[7 : 8 + levels]
    field_ref, pair_ref, side_ref, dirs_ref, sem = refs[8 + levels :]
    f32, bf16 = jnp.float32, jnp.bfloat16
    copy = pltpu.make_async_copy(dirs_hbm, dirs_ref, sem)
    copy.start()
    lines = cells_x * cells_y
    order, vectors = halo_x_ref.shape[2], halo_x_ref.shape[3]
    for k, (d, line) in enumerate(halo_fields(cells_x, cells_y)):
        x, y = line // cells_y, line % cells_y
        ahead = halo_x_ref[0, y] if d == 0 else halo_y_ref[x, 0]
        field_ref[d, line] = jnp.dot(matrix_ref[k], ahead, preferred_element_type=f32)
    for k, (code, line) in enumerate(local_fields(cells_x, cells_y)):
        field_ref[code, line] = local_ref[k]
    side_ref[0] = left_ref[0]
    side_ref[3] = left_ref[1]
    for line in range(lines):
        x, y = line // cells_y, line % cells_y
        columns = slice(line * order, (line + 1) * order)
        if x + 1 < cells_x:
            ahead = slice((line + cells_y) * order, (line + cells_y + 1) * order)
            side_ref[1, :, columns] = left_ref[0, :, ahead]
        else:
            side_ref[1, :, columns] = halo_x_ref[0, y].astype(f32).T.astype(bf16)
        if y + 1 < cells_y:
            ahead = slice((line + 1) * order, (line + 2) * order)
            side_ref[2, :, columns] = left_ref[0, :, ahead]
        else:
            side_ref[2, :, columns] = halo_y_ref[x, 0].astype(f32).T.astype(bf16)
    copy.wait()
    count_ops = dirs_ref.shape[0]
    own_ops = count_ops // groups
    me = lax.axis_index("gy")
    for j in range(groups):
        for i in range(own_ops):
            o = (me ^ j) * own_ops + i
            code = dirs_ref[o]
            side = jnp.where((code >= 3) & (code < 6), code - 2, 0)
            slot = j * own_ops + i
            for line in range(lines):
                plain = field_ref[code, line, 0:order]
                turned = field_ref[code, line, order : 2 * order]
                cosine = phase_ref[o, :, 0:vectors]
                sine = phase_ref[o, :, vectors : 2 * vectors]
                rows = slice(line * order, (line + 1) * order)
                pair_ref[slot, rows, 0:vectors] = (cosine * plain + sine * turned).astype(bf16)
                pair_ref[slot, rows, vectors : 2 * vectors] = (
                    sine * plain - cosine * turned
                ).astype(bf16)
            product = jnp.dot(side_ref[side], pair_ref[slot], preferred_element_type=f32)
            level = levels if j == 0 else low_bit(j)
            out_ref = out_refs[level]
            place = 0 if j == 0 else j >> (level + 1)
            first = 2 * i * vectors
            out_ref[place, first : first + vectors] = product[:, :vectors].astype(out_ref.dtype)
            out_ref[place, first + vectors : first + 2 * vectors] = product[:, vectors:].astype(
                out_ref.dtype
            )


def fold_kernel(level, *refs):
    held_ref, received, out_ref = refs[0], refs[1:-1], refs[-1]
    f32 = jnp.float32
    for k in range(held_ref.shape[0]):
        j = (2 * k + 1) << level
        total = held_ref[k]
        for b, ref in enumerate(received):
            total = total + ref[j >> (b + 1)].astype(f32)
        out_ref[k] = total.astype(out_ref.dtype)


def share_kernel(levels, *refs):
    held_ref, received, outs = refs[0], refs[1 : 1 + levels], refs[1 + levels :]
    f32 = jnp.float32
    count = len(outs)
    rows = outs[0].shape[0]
    me = lax.axis_index("gx")
    for step, out_ref in enumerate(outs):
        chunk = lax.rem(me + step, count)
        span = pl.ds(pl.multiple_of(chunk * rows, rows), rows)
        total = held_ref[0, span]
        for ref in received:
            total = total + ref[0, span].astype(f32)
        out_ref[...] = total.astype(out_ref.dtype)


def sum_kernel(norm_factor, *refs):
    own_ref, received, out_ref = refs[0], refs[1:-1], refs[-1]
    total = own_ref[...]
    for ref in received:
        total = total + ref[...].astype(jnp.float32)
    out_ref[...] = (total * norm_factor).astype(out_ref.dtype)


def contract_kernel(times, shares, count_chunks, *refs):
    pair_hbm, live_hbm = refs[:2]
    chunks, refs = refs[2 : 2 + count_chunks], refs[2 + count_chunks :]
    tau_ref, margin_ref, corr_ref = refs[:3]
    every_ref, left_ref, right_ref, pair_ref, live_ref, sems = refs[3:]
    f32 = jnp.float32
    copies = [
        pltpu.make_async_copy(src, dst, sems.at[k])
        for k, (src, dst) in enumerate(
            ((pair_hbm, pair_ref), (live_hbm, live_ref))
        )
    ]
    for copy in copies:
        copy.start()
    vectors = every_ref.shape[2]
    count_ops = margin_ref.shape[1]
    order = tau_ref.shape[2]
    spins = order // vectors
    me_t, me_x = lax.axis_index("ta"), lax.axis_index("gx")
    if count_chunks == 1:
        every_ref[...] = chunks[0][...]
    else:
        rows = chunks[0].shape[0]
        for k in range(count_chunks):
            at_t = lax.rem(me_t + k // shares, times)
            at_x = lax.rem(me_x + k % shares, shares)
            span = pl.ds(pl.multiple_of(at_x * rows, rows), rows)
            every_ref[at_t, span] = chunks[k][...]
    for copy in copies:
        copy.wait()
    sink, source = pair_ref[0, 0], pair_ref[0, 1]
    live = live_ref[0] > 0
    for o in range(count_ops):
        first = 2 * o * vectors
        part = lambda t, k: every_ref[t, first + k * vectors : first + (k + 1) * vectors]
        margin_ref[0, o, 0] = part(me_t, 0).astype(f32)
        margin_ref[0, o, 1] = part(me_t, 1).astype(f32)
        a_r, a_i = part(sink, 0), part(sink, 1)
        b_r, b_i = part(source, 0).T, part(source, 1).T
        left_ref[o, 0:vectors, 0:vectors] = a_r
        left_ref[o, 0:vectors, vectors:] = -a_i
        left_ref[o, vectors:, 0:vectors] = a_i
        left_ref[o, vectors:, vectors:] = a_r
        right_ref[o, 0:vectors, 0:vectors] = b_r
        right_ref[o, 0:vectors, vectors:] = -b_i
        right_ref[o, vectors:, 0:vectors] = b_i
        right_ref[o, vectors:, vectors:] = b_r
        real = jnp.zeros((8, vectors), f32)
        imag = jnp.zeros((8, vectors), f32)
        fold = lambda t: jnp.sum(t.reshape(vectors // 8, 8, vectors), axis=0)
        for s in range(spins):
            rows = slice(s * vectors, (s + 1) * vectors)
            x = jnp.dot(
                left_ref[o],
                jnp.concatenate([tau_ref[0, rows], tau_ref[1, rows]], axis=0),
                preferred_element_type=f32,
            )
            for c in range(spins):
                cols = slice(c * vectors, (c + 1) * vectors)
                y = jnp.dot(
                    jnp.concatenate([tau_ref[0, rows, cols], tau_ref[1, rows, cols]], axis=1),
                    right_ref[o],
                    preferred_element_type=f32,
                )
                x_r, x_i = x[:vectors, cols], x[vectors:, cols]
                y_r, y_i = y[:, :vectors], y[:, vectors:]
                real = real + fold(x_r * y_r + x_i * y_i)
                imag = imag + fold(x_i * y_r - x_r * y_i)
        scale = 1.0 / vectors
        corr_ref[0, o, 0] = jnp.where(live, jnp.sum(real) * scale, 0.0)
        corr_ref[0, o, 1] = jnp.where(live, jnp.sum(imag) * scale, 0.0)


def vmem_spec():
    return pl.BlockSpec(memory_space=pltpu.VMEM)


def smem_spec():
    return pl.BlockSpec(memory_space=pltpu.SMEM)


def hbm_spec():
    return pl.BlockSpec(memory_space=pltpu.HBM)


def local_call(body, name, outs, in_specs, out_specs, scratch=(), cost=None):
    return pl.pallas_call(
        body,
        out_shape=outs,
        in_specs=in_specs,
        out_specs=out_specs,
        scratch_shapes=list(scratch),
        compiler_params=pltpu.CompilerParams(vmem_limit_bytes=VMEM_LIMIT),
        cost_estimate=cost,
        name=name,
    )


def from_ahead(block, axis):
    count = lax.axis_size(axis)
    return lax.ppermute(block, axis, [((i + 1) % count, i) for i in range(count)])


def per_device(eigvecs, links, op_dirs, op_moms, perams, pair_times, slot_counts):
    f32, bf16 = jnp.float32, jnp.bfloat16
    _, cells_x, cells_y, cells_z, colors, _, vectors = eigvecs.shape
    order = cells_z * colors * 2
    lines = cells_x * cells_y
    count_ops = op_dirs.shape[0]
    times, shares, groups = lax.axis_size("ta"), lax.axis_size("gx"), lax.axis_size("gy")
    levels = groups.bit_length() - 1
    own_ops = count_ops // groups
    own_rows = own_ops * 2 * vectors
    field = eigvecs.reshape(cells_x, cells_y, order, vectors)
    halo_x = from_ahead(field[0:1], "gx")
    halo_y = from_ahead(field, "gy")
    link_field = links[0].transpose(0, 1, 3, 5, 6, 4, 2).reshape(lines, 27, 2, cells_z)
    constants = line_constants(cells_z)
    outside, inside = halo_fields(cells_x, cells_y), local_fields(cells_x, cells_y)
    inputs = (field, link_field, op_dirs, op_moms) + constants
    held = [
        pltpu.SMEM(x.shape, x.dtype) if x.ndim == 1 else pltpu.VMEM(x.shape, x.dtype)
        for x in inputs
    ]
    matrices, local, left, phases = local_call(
        functools.partial(prepare_kernel, cells_x, cells_y),
        "prepare_lines",
        (
            jax.ShapeDtypeStruct((len(outside), 2 * order, order), bf16),
            jax.ShapeDtypeStruct((len(inside), 2 * order, vectors), f32),
            jax.ShapeDtypeStruct((2, vectors, lines * order), bf16),
            jax.ShapeDtypeStruct((count_ops, order, 2 * vectors), f32),
        ),
        [hbm_spec()] * len(inputs),
        (vmem_spec(),) * 4,
        held
        + [
            pltpu.VMEM((lines, 128, cells_z), f32),
            pltpu.SemaphoreType.DMA((len(inputs),)),
        ],
    )(*inputs)
    part_shapes = [
        jax.ShapeDtypeStruct((groups >> (b + 1), own_rows, vectors), f32)
        for b in range(levels)
    ] + [jax.ShapeDtypeStruct((1, own_rows, vectors), f32)]
    parts = local_call(
        functools.partial(margin_kernel, cells_x, cells_y, groups),
        "partial_margins",
        tuple(part_shapes),
        [vmem_spec()] * 6 + [hbm_spec()],
        (vmem_spec(),) * len(part_shapes),
        [
            pltpu.VMEM((7, lines, 2 * order, vectors), f32),
            pltpu.VMEM((count_ops, lines * order, 2 * vectors), bf16),
            pltpu.VMEM((4, vectors, lines * order), bf16),
            pltpu.SMEM((count_ops,), jnp.int32),
            pltpu.SemaphoreType.DMA,
        ],
    )(matrices, local, left, phases, halo_x, halo_y, op_dirs)
    received = []
    for b in range(levels):
        sent = parts[b]
        if b:
            sent = local_call(
                functools.partial(fold_kernel, b),
                "fold_groups",
                jax.ShapeDtypeStruct(sent.shape, f32),
                [vmem_spec()] * (1 + b),
                vmem_spec(),
            )(sent, *received)
        received.append(lax.ppermute(sent, "gy", [(i, i ^ (1 << b)) for i in range(groups)]))
    norm_factor = 1.0 / math.sqrt(3.0 * cells_x * shares * cells_y * groups * cells_z)
    direct = times * shares <= DIRECT_LIMIT and own_rows % shares == 0
    steps = shares if direct else 1
    rows = own_rows // steps
    chunk_shapes = [jax.ShapeDtypeStruct((rows, vectors), f32) for k in range(steps)]
    chunks = local_call(
        functools.partial(share_kernel, levels),
        "share_rows",
        tuple(chunk_shapes),
        [vmem_spec()] * (1 + levels),
        (vmem_spec(),) * steps,
    )(parts[levels], *received)
    if direct:
        arrived = [
            lax.ppermute(chunks[k], "gx", [(i, (i + k) % shares) for i in range(shares)])
            for k in range(1, shares)
        ]
        own = local_call(
            functools.partial(sum_kernel, norm_factor),
            "sum_shares",
            jax.ShapeDtypeStruct((rows, vectors), bf16),
            [vmem_spec()] * shares,
            vmem_spec(),
        )(chunks[0], *arrived)
        every = [own]
        for k in range(1, times * shares):
            step_t, step_x = k // shares, k % shares
            perm = []
            for t in range(times):
                for x in range(shares):
                    source = ((t + step_t) % times) * shares + (x + step_x) % shares
                    perm.append((source, t * shares + x))
            every.append(lax.ppermute(own, ("ta", "gx"), perm))
    else:
        own = (lax.psum(chunks[0], "gx") * norm_factor).astype(bf16)
        every = [lax.all_gather(own, "ta", axis=0, tiled=False)]
    margins, correlators = local_call(
        functools.partial(contract_kernel, times, shares, len(every)),
        "contraction",
        (
            jax.ShapeDtypeStruct((1, own_ops, 2, vectors, vectors), f32),
            jax.ShapeDtypeStruct((1, own_ops, 2), f32),
        ),
        [hbm_spec()] * 2 + [vmem_spec()] * (len(every) + 1),
        (vmem_spec(), smem_spec()),
        [
            pltpu.VMEM((times, own_rows, vectors), bf16),
            pltpu.VMEM((own_ops, 2 * vectors, 2 * vectors), bf16),
            pltpu.VMEM((own_ops, 2 * vectors, 2 * vectors), bf16),
            pltpu.SMEM((1, 2), jnp.int32),
            pltpu.SMEM((1,), jnp.int32),
            pltpu.SemaphoreType.DMA((2,)),
        ],
    )(pair_times, slot_counts, *every, perams[0])
    return (margins, correlators)


def solution(mesh):
    placed = (
        P("ta", "gx", "gy", None, None, None, None),
        P("ta", "gx", "gy", None, None, None, None, None),
        P(),
        P(),
        P(("ta", "gx"), None, None, None),
        P(("ta", "gx"), None),
        P(("ta", "gx")),
    )
    return jax.shard_map(
        per_device,
        mesh=mesh,
        in_specs=placed,
        out_specs=(P("ta", "gy", None, None, None), P(("ta", "gx"), "gy", None)),
        check_vma=False,
    )
```

time: 156 us -> 56.3 us (0.36)
  waiting for transfers between devices: 57 us -> 18.1 us
  between operations: 39.6 us -> 1.39 us
  matrix products: 21 us -> 0 us
  starting transfers between devices: 5.92 us -> 20.4 us
  local copies, waits for them, and re-layouts: 22.1 us -> 8.23 us
  Pallas kernels: 0 us -> 7.65 us
  blocking collectives: 5.83 us -> 0 us
  other arithmetic: 3.83 us -> 0 us
    psum x1 -> x0, waiting for transfers between devices: 33.7 us -> none  [per_device(): own_ops = lax.psum(shared, 'gx')]
    reduce_scatter x1 -> x0, waiting for transfers between devices: 23.3 us -> none  [per_device(): lax.psum_scatter(partial_sums, 'gy', scatter_dimension=0, tiled=True)]
    dot_general x40 -> x0, matrix products: 21 us -> none  [the longest x1 3.84 us: contract(): jnp.einsum('oab,sbc->osac', sink_imag, rows_real, preferred_element_type=...]
    ppermute x4 -> x14, waiting for transfers between devices: 0.01 us -> 18.1 us  [the longest x2 9.25 us: per_device(): lax.ppermute(sent, 'gy', [(i, i ^ 1 << b) for i in range(groups)])]
    ppermute x4 -> x14, starting transfers between devices: 5.84 us -> 20.4 us  [the longest x7 9.61 us: per_device(): every.append(lax.ppermute(own, ('ta', 'gx'), perm))]
    reshape x12 -> x0, local copies, waits for them, and re-layouts: 12.6 us -> none  [the longest x2 5.93 us: contract(): right_real = right_real.reshape(count_ops, order, order)]
    pallas_call x0 -> x6, Pallas kernels: none -> 7.65 us  [the longest x1 3.57 us: per_device(): local_call(functools.partial(prepare_kernel, cells_x, cells_y), 'prepare_...]
    all_gather x1 -> x0, blocking collectives: 5.83 us -> none  [per_device(): lax.all_gather(own_ops.astype(jnp.bfloat16)[None], 'ta', axis=0, tiled=True)]
  transfers between devices with their start and end apart: 6 -> 14, of which waited for: 2 -> 7; matrix products, arithmetic and copies ran while one was open for 5% -> 0% of each run, Pallas kernels for 0% -> 6%
where the time goes in v1:
time: 56.3 us; the launch traced here: 55.8 us
  starting transfers between devices  20.4 us (36%)
  waiting for transfers between devices  18.1 us (32%)
  local copies, waits for them, and re-layouts  8.23 us (15%)
  Pallas kernels  7.65 us (14%)
  between operations  1.39 us (2%)
    ppermute x7, starting transfers between devices, per_device(): every.append(lax.ppermute(own, ('ta', 'gx'), perm))  9.61 us
    ppermute x2, waiting for transfers between devices, per_device(): lax.ppermute(sent, 'gy', [(i, i ^ 1 << b) for i in range(groups)])  9.25 us
    unnamed x24, local copies, waits for them, and re-layouts  8.23 us
    ppermute x2, starting transfers between devices, from_ahead(): lax.ppermute(block, axis, [((i + 1) % count, i) for i in range(count)])  5.78 us
    ppermute x7, waiting for transfers between devices, per_device(): every.append(lax.ppermute(own, ('ta', 'gx'), perm))  4.87 us
    ppermute x3, waiting for transfers between devices, per_device(): lax.ppermute(chunks[k], 'gx', [(i, (i + k) % shares) for i in range(share...  4.02 us
    ppermute x3, starting transfers between devices, per_device(): lax.ppermute(chunks[k], 'gx', [(i, (i + k) % shares) for i in range(share...  3.87 us
    pallas_call x1, Pallas kernels, per_device(): local_call(functools.partial(prepare_kernel, cells_x, cells_y), 'prepare_...  3.57 us
  transfers between devices with their start and end apart: 14, of which 7 were waited for; matrix products, arithmetic and copies ran while one was open for 0% of the time, Pallas kernels for 6%

profile of v1, /device:TPU:0, one launch (start us, length us, event | category | flops | bytes accessed | tf_op | source)
XLA Modules:
  0.0 55.8 jit_solution(6055954928708369289)
XLA Ops:
  0.6 5.1 %collective-permute-start = (bf16[1,2,144,128]{3,2,1,0:T(8,128)(2,1)}, bf16[1,2,144,128]{3,2,1,0:T(8,128)(2,1)S(1)}, u32[]{:S(2)}, u32[]{:S(2)}) collective-permute-start(bf16[1,2,144,128]{3,2,1,0:T(8,128)(2,1)} %bitcast.8), channel_id=1, source_target_pairs={{4,0},{8,4},{12,8},{0,12},{5,1},{9,5},{13,9},{1,13},{6,2},{10,6},{... | collective-permute-start | bytes 221192 | tf_op jit(solution)/shard_map/ppermute | solution.py:361
  5.7 0.7 %collective-permute-start.1 = (bf16[1,2,144,128]{3,2,1,0:T(8,128)(2,1)}, bf16[1,2,144,128]{3,2,1,0:T(8,128)(2,1)S(1)}, u32[]{:S(2)}, u32[]{:S(2)}) collective-permute-start(bf16[1,2,144,128]{3,2,1,0:T(8,128)(2,1)} %bitcast.9), channel_id=1, source_target_pairs={{1,0},{2,1},{3,2},{0,3},{5,4},{6,5},{7,6},{4,7},{9,8},{10,9},{11,1... | collective-permute-start | bytes 221192 | tf_op jit(solution)/shard_map/ppermute | solution.py:361
  6.4 0.0 copy-start.1
  6.4 0.9 %copy-done.1 = bf16[3,128,144]{2,1,0:T(8,128)(2,1)S(1)} copy-done((bf16[3,128,144]{2,1,0:T(8,128)(2,1)S(1)}, bf16[3,128,144]{2,1,0:T(8,128)(2,1)}, u32[]{:S(2)}) %copy-start.1) | copy-done | bytes 110616
  7.3 0.0 copy-start.2
  7.3 0.9 %copy-done.2 = bf16[288,144]{1,0:T(8,128)(2,1)S(1)} copy-done((bf16[288,144]{1,0:T(8,128)(2,1)S(1)}, bf16[288,144]{1,0:T(8,128)(2,1)}, u32[]{:S(2)}) %copy-start.2) | copy-done | bytes 82968
  8.2 0.0 copy-start.3
  8.3 0.9 %copy-done.3 = bf16[288,144]{1,0:T(8,128)(2,1)S(1)} copy-done((bf16[288,144]{1,0:T(8,128)(2,1)S(1)}, bf16[288,144]{1,0:T(8,128)(2,1)}, u32[]{:S(2)}) %copy-start.3) | copy-done | bytes 82968
  9.2 0.9 %copy-done.4 = bf16[1,1,2,24,3,2,128]{6,5,4,3,2,1,0:T(2,128)(2,1)S(1)} copy-done((bf16[1,1,2,24,3,2,128]{6,5,4,3,2,1,0:T(2,128)(2,1)S(1)}, bf16[1,1,2,24,3,2,128]{6,5,4,3,2,1,0:T(2,128)(2,1)}, u32[]{:S(2)}) %copy-start.4) | copy-done | bytes 73752
  10.0 0.9 %copy-done.5 = bf16[288,24]{1,0:T(8,128)(2,1)S(1)} copy-done((bf16[288,24]{1,0:T(8,128)(2,1)S(1)}, bf16[288,24]{1,0:T(8,128)(2,1)}, u32[]{:S(2)}) %copy-start.5) | copy-done | bytes 13848
  10.9 0.9 %copy-done.6 = bf16[288,128]{1,0:T(8,128)(2,1)S(1)} copy-done((bf16[288,128]{1,0:T(8,128)(2,1)S(1)}, bf16[288,128]{1,0:T(8,128)(2,1)}, u32[]{:S(2)}) %copy-start.6) | copy-done | bytes 73752
  11.8 0.8 %copy-done.7 = bf16[144,36]{1,0:T(8,128)(2,1)S(1)} copy-done((bf16[144,36]{1,0:T(8,128)(2,1)S(1)}, bf16[144,36]{1,0:T(8,128)(2,1)}, u32[]{:S(2)}) %copy-start.7) | copy-done | bytes 10392
  12.6 0.7 %copy-done.8 = bf16[1,1,2,24,3,2,3,3]{3,5,7,6,4,2,1,0:T(2,128)(2,1)S(1)} copy-done((bf16[1,1,2,24,3,2,3,3]{3,5,7,6,4,2,1,0:T(2,128)(2,1)S(1)}, bf16[1,1,2,24,3,2,3,3]{3,5,7,6,4,2,1,0:T(2,128)(2,1)}, u32[]{:S(2)}) %copy-start.8) | copy-done | bytes 5208
  13.3 0.7 %copy-done.9 = s32[8]{0:T(128)S(1)} copy-done((s32[8]{0:T(128)S(1)}, s32[8]{0:T(128)}, u32[]{:S(2)}) %copy-start.9) | copy-done | bytes 56
  14.0 0.7 %copy-done.10 = s32[8]{0:T(128)S(1)} copy-done((s32[8]{0:T(128)S(1)}, s32[8]{0:T(128)}, u32[]{:S(2)}) %copy-start.10) | copy-done | bytes 56
  14.6 3.6 %prepare_lines.1 = (bf16[3,288,144]{2,1,0:T(8,128)(2,1)S(1)}, f32[11,288,128]{2,1,0:T(8,128)S(1)}, bf16[2,128,288]{2,1,0:T(8,128)(2,1)S(1)}, f32[8,144,256]{2,1,0:T(8,128)S(1)}) custom-call(bf16[1,2,144,128]{3,2,1,0:T(8,128)(2,1)S(1)} %bitcast.10, bf16[2,27,2,24]{3,2,1,0:T(2,128)(2,1)S(1)} %bitcast.11, s32[8]{0:T(128)S(1)} %copy-done.9, s32[8]{0:T(128)S(1)} %copy-done.10, ...), custom_call_target="tpu_custom_call" | custom-call | tf_op jit(solution)/shard_map/prepare_lines/pallas_call | solution.py:385
  18.2 0.0 collective-permute-done.refs_4_
  18.2 0.0 collective-permute-done.1.refs_5_
  18.2 1.4 %partial_margins.1 = (f32[2,512,128]{2,1,0:T(8,128)S(1)}, f32[1,512,128]{2,1,0:T(8,128)S(1)}, f32[1,512,128]{2,1,0:T(8,128)S(1)}) custom-call(bf16[3,288,144]{2,1,0:T(8,128)(2,1)S(1)} %get-tuple-element.13.refs_0_, f32[11,288,128]{2,1,0:T(8,128)S(1)} %get-tuple-element.14.refs_1_, bf16[2,128,288]{2,1,0:T(8,128)(2,1)S(1)} %get-tuple-element.15.refs_2_, ...), custom_call_target="tpu_custom_call" | custom-call | tf_op jit(solution)/shard_map/partial_margins/pallas_call | solution.py:406
  19.6 0.0 copy-start
  19.6 0.0 copy-start.11
  19.6 0.1 collective-permute-start.2
  19.7 1.9 %collective-permute-done.2.refs_1_ = f32[2,512,128]{2,1,0:T(8,128)S(1)} collective-permute-done((f32[2,512,128]{2,1,0:T(8,128)S(1)}, f32[2,512,128]{2,1,0:T(8,128)S(1)}, u32[]{:S(2)}, u32[]{:S(2)}) %collective-permute-start.2) | collective-permute-done | bytes 524320 | tf_op jit(solution)/shard_map/ppermute | solution.py:431
  21.6 1.1 %collective-permute-start.3 = (f32[1,512,128]{2,1,0:T(8,128)S(1)}, f32[1,512,128]{2,1,0:T(8,128)S(1)}, u32[]{:S(2)}, u32[]{:S(2)}) collective-permute-start(f32[1,512,128]{2,1,0:T(8,128)S(1)} %fold_groups.1), channel_id=1, source_target_pairs={{0,2},{1,3},{2,0},{3,1},{4,6},{5,7},{6,4},{7,5},{8,10},{9,11},{10,... | collective-permute-start | bytes 786440 | tf_op jit(solution)/shard_map/ppermute | solution.py:431
  22.7 7.4 %collective-permute-done.3.refs_2_ = f32[1,512,128]{2,1,0:T(8,128)S(1)} collective-permute-done((f32[1,512,128]{2,1,0:T(8,128)S(1)}, f32[1,512,128]{2,1,0:T(8,128)S(1)}, u32[]{:S(2)}, u32[]{:S(2)}) %collective-permute-start.3) | collective-permute-done | bytes 262176 | tf_op jit(solution)/shard_map/ppermute | solution.py:431
  30.1 0.1 collective-permute-start.4
  30.2 1.0 %collective-permute-start.5 = (f32[128,128]{1,0:T(8,128)S(1)}, f32[128,128]{1,0:T(8,128)S(1)}, u32[]{:S(2)}, u32[]{:S(2)}) collective-permute-start(f32[128,128]{1,0:T(8,128)S(1)} %get-tuple-element.22), channel_id=1, source_target_pairs={{0,8},{4,12},{8,0},{12,4},{1,9},{5,13},{9,1},{13,5},{2,10},{6,14},... | collective-permute-start | bytes 196616 | tf_op jit(solution)/shard_map/ppermute | solution.py:446
  31.2 2.8 %collective-permute-start.6 = (f32[128,128]{1,0:T(8,128)S(1)}, f32[128,128]{1,0:T(8,128)S(1)}, u32[]{:S(2)}, u32[]{:S(2)}) collective-permute-start(f32[128,128]{1,0:T(8,128)S(1)} %get-tuple-element.23), channel_id=1, source_target_pairs={{0,12},{4,0},{8,4},{12,8},{1,13},{5,1},{9,5},{13,9},{2,14},{6,2},{... | collective-permute-start | bytes 196616 | tf_op jit(solution)/shard_map/ppermute | solution.py:446
  34.0 2.7 %collective-permute-done.4.refs_1_ = f32[128,128]{1,0:T(8,128)S(1)} collective-permute-done((f32[128,128]{1,0:T(8,128)S(1)}, f32[128,128]{1,0:T(8,128)S(1)}, u32[]{:S(2)}, u32[]{:S(2)}) %collective-permute-start.4) | collective-permute-done | bytes 65568 | tf_op jit(solution)/shard_map/ppermute | solution.py:446
  36.7 1.3 %collective-permute-done.5.refs_2_ = f32[128,128]{1,0:T(8,128)S(1)} collective-permute-done((f32[128,128]{1,0:T(8,128)S(1)}, f32[128,128]{1,0:T(8,128)S(1)}, u32[]{:S(2)}, u32[]{:S(2)}) %collective-permute-start.5) | collective-permute-done | bytes 65568 | tf_op jit(solution)/shard_map/ppermute | solution.py:446
  38.0 0.0 collective-permute-done.6.refs_3_
  38.0 1.6 %collective-permute-start.10 = (bf16[128,128]{1,0:T(8,128)(2,1)S(1)}, bf16[128,128]{1,0:T(8,128)(2,1)S(1)}, u32[]{:S(2)}, u32[]{:S(2)}) collective-permute-start(bf16[128,128]{1,0:T(8,128)(2,1)S(1)} %sum_shares.1.refs_2_), channel_id=1, source_target_pairs={{16,0},{20,4},{24,8},{28,12},{0,16},{4,20},{8,24},{12,28},{17,1},{... | collective-permute-start | bytes 98312 | tf_op jit(solution)/shard_map/ppermute | solution.py:464
  39.6 2.0 %collective-permute-start.11 = (bf16[128,128]{1,0:T(8,128)(2,1)S(1)}, bf16[128,128]{1,0:T(8,128)(2,1)S(1)}, u32[]{:S(2)}, u32[]{:S(2)}) collective-permute-start(bf16[128,128]{1,0:T(8,128)(2,1)S(1)} %sum_shares.1.refs_2_), channel_id=1, source_target_pairs={{20,0},{24,4},{28,8},{16,12},{4,16},{8,20},{12,24},{0,28},{21,1},{... | collective-permute-start | bytes 98312 | tf_op jit(solution)/shard_map/ppermute | solution.py:464
  41.6 1.7 %collective-permute-start.12 = (bf16[128,128]{1,0:T(8,128)(2,1)S(1)}, bf16[128,128]{1,0:T(8,128)(2,1)S(1)}, u32[]{:S(2)}, u32[]{:S(2)}) collective-permute-start(bf16[128,128]{1,0:T(8,128)(2,1)S(1)} %sum_shares.1.refs_2_), channel_id=1, source_target_pairs={{24,0},{28,4},{16,8},{20,12},{8,16},{12,20},{0,24},{4,28},{25,1},{... | collective-permute-start | bytes 98312 | tf_op jit(solution)/shard_map/ppermute | solution.py:464
  43.3 0.0 collective-permute-start.13
  43.3 3.8 %collective-permute-start.7 = (bf16[128,128]{1,0:T(8,128)(2,1)S(1)}, bf16[128,128]{1,0:T(8,128)(2,1)S(1)}, u32[]{:S(2)}, u32[]{:S(2)}) collective-permute-start(bf16[128,128]{1,0:T(8,128)(2,1)S(1)} %sum_shares.1.refs_2_), channel_id=1, source_target_pairs={{4,0},{8,4},{12,8},{0,12},{20,16},{24,20},{28,24},{16,28},{5,1},{9... | collective-permute-start | bytes 98312 | tf_op jit(solution)/shard_map/ppermute | solution.py:464
  47.1 0.0 collective-permute-done.10.refs_6_
  47.1 0.4 collective-permute-start.8
  47.5 0.0 collective-permute-done.11.refs_7_
  47.5 0.2 collective-permute-start.9
  48.3 0.0 collective-permute-done.12.refs_8_
  48.3 1.6 %collective-permute-done.13.refs_9_ = bf16[128,128]{1,0:T(8,128)(2,1)S(1)} collective-permute-done((bf16[128,128]{1,0:T(8,128)(2,1)S(1)}, bf16[128,128]{1,0:T(8,128)(2,1)S(1)}, u32[]{:S(2)}, u32[]{:S(2)}) %collective-permute-start.13) | collective-permute-done | bytes 32800 | tf_op jit(solution)/shard_map/ppermute | solution.py:464
  49.9 0.0 collective-permute-done.7.refs_3_
  49.9 2.0 %collective-permute-done.8.refs_4_ = bf16[128,128]{1,0:T(8,128)(2,1)S(1)} collective-permute-done((bf16[128,128]{1,0:T(8,128)(2,1)S(1)}, bf16[128,128]{1,0:T(8,128)(2,1)S(1)}, u32[]{:S(2)}, u32[]{:S(2)}) %collective-permute-start.8) | collective-permute-done | bytes 32800 | tf_op jit(solution)/shard_map/ppermute | solution.py:464
  51.9 1.3 %collective-permute-done.9.refs_5_ = bf16[128,128]{1,0:T(8,128)(2,1)S(1)} collective-permute-done((bf16[128,128]{1,0:T(8,128)(2,1)S(1)}, bf16[128,128]{1,0:T(8,128)(2,1)S(1)}, u32[]{:S(2)}, u32[]{:S(2)}) %collective-permute-start.9) | collective-permute-done | bytes 32800 | tf_op jit(solution)/shard_map/ppermute | solution.py:464
  53.2 0.0 copy-done
  53.2 0.0 copy-done.11
  53.2 2.6 %contraction.1 = (f32[1,2,2,128,128]{4,3,2,1,0:T(8,128)}, f32[1,2,2]{2,1,0:T(2,128)}) custom-call(s32[1,2]{1,0:T(1,128)S(1)} %copy-done.11, s32[1]{0:T(128)S(6)} %copy.15.refs_1_, bf16[128,128]{1,0:T(8,128)(2,1)S(1)} %sum_shares.1.refs_2_, bf16[128,128]{1,0:T(8,128)(2,1)S(1)} %collective-permute-done.7.refs_3_, ...), custom_call_target="tpu_custom_call" | custom-call | tf_op jit(solution)/shard_map/contraction/pallas_call | solution.py:468
  (10 shorter events, 0.1 us)
Async XLA Ops:
  0.6 17.6 %collective-permute-start = (bf16[1,2,144,128]{3,2,1,0:T(8,128)(2,1)}, bf16[1,2,144,128]{3,2,1,0:T(8,128)(2,1)S(1)}, u32[]{:S(2)}, u32[]{:S(2)}) collective-permute-start(bf16[1,2,144,128]{3,2,1,0:T(8,128)(2,1)} %bitcast.8), channel_id=1, source_target_pairs={{4,0},{8,4},{12,8},{0,12},{5,1},{9,5},{13,9},{1,13},{6,2},{10,6},{... | collective-permute-start | bytes 221192 | tf_op jit(solution)/shard_map/ppermute | solution.py:361
  5.7 12.5 %collective-permute-start.1 = (bf16[1,2,144,128]{3,2,1,0:T(8,128)(2,1)}, bf16[1,2,144,128]{3,2,1,0:T(8,128)(2,1)S(1)}, u32[]{:S(2)}, u32[]{:S(2)}) collective-permute-start(bf16[1,2,144,128]{3,2,1,0:T(8,128)(2,1)} %bitcast.9), channel_id=1, source_target_pairs={{1,0},{2,1},{3,2},{0,3},{5,4},{6,5},{7,6},{4,7},{9,8},{10,9},{11,1... | collective-permute-start | bytes 221192 | tf_op jit(solution)/shard_map/ppermute | solution.py:361
  6.4 0.9 %copy-start.1 = (bf16[3,128,144]{2,1,0:T(8,128)(2,1)S(1)}, bf16[3,128,144]{2,1,0:T(8,128)(2,1)}, u32[]{:S(2)}) copy-start(bf16[3,128,144]{2,1,0:T(8,128)(2,1)} %constant.14.clone.refs_6_) | copy-start | bytes 331780
  7.3 0.9 %copy-start.2 = (bf16[288,144]{1,0:T(8,128)(2,1)S(1)}, bf16[288,144]{1,0:T(8,128)(2,1)}, u32[]{:S(2)}) copy-start(bf16[288,144]{1,0:T(8,128)(2,1)} %constant.15.clone.refs_7_) | copy-start | bytes 248836
  8.2 0.9 %copy-start.3 = (bf16[288,144]{1,0:T(8,128)(2,1)S(1)}, bf16[288,144]{1,0:T(8,128)(2,1)}, u32[]{:S(2)}) copy-start(bf16[288,144]{1,0:T(8,128)(2,1)} %constant.16.clone.refs_8_) | copy-start | bytes 248836
  9.2 0.9 %copy-start.4 = (bf16[1,1,2,24,3,2,128]{6,5,4,3,2,1,0:T(2,128)(2,1)S(1)}, bf16[1,1,2,24,3,2,128]{6,5,4,3,2,1,0:T(2,128)(2,1)}, u32[]{:S(2)}) copy-start(bf16[1,1,2,24,3,2,128]{6,5,4,3,2,1,0:T(2,128)(2,1)} %param.13) | copy-start | bytes 221188
  10.0 0.9 %copy-start.5 = (bf16[288,24]{1,0:T(8,128)(2,1)S(1)}, bf16[288,24]{1,0:T(8,128)(2,1)}, u32[]{:S(2)}) copy-start(bf16[288,24]{1,0:T(8,128)(2,1)} %constant.12.clone.refs_4_) | copy-start | bytes 41476
  10.9 0.9 %copy-start.6 = (bf16[288,128]{1,0:T(8,128)(2,1)S(1)}, bf16[288,128]{1,0:T(8,128)(2,1)}, u32[]{:S(2)}) copy-start(bf16[288,128]{1,0:T(8,128)(2,1)} %constant.13.clone.refs_5_) | copy-start | bytes 221188
  11.8 0.8 %copy-start.7 = (bf16[144,36]{1,0:T(8,128)(2,1)S(1)}, bf16[144,36]{1,0:T(8,128)(2,1)}, u32[]{:S(2)}) copy-start(bf16[144,36]{1,0:T(8,128)(2,1)} %constant.17.clone.refs_9_) | copy-start | bytes 31108
  12.6 0.7 %copy-start.8 = (bf16[1,1,2,24,3,2,3,3]{3,5,7,6,4,2,1,0:T(2,128)(2,1)S(1)}, bf16[1,1,2,24,3,2,3,3]{3,5,7,6,4,2,1,0:T(2,128)(2,1)}, u32[]{:S(2)}) copy-start(bf16[1,1,2,24,3,2,3,3]{3,5,7,6,4,2,1,0:T(2,128)(2,1)} %param.14) | copy-start | bytes 15556
  13.3 0.7 %copy-start.9 = (s32[8]{0:T(128)S(1)}, s32[8]{0:T(128)}, u32[]{:S(2)}) copy-start(s32[8]{0:T(128)} %refs_6_.2) | copy-start | bytes 100
  14.0 0.7 %copy-start.10 = (s32[8]{0:T(128)S(1)}, s32[8]{0:T(128)}, u32[]{:S(2)}) copy-start(s32[8]{0:T(128)} %refs_3_.1) | copy-start | bytes 100
  19.6 33.6 %copy-start = (bf16[1,2,512,512]{3,2,1,0:T(8,128)(2,1)S(1)}, bf16[1,2,512,512]{3,2,1,0:T(8,128)(2,1)}, u32[]{:S(2)}) copy-start(bf16[1,2,512,512]{3,2,1,0:T(8,128)(2,1)} %param.17) | copy-start | bytes 3145732
  19.6 33.5 %copy-start.11 = (s32[1,2]{1,0:T(1,128)S(1)}, s32[1,2]{1,0:T(1,128)}, u32[]{:S(2)}) copy-start(s32[1,2]{1,0:T(1,128)} %refs_0_.1) | copy-start | bytes 28
  19.6 2.0 %collective-permute-start.2 = (f32[2,512,128]{2,1,0:T(8,128)S(1)}, f32[2,512,128]{2,1,0:T(8,128)S(1)}, u32[]{:S(2)}, u32[]{:S(2)}) collective-permute-start(f32[2,512,128]{2,1,0:T(8,128)S(1)} %get-tuple-element.18), channel_id=1, source_target_pairs={{0,1},{1,0},{2,3},{3,2},{4,5},{5,4},{6,7},{7,6},{8,9},{9,8},{10,11... | collective-permute-start | bytes 1572872 | tf_op jit(solution)/shard_map/ppermute | solution.py:431
  21.6 8.4 %collective-permute-start.3 = (f32[1,512,128]{2,1,0:T(8,128)S(1)}, f32[1,512,128]{2,1,0:T(8,128)S(1)}, u32[]{:S(2)}, u32[]{:S(2)}) collective-permute-start(f32[1,512,128]{2,1,0:T(8,128)S(1)} %fold_groups.1), channel_id=1, source_target_pairs={{0,2},{1,3},{2,0},{3,1},{4,6},{5,7},{6,4},{7,5},{8,10},{9,11},{10,... | collective-permute-start | bytes 786440 | tf_op jit(solution)/shard_map/ppermute | solution.py:431
  30.1 6.6 %collective-permute-start.4 = (f32[128,128]{1,0:T(8,128)S(1)}, f32[128,128]{1,0:T(8,128)S(1)}, u32[]{:S(2)}, u32[]{:S(2)}) collective-permute-start(f32[128,128]{1,0:T(8,128)S(1)} %get-tuple-element.21), channel_id=1, source_target_pairs={{0,4},{4,8},{8,12},{12,0},{1,5},{5,9},{9,13},{13,1},{2,6},{6,10},{... | collective-permute-start | bytes 196616 | tf_op jit(solution)/shard_map/ppermute | solution.py:446
  30.2 7.8 %collective-permute-start.5 = (f32[128,128]{1,0:T(8,128)S(1)}, f32[128,128]{1,0:T(8,128)S(1)}, u32[]{:S(2)}, u32[]{:S(2)}) collective-permute-start(f32[128,128]{1,0:T(8,128)S(1)} %get-tuple-element.22), channel_id=1, source_target_pairs={{0,8},{4,12},{8,0},{12,4},{1,9},{5,13},{9,1},{13,5},{2,10},{6,14},... | collective-permute-start | bytes 196616 | tf_op jit(solution)/shard_map/ppermute | solution.py:446
  31.2 6.8 %collective-permute-start.6 = (f32[128,128]{1,0:T(8,128)S(1)}, f32[128,128]{1,0:T(8,128)S(1)}, u32[]{:S(2)}, u32[]{:S(2)}) collective-permute-start(f32[128,128]{1,0:T(8,128)S(1)} %get-tuple-element.23), channel_id=1, source_target_pairs={{0,12},{4,0},{8,4},{12,8},{1,13},{5,1},{9,5},{13,9},{2,14},{6,2},{... | collective-permute-start | bytes 196616 | tf_op jit(solution)/shard_map/ppermute | solution.py:446
  38.0 9.0 %collective-permute-start.10 = (bf16[128,128]{1,0:T(8,128)(2,1)S(1)}, bf16[128,128]{1,0:T(8,128)(2,1)S(1)}, u32[]{:S(2)}, u32[]{:S(2)}) collective-permute-start(bf16[128,128]{1,0:T(8,128)(2,1)S(1)} %sum_shares.1.refs_2_), channel_id=1, source_target_pairs={{16,0},{20,4},{24,8},{28,12},{0,16},{4,20},{8,24},{12,28},{17,1},{... | collective-permute-start | bytes 98312 | tf_op jit(solution)/shard_map/ppermute | solution.py:464
  39.6 7.9 %collective-permute-start.11 = (bf16[128,128]{1,0:T(8,128)(2,1)S(1)}, bf16[128,128]{1,0:T(8,128)(2,1)S(1)}, u32[]{:S(2)}, u32[]{:S(2)}) collective-permute-start(bf16[128,128]{1,0:T(8,128)(2,1)S(1)} %sum_shares.1.refs_2_), channel_id=1, source_target_pairs={{20,0},{24,4},{28,8},{16,12},{4,16},{8,20},{12,24},{0,28},{21,1},{... | collective-permute-start | bytes 98312 | tf_op jit(solution)/shard_map/ppermute | solution.py:464
  41.6 6.7 %collective-permute-start.12 = (bf16[128,128]{1,0:T(8,128)(2,1)S(1)}, bf16[128,128]{1,0:T(8,128)(2,1)S(1)}, u32[]{:S(2)}, u32[]{:S(2)}) collective-permute-start(bf16[128,128]{1,0:T(8,128)(2,1)S(1)} %sum_shares.1.refs_2_), channel_id=1, source_target_pairs={{24,0},{28,4},{16,8},{20,12},{8,16},{12,20},{0,24},{4,28},{25,1},{... | collective-permute-start | bytes 98312 | tf_op jit(solution)/shard_map/ppermute | solution.py:464
  43.3 6.6 %collective-permute-start.13 = (bf16[128,128]{1,0:T(8,128)(2,1)S(1)}, bf16[128,128]{1,0:T(8,128)(2,1)S(1)}, u32[]{:S(2)}, u32[]{:S(2)}) collective-permute-start(bf16[128,128]{1,0:T(8,128)(2,1)S(1)} %sum_shares.1.refs_2_), channel_id=1, source_target_pairs={{28,0},{16,4},{20,8},{24,12},{12,16},{0,20},{4,24},{8,28},{29,1},{... | collective-permute-start | bytes 98312 | tf_op jit(solution)/shard_map/ppermute | solution.py:464
  43.3 6.6 %collective-permute-start.7 = (bf16[128,128]{1,0:T(8,128)(2,1)S(1)}, bf16[128,128]{1,0:T(8,128)(2,1)S(1)}, u32[]{:S(2)}, u32[]{:S(2)}) collective-permute-start(bf16[128,128]{1,0:T(8,128)(2,1)S(1)} %sum_shares.1.refs_2_), channel_id=1, source_target_pairs={{4,0},{8,4},{12,8},{0,12},{20,16},{24,20},{28,24},{16,28},{5,1},{9... | collective-permute-start | bytes 98312 | tf_op jit(solution)/shard_map/ppermute | solution.py:464
  47.1 4.8 %collective-permute-start.8 = (bf16[128,128]{1,0:T(8,128)(2,1)S(1)}, bf16[128,128]{1,0:T(8,128)(2,1)S(1)}, u32[]{:S(2)}, u32[]{:S(2)}) collective-permute-start(bf16[128,128]{1,0:T(8,128)(2,1)S(1)} %sum_shares.1.refs_2_), channel_id=1, source_target_pairs={{8,0},{12,4},{0,8},{4,12},{24,16},{28,20},{16,24},{20,28},{9,1},{1... | collective-permute-start | bytes 98312 | tf_op jit(solution)/shard_map/ppermute | solution.py:464
  47.5 5.7 %collective-permute-start.9 = (bf16[128,128]{1,0:T(8,128)(2,1)S(1)}, bf16[128,128]{1,0:T(8,128)(2,1)S(1)}, u32[]{:S(2)}, u32[]{:S(2)}) collective-permute-start(bf16[128,128]{1,0:T(8,128)(2,1)S(1)} %sum_shares.1.refs_2_), channel_id=1, source_target_pairs={{12,0},{0,4},{4,8},{8,12},{28,16},{16,20},{20,24},{24,28},{13,1},{... | collective-permute-start | bytes 98312 | tf_op jit(solution)/shard_map/ppermute | solution.py:464

commit v2 on v1

v2 whole, which is shorter than its diff:
```python
import functools
import math

import jax
import jax.numpy as jnp
import numpy as np
from jax import lax
from jax.experimental import pallas as pl
from jax.experimental.pallas import tpu as pltpu
from jax.sharding import PartitionSpec as P

VMEM_LIMIT = 24 * 1024 * 1024
MOMENTA = 3
LINK_COLS = 54
DIRECT_LIMIT = 8


def wave_constants(cells_z):
    z_row = np.arange(3 * cells_z) // 3
    columns = []
    for ahead in range(2):
        for momentum in range(MOMENTA):
            angle = 2.0 * math.pi * momentum * ((z_row + ahead) % cells_z) / cells_z
            columns.append(np.cos(angle))
            columns.append(np.sin(angle))
    left = np.stack(columns, axis=1).astype(np.float32)
    terms = []
    for _ in range(3):
        term = left.astype(jnp.bfloat16).astype(np.float32)
        terms.append(term)
        left = left - term
    return jnp.asarray(np.concatenate(terms, axis=1), jnp.bfloat16)


def iota(shape, axis):
    return lax.broadcasted_iota(jnp.int32, shape, axis)


def third(x):
    return (x * 21846) >> 16


def one_hot(condition):
    return condition.astype(jnp.float32).astype(jnp.bfloat16)


def planar_order(order):
    row, col = iota((order, order), 0), iota((order, order), 1)
    half = order // 2
    source = jnp.where(row < half, 2 * row, 2 * (row - half) + 1)
    return one_hot(col == source)


def side_by_side(planar):
    half = planar.shape[0] // 2
    return jnp.concatenate([planar[:half], planar[half:]], axis=1).astype(jnp.bfloat16)


def transport(matrix, pair, sign):
    half, vectors = matrix.shape[0] // 2, pair.shape[1] // 2
    parts = jnp.dot(matrix, pair, preferred_element_type=jnp.float32)
    real, imag = parts[:half], parts[half:]
    if sign > 0:
        return jnp.concatenate(
            [real[:, :vectors] - imag[:, vectors:], real[:, vectors:] + imag[:, :vectors]], axis=0
        )
    return jnp.concatenate(
        [real[:, :vectors] + imag[:, vectors:], real[:, vectors:] - imag[:, :vectors]], axis=0
    )


def halo_fields(cells_x, cells_y):
    pairs = [(0, (cells_x - 1) * cells_y + y) for y in range(cells_y)]
    return pairs + [(1, x * cells_y + cells_y - 1) for x in range(cells_x)]


def local_fields(cells_x, cells_y):
    lines = cells_x * cells_y
    outside = halo_fields(cells_x, cells_y)
    every = [(code, line) for code in range(7) for line in range(lines)]
    return [pair for pair in every if pair not in outside]


def prepare_kernel(cells_x, cells_y, *refs):
    inputs, refs = refs[:5], refs[5:]
    matrix_ref, local_ref, left_ref, phase_ref = refs[:4]
    held, link_rows_ref, sems = refs[4:9], refs[9], refs[10]
    copies = [
        pltpu.make_async_copy(src, dst, sems.at[k])
        for k, (src, dst) in enumerate(zip(inputs, held))
    ]
    for copy in copies:
        copy.start()
    v_ref, link_ref, dirs_ref, moms_ref, waves_ref = held
    f32, bf16 = jnp.float32, jnp.bfloat16
    order, vectors = v_ref.shape[2], v_ref.shape[3]
    half, cells_z = order // 2, order // 6
    lines = cells_x * cells_y
    spread = one_hot(third(iota((half, cells_z), 0)) == iota((half, cells_z), 1))
    row, col = iota((half, LINK_COLS), 0), iota((half, LINK_COLS), 1)
    row_color = row - 3 * third(row)
    pair_at = third(col >> 1)
    col_in, col_out = (col >> 1) - 3 * pair_at, pair_at - 3 * third(pair_at)
    pick = [(row_color == col_out).astype(f32), (row_color == col_in).astype(f32)]
    wide = (LINK_COLS, 6 * 128)
    row, col = iota(wide, 0), iota(wide, 1)
    block, place = col >> 7, col & 127
    color = place - 3 * third(place)
    pair_at = third(row >> 1)
    row_in, row_out = (row >> 1) - 3 * pair_at, pair_at - 3 * third(pair_at)
    fits = 2 * third(pair_at) + (row & 1) == block
    expand = [one_hot(fits & (row_in == color)), one_hot(fits & (row_out == color))]
    row, col = iota((half, 128), 0), iota((half, 128), 1)
    near = ((third(row) == third(col)) & (col < half)).astype(f32)
    planar = planar_order(order)
    for copy in copies:
        copy.wait()
    for line in range(lines):
        for k in range(LINK_COLS // 2):
            link_rows_ref[line, 2 * k : 2 * k + 2] = link_ref[line, k].astype(f32)
    outside = halo_fields(cells_x, cells_y)
    inside = local_fields(cells_x, cells_y)
    ordered = []
    for line in range(lines):
        here = jnp.dot(
            planar, v_ref[line // cells_y, line % cells_y], preferred_element_type=f32
        )
        ordered.append(here)
        local_ref[inside.index((6, line))] = here
    for line in range(lines):
        here = ordered[line]
        ahead_z = jnp.concatenate(
            [here[3:half], here[:3], here[half + 3 :], here[half : half + 3]], axis=0
        )
        columns = slice(line * order, (line + 1) * order)
        left_ref[0, :, columns] = here.T.astype(bf16)
        left_ref[1, :, columns] = ahead_z.T.astype(bf16)
        seen = lax.dot_general(
            spread,
            link_rows_ref[line].astype(bf16),
            (((1,), (1,)), ((), ())),
            preferred_element_type=f32,
        )
        pair = side_by_side(here)
        for way in range(2):
            blocks = jnp.dot(
                (seen * pick[way]).astype(bf16), expand[way], preferred_element_type=f32
            )
            for d in range(3):
                matrix = jnp.concatenate(
                    [
                        blocks[:, 256 * d : 256 * d + 128] * near,
                        blocks[:, 256 * d + 128 : 256 * d + 256] * near,
                    ],
                    axis=0,
                ).astype(bf16)
                if way == 1:
                    carried = transport(matrix[:, :half], pair, -1)
                    local_ref[inside.index((3 + d, line))] = carried.astype(bf16).astype(f32)
                elif (d, line) in outside:
                    matrix_ref[outside.index((d, line))] = matrix
                else:
                    ahead = ahead_z if d == 2 else ordered[line + (cells_y if d == 0 else 1)]
                    local_ref[inside.index((d, line))] = transport(
                        matrix[:, :half], side_by_side(ahead), 1
                    )
    wave_cols = waves_ref.shape[1]
    per_term = wave_cols // 3
    row, col = iota((wave_cols, 2 * vectors), 0), iota((wave_cols, 2 * vectors), 1)
    term = (row >= per_term).astype(jnp.int32) + (row >= 2 * per_term).astype(jnp.int32)
    wave_at = row - per_term * term - (col >= vectors).astype(jnp.int32)
    for o in range(phase_ref.shape[0]):
        column = 2 * (jnp.where(dirs_ref[o] == 5, MOMENTA, 0) + moms_ref[o])
        phase_ref[o] = jnp.dot(
            waves_ref[...], one_hot(wave_at == column), preferred_element_type=f32
        )


def low_bit(j):
    return (j & -j).bit_length() - 1


def margin_kernel(cells_x, cells_y, groups, *refs):
    matrix_ref, local_ref, left_ref, phase_ref, halo_x_ref, halo_y_ref, dirs_hbm = refs[:7]
    levels = groups.bit_length() - 1
    out_refs = refs[7 : 8 + levels]
    field_ref, side_ref, dirs_ref, sem = refs[8 + levels :]
    f32, bf16 = jnp.float32, jnp.bfloat16
    copy = pltpu.make_async_copy(dirs_hbm, dirs_ref, sem)
    copy.start()
    lines = cells_x * cells_y
    order, vectors = halo_x_ref.shape[2], halo_x_ref.shape[3]
    half = order // 2
    planar = planar_order(order)
    side_ref[0] = left_ref[0]
    side_ref[3] = left_ref[1]
    outside = halo_fields(cells_x, cells_y)
    for d in range(2):
        for line in range(lines):
            x, y = line // cells_y, line % cells_y
            columns = slice(line * order, (line + 1) * order)
            if (d, line) not in outside:
                ahead = line + (cells_y if d == 0 else 1)
                side_ref[1 + d, :, columns] = left_ref[0, :, ahead * order : (ahead + 1) * order]
                continue
            halo = halo_x_ref[0, y] if d == 0 else halo_y_ref[x, 0]
            ahead = jnp.dot(planar, halo, preferred_element_type=f32)
            side_ref[1 + d, :, columns] = ahead.T.astype(bf16)
            matrix = matrix_ref[outside.index((d, line))]
            field_ref[d, line] = transport(matrix[:, :half], side_by_side(ahead), 1)
    for k, (code, line) in enumerate(local_fields(cells_x, cells_y)):
        field_ref[code, line] = local_ref[k]
    copy.wait()
    count_ops = dirs_ref.shape[0]
    own_ops = count_ops // groups
    me = lax.axis_index("gy")
    for j in range(groups):
        for i in range(own_ops):
            o = (me ^ j) * own_ops + i
            code = dirs_ref[o]
            side = jnp.where((code >= 3) & (code < 6), code - 2, 0)
            cosine = phase_ref[o, :, 0:vectors]
            sine = phase_ref[o, :, vectors : 2 * vectors]
            pairs = []
            for line in range(lines):
                real, imag = field_ref[code, line, 0:half], field_ref[code, line, half:order]
                turned_r, turned_i = cosine * real - sine * imag, sine * real + cosine * imag
                pairs.append(jnp.concatenate([turned_r, turned_i], axis=1))
                pairs.append(jnp.concatenate([turned_i, -turned_r], axis=1))
            product = jnp.dot(
                side_ref[side],
                jnp.concatenate(pairs, axis=0).astype(bf16),
                preferred_element_type=f32,
            )
            level = levels if j == 0 else low_bit(j)
            out_ref = out_refs[level]
            place = 0 if j == 0 else j >> (level + 1)
            first = 2 * i * vectors
            out_ref[place, first : first + vectors] = product[:, :vectors]
            out_ref[place, first + vectors : first + 2 * vectors] = product[:, vectors:]


def fold_kernel(level, *refs):
    held_ref, received, out_ref = refs[0], refs[1:-1], refs[-1]
    f32 = jnp.float32
    for k in range(held_ref.shape[0]):
        j = (2 * k + 1) << level
        total = held_ref[k]
        for b, ref in enumerate(received):
            total = total + ref[j >> (b + 1)].astype(f32)
        out_ref[k] = total.astype(out_ref.dtype)


def share_kernel(levels, *refs):
    held_ref, received, outs = refs[0], refs[1 : 1 + levels], refs[1 + levels :]
    f32 = jnp.float32
    count = len(outs)
    rows = outs[0].shape[0]
    me = lax.axis_index("gx")
    for step, out_ref in enumerate(outs):
        chunk = lax.rem(me + step, count)
        span = pl.ds(pl.multiple_of(chunk * rows, rows), rows)
        total = held_ref[0, span]
        for ref in received:
            total = total + ref[0, span].astype(f32)
        out_ref[...] = total.astype(out_ref.dtype)


def sum_kernel(norm_factor, *refs):
    own_ref, received, out_ref = refs[0], refs[1:-1], refs[-1]
    total = own_ref[...]
    for ref in received:
        total = total + ref[...].astype(jnp.float32)
    out_ref[...] = (total * norm_factor).astype(out_ref.dtype)


def pack_kernel(*refs):
    chunks, out_ref = refs[:-1], refs[-1]
    rows = chunks[0].shape[0]
    me = lax.axis_index("gx")
    for k, ref in enumerate(chunks):
        place = lax.rem(me + k, len(chunks))
        out_ref[pl.ds(pl.multiple_of(place * rows, rows), rows)] = ref[...]


def contract_kernel(times, *refs):
    pair_hbm, live_ref = refs[:2]
    blocks, refs = refs[2 : 2 + times], refs[2 + times :]
    tau_ref, margin_ref, corr_ref = refs[:3]
    every_ref, left_ref, right_ref, pair_ref, sem = refs[3:]
    f32 = jnp.float32
    copy = pltpu.make_async_copy(pair_hbm, pair_ref, sem)
    copy.start()
    vectors = every_ref.shape[2]
    count_ops = margin_ref.shape[1]
    order = tau_ref.shape[2]
    spins = order // vectors
    me_t = lax.axis_index("ta")
    for k in range(times):
        every_ref[lax.rem(me_t + k, times)] = blocks[k][...]
    copy.wait()
    sink, source = pair_ref[0, 0], pair_ref[0, 1]
    live = live_ref[0] > 0
    for o in range(count_ops):
        first = 2 * o * vectors
        part = lambda t, k: every_ref[t, first + k * vectors : first + (k + 1) * vectors]
        margin_ref[0, o, 0] = part(me_t, 0).astype(f32)
        margin_ref[0, o, 1] = part(me_t, 1).astype(f32)
        a_r, a_i = part(sink, 0), part(sink, 1)
        b_r, b_i = part(source, 0).T, part(source, 1).T
        left_ref[o, 0:vectors, 0:vectors] = a_r
        left_ref[o, 0:vectors, vectors:] = -a_i
        left_ref[o, vectors:, 0:vectors] = a_i
        left_ref[o, vectors:, vectors:] = a_r
        right_ref[o, 0:vectors, 0:vectors] = b_r
        right_ref[o, 0:vectors, vectors:] = -b_i
        right_ref[o, vectors:, 0:vectors] = b_i
        right_ref[o, vectors:, vectors:] = b_r
        real = jnp.zeros((8, vectors), f32)
        imag = jnp.zeros((8, vectors), f32)
        fold = lambda t: jnp.sum(t.reshape(vectors // 8, 8, vectors), axis=0)
        for s in range(spins):
            rows = slice(s * vectors, (s + 1) * vectors)
            x = jnp.dot(
                left_ref[o],
                jnp.concatenate([tau_ref[0, rows], tau_ref[1, rows]], axis=0),
                preferred_element_type=f32,
            )
            for c in range(spins):
                cols = slice(c * vectors, (c + 1) * vectors)
                y = jnp.dot(
                    jnp.concatenate([tau_ref[0, rows, cols], tau_ref[1, rows, cols]], axis=1),
                    right_ref[o],
                    preferred_element_type=f32,
                )
                x_r, x_i = x[:vectors, cols], x[vectors:, cols]
                y_r, y_i = y[:, :vectors], y[:, vectors:]
                real = real + fold(x_r * y_r + x_i * y_i)
                imag = imag + fold(x_i * y_r - x_r * y_i)
        scale = 1.0 / vectors
        corr_ref[0, o, 0] = jnp.where(live, jnp.sum(real) * scale, 0.0)
        corr_ref[0, o, 1] = jnp.where(live, jnp.sum(imag) * scale, 0.0)


def vmem_spec():
    return pl.BlockSpec(memory_space=pltpu.VMEM)


def smem_spec():
    return pl.BlockSpec(memory_space=pltpu.SMEM)


def hbm_spec():
    return pl.BlockSpec(memory_space=pltpu.HBM)


def in_hbm(x):
    return pltpu.with_memory_space_constraint(x, pltpu.HBM)


def local_call(body, name, outs, in_specs, out_specs, scratch=(), cost=None):
    return pl.pallas_call(
        body,
        out_shape=outs,
        in_specs=in_specs,
        out_specs=out_specs,
        scratch_shapes=list(scratch),
        compiler_params=pltpu.CompilerParams(vmem_limit_bytes=VMEM_LIMIT),
        cost_estimate=cost,
        name=name,
    )


def from_step(block, axis, step):
    count = lax.axis_size(axis)
    return lax.ppermute(block, axis, [((i + step) % count, i) for i in range(count)])


def per_device(eigvecs, links, op_dirs, op_moms, perams, pair_times, slot_counts):
    f32, bf16 = jnp.float32, jnp.bfloat16
    _, cells_x, cells_y, cells_z, colors, _, vectors = eigvecs.shape
    order = cells_z * colors * 2
    lines = cells_x * cells_y
    count_ops = op_dirs.shape[0]
    times, shares, groups = lax.axis_size("ta"), lax.axis_size("gx"), lax.axis_size("gy")
    levels = groups.bit_length() - 1
    own_ops = count_ops // groups
    own_rows = own_ops * 2 * vectors
    field = eigvecs.reshape(cells_x, cells_y, order, vectors)
    halo_x = from_step(field[0:1], "gx", 1)
    halo_y = from_step(field, "gy", 1)
    link_field = links[0].transpose(0, 1, 3, 5, 6, 4, 2).reshape(lines, 27, 2, cells_z)
    outside, inside = halo_fields(cells_x, cells_y), local_fields(cells_x, cells_y)
    inputs = [field, link_field, op_dirs, op_moms, wave_constants(cells_z)]
    inputs = [in_hbm(x) for x in inputs]
    held = [
        pltpu.SMEM(x.shape, x.dtype) if x.ndim == 1 else pltpu.VMEM(x.shape, x.dtype)
        for x in inputs
    ]
    matrices, local, left, phases = local_call(
        functools.partial(prepare_kernel, cells_x, cells_y),
        "prepare_lines",
        (
            jax.ShapeDtypeStruct((len(outside), order, 128), bf16),
            jax.ShapeDtypeStruct((len(inside), order, vectors), f32),
            jax.ShapeDtypeStruct((2, vectors, lines * order), bf16),
            jax.ShapeDtypeStruct((count_ops, order // 2, 2 * vectors), f32),
        ),
        [hbm_spec()] * len(inputs),
        (vmem_spec(),) * 4,
        held
        + [
            pltpu.VMEM((lines, LINK_COLS, cells_z), f32),
            pltpu.SemaphoreType.DMA((len(inputs),)),
        ],
    )(*inputs)
    part_shapes = [
        jax.ShapeDtypeStruct((groups >> (b + 1), own_rows, vectors), f32)
        for b in range(levels)
    ] + [jax.ShapeDtypeStruct((1, own_rows, vectors), f32)]
    parts = local_call(
        functools.partial(margin_kernel, cells_x, cells_y, groups),
        "partial_margins",
        tuple(part_shapes),
        [vmem_spec()] * 6 + [hbm_spec()],
        (vmem_spec(),) * len(part_shapes),
        [
            pltpu.VMEM((7, lines, order, vectors), f32),
            pltpu.VMEM((4, vectors, lines * order), bf16),
            pltpu.SMEM((count_ops,), jnp.int32),
            pltpu.SemaphoreType.DMA,
        ],
    )(matrices, local, left, phases, halo_x, halo_y, in_hbm(op_dirs))
    received = []
    for b in range(levels):
        sent = parts[b]
        if b:
            sent = local_call(
                functools.partial(fold_kernel, b),
                "fold_groups",
                jax.ShapeDtypeStruct(sent.shape, f32),
                [vmem_spec()] * (1 + b),
                vmem_spec(),
            )(sent, *received)
        received.append(lax.ppermute(sent, "gy", [(i, i ^ (1 << b)) for i in range(groups)]))
    norm_factor = 1.0 / math.sqrt(3.0 * cells_x * shares * cells_y * groups * cells_z)
    direct = shares <= DIRECT_LIMIT and own_rows % (16 * shares) == 0
    steps = shares if direct else 1
    rows = own_rows // steps
    chunk_shapes = [jax.ShapeDtypeStruct((rows, vectors), f32) for k in range(steps)]
    chunks = local_call(
        functools.partial(share_kernel, levels),
        "share_rows",
        tuple(chunk_shapes),
        [vmem_spec()] * (1 + levels),
        (vmem_spec(),) * steps,
    )(parts[levels], *received)
    if direct:
        arrived = [from_step(chunks[k], "gx", -k) for k in range(1, shares)]
        own = local_call(
            functools.partial(sum_kernel, norm_factor),
            "sum_shares",
            jax.ShapeDtypeStruct((rows, vectors), bf16),
            [vmem_spec()] * shares,
            vmem_spec(),
        )(chunks[0], *arrived)
        own = local_call(
            pack_kernel,
            "pack_rows",
            jax.ShapeDtypeStruct((own_rows, vectors), bf16),
            [vmem_spec()] * shares,
            vmem_spec(),
        )(own, *[from_step(own, "gx", k) for k in range(1, shares)])
    else:
        own = (lax.psum(chunks[0], "gx") * norm_factor).astype(bf16)
    every = [own] + [from_step(own, "ta", k) for k in range(1, times)]
    margins, correlators = local_call(
        functools.partial(contract_kernel, times),
        "contraction",
        (
            jax.ShapeDtypeStruct((1, own_ops, 2, vectors, vectors), f32),
            jax.ShapeDtypeStruct((1, own_ops, 2), f32),
        ),
        [hbm_spec(), smem_spec()] + [vmem_spec()] * (len(every) + 1),
        (vmem_spec(), smem_spec()),
        [
            pltpu.VMEM((times, own_rows, vectors), bf16),
            pltpu.VMEM((own_ops, 2 * vectors, 2 * vectors), bf16),
            pltpu.VMEM((own_ops, 2 * vectors, 2 * vectors), bf16),
            pltpu.SMEM((1, 2), jnp.int32),
            pltpu.SemaphoreType.DMA,
        ],
    )(in_hbm(pair_times), slot_counts, *every, perams[0])
    return (margins, correlators)


def solution(mesh):
    placed = (
        P("ta", "gx", "gy", None, None, None, None),
        P("ta", "gx", "gy", None, None, None, None, None),
        P(),
        P(),
        P(("ta", "gx"), None, None, None),
        P(("ta", "gx"), None),
        P(("ta", "gx")),
    )
    return jax.shard_map(
        per_device,
        mesh=mesh,
        in_specs=placed,
        out_specs=(P("ta", "gy", None, None, None), P(("ta", "gx"), "gy", None)),
        check_vma=False,
    )
```

time: 56.3 us -> 46 us (0.82)
  local copies, waits for them, and re-layouts: 8.23 us -> 0.01 us
  starting transfers between devices: 20.4 us -> 16.8 us
  waiting for transfers between devices: 18.1 us -> 21.3 us
  Pallas kernels: 7.65 us -> 6.39 us
    unnamed x24 -> x2, local copies, waits for them, and re-layouts: 8.23 us -> 0.01 us
    ppermute x12 -> x9, starting transfers between devices: 19.3 us -> 14.6 us  [from_step(): lax.ppermute(block, axis, [((i + step) % count, i) for i in range(count)])]
    ppermute x12 -> x9, waiting for transfers between devices: 8.89 us -> 12.3 us  [from_step(): lax.ppermute(block, axis, [((i + step) % count, i) for i in range(count)])]
    pallas_call x1, Pallas kernels: 3.57 us -> 2.24 us  [per_device(): local_call(functools.partial(prepare_kernel, cells_x, cells_y), 'prepare_...]
    ppermute x2, starting transfers between devices: 1.13 us -> 2.23 us  [per_device(): lax.ppermute(sent, 'gy', [(i, i ^ 1 << b) for i in range(groups)])]
    pallas_call x1 -> x2, Pallas kernels: 2.63 us -> 2.72 us  [the longest x1 2.71 us: per_device(): local_call(functools.partial(contract_kernel, times), 'contraction', (jax...]
  transfers between devices with their start and end apart: 14 -> 11, of which waited for: 7 -> 8; matrix products, arithmetic and copies ran while one was open for 0% -> 0% of each run, Pallas kernels for 6% -> 5%
where the time goes in v2:
time: 46 us; the launch traced here: 45.8 us
  waiting for transfers between devices  21.3 us (46%)
  starting transfers between devices  16.8 us (37%)
  Pallas kernels  6.39 us (14%)
  between operations  1.35 us (3%)
    ppermute x9, starting transfers between devices, from_step(): lax.ppermute(block, axis, [((i + step) % count, i) for i in range(count)])  14.6 us
    ppermute x9, waiting for transfers between devices, from_step(): lax.ppermute(block, axis, [((i + step) % count, i) for i in range(count)])  12.3 us
    ppermute x2, waiting for transfers between devices, per_device(): lax.ppermute(sent, 'gy', [(i, i ^ 1 << b) for i in range(groups)])  8.96 us
    pallas_call x1, Pallas kernels, per_device(): local_call(functools.partial(contract_kernel, times), 'contraction', (jax...  2.71 us
    pallas_call x1, Pallas kernels, per_device(): local_call(functools.partial(prepare_kernel, cells_x, cells_y), 'prepare_...  2.24 us
    ppermute x2, starting transfers between devices, per_device(): lax.ppermute(sent, 'gy', [(i, i ^ 1 << b) for i in range(groups)])  2.23 us
    pallas_call x1, Pallas kernels, per_device(): local_call(functools.partial(margin_kernel, cells_x, cells_y, groups), 'p...  1.34 us
  transfers between devices with their start and end apart: 11, of which 8 were waited for; matrix products, arithmetic and copies ran while one was open for 0% of the time, Pallas kernels for 5%

profile of v2, /device:TPU:0, one launch (start us, length us, event | category | flops | bytes accessed | tf_op | source)
XLA Modules:
  0.0 45.8 jit_solution(3329034401790190491)
XLA Ops:
  0.6 5.1 %collective-permute-start = (bf16[1,2,144,128]{3,2,1,0:T(8,128)(2,1)}, bf16[1,2,144,128]{3,2,1,0:T(8,128)(2,1)S(1)}, u32[]{:S(2)}, u32[]{:S(2)}) collective-permute-start(bf16[1,2,144,128]{3,2,1,0:T(8,128)(2,1)} %bitcast.8), channel_id=1, source_target_pairs={{4,0},{8,4},{12,8},{0,12},{5,1},{9,5},{13,9},{1,13},{6,2},{10,6},{... | collective-permute-start | bytes 221192 | tf_op jit(solution)/shard_map/ppermute | solution.py:376
  5.7 0.7 %collective-permute-start.1 = (bf16[1,2,144,128]{3,2,1,0:T(8,128)(2,1)}, bf16[1,2,144,128]{3,2,1,0:T(8,128)(2,1)S(1)}, u32[]{:S(2)}, u32[]{:S(2)}) collective-permute-start(bf16[1,2,144,128]{3,2,1,0:T(8,128)(2,1)} %bitcast.9), channel_id=1, source_target_pairs={{1,0},{2,1},{3,2},{0,3},{5,4},{6,5},{7,6},{4,7},{9,8},{10,9},{11,1... | collective-permute-start | bytes 221192 | tf_op jit(solution)/shard_map/ppermute | solution.py:376
  6.4 2.2 %prepare_lines.1 = (bf16[3,144,128]{2,1,0:T(8,128)(2,1)S(1)}, f32[11,144,128]{2,1,0:T(8,128)S(1)}, bf16[2,128,288]{2,1,0:T(8,128)(2,1)S(1)}, f32[8,72,256]{2,1,0:T(8,128)S(1)}) custom-call(bf16[1,2,144,128]{3,2,1,0:T(8,128)(2,1)} %bitcast.10, bf16[2,27,2,24]{3,2,1,0:T(2,128)(2,1)} %bitcast.11, s32[8]{0:T(128)} %refs_6_.1, s32[8]{0:T(128)} %refs_3_.1, ...), custom_call_target="tpu_custom_call" | custom-call | tf_op jit(solution)/shard_map/prepare_lines/pallas_call | solution.py:400
  8.7 0.0 collective-permute-done.refs_4_
  8.7 0.0 collective-permute-done.1.refs_5_
  8.7 1.3 %partial_margins.1 = (f32[2,512,128]{2,1,0:T(8,128)S(1)}, f32[1,512,128]{2,1,0:T(8,128)S(1)}, f32[1,512,128]{2,1,0:T(8,128)S(1)}) custom-call(bf16[3,144,128]{2,1,0:T(8,128)(2,1)S(1)} %get-tuple-element.13.refs_0_, f32[11,144,128]{2,1,0:T(8,128)S(1)} %get-tuple-element.14.refs_1_, bf16[2,128,288]{2,1,0:T(8,128)(2,1)S(1)} %get-tuple-element.15.refs_2_, ...), custom_call_target="tpu_custom_call" | custom-call | tf_op jit(solution)/shard_map/partial_margins/pallas_call | solution.py:421
  10.1 1.0 %collective-permute-start.2 = (f32[2,512,128]{2,1,0:T(8,128)S(1)}, f32[2,512,128]{2,1,0:T(8,128)S(1)}, u32[]{:S(2)}, u32[]{:S(2)}) collective-permute-start(f32[2,512,128]{2,1,0:T(8,128)S(1)} %get-tuple-element.18), channel_id=1, source_target_pairs={{0,1},{1,0},{2,3},{3,2},{4,5},{5,4},{6,7},{7,6},{8,9},{9,8},{10,11... | collective-permute-start | bytes 1572872 | tf_op jit(solution)/shard_map/ppermute | solution.py:445
  11.1 1.5 %collective-permute-done.2.refs_1_ = f32[2,512,128]{2,1,0:T(8,128)S(1)} collective-permute-done((f32[2,512,128]{2,1,0:T(8,128)S(1)}, f32[2,512,128]{2,1,0:T(8,128)S(1)}, u32[]{:S(2)}, u32[]{:S(2)}) %collective-permute-start.2) | collective-permute-done | bytes 524320 | tf_op jit(solution)/shard_map/ppermute | solution.py:445
  12.6 0.0 copy-start
  12.6 1.2 %collective-permute-start.3 = (f32[1,512,128]{2,1,0:T(8,128)S(1)}, f32[1,512,128]{2,1,0:T(8,128)S(1)}, u32[]{:S(2)}, u32[]{:S(2)}) collective-permute-start(f32[1,512,128]{2,1,0:T(8,128)S(1)} %fold_groups.1), channel_id=1, source_target_pairs={{0,2},{1,3},{2,0},{3,1},{4,6},{5,7},{6,4},{7,5},{8,10},{9,11},{10,... | collective-permute-start | bytes 786440 | tf_op jit(solution)/shard_map/ppermute | solution.py:445
  13.9 7.4 %collective-permute-done.3.refs_2_ = f32[1,512,128]{2,1,0:T(8,128)S(1)} collective-permute-done((f32[1,512,128]{2,1,0:T(8,128)S(1)}, f32[1,512,128]{2,1,0:T(8,128)S(1)}, u32[]{:S(2)}, u32[]{:S(2)}) %collective-permute-start.3) | collective-permute-done | bytes 262176 | tf_op jit(solution)/shard_map/ppermute | solution.py:445
  21.3 0.1 collective-permute-start.4
  21.4 3.1 %collective-permute-start.5 = (f32[128,128]{1,0:T(8,128)S(1)}, f32[128,128]{1,0:T(8,128)S(1)}, u32[]{:S(2)}, u32[]{:S(2)}) collective-permute-start(f32[128,128]{1,0:T(8,128)S(1)} %get-tuple-element.22), channel_id=1, source_target_pairs={{8,0},{12,4},{0,8},{4,12},{9,1},{13,5},{1,9},{5,13},{10,2},{14,6},... | collective-permute-start | bytes 196616 | tf_op jit(solution)/shard_map/ppermute | solution.py:376
  24.5 0.7 %collective-permute-start.6 = (f32[128,128]{1,0:T(8,128)S(1)}, f32[128,128]{1,0:T(8,128)S(1)}, u32[]{:S(2)}, u32[]{:S(2)}) collective-permute-start(f32[128,128]{1,0:T(8,128)S(1)} %get-tuple-element.23), channel_id=1, source_target_pairs={{4,0},{8,4},{12,8},{0,12},{5,1},{9,5},{13,9},{1,13},{6,2},{10,6},{... | collective-permute-start | bytes 196616 | tf_op jit(solution)/shard_map/ppermute | solution.py:376
  25.2 2.9 %collective-permute-done.4.refs_1_ = f32[128,128]{1,0:T(8,128)S(1)} collective-permute-done((f32[128,128]{1,0:T(8,128)S(1)}, f32[128,128]{1,0:T(8,128)S(1)}, u32[]{:S(2)}, u32[]{:S(2)}) %collective-permute-start.4) | collective-permute-done | bytes 65568 | tf_op jit(solution)/shard_map/ppermute | solution.py:376
  28.1 1.3 %collective-permute-done.5.refs_2_ = f32[128,128]{1,0:T(8,128)S(1)} collective-permute-done((f32[128,128]{1,0:T(8,128)S(1)}, f32[128,128]{1,0:T(8,128)S(1)}, u32[]{:S(2)}, u32[]{:S(2)}) %collective-permute-start.5) | collective-permute-done | bytes 65568 | tf_op jit(solution)/shard_map/ppermute | solution.py:376
  29.5 0.0 collective-permute-done.6.refs_3_
  29.5 2.7 %collective-permute-start.7 = (bf16[128,128]{1,0:T(8,128)(2,1)S(1)}, bf16[128,128]{1,0:T(8,128)(2,1)S(1)}, u32[]{:S(2)}, u32[]{:S(2)}) collective-permute-start(bf16[128,128]{1,0:T(8,128)(2,1)S(1)} %sum_shares.1.refs_0_), channel_id=1, source_target_pairs={{4,0},{8,4},{12,8},{0,12},{5,1},{9,5},{13,9},{1,13},{6,2},{10,6},{... | collective-permute-start | bytes 98312 | tf_op jit(solution)/shard_map/ppermute | solution.py:376
  32.3 0.1 collective-permute-start.8
  32.4 0.5 %collective-permute-start.9 = (bf16[128,128]{1,0:T(8,128)(2,1)S(1)}, bf16[128,128]{1,0:T(8,128)(2,1)S(1)}, u32[]{:S(2)}, u32[]{:S(2)}) collective-permute-start(bf16[128,128]{1,0:T(8,128)(2,1)S(1)} %sum_shares.1.refs_0_), channel_id=1, source_target_pairs={{12,0},{0,4},{4,8},{8,12},{13,1},{1,5},{5,9},{9,13},{14,2},{2,6},{... | collective-permute-start | bytes 98312 | tf_op jit(solution)/shard_map/ppermute | solution.py:376
  32.9 1.0 %collective-permute-done.7.refs_1_ = bf16[128,128]{1,0:T(8,128)(2,1)S(1)} collective-permute-done((bf16[128,128]{1,0:T(8,128)(2,1)S(1)}, bf16[128,128]{1,0:T(8,128)(2,1)S(1)}, u32[]{:S(2)}, u32[]{:S(2)}) %collective-permute-start.7) | collective-permute-done | bytes 32800 | tf_op jit(solution)/shard_map/ppermute | solution.py:376
  33.9 3.2 %collective-permute-done.8.refs_2_ = bf16[128,128]{1,0:T(8,128)(2,1)S(1)} collective-permute-done((bf16[128,128]{1,0:T(8,128)(2,1)S(1)}, bf16[128,128]{1,0:T(8,128)(2,1)S(1)}, u32[]{:S(2)}, u32[]{:S(2)}) %collective-permute-start.8) | collective-permute-done | bytes 32800 | tf_op jit(solution)/shard_map/ppermute | solution.py:376
  37.1 1.0 %collective-permute-done.9.refs_3_ = bf16[128,128]{1,0:T(8,128)(2,1)S(1)} collective-permute-done((bf16[128,128]{1,0:T(8,128)(2,1)S(1)}, bf16[128,128]{1,0:T(8,128)(2,1)S(1)}, u32[]{:S(2)}, u32[]{:S(2)}) %collective-permute-start.9) | collective-permute-done | bytes 32800 | tf_op jit(solution)/shard_map/ppermute | solution.py:376
  38.1 1.6 %collective-permute-start.10 = (bf16[512,128]{1,0:T(8,128)(2,1)S(1)}, bf16[512,128]{1,0:T(8,128)(2,1)S(1)}, u32[]{:S(2)}, u32[]{:S(2)}) collective-permute-start(bf16[512,128]{1,0:T(8,128)(2,1)S(1)} %pack_rows.1.refs_2_), channel_id=1, source_target_pairs={{16,0},{0,16},{17,1},{1,17},{18,2},{2,18},{19,3},{3,19},{20,4},{4,... | collective-permute-start | bytes 393224 | tf_op jit(solution)/shard_map/ppermute | solution.py:376
  40.3 2.8 %collective-permute-done.10.refs_3_ = bf16[512,128]{1,0:T(8,128)(2,1)S(1)} collective-permute-done((bf16[512,128]{1,0:T(8,128)(2,1)S(1)}, bf16[512,128]{1,0:T(8,128)(2,1)S(1)}, u32[]{:S(2)}, u32[]{:S(2)}) %collective-permute-start.10) | collective-permute-done | bytes 131104 | tf_op jit(solution)/shard_map/ppermute | solution.py:376
  43.1 0.0 copy-done
  43.1 2.7 %contraction.1 = (f32[1,2,2,128,128]{4,3,2,1,0:T(8,128)}, f32[1,2,2]{2,1,0:T(2,128)}) custom-call(s32[1,2]{1,0:T(1,128)} %refs_0_.1, s32[1]{0:T(128)S(6)} %copy.10.refs_1_, bf16[512,128]{1,0:T(8,128)(2,1)S(1)} %pack_rows.1.refs_2_, bf16[512,128]{1,0:T(8,128)(2,1)S(1)} %collective-permute-done.10.refs_3_, bf16[2,512,512]{2,1,0:T(8,128)(2,1)S(1)} %bitcast.7), custom_call_target="tpu_custom_call" | custom-call | tf_op jit(solution)/shard_map/contraction/pallas_call | solution.py:477
  (4 shorter events, 0.1 us)
Async XLA Ops:
  0.6 8.0 %collective-permute-start = (bf16[1,2,144,128]{3,2,1,0:T(8,128)(2,1)}, bf16[1,2,144,128]{3,2,1,0:T(8,128)(2,1)S(1)}, u32[]{:S(2)}, u32[]{:S(2)}) collective-permute-start(bf16[1,2,144,128]{3,2,1,0:T(8,128)(2,1)} %bitcast.8), channel_id=1, source_target_pairs={{4,0},{8,4},{12,8},{0,12},{5,1},{9,5},{13,9},{1,13},{6,2},{10,6},{... | collective-permute-start | bytes 221192 | tf_op jit(solution)/shard_map/ppermute | solution.py:376
  5.7 3.0 %collective-permute-start.1 = (bf16[1,2,144,128]{3,2,1,0:T(8,128)(2,1)}, bf16[1,2,144,128]{3,2,1,0:T(8,128)(2,1)S(1)}, u32[]{:S(2)}, u32[]{:S(2)}) collective-permute-start(bf16[1,2,144,128]{3,2,1,0:T(8,128)(2,1)} %bitcast.9), channel_id=1, source_target_pairs={{1,0},{2,1},{3,2},{0,3},{5,4},{6,5},{7,6},{4,7},{9,8},{10,9},{11,1... | collective-permute-start | bytes 221192 | tf_op jit(solution)/shard_map/ppermute | solution.py:376
  10.1 2.5 %collective-permute-start.2 = (f32[2,512,128]{2,1,0:T(8,128)S(1)}, f32[2,512,128]{2,1,0:T(8,128)S(1)}, u32[]{:S(2)}, u32[]{:S(2)}) collective-permute-start(f32[2,512,128]{2,1,0:T(8,128)S(1)} %get-tuple-element.18), channel_id=1, source_target_pairs={{0,1},{1,0},{2,3},{3,2},{4,5},{5,4},{6,7},{7,6},{8,9},{9,8},{10,11... | collective-permute-start | bytes 1572872 | tf_op jit(solution)/shard_map/ppermute | solution.py:445
  12.6 30.5 %copy-start = (bf16[1,2,512,512]{3,2,1,0:T(8,128)(2,1)S(1)}, bf16[1,2,512,512]{3,2,1,0:T(8,128)(2,1)}, u32[]{:S(2)}) copy-start(bf16[1,2,512,512]{3,2,1,0:T(8,128)(2,1)} %param.12) | copy-start | bytes 3145732
  12.6 8.7 %collective-permute-start.3 = (f32[1,512,128]{2,1,0:T(8,128)S(1)}, f32[1,512,128]{2,1,0:T(8,128)S(1)}, u32[]{:S(2)}, u32[]{:S(2)}) collective-permute-start(f32[1,512,128]{2,1,0:T(8,128)S(1)} %fold_groups.1), channel_id=1, source_target_pairs={{0,2},{1,3},{2,0},{3,1},{4,6},{5,7},{6,4},{7,5},{8,10},{9,11},{10,... | collective-permute-start | bytes 786440 | tf_op jit(solution)/shard_map/ppermute | solution.py:445
  21.3 6.8 %collective-permute-start.4 = (f32[128,128]{1,0:T(8,128)S(1)}, f32[128,128]{1,0:T(8,128)S(1)}, u32[]{:S(2)}, u32[]{:S(2)}) collective-permute-start(f32[128,128]{1,0:T(8,128)S(1)} %get-tuple-element.21), channel_id=1, source_target_pairs={{12,0},{0,4},{4,8},{8,12},{13,1},{1,5},{5,9},{9,13},{14,2},{2,6},{... | collective-permute-start | bytes 196616 | tf_op jit(solution)/shard_map/ppermute | solution.py:376
  21.4 8.1 %collective-permute-start.5 = (f32[128,128]{1,0:T(8,128)S(1)}, f32[128,128]{1,0:T(8,128)S(1)}, u32[]{:S(2)}, u32[]{:S(2)}) collective-permute-start(f32[128,128]{1,0:T(8,128)S(1)} %get-tuple-element.22), channel_id=1, source_target_pairs={{8,0},{12,4},{0,8},{4,12},{9,1},{13,5},{1,9},{5,13},{10,2},{14,6},... | collective-permute-start | bytes 196616 | tf_op jit(solution)/shard_map/ppermute | solution.py:376
  24.5 4.9 %collective-permute-start.6 = (f32[128,128]{1,0:T(8,128)S(1)}, f32[128,128]{1,0:T(8,128)S(1)}, u32[]{:S(2)}, u32[]{:S(2)}) collective-permute-start(f32[128,128]{1,0:T(8,128)S(1)} %get-tuple-element.23), channel_id=1, source_target_pairs={{4,0},{8,4},{12,8},{0,12},{5,1},{9,5},{13,9},{1,13},{6,2},{10,6},{... | collective-permute-start | bytes 196616 | tf_op jit(solution)/shard_map/ppermute | solution.py:376
  29.5 4.3 %collective-permute-start.7 = (bf16[128,128]{1,0:T(8,128)(2,1)S(1)}, bf16[128,128]{1,0:T(8,128)(2,1)S(1)}, u32[]{:S(2)}, u32[]{:S(2)}) collective-permute-start(bf16[128,128]{1,0:T(8,128)(2,1)S(1)} %sum_shares.1.refs_0_), channel_id=1, source_target_pairs={{4,0},{8,4},{12,8},{0,12},{5,1},{9,5},{13,9},{1,13},{6,2},{10,6},{... | collective-permute-start | bytes 98312 | tf_op jit(solution)/shard_map/ppermute | solution.py:376
  32.3 4.8 %collective-permute-start.8 = (bf16[128,128]{1,0:T(8,128)(2,1)S(1)}, bf16[128,128]{1,0:T(8,128)(2,1)S(1)}, u32[]{:S(2)}, u32[]{:S(2)}) collective-permute-start(bf16[128,128]{1,0:T(8,128)(2,1)S(1)} %sum_shares.1.refs_0_), channel_id=1, source_target_pairs={{8,0},{12,4},{0,8},{4,12},{9,1},{13,5},{1,9},{5,13},{10,2},{14,6},... | collective-permute-start | bytes 98312 | tf_op jit(solution)/shard_map/ppermute | solution.py:376
  32.4 5.7 %collective-permute-start.9 = (bf16[128,128]{1,0:T(8,128)(2,1)S(1)}, bf16[128,128]{1,0:T(8,128)(2,1)S(1)}, u32[]{:S(2)}, u32[]{:S(2)}) collective-permute-start(bf16[128,128]{1,0:T(8,128)(2,1)S(1)} %sum_shares.1.refs_0_), channel_id=1, source_target_pairs={{12,0},{0,4},{4,8},{8,12},{13,1},{1,5},{5,9},{9,13},{14,2},{2,6},{... | collective-permute-start | bytes 98312 | tf_op jit(solution)/shard_map/ppermute | solution.py:376
  38.1 5.0 %collective-permute-start.10 = (bf16[512,128]{1,0:T(8,128)(2,1)S(1)}, bf16[512,128]{1,0:T(8,128)(2,1)S(1)}, u32[]{:S(2)}, u32[]{:S(2)}) collective-permute-start(bf16[512,128]{1,0:T(8,128)(2,1)S(1)} %pack_rows.1.refs_2_), channel_id=1, source_target_pairs={{16,0},{0,16},{17,1},{1,17},{18,2},{2,18},{19,3},{3,19},{20,4},{4,... | collective-permute-start | bytes 393224 | tf_op jit(solution)/shard_map/ppermute | solution.py:376

commit v3 on v2

--- a/solution.py
+++ b/solution.py
@@ -12,6 +12,8 @@
 VMEM_LIMIT = 24 * 1024 * 1024
 MOMENTA = 3
 LINK_COLS = 54
+TAIL = 16
+FIXED_BITS = 14.0
 DIRECT_LIMIT = 8
 
 
@@ -240,52 +242,78 @@
             out_ref[place, first + vectors : first + 2 * vectors] = product[:, vectors:]
 
 
-def fold_kernel(level, *refs):
+def scale_of(block):
+    top = jnp.max(jnp.abs(block), axis=0, keepdims=True)
+    return jnp.floor(jnp.log2(jnp.maximum(top, 1e-30))) + 1.0
+
+
+def put_fixed(out_ref, blocks):
+    rows, vectors = blocks[0].shape
+    tail = iota((TAIL, vectors), 0)
+    scales = jnp.zeros((TAIL, vectors), jnp.float32)
+    for k, block in enumerate(blocks):
+        scale = scale_of(block)
+        scales = jnp.where(tail == k, scale, scales)
+        fixed = jnp.floor(block * jnp.exp2(FIXED_BITS - scale) + 0.5)
+        out_ref[k * rows : (k + 1) * rows] = fixed.astype(jnp.int32).astype(jnp.int16)
+    out_ref[len(blocks) * rows :] = scales.astype(jnp.int32).astype(jnp.int16)
+
+
+def from_fixed(ref, rows, k):
+    scales = ref[ref.shape[0] - TAIL :].astype(jnp.int32).astype(jnp.float32)
+    block = ref[k * rows : (k + 1) * rows].astype(jnp.int32).astype(jnp.float32)
+    return block * jnp.exp2(scales[k : k + 1] - FIXED_BITS)
+
+
+def fold_kernel(level, count_blocks, *refs):
     held_ref, received, out_ref = refs[0], refs[1:-1], refs[-1]
-    f32 = jnp.float32
+    rows = held_ref.shape[1] // count_blocks
     for k in range(held_ref.shape[0]):
         j = (2 * k + 1) << level
-        total = held_ref[k]
+        blocks = []
+        for p in range(count_blocks):
+            total = held_ref[k, p * rows : (p + 1) * rows]
+            for b, ref in enumerate(received):
+                total = total + arrived_block(ref.at[j >> (b + 1)], b, rows, p)
+            blocks.append(total)
+        put_fixed(out_ref.at[k], blocks)
+
+
+def arrived_block(ref, level, rows, p):
+    return ref[p * rows : (p + 1) * rows] if level == 0 else from_fixed(ref, rows, p)
+
+
+def share_kernel(levels, count_blocks, *refs):
+    held_ref, received, refs = refs[0], refs[1 : 1 + levels], refs[1 + levels :]
+    outs, total_ref = refs[:-1], refs[-1]
+    span = held_ref.shape[1] // count_blocks
+    for p in range(count_blocks):
+        total = held_ref[0, p * span : (p + 1) * span]
         for b, ref in enumerate(received):
-            total = total + ref[j >> (b + 1)].astype(f32)
-        out_ref[k] = total.astype(out_ref.dtype)
-
-
-def share_kernel(levels, *refs):
-    held_ref, received, outs = refs[0], refs[1 : 1 + levels], refs[1 + levels :]
-    f32 = jnp.float32
-    count = len(outs)
+            total = total + arrived_block(ref.at[0], b, span, p)
+        total_ref[p * span : (p + 1) * span] = total
     rows = outs[0].shape[0]
     me = lax.axis_index("gx")
     for step, out_ref in enumerate(outs):
-        chunk = lax.rem(me + step, count)
-        span = pl.ds(pl.multiple_of(chunk * rows, rows), rows)
-        total = held_ref[0, span]
-        for ref in received:
-            total = total + ref[0, span].astype(f32)
-        out_ref[...] = total.astype(out_ref.dtype)
+        chunk = lax.rem(me + step, len(outs))
+        total = total_ref[pl.ds(pl.multiple_of(chunk * rows, rows), rows)]
+        if step:
+            put_fixed(out_ref, [total])
+        else:
+            out_ref[...] = total
 
 
 def sum_kernel(norm_factor, *refs):
     own_ref, received, out_ref = refs[0], refs[1:-1], refs[-1]
     total = own_ref[...]
     for ref in received:
-        total = total + ref[...].astype(jnp.float32)
+        total = total + from_fixed(ref, total.shape[0], 0)
     out_ref[...] = (total * norm_factor).astype(out_ref.dtype)
 
 
-def pack_kernel(*refs):
-    chunks, out_ref = refs[:-1], refs[-1]
-    rows = chunks[0].shape[0]
-    me = lax.axis_index("gx")
-    for k, ref in enumerate(chunks):
-        place = lax.rem(me + k, len(chunks))
-        out_ref[pl.ds(pl.multiple_of(place * rows, rows), rows)] = ref[...]
-
-
-def contract_kernel(times, *refs):
+def contract_kernel(times, steps, *refs):
     pair_hbm, live_ref = refs[:2]
-    blocks, refs = refs[2 : 2 + times], refs[2 + times :]
+    chunks, refs = refs[2 : 2 + times * steps], refs[2 + times * steps :]
     tau_ref, margin_ref, corr_ref = refs[:3]
     every_ref, left_ref, right_ref, pair_ref, sem = refs[3:]
     f32 = jnp.float32
@@ -295,9 +323,12 @@
     count_ops = margin_ref.shape[1]
     order = tau_ref.shape[2]
     spins = order // vectors
-    me_t = lax.axis_index("ta")
-    for k in range(times):
-        every_ref[lax.rem(me_t + k, times)] = blocks[k][...]
+    me_t, me_x = lax.axis_index("ta"), lax.axis_index("gx")
+    rows = chunks[0].shape[0]
+    for k, ref in enumerate(chunks):
+        at_t = lax.rem(me_t + k // steps, times)
+        place = lax.rem(me_x + k % steps, steps) if steps > 1 else 0
+        every_ref[at_t, pl.ds(pl.multiple_of(place * rows, rows), rows)] = ref[...]
     copy.wait()
     sink, source = pair_ref[0, 0], pair_ref[0, 1]
     live = live_ref[0] > 0
@@ -436,9 +467,9 @@
         sent = parts[b]
         if b:
             sent = local_call(
-                functools.partial(fold_kernel, b),
+                functools.partial(fold_kernel, b, 2 * own_ops),
                 "fold_groups",
-                jax.ShapeDtypeStruct(sent.shape, f32),
+                jax.ShapeDtypeStruct((sent.shape[0], own_rows + TAIL, vectors), jnp.int16),
                 [vmem_spec()] * (1 + b),
                 vmem_spec(),
             )(sent, *received)
@@ -447,13 +478,15 @@
     direct = shares <= DIRECT_LIMIT and own_rows % (16 * shares) == 0
     steps = shares if direct else 1
     rows = own_rows // steps
-    chunk_shapes = [jax.ShapeDtypeStruct((rows, vectors), f32) for k in range(steps)]
+    chunk_shapes = [jax.ShapeDtypeStruct((rows, vectors), f32)]
+    chunk_shapes += [jax.ShapeDtypeStruct((rows + TAIL, vectors), jnp.int16)] * (steps - 1)
     chunks = local_call(
-        functools.partial(share_kernel, levels),
+        functools.partial(share_kernel, levels, 2 * own_ops),
         "share_rows",
         tuple(chunk_shapes),
         [vmem_spec()] * (1 + levels),
         (vmem_spec(),) * steps,
+        [pltpu.VMEM((own_rows, vectors), f32)],
     )(parts[levels], *received)
     if direct:
         arrived = [from_step(chunks[k], "gx", -k) for k in range(1, shares)]
@@ -464,18 +497,12 @@
             [vmem_spec()] * shares,
             vmem_spec(),
         )(chunks[0], *arrived)
-        own = local_call(
-            pack_kernel,
-            "pack_rows",
-            jax.ShapeDtypeStruct((own_rows, vectors), bf16),
-            [vmem_spec()] * shares,
-            vmem_spec(),
-        )(own, *[from_step(own, "gx", k) for k in range(1, shares)])
+        every = [own] + [from_step(own, "gx", k) for k in range(1, shares)]
     else:
-        own = (lax.psum(chunks[0], "gx") * norm_factor).astype(bf16)
-    every = [own] + [from_step(own, "ta", k) for k in range(1, times)]
+        every = [(lax.psum(chunks[0], "gx") * norm_factor).astype(bf16)]
+    every += [from_step(every[k], "ta", t) for t in range(1, times) for k in range(steps)]
     margins, correlators = local_call(
-        functools.partial(contract_kernel, times),
+        functools.partial(contract_kernel, times, steps),
         "contraction",
         (
             jax.ShapeDtypeStruct((1, own_ops, 2, vectors, vectors), f32),

time: 46 us -> 41.7 us (0.907)
  waiting for transfers between devices: 21.3 us -> 13.2 us
  starting transfers between devices: 16.8 us -> 20.3 us
    ppermute x9 -> x12, waiting for transfers between devices: 12.3 us -> 6.99 us  [from_step(): lax.ppermute(block, axis, [((i + step) % count, i) for i in range(count)])]
    ppermute x9 -> x12, starting transfers between devices: 14.6 us -> 18.1 us  [from_step(): lax.ppermute(block, axis, [((i + step) % count, i) for i in range(count)])]
    ppermute x2, waiting for transfers between devices: 8.96 us -> 6.23 us  [per_device(): lax.ppermute(sent, 'gy', [(i, i ^ 1 << b) for i in range(groups)])]
    pallas_call x4 -> x3, Pallas kernels: 2.79 us -> 2.97 us  [the longest x1 2.72 us: per_device(): local_call(functools.partial(contract_kernel, times, steps), 'contraction...]
  transfers between devices with their start and end apart: 11 -> 14, of which waited for: 8 -> 7; matrix products, arithmetic and copies ran while one was open for 0% -> 0% of each run, Pallas kernels for 5% -> 5%
where the time goes in v3:
time: 41.7 us; the launch traced here: 41.5 us
  starting transfers between devices  20.3 us (49%)
  waiting for transfers between devices  13.2 us (32%)
  Pallas kernels  6.58 us (16%)
  between operations  1.36 us (3%)
    ppermute x12, starting transfers between devices, from_step(): lax.ppermute(block, axis, [((i + step) % count, i) for i in range(count)])  18.1 us
    ppermute x12, waiting for transfers between devices, from_step(): lax.ppermute(block, axis, [((i + step) % count, i) for i in range(count)])  6.99 us
    ppermute x2, waiting for transfers between devices, per_device(): lax.ppermute(sent, 'gy', [(i, i ^ 1 << b) for i in range(groups)])  6.23 us
    pallas_call x1, Pallas kernels, per_device(): local_call(functools.partial(contract_kernel, times, steps), 'contraction...  2.72 us
    pallas_call x1, Pallas kernels, per_device(): local_call(functools.partial(prepare_kernel, cells_x, cells_y), 'prepare_...  2.24 us
    ppermute x2, starting transfers between devices, per_device(): lax.ppermute(sent, 'gy', [(i, i ^ 1 << b) for i in range(groups)])  2.23 us
    pallas_call x1, Pallas kernels, per_device(): local_call(functools.partial(margin_kernel, cells_x, cells_y, groups), 'p...  1.34 us
  transfers between devices with their start and end apart: 14, of which 7 were waited for; matrix products, arithmetic and copies ran while one was open for 0% of the time, Pallas kernels for 5%

profile of v3, /device:TPU:0, one launch (start us, length us, event | category | flops | bytes accessed | tf_op | source)
XLA Modules:
  0.0 41.5 jit_solution(7994712561193215109)
XLA Ops:
  0.6 5.1 %collective-permute-start = (bf16[1,2,144,128]{3,2,1,0:T(8,128)(2,1)}, bf16[1,2,144,128]{3,2,1,0:T(8,128)(2,1)S(1)}, u32[]{:S(2)}, u32[]{:S(2)}) collective-permute-start(bf16[1,2,144,128]{3,2,1,0:T(8,128)(2,1)} %bitcast.8), channel_id=1, source_target_pairs={{4,0},{8,4},{12,8},{0,12},{5,1},{9,5},{13,9},{1,13},{6,2},{10,6},{... | collective-permute-start | bytes 221192 | tf_op jit(solution)/shard_map/ppermute | solution.py:407
  5.7 0.7 %collective-permute-start.1 = (bf16[1,2,144,128]{3,2,1,0:T(8,128)(2,1)}, bf16[1,2,144,128]{3,2,1,0:T(8,128)(2,1)S(1)}, u32[]{:S(2)}, u32[]{:S(2)}) collective-permute-start(bf16[1,2,144,128]{3,2,1,0:T(8,128)(2,1)} %bitcast.9), channel_id=1, source_target_pairs={{1,0},{2,1},{3,2},{0,3},{5,4},{6,5},{7,6},{4,7},{9,8},{10,9},{11,1... | collective-permute-start | bytes 221192 | tf_op jit(solution)/shard_map/ppermute | solution.py:407
  6.4 2.2 %prepare_lines.1 = (bf16[3,144,128]{2,1,0:T(8,128)(2,1)S(1)}, f32[11,144,128]{2,1,0:T(8,128)S(1)}, bf16[2,128,288]{2,1,0:T(8,128)(2,1)S(1)}, f32[8,72,256]{2,1,0:T(8,128)S(1)}) custom-call(bf16[1,2,144,128]{3,2,1,0:T(8,128)(2,1)} %bitcast.10, bf16[2,27,2,24]{3,2,1,0:T(2,128)(2,1)} %bitcast.11, s32[8]{0:T(128)} %refs_6_.1, s32[8]{0:T(128)} %refs_3_.1, ...), custom_call_target="tpu_custom_call" | custom-call | tf_op jit(solution)/shard_map/prepare_lines/pallas_call | solution.py:431
  8.7 0.0 collective-permute-done.refs_4_
  8.7 0.0 collective-permute-done.1.refs_5_
  8.7 1.3 %partial_margins.1 = (f32[2,512,128]{2,1,0:T(8,128)S(1)}, f32[1,512,128]{2,1,0:T(8,128)S(1)}, f32[1,512,128]{2,1,0:T(8,128)S(1)}) custom-call(bf16[3,144,128]{2,1,0:T(8,128)(2,1)S(1)} %get-tuple-element.13.refs_0_, f32[11,144,128]{2,1,0:T(8,128)S(1)} %get-tuple-element.14.refs_1_, bf16[2,128,288]{2,1,0:T(8,128)(2,1)S(1)} %get-tuple-element.15.refs_2_, ...), custom_call_target="tpu_custom_call" | custom-call | tf_op jit(solution)/shard_map/partial_margins/pallas_call | solution.py:452
  10.1 0.0 copy-start
  10.1 1.0 %collective-permute-start.2 = (f32[2,512,128]{2,1,0:T(8,128)S(1)}, f32[2,512,128]{2,1,0:T(8,128)S(1)}, u32[]{:S(2)}, u32[]{:S(2)}) collective-permute-start(f32[2,512,128]{2,1,0:T(8,128)S(1)} %get-tuple-element.18), channel_id=1, source_target_pairs={{0,1},{1,0},{2,3},{3,2},{4,5},{5,4},{6,7},{7,6},{8,9},{9,8},{10,11... | collective-permute-start | bytes 1572872 | tf_op jit(solution)/shard_map/ppermute | solution.py:476
  11.1 1.5 %collective-permute-done.2.refs_1_ = f32[2,512,128]{2,1,0:T(8,128)S(1)} collective-permute-done((f32[2,512,128]{2,1,0:T(8,128)S(1)}, f32[2,512,128]{2,1,0:T(8,128)S(1)}, u32[]{:S(2)}, u32[]{:S(2)}) %collective-permute-start.2) | collective-permute-done | bytes 524320 | tf_op jit(solution)/shard_map/ppermute | solution.py:476
  12.6 0.1 fold_groups.1
  12.7 1.2 %collective-permute-start.3 = (s16[1,528,128]{2,1,0:T(8,128)(2,1)S(1)}, s16[1,528,128]{2,1,0:T(8,128)(2,1)S(1)}, u32[]{:S(2)}, u32[]{:S(2)}) collective-permute-start(s16[1,528,128]{2,1,0:T(8,128)(2,1)S(1)} %fold_groups.1), channel_id=1, source_target_pairs={{0,2},{1,3},{2,0},{3,1},{4,6},{5,7},{6,4},{7,5},{8,10},{9,11},{10,... | collective-permute-start | bytes 405512 | tf_op jit(solution)/shard_map/ppermute | solution.py:476
  13.9 4.7 %collective-permute-done.3.refs_2_ = s16[1,528,128]{2,1,0:T(8,128)(2,1)S(1)} collective-permute-done((s16[1,528,128]{2,1,0:T(8,128)(2,1)S(1)}, s16[1,528,128]{2,1,0:T(8,128)(2,1)S(1)}, u32[]{:S(2)}, u32[]{:S(2)}) %collective-permute-start.3) | collective-permute-done | bytes 135200 | tf_op jit(solution)/shard_map/ppermute | solution.py:476
  18.6 0.1 share_rows.1
  18.8 0.1 collective-permute-start.4
  18.9 3.1 %collective-permute-start.5 = (s16[144,128]{1,0:T(8,128)(2,1)S(1)}, s16[144,128]{1,0:T(8,128)(2,1)S(1)}, u32[]{:S(2)}, u32[]{:S(2)}) collective-permute-start(s16[144,128]{1,0:T(8,128)(2,1)S(1)} %get-tuple-element.22), channel_id=1, source_target_pairs={{8,0},{12,4},{0,8},{4,12},{9,1},{13,5},{1,9},{5,13},{10,2},{14,6},... | collective-permute-start | bytes 110600 | tf_op jit(solution)/shard_map/ppermute | solution.py:407
  22.0 0.7 %collective-permute-start.6 = (s16[144,128]{1,0:T(8,128)(2,1)S(1)}, s16[144,128]{1,0:T(8,128)(2,1)S(1)}, u32[]{:S(2)}, u32[]{:S(2)}) collective-permute-start(s16[144,128]{1,0:T(8,128)(2,1)S(1)} %get-tuple-element.23), channel_id=1, source_target_pairs={{4,0},{8,4},{12,8},{0,12},{5,1},{9,5},{13,9},{1,13},{6,2},{10,6},{... | collective-permute-start | bytes 110600 | tf_op jit(solution)/shard_map/ppermute | solution.py:407
  22.7 2.0 %collective-permute-done.4.refs_1_ = s16[144,128]{1,0:T(8,128)(2,1)S(1)} collective-permute-done((s16[144,128]{1,0:T(8,128)(2,1)S(1)}, s16[144,128]{1,0:T(8,128)(2,1)S(1)}, u32[]{:S(2)}, u32[]{:S(2)}) %collective-permute-start.4) | collective-permute-done | bytes 36896 | tf_op jit(solution)/shard_map/ppermute | solution.py:407
  24.6 0.0 collective-permute-done.5.refs_2_
  24.6 1.3 %collective-permute-done.6.refs_3_ = s16[144,128]{1,0:T(8,128)(2,1)S(1)} collective-permute-done((s16[144,128]{1,0:T(8,128)(2,1)S(1)}, s16[144,128]{1,0:T(8,128)(2,1)S(1)}, u32[]{:S(2)}, u32[]{:S(2)}) %collective-permute-start.6) | collective-permute-done | bytes 36896 | tf_op jit(solution)/shard_map/ppermute | solution.py:407
  26.0 2.5 %collective-permute-start.7 = (bf16[128,128]{1,0:T(8,128)(2,1)S(1)}, bf16[128,128]{1,0:T(8,128)(2,1)S(1)}, u32[]{:S(2)}, u32[]{:S(2)}) collective-permute-start(bf16[128,128]{1,0:T(8,128)(2,1)S(1)} %sum_shares.1.refs_2_), channel_id=1, source_target_pairs={{4,0},{8,4},{12,8},{0,12},{5,1},{9,5},{13,9},{1,13},{6,2},{10,6},{... | collective-permute-start | bytes 98312 | tf_op jit(solution)/shard_map/ppermute | solution.py:407
  28.5 0.2 collective-permute-start.8
  28.8 0.4 %collective-permute-start.9 = (bf16[128,128]{1,0:T(8,128)(2,1)S(1)}, bf16[128,128]{1,0:T(8,128)(2,1)S(1)}, u32[]{:S(2)}, u32[]{:S(2)}) collective-permute-start(bf16[128,128]{1,0:T(8,128)(2,1)S(1)} %sum_shares.1.refs_2_), channel_id=1, source_target_pairs={{12,0},{0,4},{4,8},{8,12},{13,1},{1,5},{5,9},{9,13},{14,2},{2,6},{... | collective-permute-start | bytes 98312 | tf_op jit(solution)/shard_map/ppermute | solution.py:407
  29.2 1.5 %collective-permute-start.10 = (bf16[128,128]{1,0:T(8,128)(2,1)S(1)}, bf16[128,128]{1,0:T(8,128)(2,1)S(1)}, u32[]{:S(2)}, u32[]{:S(2)}) collective-permute-start(bf16[128,128]{1,0:T(8,128)(2,1)S(1)} %sum_shares.1.refs_2_), channel_id=1, source_target_pairs={{16,0},{0,16},{17,1},{1,17},{18,2},{2,18},{19,3},{3,19},{20,4},{4,... | collective-permute-start | bytes 98312 | tf_op jit(solution)/shard_map/ppermute | solution.py:407
  30.7 0.0 collective-permute-done.7.refs_3_
  30.7 1.1 %collective-permute-start.11 = (bf16[128,128]{1,0:T(8,128)(2,1)S(1)}, bf16[128,128]{1,0:T(8,128)(2,1)S(1)}, u32[]{:S(2)}, u32[]{:S(2)}) collective-permute-start(bf16[128,128]{1,0:T(8,128)(2,1)S(1)} %collective-permute-done.7.refs_3_), channel_id=1, source_target_pairs={{16,0},{0,16},{17,1},{1,17},{18,2},{2,18},{19,3},{3,19},{20,4},{4,... | collective-permute-start | bytes 98312 | tf_op jit(solution)/shard_map/ppermute | solution.py:407
  31.8 1.5 %collective-permute-done.8.refs_4_ = bf16[128,128]{1,0:T(8,128)(2,1)S(1)} collective-permute-done((bf16[128,128]{1,0:T(8,128)(2,1)S(1)}, bf16[128,128]{1,0:T(8,128)(2,1)S(1)}, u32[]{:S(2)}, u32[]{:S(2)}) %collective-permute-start.8) | collective-permute-done | bytes 32800 | tf_op jit(solution)/shard_map/ppermute | solution.py:407
  33.3 1.5 %collective-permute-start.12 = (bf16[128,128]{1,0:T(8,128)(2,1)S(1)}, bf16[128,128]{1,0:T(8,128)(2,1)S(1)}, u32[]{:S(2)}, u32[]{:S(2)}) collective-permute-start(bf16[128,128]{1,0:T(8,128)(2,1)S(1)} %collective-permute-done.8.refs_4_), channel_id=1, source_target_pairs={{16,0},{0,16},{17,1},{1,17},{18,2},{2,18},{19,3},{3,19},{20,4},{4,... | collective-permute-start | bytes 98312 | tf_op jit(solution)/shard_map/ppermute | solution.py:407
  34.8 0.0 collective-permute-done.9.refs_5_
  34.8 1.1 %collective-permute-start.13 = (bf16[128,128]{1,0:T(8,128)(2,1)S(1)}, bf16[128,128]{1,0:T(8,128)(2,1)S(1)}, u32[]{:S(2)}, u32[]{:S(2)}) collective-permute-start(bf16[128,128]{1,0:T(8,128)(2,1)S(1)} %collective-permute-done.9.refs_5_), channel_id=1, source_target_pairs={{16,0},{0,16},{17,1},{1,17},{18,2},{2,18},{19,3},{3,19},{20,4},{4,... | collective-permute-start | bytes 98312 | tf_op jit(solution)/shard_map/ppermute | solution.py:407
  36.6 0.0 collective-permute-done.10.refs_6_
  36.6 0.0 collective-permute-done.11.refs_7_
  36.6 0.6 %collective-permute-done.12.refs_8_ = bf16[128,128]{1,0:T(8,128)(2,1)S(1)} collective-permute-done((bf16[128,128]{1,0:T(8,128)(2,1)S(1)}, bf16[128,128]{1,0:T(8,128)(2,1)S(1)}, u32[]{:S(2)}, u32[]{:S(2)}) %collective-permute-start.12) | collective-permute-done | bytes 32800 | tf_op jit(solution)/shard_map/ppermute | solution.py:407
  37.3 1.5 %collective-permute-done.13.refs_9_ = bf16[128,128]{1,0:T(8,128)(2,1)S(1)} collective-permute-done((bf16[128,128]{1,0:T(8,128)(2,1)S(1)}, bf16[128,128]{1,0:T(8,128)(2,1)S(1)}, u32[]{:S(2)}, u32[]{:S(2)}) %collective-permute-start.13) | collective-permute-done | bytes 32800 | tf_op jit(solution)/shard_map/ppermute | solution.py:407
  38.8 0.0 copy-done
  38.8 2.7 %contraction.1 = (f32[1,2,2,128,128]{4,3,2,1,0:T(8,128)}, f32[1,2,2]{2,1,0:T(2,128)}) custom-call(s32[1,2]{1,0:T(1,128)} %refs_0_.1, s32[1]{0:T(128)S(6)} %copy.10.refs_1_, bf16[128,128]{1,0:T(8,128)(2,1)S(1)} %sum_shares.1.refs_2_, bf16[128,128]{1,0:T(8,128)(2,1)S(1)} %collective-permute-done.7.refs_3_, ...), custom_call_target="tpu_custom_call" | custom-call | tf_op jit(solution)/shard_map/contraction/pallas_call | solution.py:504
  (1 shorter events, 0.0 us)
Async XLA Ops:
  0.6 8.0 %collective-permute-start = (bf16[1,2,144,128]{3,2,1,0:T(8,128)(2,1)}, bf16[1,2,144,128]{3,2,1,0:T(8,128)(2,1)S(1)}, u32[]{:S(2)}, u32[]{:S(2)}) collective-permute-start(bf16[1,2,144,128]{3,2,1,0:T(8,128)(2,1)} %bitcast.8), channel_id=1, source_target_pairs={{4,0},{8,4},{12,8},{0,12},{5,1},{9,5},{13,9},{1,13},{6,2},{10,6},{... | collective-permute-start | bytes 221192 | tf_op jit(solution)/shard_map/ppermute | solution.py:407
  5.7 3.0 %collective-permute-start.1 = (bf16[1,2,144,128]{3,2,1,0:T(8,128)(2,1)}, bf16[1,2,144,128]{3,2,1,0:T(8,128)(2,1)S(1)}, u32[]{:S(2)}, u32[]{:S(2)}) collective-permute-start(bf16[1,2,144,128]{3,2,1,0:T(8,128)(2,1)} %bitcast.9), channel_id=1, source_target_pairs={{1,0},{2,1},{3,2},{0,3},{5,4},{6,5},{7,6},{4,7},{9,8},{10,9},{11,1... | collective-permute-start | bytes 221192 | tf_op jit(solution)/shard_map/ppermute | solution.py:407
  10.1 28.7 %copy-start = (bf16[1,2,512,512]{3,2,1,0:T(8,128)(2,1)S(1)}, bf16[1,2,512,512]{3,2,1,0:T(8,128)(2,1)}, u32[]{:S(2)}) copy-start(bf16[1,2,512,512]{3,2,1,0:T(8,128)(2,1)} %param.12) | copy-start | bytes 3145732
  10.1 2.5 %collective-permute-start.2 = (f32[2,512,128]{2,1,0:T(8,128)S(1)}, f32[2,512,128]{2,1,0:T(8,128)S(1)}, u32[]{:S(2)}, u32[]{:S(2)}) collective-permute-start(f32[2,512,128]{2,1,0:T(8,128)S(1)} %get-tuple-element.18), channel_id=1, source_target_pairs={{0,1},{1,0},{2,3},{3,2},{4,5},{5,4},{6,7},{7,6},{8,9},{9,8},{10,11... | collective-permute-start | bytes 1572872 | tf_op jit(solution)/shard_map/ppermute | solution.py:476
  12.7 5.9 %collective-permute-start.3 = (s16[1,528,128]{2,1,0:T(8,128)(2,1)S(1)}, s16[1,528,128]{2,1,0:T(8,128)(2,1)S(1)}, u32[]{:S(2)}, u32[]{:S(2)}) collective-permute-start(s16[1,528,128]{2,1,0:T(8,128)(2,1)S(1)} %fold_groups.1), channel_id=1, source_target_pairs={{0,2},{1,3},{2,0},{3,1},{4,6},{5,7},{6,4},{7,5},{8,10},{9,11},{10,... | collective-permute-start | bytes 405512 | tf_op jit(solution)/shard_map/ppermute | solution.py:476
  18.8 5.8 %collective-permute-start.4 = (s16[144,128]{1,0:T(8,128)(2,1)S(1)}, s16[144,128]{1,0:T(8,128)(2,1)S(1)}, u32[]{:S(2)}, u32[]{:S(2)}) collective-permute-start(s16[144,128]{1,0:T(8,128)(2,1)S(1)} %get-tuple-element.21), channel_id=1, source_target_pairs={{12,0},{0,4},{4,8},{8,12},{13,1},{1,5},{5,9},{9,13},{14,2},{2,6},{... | collective-permute-start | bytes 110600 | tf_op jit(solution)/shard_map/ppermute | solution.py:407
  18.9 5.8 %collective-permute-start.5 = (s16[144,128]{1,0:T(8,128)(2,1)S(1)}, s16[144,128]{1,0:T(8,128)(2,1)S(1)}, u32[]{:S(2)}, u32[]{:S(2)}) collective-permute-start(s16[144,128]{1,0:T(8,128)(2,1)S(1)} %get-tuple-element.22), channel_id=1, source_target_pairs={{8,0},{12,4},{0,8},{4,12},{9,1},{13,5},{1,9},{5,13},{10,2},{14,6},... | collective-permute-start | bytes 110600 | tf_op jit(solution)/shard_map/ppermute | solution.py:407
  22.0 4.0 %collective-permute-start.6 = (s16[144,128]{1,0:T(8,128)(2,1)S(1)}, s16[144,128]{1,0:T(8,128)(2,1)S(1)}, u32[]{:S(2)}, u32[]{:S(2)}) collective-permute-start(s16[144,128]{1,0:T(8,128)(2,1)S(1)} %get-tuple-element.23), channel_id=1, source_target_pairs={{4,0},{8,4},{12,8},{0,12},{5,1},{9,5},{13,9},{1,13},{6,2},{10,6},{... | collective-permute-start | bytes 110600 | tf_op jit(solution)/shard_map/ppermute | solution.py:407
  26.0 4.7 %collective-permute-start.7 = (bf16[128,128]{1,0:T(8,128)(2,1)S(1)}, bf16[128,128]{1,0:T(8,128)(2,1)S(1)}, u32[]{:S(2)}, u32[]{:S(2)}) collective-permute-start(bf16[128,128]{1,0:T(8,128)(2,1)S(1)} %sum_shares.1.refs_2_), channel_id=1, source_target_pairs={{4,0},{8,4},{12,8},{0,12},{5,1},{9,5},{13,9},{1,13},{6,2},{10,6},{... | collective-permute-start | bytes 98312 | tf_op jit(solution)/shard_map/ppermute | solution.py:407
  28.5 4.8 %collective-permute-start.8 = (bf16[128,128]{1,0:T(8,128)(2,1)S(1)}, bf16[128,128]{1,0:T(8,128)(2,1)S(1)}, u32[]{:S(2)}, u32[]{:S(2)}) collective-permute-start(bf16[128,128]{1,0:T(8,128)(2,1)S(1)} %sum_shares.1.refs_2_), channel_id=1, source_target_pairs={{8,0},{12,4},{0,8},{4,12},{9,1},{13,5},{1,9},{5,13},{10,2},{14,6},... | collective-permute-start | bytes 98312 | tf_op jit(solution)/shard_map/ppermute | solution.py:407
  28.8 6.1 %collective-permute-start.9 = (bf16[128,128]{1,0:T(8,128)(2,1)S(1)}, bf16[128,128]{1,0:T(8,128)(2,1)S(1)}, u32[]{:S(2)}, u32[]{:S(2)}) collective-permute-start(bf16[128,128]{1,0:T(8,128)(2,1)S(1)} %sum_shares.1.refs_2_), channel_id=1, source_target_pairs={{12,0},{0,4},{4,8},{8,12},{13,1},{1,5},{5,9},{9,13},{14,2},{2,6},{... | collective-permute-start | bytes 98312 | tf_op jit(solution)/shard_map/ppermute | solution.py:407
  29.2 7.4 %collective-permute-start.10 = (bf16[128,128]{1,0:T(8,128)(2,1)S(1)}, bf16[128,128]{1,0:T(8,128)(2,1)S(1)}, u32[]{:S(2)}, u32[]{:S(2)}) collective-permute-start(bf16[128,128]{1,0:T(8,128)(2,1)S(1)} %sum_shares.1.refs_2_), channel_id=1, source_target_pairs={{16,0},{0,16},{17,1},{1,17},{18,2},{2,18},{19,3},{3,19},{20,4},{4,... | collective-permute-start | bytes 98312 | tf_op jit(solution)/shard_map/ppermute | solution.py:407
  30.7 6.0 %collective-permute-start.11 = (bf16[128,128]{1,0:T(8,128)(2,1)S(1)}, bf16[128,128]{1,0:T(8,128)(2,1)S(1)}, u32[]{:S(2)}, u32[]{:S(2)}) collective-permute-start(bf16[128,128]{1,0:T(8,128)(2,1)S(1)} %collective-permute-done.7.refs_3_), channel_id=1, source_target_pairs={{16,0},{0,16},{17,1},{1,17},{18,2},{2,18},{19,3},{3,19},{20,4},{4,... | collective-permute-start | bytes 98312 | tf_op jit(solution)/shard_map/ppermute | solution.py:407
  33.3 3.9 %collective-permute-start.12 = (bf16[128,128]{1,0:T(8,128)(2,1)S(1)}, bf16[128,128]{1,0:T(8,128)(2,1)S(1)}, u32[]{:S(2)}, u32[]{:S(2)}) collective-permute-start(bf16[128,128]{1,0:T(8,128)(2,1)S(1)} %collective-permute-done.8.refs_4_), channel_id=1, source_target_pairs={{16,0},{0,16},{17,1},{1,17},{18,2},{2,18},{19,3},{3,19},{20,4},{4,... | collective-permute-start | bytes 98312 | tf_op jit(solution)/shard_map/ppermute | solution.py:407
  34.8 3.9 %collective-permute-start.13 = (bf16[128,128]{1,0:T(8,128)(2,1)S(1)}, bf16[128,128]{1,0:T(8,128)(2,1)S(1)}, u32[]{:S(2)}, u32[]{:S(2)}) collective-permute-start(bf16[128,128]{1,0:T(8,128)(2,1)S(1)} %collective-permute-done.9.refs_5_), channel_id=1, source_target_pairs={{16,0},{0,16},{17,1},{1,17},{18,2},{2,18},{19,3},{3,19},{20,4},{4,... | collective-permute-start | bytes 98312 | tf_op jit(solution)/shard_map/ppermute | solution.py:407

commit v4 on v3

--- a/solution.py
+++ b/solution.py
@@ -292,28 +292,31 @@
         for b, ref in enumerate(received):
             total = total + arrived_block(ref.at[0], b, span, p)
         total_ref[p * span : (p + 1) * span] = total
-    rows = outs[0].shape[0]
+    if len(outs) == 1:
+        outs[0][...] = total_ref[...]
+        return
+    own_ref, sent_ref = outs
+    rows, count = own_ref.shape[0], sent_ref.shape[0]
     me = lax.axis_index("gx")
-    for step, out_ref in enumerate(outs):
-        chunk = lax.rem(me + step, len(outs))
-        total = total_ref[pl.ds(pl.multiple_of(chunk * rows, rows), rows)]
-        if step:
-            put_fixed(out_ref, [total])
-        else:
-            out_ref[...] = total
-
-
-def sum_kernel(norm_factor, *refs):
-    own_ref, received, out_ref = refs[0], refs[1:-1], refs[-1]
+    own_ref[...] = total_ref[pl.ds(pl.multiple_of(me * rows, rows), rows)]
+    for chunk in range(count):
+        put_fixed(sent_ref.at[chunk], [total_ref[chunk * rows : (chunk + 1) * rows]])
+
+
+def sum_kernel(norm_factor, own_ref, arrived_ref, out_ref):
     total = own_ref[...]
-    for ref in received:
-        total = total + from_fixed(ref, total.shape[0], 0)
-    out_ref[...] = (total * norm_factor).astype(out_ref.dtype)
-
-
-def contract_kernel(times, steps, *refs):
+    me = lax.axis_index("gx")
+    count = arrived_ref.shape[0]
+    for k in range(1, count):
+        total = total + from_fixed(arrived_ref.at[lax.rem(me + k, count)], total.shape[0], 0)
+    total = (total * norm_factor).astype(out_ref.dtype)
+    for k in range(count):
+        out_ref[k] = total
+
+
+def contract_kernel(times, *refs):
     pair_hbm, live_ref = refs[:2]
-    chunks, refs = refs[2 : 2 + times * steps], refs[2 + times * steps :]
+    blocks, refs = refs[2 : 2 + times], refs[2 + times :]
     tau_ref, margin_ref, corr_ref = refs[:3]
     every_ref, left_ref, right_ref, pair_ref, sem = refs[3:]
     f32 = jnp.float32
@@ -323,12 +326,9 @@
     count_ops = margin_ref.shape[1]
     order = tau_ref.shape[2]
     spins = order // vectors
-    me_t, me_x = lax.axis_index("ta"), lax.axis_index("gx")
-    rows = chunks[0].shape[0]
-    for k, ref in enumerate(chunks):
-        at_t = lax.rem(me_t + k // steps, times)
-        place = lax.rem(me_x + k % steps, steps) if steps > 1 else 0
-        every_ref[at_t, pl.ds(pl.multiple_of(place * rows, rows), rows)] = ref[...]
+    me_t = lax.axis_index("ta")
+    for k, ref in enumerate(blocks):
+        every_ref[lax.rem(me_t + k, times)] = ref[...]
     copy.wait()
     sink, source = pair_ref[0, 0], pair_ref[0, 1]
     live = live_ref[0] > 0
@@ -479,30 +479,30 @@
     steps = shares if direct else 1
     rows = own_rows // steps
     chunk_shapes = [jax.ShapeDtypeStruct((rows, vectors), f32)]
-    chunk_shapes += [jax.ShapeDtypeStruct((rows + TAIL, vectors), jnp.int16)] * (steps - 1)
+    if direct:
+        chunk_shapes.append(jax.ShapeDtypeStruct((steps, rows + TAIL, vectors), jnp.int16))
     chunks = local_call(
         functools.partial(share_kernel, levels, 2 * own_ops),
         "share_rows",
         tuple(chunk_shapes),
         [vmem_spec()] * (1 + levels),
-        (vmem_spec(),) * steps,
+        (vmem_spec(),) * len(chunk_shapes),
         [pltpu.VMEM((own_rows, vectors), f32)],
     )(parts[levels], *received)
     if direct:
-        arrived = [from_step(chunks[k], "gx", -k) for k in range(1, shares)]
         own = local_call(
             functools.partial(sum_kernel, norm_factor),
             "sum_shares",
-            jax.ShapeDtypeStruct((rows, vectors), bf16),
-            [vmem_spec()] * shares,
+            jax.ShapeDtypeStruct((steps, rows, vectors), bf16),
+            [vmem_spec()] * 2,
             vmem_spec(),
-        )(chunks[0], *arrived)
-        every = [own] + [from_step(own, "gx", k) for k in range(1, shares)]
+        )(chunks[0], lax.all_to_all(chunks[1], "gx", 0, 0, tiled=True))
+        own = lax.all_to_all(own, "gx", 0, 0, tiled=True).reshape(own_rows, vectors)
     else:
-        every = [(lax.psum(chunks[0], "gx") * norm_factor).astype(bf16)]
-    every += [from_step(every[k], "ta", t) for t in range(1, times) for k in range(steps)]
+        own = (lax.psum(chunks[0], "gx") * norm_factor).astype(bf16)
+    every = [own] + [from_step(own, "ta", t) for t in range(1, times)]
     margins, correlators = local_call(
-        functools.partial(contract_kernel, times, steps),
+        functools.partial(contract_kernel, times),
         "contraction",
         (
             jax.ShapeDtypeStruct((1, own_ops, 2, vectors, vectors), f32),

time: 41.7 us -> 45.5 us (1.091)
  blocking collectives: 0 us -> 18.6 us
  starting transfers between devices: 20.3 us -> 9.5 us
  waiting for transfers between devices: 13.2 us -> 9.1 us
    all_to_all x0 -> x2, blocking collectives: none -> 18.6 us  [the longest x1 10.3 us: per_device(): lax.all_to_all(chunks[1], 'gx', 0, 0, tiled=True)]
    ppermute x12 -> x3, starting transfers between devices: 18.1 us -> 7.27 us  [from_step(): lax.ppermute(block, axis, [((i + step) % count, i) for i in range(count)])]
    ppermute x12 -> x3, waiting for transfers between devices: 6.99 us -> 2.87 us  [from_step(): lax.ppermute(block, axis, [((i + step) % count, i) for i in range(count)])]
  transfers between devices with their start and end apart: 14 -> 5, of which waited for: 7 -> 3; matrix products, arithmetic and copies ran while one was open for 0% -> 0% of each run, Pallas kernels for 5% -> 5%
where the time goes in v4:
time: 45.5 us; the launch traced here: 45.2 us
  blocking collectives  18.6 us (41%)
  starting transfers between devices  9.5 us (21%)
  waiting for transfers between devices  9.1 us (20%)
  Pallas kernels  6.65 us (15%)
  between operations  1.33 us (3%)
    all_to_all x1, blocking collectives, per_device(): lax.all_to_all(chunks[1], 'gx', 0, 0, tiled=True)  10.3 us
    all_to_all x1, blocking collectives, per_device(): own = lax.all_to_all(own, 'gx', 0, 0, tiled=True).reshape(own_rows, vectors)  8.31 us
    ppermute x3, starting transfers between devices, from_step(): lax.ppermute(block, axis, [((i + step) % count, i) for i in range(count)])  7.27 us
    ppermute x2, waiting for transfers between devices, per_device(): lax.ppermute(sent, 'gy', [(i, i ^ 1 << b) for i in range(groups)])  6.23 us
    ppermute x3, waiting for transfers between devices, from_step(): lax.ppermute(block, axis, [((i + step) % count, i) for i in range(count)])  2.87 us
    pallas_call x1, Pallas kernels, per_device(): local_call(functools.partial(contract_kernel, times), 'contraction', (jax...  2.79 us
    pallas_call x1, Pallas kernels, per_device(): local_call(functools.partial(prepare_kernel, cells_x, cells_y), 'prepare_...  2.24 us
    ppermute x2, starting transfers between devices, per_device(): lax.ppermute(sent, 'gy', [(i, i ^ 1 << b) for i in range(groups)])  2.23 us
  transfers between devices with their start and end apart: 5, of which 3 were waited for; matrix products, arithmetic and copies ran while one was open for 0% of the time, Pallas kernels for 5%

profile of v4, /device:TPU:0, one launch (start us, length us, event | category | flops | bytes accessed | tf_op | source)
XLA Modules:
  0.0 45.2 jit_solution(8289817826864700310)
XLA Ops:
  0.6 5.1 %collective-permute-start = (bf16[1,2,144,128]{3,2,1,0:T(8,128)(2,1)}, bf16[1,2,144,128]{3,2,1,0:T(8,128)(2,1)S(1)}, u32[]{:S(2)}, u32[]{:S(2)}) collective-permute-start(bf16[1,2,144,128]{3,2,1,0:T(8,128)(2,1)} %bitcast.11), channel_id=1, source_target_pairs={{4,0},{8,4},{12,8},{0,12},{5,1},{9,5},{13,9},{1,13},{6,2},{10,6},{... | collective-permute-start | bytes 221192 | tf_op jit(solution)/shard_map/ppermute | solution.py:407
  5.7 0.7 %collective-permute-start.1 = (bf16[1,2,144,128]{3,2,1,0:T(8,128)(2,1)}, bf16[1,2,144,128]{3,2,1,0:T(8,128)(2,1)S(1)}, u32[]{:S(2)}, u32[]{:S(2)}) collective-permute-start(bf16[1,2,144,128]{3,2,1,0:T(8,128)(2,1)} %bitcast.12), channel_id=1, source_target_pairs={{1,0},{2,1},{3,2},{0,3},{5,4},{6,5},{7,6},{4,7},{9,8},{10,9},{11,1... | collective-permute-start | bytes 221192 | tf_op jit(solution)/shard_map/ppermute | solution.py:407
  6.4 2.2 %prepare_lines.1 = (bf16[3,144,128]{2,1,0:T(8,128)(2,1)S(1)}, f32[11,144,128]{2,1,0:T(8,128)S(1)}, bf16[2,128,288]{2,1,0:T(8,128)(2,1)S(1)}, f32[8,72,256]{2,1,0:T(8,128)S(1)}) custom-call(bf16[1,2,144,128]{3,2,1,0:T(8,128)(2,1)} %bitcast.13, bf16[2,27,2,24]{3,2,1,0:T(2,128)(2,1)} %bitcast.14, s32[8]{0:T(128)} %refs_6_.1, s32[8]{0:T(128)} %refs_3_.1, ...), custom_call_target="tpu_custom_call" | custom-call | tf_op jit(solution)/shard_map/prepare_lines/pallas_call | solution.py:431
  8.7 0.0 collective-permute-done.refs_4_
  8.7 0.0 collective-permute-done.1.refs_5_
  8.7 1.3 %partial_margins.1 = (f32[2,512,128]{2,1,0:T(8,128)S(1)}, f32[1,512,128]{2,1,0:T(8,128)S(1)}, f32[1,512,128]{2,1,0:T(8,128)S(1)}) custom-call(bf16[3,144,128]{2,1,0:T(8,128)(2,1)S(1)} %get-tuple-element.11.refs_0_, f32[11,144,128]{2,1,0:T(8,128)S(1)} %get-tuple-element.12.refs_1_, bf16[2,128,288]{2,1,0:T(8,128)(2,1)S(1)} %get-tuple-element.13.refs_2_, ...), custom_call_target="tpu_custom_call" | custom-call | tf_op jit(solution)/shard_map/partial_margins/pallas_call | solution.py:452
  10.1 1.0 %collective-permute-start.2 = (f32[2,512,128]{2,1,0:T(8,128)S(1)}, f32[2,512,128]{2,1,0:T(8,128)S(1)}, u32[]{:S(2)}, u32[]{:S(2)}) collective-permute-start(f32[2,512,128]{2,1,0:T(8,128)S(1)} %get-tuple-element.16), channel_id=1, source_target_pairs={{0,1},{1,0},{2,3},{3,2},{4,5},{5,4},{6,7},{7,6},{8,9},{9,8},{10,11... | collective-permute-start | bytes 1572872 | tf_op jit(solution)/shard_map/ppermute | solution.py:476
  11.1 1.5 %collective-permute-done.2.refs_1_ = f32[2,512,128]{2,1,0:T(8,128)S(1)} collective-permute-done((f32[2,512,128]{2,1,0:T(8,128)S(1)}, f32[2,512,128]{2,1,0:T(8,128)S(1)}, u32[]{:S(2)}, u32[]{:S(2)}) %collective-permute-start.2) | collective-permute-done | bytes 524320 | tf_op jit(solution)/shard_map/ppermute | solution.py:476
  12.6 0.1 fold_groups.1
  12.7 0.0 copy-start
  12.7 1.2 %collective-permute-start.3 = (s16[1,528,128]{2,1,0:T(8,128)(2,1)S(1)}, s16[1,528,128]{2,1,0:T(8,128)(2,1)S(1)}, u32[]{:S(2)}, u32[]{:S(2)}) collective-permute-start(s16[1,528,128]{2,1,0:T(8,128)(2,1)S(1)} %fold_groups.1), channel_id=1, source_target_pairs={{0,2},{1,3},{2,0},{3,1},{4,6},{5,7},{6,4},{7,5},{8,10},{9,11},{10,... | collective-permute-start | bytes 405512 | tf_op jit(solution)/shard_map/ppermute | solution.py:476
  13.9 4.7 %collective-permute-done.3.refs_2_ = s16[1,528,128]{2,1,0:T(8,128)(2,1)S(1)} collective-permute-done((s16[1,528,128]{2,1,0:T(8,128)(2,1)S(1)}, s16[1,528,128]{2,1,0:T(8,128)(2,1)S(1)}, u32[]{:S(2)}, u32[]{:S(2)}) %collective-permute-start.3) | collective-permute-done | bytes 135200 | tf_op jit(solution)/shard_map/ppermute | solution.py:476
  18.6 0.1 share_rows.1
  18.8 10.3 %all_to_all.10.arrived_ref = s16[4,144,128]{2,1,0:T(8,128)(2,1)S(1)} all-to-all(s16[4,144,128]{2,1,0:T(8,128)(2,1)S(1)} %get-tuple-element.19), channel_id=1, replica_groups=mesh['ta'=2,'gx'=4,'gy'=4] {'gx'}, dimensions={0} | all-to-all | bytes 294912 | tf_op jit(solution)/shard_map/all_to_all | solution.py:499
  29.2 8.3 %all_to_all.11 = bf16[4,128,128]{2,1,0:T(8,128)(2,1)S(1)} all-to-all(bf16[4,128,128]{2,1,0:T(8,128)(2,1)S(1)} %sum_shares.1), channel_id=1, replica_groups=mesh['ta'=2,'gx'=4,'gy'=4] {'gx'}, dimensions={0} | all-to-all | bytes 262144 | tf_op jit(solution)/shard_map/all_to_all | solution.py:500
  37.5 1.5 %collective-permute-start.4 = (bf16[512,128]{1,0:T(8,128)(2,1)S(1)}, bf16[512,128]{1,0:T(8,128)(2,1)S(1)}, u32[]{:S(2)}, u32[]{:S(2)}) collective-permute-start(bf16[512,128]{1,0:T(8,128)(2,1)S(1)} %bitcast.9), channel_id=1, source_target_pairs={{16,0},{0,16},{17,1},{1,17},{18,2},{2,18},{19,3},{3,19},{20,4},{4,... | collective-permute-start | bytes 393224 | tf_op jit(solution)/shard_map/ppermute | solution.py:407
  39.6 2.8 %collective-permute-done.4.refs_3_ = bf16[512,128]{1,0:T(8,128)(2,1)S(1)} collective-permute-done((bf16[512,128]{1,0:T(8,128)(2,1)S(1)}, bf16[512,128]{1,0:T(8,128)(2,1)S(1)}, u32[]{:S(2)}, u32[]{:S(2)}) %collective-permute-start.4) | collective-permute-done | bytes 131104 | tf_op jit(solution)/shard_map/ppermute | solution.py:407
  42.4 0.0 copy-done
  42.4 2.8 %contraction.1 = (f32[1,2,2,128,128]{4,3,2,1,0:T(8,128)}, f32[1,2,2]{2,1,0:T(2,128)}) custom-call(s32[1,2]{1,0:T(1,128)} %refs_0_.1, s32[1]{0:T(128)S(6)} %copy.10.refs_1_, bf16[512,128]{1,0:T(8,128)(2,1)S(1)} %bitcast.10, bf16[512,128]{1,0:T(8,128)(2,1)S(1)} %collective-permute-done.4.refs_3_, bf16[2,512,512]{2,1,0:T(8,128)(2,1)S(1)} %bitcast.8), custom_call_target="tpu_custom_call" | custom-call | tf_op jit(solution)/shard_map/contraction/pallas_call | solution.py:504
  (1 shorter events, 0.0 us)
Async XLA Ops:
  0.6 8.0 %collective-permute-start = (bf16[1,2,144,128]{3,2,1,0:T(8,128)(2,1)}, bf16[1,2,144,128]{3,2,1,0:T(8,128)(2,1)S(1)}, u32[]{:S(2)}, u32[]{:S(2)}) collective-permute-start(bf16[1,2,144,128]{3,2,1,0:T(8,128)(2,1)} %bitcast.11), channel_id=1, source_target_pairs={{4,0},{8,4},{12,8},{0,12},{5,1},{9,5},{13,9},{1,13},{6,2},{10,6},{... | collective-permute-start | bytes 221192 | tf_op jit(solution)/shard_map/ppermute | solution.py:407
  5.7 3.0 %collective-permute-start.1 = (bf16[1,2,144,128]{3,2,1,0:T(8,128)(2,1)}, bf16[1,2,144,128]{3,2,1,0:T(8,128)(2,1)S(1)}, u32[]{:S(2)}, u32[]{:S(2)}) collective-permute-start(bf16[1,2,144,128]{3,2,1,0:T(8,128)(2,1)} %bitcast.12), channel_id=1, source_target_pairs={{1,0},{2,1},{3,2},{0,3},{5,4},{6,5},{7,6},{4,7},{9,8},{10,9},{11,1... | collective-permute-start | bytes 221192 | tf_op jit(solution)/shard_map/ppermute | solution.py:407
  10.1 2.5 %collective-permute-start.2 = (f32[2,512,128]{2,1,0:T(8,128)S(1)}, f32[2,512,128]{2,1,0:T(8,128)S(1)}, u32[]{:S(2)}, u32[]{:S(2)}) collective-permute-start(f32[2,512,128]{2,1,0:T(8,128)S(1)} %get-tuple-element.16), channel_id=1, source_target_pairs={{0,1},{1,0},{2,3},{3,2},{4,5},{5,4},{6,7},{7,6},{8,9},{9,8},{10,11... | collective-permute-start | bytes 1572872 | tf_op jit(solution)/shard_map/ppermute | solution.py:476
  12.7 29.7 %copy-start = (bf16[1,2,512,512]{3,2,1,0:T(8,128)(2,1)S(1)}, bf16[1,2,512,512]{3,2,1,0:T(8,128)(2,1)}, u32[]{:S(2)}) copy-start(bf16[1,2,512,512]{3,2,1,0:T(8,128)(2,1)} %param.12) | copy-start | bytes 3145732
  12.7 5.9 %collective-permute-start.3 = (s16[1,528,128]{2,1,0:T(8,128)(2,1)S(1)}, s16[1,528,128]{2,1,0:T(8,128)(2,1)S(1)}, u32[]{:S(2)}, u32[]{:S(2)}) collective-permute-start(s16[1,528,128]{2,1,0:T(8,128)(2,1)S(1)} %fold_groups.1), channel_id=1, source_target_pairs={{0,2},{1,3},{2,0},{3,1},{4,6},{5,7},{6,4},{7,5},{8,10},{9,11},{10,... | collective-permute-start | bytes 405512 | tf_op jit(solution)/shard_map/ppermute | solution.py:476
  37.5 5.0 %collective-permute-start.4 = (bf16[512,128]{1,0:T(8,128)(2,1)S(1)}, bf16[512,128]{1,0:T(8,128)(2,1)S(1)}, u32[]{:S(2)}, u32[]{:S(2)}) collective-permute-start(bf16[512,128]{1,0:T(8,128)(2,1)S(1)} %bitcast.9), channel_id=1, source_target_pairs={{16,0},{0,16},{17,1},{1,17},{18,2},{2,18},{19,3},{3,19},{20,4},{4,... | collective-permute-start | bytes 393224 | tf_op jit(solution)/shard_map/ppermute | solution.py:407

commit v5 on v3

--- a/solution.py
+++ b/solution.py
@@ -178,20 +178,46 @@
         )
 
 
+def write_margins(slots, own_ops, field_ref, side_ref, phase_ref, dirs_ref, lines):
+    f32, bf16 = jnp.float32, jnp.bfloat16
+    order, vectors = field_ref.shape[2], field_ref.shape[3]
+    half = order // 2
+    me = lax.axis_index("gy")
+    for j, out_ref, place in slots:
+        for i in range(own_ops):
+            o = (me ^ j) * own_ops + i
+            code = dirs_ref[o]
+            side = jnp.where((code >= 3) & (code < 6), code - 2, 0)
+            cosine = phase_ref[o, :, 0:vectors]
+            sine = phase_ref[o, :, vectors : 2 * vectors]
+            pairs = []
+            for line in range(lines):
+                real, imag = field_ref[code, line, 0:half], field_ref[code, line, half:order]
+                turned_r, turned_i = cosine * real - sine * imag, sine * real + cosine * imag
+                pairs.append(jnp.concatenate([turned_r, turned_i], axis=1))
+                pairs.append(jnp.concatenate([turned_i, -turned_r], axis=1))
+            product = jnp.dot(
+                side_ref[side],
+                jnp.concatenate(pairs, axis=0).astype(bf16),
+                preferred_element_type=f32,
+            )
+            first = 2 * i * vectors
+            out_ref[place, first : first + vectors] = product[:, :vectors]
+            out_ref[place, first + vectors : first + 2 * vectors] = product[:, vectors:]
+
+
 def low_bit(j):
     return (j & -j).bit_length() - 1
 
 
-def margin_kernel(cells_x, cells_y, groups, *refs):
+def first_margin_kernel(cells_x, cells_y, groups, own_ops, *refs):
     matrix_ref, local_ref, left_ref, phase_ref, halo_x_ref, halo_y_ref, dirs_hbm = refs[:7]
-    levels = groups.bit_length() - 1
-    out_refs = refs[7 : 8 + levels]
-    field_ref, side_ref, dirs_ref, sem = refs[8 + levels :]
+    swap_ref, hold_ref, field_ref, side_ref, dirs_ref, sem = refs[7:]
     f32, bf16 = jnp.float32, jnp.bfloat16
     copy = pltpu.make_async_copy(dirs_hbm, dirs_ref, sem)
     copy.start()
     lines = cells_x * cells_y
-    order, vectors = halo_x_ref.shape[2], halo_x_ref.shape[3]
+    order = halo_x_ref.shape[2]
     half = order // 2
     planar = planar_order(order)
     side_ref[0] = left_ref[0]
@@ -213,33 +239,22 @@
     for k, (code, line) in enumerate(local_fields(cells_x, cells_y)):
         field_ref[code, line] = local_ref[k]
     copy.wait()
-    count_ops = dirs_ref.shape[0]
-    own_ops = count_ops // groups
-    me = lax.axis_index("gy")
-    for j in range(groups):
-        for i in range(own_ops):
-            o = (me ^ j) * own_ops + i
-            code = dirs_ref[o]
-            side = jnp.where((code >= 3) & (code < 6), code - 2, 0)
-            cosine = phase_ref[o, :, 0:vectors]
-            sine = phase_ref[o, :, vectors : 2 * vectors]
-            pairs = []
-            for line in range(lines):
-                real, imag = field_ref[code, line, 0:half], field_ref[code, line, half:order]
-                turned_r, turned_i = cosine * real - sine * imag, sine * real + cosine * imag
-                pairs.append(jnp.concatenate([turned_r, turned_i], axis=1))
-                pairs.append(jnp.concatenate([turned_i, -turned_r], axis=1))
-            product = jnp.dot(
-                side_ref[side],
-                jnp.concatenate(pairs, axis=0).astype(bf16),
-                preferred_element_type=f32,
-            )
-            level = levels if j == 0 else low_bit(j)
-            out_ref = out_refs[level]
-            place = 0 if j == 0 else j >> (level + 1)
-            first = 2 * i * vectors
-            out_ref[place, first : first + vectors] = product[:, :vectors]
-            out_ref[place, first + vectors : first + 2 * vectors] = product[:, vectors:]
+    slots = [(j, swap_ref if j & 1 else hold_ref, j >> 2) for j in range(groups) if j & 2]
+    slots.sort(key=lambda slot: -(slot[0] & 1))
+    write_margins(slots, own_ops, field_ref, side_ref, phase_ref, dirs_ref, lines)
+
+
+def second_margin_kernel(lines, groups, own_ops, *refs):
+    field_ref, side_ref, phase_ref, dirs_hbm, swap_ref = refs[:5]
+    hold_refs, dirs_ref, sem = refs[5:-2], refs[-2], refs[-1]
+    copy = pltpu.make_async_copy(dirs_hbm, dirs_ref, sem)
+    copy.start()
+    copy.wait()
+    slots = [(j, swap_ref, j >> 2) for j in range(groups) if j & 3 == 1]
+    for j in range(0, groups, 4):
+        level = low_bit(j) if j else groups.bit_length() - 1
+        slots.append((j, hold_refs[level - 2], j >> (level + 1)))
+    write_margins(slots, own_ops, field_ref, side_ref, phase_ref, dirs_ref, lines)
 
 
 def scale_of(block):
@@ -265,22 +280,23 @@
     return block * jnp.exp2(scales[k : k + 1] - FIXED_BITS)
 
 
+def arrived_block(received, j, rows, p):
+    total = received[0][j >> 2, p * rows : (p + 1) * rows]
+    for b, ref in enumerate(received[1:], 1):
+        total = total + from_fixed(ref.at[j >> (b + 1)], rows, p)
+    return total
+
+
 def fold_kernel(level, count_blocks, *refs):
     held_ref, received, out_ref = refs[0], refs[1:-1], refs[-1]
     rows = held_ref.shape[1] // count_blocks
     for k in range(held_ref.shape[0]):
         j = (2 * k + 1) << level
-        blocks = []
-        for p in range(count_blocks):
-            total = held_ref[k, p * rows : (p + 1) * rows]
-            for b, ref in enumerate(received):
-                total = total + arrived_block(ref.at[j >> (b + 1)], b, rows, p)
-            blocks.append(total)
+        blocks = [
+            held_ref[k, p * rows : (p + 1) * rows] + arrived_block(received, j, rows, p)
+            for p in range(count_blocks)
+        ]
         put_fixed(out_ref.at[k], blocks)
-
-
-def arrived_block(ref, level, rows, p):
-    return ref[p * rows : (p + 1) * rows] if level == 0 else from_fixed(ref, rows, p)
 
 
 def share_kernel(levels, count_blocks, *refs):
@@ -288,19 +304,23 @@
     outs, total_ref = refs[:-1], refs[-1]
     span = held_ref.shape[1] // count_blocks
     for p in range(count_blocks):
-        total = held_ref[0, p * span : (p + 1) * span]
-        for b, ref in enumerate(received):
-            total = total + arrived_block(ref.at[0], b, span, p)
-        total_ref[p * span : (p + 1) * span] = total
+        here = slice(p * span, (p + 1) * span)
+        total_ref[here] = held_ref[0, here] + arrived_block(received, 0, span, p)
     rows = outs[0].shape[0]
     me = lax.axis_index("gx")
     for step, out_ref in enumerate(outs):
-        chunk = lax.rem(me + step, len(outs))
+        chunk = partner_of(me, step, len(outs))
         total = total_ref[pl.ds(pl.multiple_of(chunk * rows, rows), rows)]
         if step:
             put_fixed(out_ref, [total])
         else:
             out_ref[...] = total
+
+
+def partner_of(me, step, count):
+    if count & (count - 1) == 0:
+        return me ^ step
+    return (me + step) % count
 
 
 def sum_kernel(norm_factor, *refs):
@@ -327,7 +347,7 @@
     rows = chunks[0].shape[0]
     for k, ref in enumerate(chunks):
         at_t = lax.rem(me_t + k // steps, times)
-        place = lax.rem(me_x + k % steps, steps) if steps > 1 else 0
+        place = partner_of(me_x, k % steps, steps)
         every_ref[at_t, pl.ds(pl.multiple_of(place * rows, rows), rows)] = ref[...]
     copy.wait()
     sink, source = pair_ref[0, 0], pair_ref[0, 1]
@@ -339,38 +359,44 @@
         margin_ref[0, o, 1] = part(me_t, 1).astype(f32)
         a_r, a_i = part(sink, 0), part(sink, 1)
         b_r, b_i = part(source, 0).T, part(source, 1).T
-        left_ref[o, 0:vectors, 0:vectors] = a_r
-        left_ref[o, 0:vectors, vectors:] = -a_i
-        left_ref[o, vectors:, 0:vectors] = a_i
-        left_ref[o, vectors:, vectors:] = a_r
-        right_ref[o, 0:vectors, 0:vectors] = b_r
-        right_ref[o, 0:vectors, vectors:] = -b_i
-        right_ref[o, vectors:, 0:vectors] = b_i
-        right_ref[o, vectors:, vectors:] = b_r
-        real = jnp.zeros((8, vectors), f32)
-        imag = jnp.zeros((8, vectors), f32)
-        fold = lambda t: jnp.sum(t.reshape(vectors // 8, 8, vectors), axis=0)
-        for s in range(spins):
-            rows = slice(s * vectors, (s + 1) * vectors)
-            x = jnp.dot(
-                left_ref[o],
-                jnp.concatenate([tau_ref[0, rows], tau_ref[1, rows]], axis=0),
+        real, imag = slice(first, first + vectors), slice(first + vectors, first + 2 * vectors)
+        left_ref[real, 0:vectors] = a_r
+        left_ref[real, vectors:] = -a_i
+        left_ref[imag, 0:vectors] = a_i
+        left_ref[imag, vectors:] = a_r
+        right_ref[0:vectors, real] = b_r
+        right_ref[0:vectors, imag] = -b_i
+        right_ref[vectors:, real] = b_i
+        right_ref[vectors:, imag] = b_r
+    lanes = 32
+    fold = lambda t: jnp.sum(t.reshape(vectors // lanes, lanes, vectors), axis=0)
+    sums = [[jnp.zeros((lanes, vectors), f32) for _ in range(2)] for _ in range(count_ops)]
+    for s in range(spins):
+        rows = slice(s * vectors, (s + 1) * vectors)
+        x = jnp.dot(
+            left_ref[...],
+            jnp.concatenate([tau_ref[0, rows], tau_ref[1, rows]], axis=0),
+            preferred_element_type=f32,
+        )
+        for c in range(spins):
+            cols = slice(c * vectors, (c + 1) * vectors)
+            y = jnp.dot(
+                jnp.concatenate([tau_ref[0, rows, cols], tau_ref[1, rows, cols]], axis=1),
+                right_ref[...],
                 preferred_element_type=f32,
             )
-            for c in range(spins):
-                cols = slice(c * vectors, (c + 1) * vectors)
-                y = jnp.dot(
-                    jnp.concatenate([tau_ref[0, rows, cols], tau_ref[1, rows, cols]], axis=1),
-                    right_ref[o],
-                    preferred_element_type=f32,
-                )
-                x_r, x_i = x[:vectors, cols], x[vectors:, cols]
-                y_r, y_i = y[:, :vectors], y[:, vectors:]
-                real = real + fold(x_r * y_r + x_i * y_i)
-                imag = imag + fold(x_i * y_r - x_r * y_i)
-        scale = 1.0 / vectors
-        corr_ref[0, o, 0] = jnp.where(live, jnp.sum(real) * scale, 0.0)
-        corr_ref[0, o, 1] = jnp.where(live, jnp.sum(imag) * scale, 0.0)
+            for o in range(count_ops):
+                first = 2 * o * vectors
+                x_r = x[first : first + vectors, cols]
+                x_i = x[first + vectors : first + 2 * vectors, cols]
+                y_r = y[:, first : first + vectors]
+                y_i = y[:, first + vectors : first + 2 * vectors]
+                sums[o][0] = sums[o][0] + fold(x_r * y_r + x_i * y_i)
+                sums[o][1] = sums[o][1] + fold(x_i * y_r - x_r * y_i)
+    scale = 1.0 / vectors
+    for o in range(count_ops):
+        for k in range(2):
+            corr_ref[0, o, k] = jnp.where(live, jnp.sum(sums[o][k]) * scale, 0.0)
 
 
 def vmem_spec():
@@ -405,6 +431,16 @@
 def from_step(block, axis, step):
     count = lax.axis_size(axis)
     return lax.ppermute(block, axis, [((i + step) % count, i) for i in range(count)])
+
+
+def from_partner(block, axis, step):
+    count = lax.axis_size(axis)
+    return lax.ppermute(block, axis, [(partner_of(i, step, count), i) for i in range(count)])
+
+
+def to_partner(block, axis, step):
+    count = lax.axis_size(axis)
+    return lax.ppermute(block, axis, [(i, partner_of(i, step, count)) for i in range(count)])
 
 
 def per_device(eigvecs, links, op_dirs, op_moms, perams, pair_times, slot_counts):
@@ -445,35 +481,43 @@
             pltpu.SemaphoreType.DMA((len(inputs),)),
         ],
     )(*inputs)
-    part_shapes = [
-        jax.ShapeDtypeStruct((groups >> (b + 1), own_rows, vectors), f32)
-        for b in range(levels)
-    ] + [jax.ShapeDtypeStruct((1, own_rows, vectors), f32)]
-    parts = local_call(
-        functools.partial(margin_kernel, cells_x, cells_y, groups),
-        "partial_margins",
-        tuple(part_shapes),
+    part = lambda count: jax.ShapeDtypeStruct((count, own_rows, vectors), f32)
+    dirs = in_hbm(op_dirs)
+    dirs_scratch = [pltpu.SMEM((count_ops,), jnp.int32), pltpu.SemaphoreType.DMA]
+    swap_a, hold_a, fields, sides = local_call(
+        functools.partial(first_margin_kernel, cells_x, cells_y, groups, own_ops),
+        "first_margins",
+        (
+            part(groups // 4),
+            part(groups // 4),
+            jax.ShapeDtypeStruct((7, lines, order, vectors), f32),
+            jax.ShapeDtypeStruct((4, vectors, lines * order), bf16),
+        ),
         [vmem_spec()] * 6 + [hbm_spec()],
-        (vmem_spec(),) * len(part_shapes),
-        [
-            pltpu.VMEM((7, lines, order, vectors), f32),
-            pltpu.VMEM((4, vectors, lines * order), bf16),
-            pltpu.SMEM((count_ops,), jnp.int32),
-            pltpu.SemaphoreType.DMA,
-        ],
-    )(matrices, local, left, phases, halo_x, halo_y, in_hbm(op_dirs))
-    received = []
-    for b in range(levels):
-        sent = parts[b]
-        if b:
-            sent = local_call(
-                functools.partial(fold_kernel, b, 2 * own_ops),
-                "fold_groups",
-                jax.ShapeDtypeStruct((sent.shape[0], own_rows + TAIL, vectors), jnp.int16),
-                [vmem_spec()] * (1 + b),
-                vmem_spec(),
-            )(sent, *received)
-        received.append(lax.ppermute(sent, "gy", [(i, i ^ (1 << b)) for i in range(groups)]))
+        (vmem_spec(),) * 4,
+        dirs_scratch,
+    )(matrices, local, left, phases, halo_x, halo_y, dirs)
+    swapped_a = from_partner(swap_a, "gy", 1)
+    held_shapes = [part(groups >> (b + 1)) for b in range(2, levels)] + [part(1)]
+    swap_b, *held = local_call(
+        functools.partial(second_margin_kernel, lines, groups, own_ops),
+        "second_margins",
+        (part(groups // 4), *held_shapes),
+        [vmem_spec()] * 3 + [hbm_spec()],
+        (vmem_spec(),) * (1 + len(held_shapes)),
+        dirs_scratch,
+    )(fields, sides, phases, dirs)
+    received = [from_partner(swap_b, "gy", 1)]
+    for b in range(1, levels):
+        inputs = (hold_a, swapped_a) if b == 1 else (held[b - 2], *received)
+        sent = local_call(
+            functools.partial(fold_kernel, b, 2 * own_ops),
+            "fold_groups",
+            jax.ShapeDtypeStruct((inputs[0].shape[0], own_rows + TAIL, vectors), jnp.int16),
+            [vmem_spec()] * len(inputs),
+            vmem_spec(),
+        )(*inputs)
+        received.append(from_partner(sent, "gy", 1 << b))
     norm_factor = 1.0 / math.sqrt(3.0 * cells_x * shares * cells_y * groups * cells_z)
     direct = shares <= DIRECT_LIMIT and own_rows % (16 * shares) == 0
     steps = shares if direct else 1
@@ -487,9 +531,9 @@
         [vmem_spec()] * (1 + levels),
         (vmem_spec(),) * steps,
         [pltpu.VMEM((own_rows, vectors), f32)],
-    )(parts[levels], *received)
+    )(held[-1], *received)
     if direct:
-        arrived = [from_step(chunks[k], "gx", -k) for k in range(1, shares)]
+        arrived = [to_partner(chunks[k], "gx", k) for k in range(1, shares)]
         own = local_call(
             functools.partial(sum_kernel, norm_factor),
             "sum_shares",
@@ -497,7 +541,7 @@
             [vmem_spec()] * shares,
             vmem_spec(),
         )(chunks[0], *arrived)
-        every = [own] + [from_step(own, "gx", k) for k in range(1, shares)]
+        every = [own] + [from_partner(own, "gx", k) for k in range(1, shares)]
     else:
         every = [(lax.psum(chunks[0], "gx") * norm_factor).astype(bf16)]
     every += [from_step(every[k], "ta", t) for t in range(1, times) for k in range(steps)]
@@ -512,8 +556,8 @@
         (vmem_spec(), smem_spec()),
         [
             pltpu.VMEM((times, own_rows, vectors), bf16),
-            pltpu.VMEM((own_ops, 2 * vectors, 2 * vectors), bf16),
-            pltpu.VMEM((own_ops, 2 * vectors, 2 * vectors), bf16),
+            pltpu.VMEM((own_rows, 2 * vectors), bf16),
+            pltpu.VMEM((2 * vectors, own_rows), bf16),
             pltpu.SMEM((1, 2), jnp.int32),
             pltpu.SemaphoreType.DMA,
         ],

time: 41.7 us -> 42.1 us (level)
  waiting for transfers between devices: 13.2 us -> 11.4 us
  starting transfers between devices: 20.3 us -> 21.6 us
  Pallas kernels: 6.58 us -> 7.47 us
    ppermute x2 -> x9, starting transfers between devices: 2.23 us -> 11.2 us  [the longest x6 6.74 us: from_partner(): lax.ppermute(block, axis, [(partner_of(i, step, count), i) for i in range...]
    ppermute x12 -> x6, starting transfers between devices: 18.1 us -> 10.5 us  [from_step(): lax.ppermute(block, axis, [((i + step) % count, i) for i in range(count)])]
    ppermute x12 -> x6, waiting for transfers between devices: 6.99 us -> 2.15 us  [from_step(): lax.ppermute(block, axis, [((i + step) % count, i) for i in range(count)])]
    ppermute x2 -> x9, waiting for transfers between devices: 6.23 us -> 9.3 us  [the longest x6 4.84 us: from_partner(): lax.ppermute(block, axis, [(partner_of(i, step, count), i) for i in range...]
    pallas_call x1 -> x2, Pallas kernels: 1.34 us -> 2.28 us  [the longest x1 1.27 us: per_device(): local_call(functools.partial(first_margin_kernel, cells_x, cells_y, group...]
  transfers between devices with their start and end apart: 14 -> 15, of which waited for: 7 -> 8; matrix products, arithmetic and copies ran while one was open for 0% -> 0% of each run, Pallas kernels for 5% -> 8%
where the time goes in v5:
time: 42.1 us; the launch traced here: 41.9 us
  starting transfers between devices  21.6 us (51%)
  waiting for transfers between devices  11.4 us (27%)
  Pallas kernels  7.47 us (18%)
  between operations  1.37 us (3%)
    ppermute x6, starting transfers between devices, from_step(): lax.ppermute(block, axis, [((i + step) % count, i) for i in range(count)])  10.5 us
    ppermute x6, starting transfers between devices, from_partner(): lax.ppermute(block, axis, [(partner_of(i, step, count), i) for i in range...  6.74 us
    ppermute x6, waiting for transfers between devices, from_partner(): lax.ppermute(block, axis, [(partner_of(i, step, count), i) for i in range...  4.84 us
    ppermute x3, waiting for transfers between devices, to_partner(): lax.ppermute(block, axis, [(i, partner_of(i, step, count)) for i in range...  4.45 us
    ppermute x3, starting transfers between devices, to_partner(): lax.ppermute(block, axis, [(i, partner_of(i, step, count)) for i in range...  4.44 us
    pallas_call x1, Pallas kernels, per_device(): local_call(functools.partial(contract_kernel, times, steps), 'contraction...  2.7 us
    pallas_call x1, Pallas kernels, per_device(): local_call(functools.partial(prepare_kernel, cells_x, cells_y), 'prepare_...  2.24 us
    ppermute x6, waiting for transfers between devices, from_step(): lax.ppermute(block, axis, [((i + step) % count, i) for i in range(count)])  2.15 us
  transfers between devices with their start and end apart: 15, of which 8 were waited for; matrix products, arithmetic and copies ran while one was open for 0% of the time, Pallas kernels for 8%

profile of v5, /device:TPU:0, one launch (start us, length us, event | category | flops | bytes accessed | tf_op | source)
XLA Modules:
  0.0 41.9 jit_solution(3672389350783551321)
XLA Ops:
  0.6 5.1 %collective-permute-start = (bf16[1,2,144,128]{3,2,1,0:T(8,128)(2,1)}, bf16[1,2,144,128]{3,2,1,0:T(8,128)(2,1)S(1)}, u32[]{:S(2)}, u32[]{:S(2)}) collective-permute-start(bf16[1,2,144,128]{3,2,1,0:T(8,128)(2,1)} %bitcast.8), channel_id=1, source_target_pairs={{4,0},{8,4},{12,8},{0,12},{5,1},{9,5},{13,9},{1,13},{6,2},{10,6},{... | collective-permute-start | bytes 221192 | tf_op jit(solution)/shard_map/ppermute | solution.py:433
  5.7 0.7 %collective-permute-start.1 = (bf16[1,2,144,128]{3,2,1,0:T(8,128)(2,1)}, bf16[1,2,144,128]{3,2,1,0:T(8,128)(2,1)S(1)}, u32[]{:S(2)}, u32[]{:S(2)}) collective-permute-start(bf16[1,2,144,128]{3,2,1,0:T(8,128)(2,1)} %bitcast.9), channel_id=1, source_target_pairs={{1,0},{2,1},{3,2},{0,3},{5,4},{6,5},{7,6},{4,7},{9,8},{10,9},{11,1... | collective-permute-start | bytes 221192 | tf_op jit(solution)/shard_map/ppermute | solution.py:433
  6.4 2.2 %prepare_lines.1 = (bf16[3,144,128]{2,1,0:T(8,128)(2,1)S(1)}, f32[11,144,128]{2,1,0:T(8,128)S(1)}, bf16[2,128,288]{2,1,0:T(8,128)(2,1)S(1)}, f32[8,72,256]{2,1,0:T(8,128)S(1)}) custom-call(bf16[1,2,144,128]{3,2,1,0:T(8,128)(2,1)} %bitcast.10, bf16[2,27,2,24]{3,2,1,0:T(2,128)(2,1)} %bitcast.11, s32[8]{0:T(128)} %refs_3_.3, s32[8]{0:T(128)} %refs_3_.2, ...), custom_call_target="tpu_custom_call" | custom-call | tf_op jit(solution)/shard_map/prepare_lines/pallas_call | solution.py:467
  8.7 0.0 collective-permute-done.refs_4_
  8.7 0.0 collective-permute-done.1.refs_5_
  8.7 1.3 %first_margins.1 = (f32[1,512,128]{2,1,0:T(8,128)S(1)}, f32[1,512,128]{2,1,0:T(8,128)S(1)}, f32[7,2,144,128]{3,2,1,0:T(8,128)S(1)}, bf16[4,128,288]{2,1,0:T(8,128)(2,1)S(1)}) custom-call(bf16[3,144,128]{2,1,0:T(8,128)(2,1)S(1)} %get-tuple-element.16.refs_0_, f32[11,144,128]{2,1,0:T(8,128)S(1)} %get-tuple-element.17.refs_1_, ...), custom_call_target="tpu_custom_call" | custom-call | tf_op jit(solution)/shard_map/first_margins/pallas_call | solution.py:487
  10.0 1.0 %collective-permute-start.3 = (f32[1,512,128]{2,1,0:T(8,128)S(1)}, f32[1,512,128]{2,1,0:T(8,128)S(1)}, u32[]{:S(2)}, u32[]{:S(2)}) collective-permute-start(f32[1,512,128]{2,1,0:T(8,128)S(1)} %get-tuple-element.25), channel_id=1, source_target_pairs={{1,0},{0,1},{3,2},{2,3},{5,4},{4,5},{7,6},{6,7},{9,8},{8,9},{11,10... | collective-permute-start | bytes 786440 | tf_op jit(solution)/shard_map/ppermute | solution.py:438
  11.0 1.0 %second_margins.1 = (f32[1,512,128]{2,1,0:T(8,128)S(1)}, f32[1,512,128]{2,1,0:T(8,128)S(1)}) custom-call(f32[7,2,144,128]{3,2,1,0:T(8,128)S(1)} %get-tuple-element.20.refs_0_, bf16[4,128,288]{2,1,0:T(8,128)(2,1)S(1)} %get-tuple-element.21.refs_1_, f32[8,72,256]{2,1,0:T(8,128)S(1)} %get-tuple-element.19.refs_3_.refs_2_, s32[8]{0:T(128)} %refs_3_.3), custom_call_target="tpu_custom_call" | custom-call | tf_op jit(solution)/shard_map/second_margins/pallas_call | solution.py:502
  12.0 0.0 copy-start
  12.0 0.1 collective-permute-start.2
  12.1 0.1 collective-permute-done.3.refs_1_
  12.2 0.1 fold_groups.1
  12.3 1.2 %collective-permute-start.4 = (s16[1,528,128]{2,1,0:T(8,128)(2,1)S(1)}, s16[1,528,128]{2,1,0:T(8,128)(2,1)S(1)}, u32[]{:S(2)}, u32[]{:S(2)}) collective-permute-start(s16[1,528,128]{2,1,0:T(8,128)(2,1)S(1)} %fold_groups.1), channel_id=1, source_target_pairs={{2,0},{3,1},{0,2},{1,3},{6,4},{7,5},{4,6},{5,7},{10,8},{11,9},{8,1... | collective-permute-start | bytes 405512 | tf_op jit(solution)/shard_map/ppermute | solution.py:438
  13.5 0.1 collective-permute-done.2.refs_1_
  13.6 4.6 %collective-permute-done.4.refs_2_ = s16[1,528,128]{2,1,0:T(8,128)(2,1)S(1)} collective-permute-done((s16[1,528,128]{2,1,0:T(8,128)(2,1)S(1)}, s16[1,528,128]{2,1,0:T(8,128)(2,1)S(1)}, u32[]{:S(2)}, u32[]{:S(2)}) %collective-permute-start.4) | collective-permute-done | bytes 135200 | tf_op jit(solution)/shard_map/ppermute | solution.py:438
  18.3 0.1 share_rows.1
  18.4 0.1 collective-permute-start.5
  18.5 3.1 %collective-permute-start.6 = (s16[144,128]{1,0:T(8,128)(2,1)S(1)}, s16[144,128]{1,0:T(8,128)(2,1)S(1)}, u32[]{:S(2)}, u32[]{:S(2)}) collective-permute-start(s16[144,128]{1,0:T(8,128)(2,1)S(1)} %get-tuple-element.28), channel_id=1, source_target_pairs={{0,8},{4,12},{8,0},{12,4},{1,9},{5,13},{9,1},{13,5},{2,10},{6,14},... | collective-permute-start | bytes 110600 | tf_op jit(solution)/shard_map/ppermute | solution.py:443
  21.5 1.3 %collective-permute-start.7 = (s16[144,128]{1,0:T(8,128)(2,1)S(1)}, s16[144,128]{1,0:T(8,128)(2,1)S(1)}, u32[]{:S(2)}, u32[]{:S(2)}) collective-permute-start(s16[144,128]{1,0:T(8,128)(2,1)S(1)} %get-tuple-element.29), channel_id=1, source_target_pairs={{0,12},{4,8},{8,4},{12,0},{1,13},{5,9},{9,5},{13,1},{2,14},{6,10},... | collective-permute-start | bytes 110600 | tf_op jit(solution)/shard_map/ppermute | solution.py:443
  22.8 0.0 collective-permute-done.5.refs_1_
  22.8 0.9 %collective-permute-done.6.refs_2_ = s16[144,128]{1,0:T(8,128)(2,1)S(1)} collective-permute-done((s16[144,128]{1,0:T(8,128)(2,1)S(1)}, s16[144,128]{1,0:T(8,128)(2,1)S(1)}, u32[]{:S(2)}, u32[]{:S(2)}) %collective-permute-start.6) | collective-permute-done | bytes 36896 | tf_op jit(solution)/shard_map/ppermute | solution.py:443
  23.8 3.5 %collective-permute-done.7.refs_3_ = s16[144,128]{1,0:T(8,128)(2,1)S(1)} collective-permute-done((s16[144,128]{1,0:T(8,128)(2,1)S(1)}, s16[144,128]{1,0:T(8,128)(2,1)S(1)}, u32[]{:S(2)}, u32[]{:S(2)}) %collective-permute-start.7) | collective-permute-done | bytes 36896 | tf_op jit(solution)/shard_map/ppermute | solution.py:443
  27.3 0.1 collective-permute-start.8
  27.4 1.9 %collective-permute-start.9 = (bf16[128,128]{1,0:T(8,128)(2,1)S(1)}, bf16[128,128]{1,0:T(8,128)(2,1)S(1)}, u32[]{:S(2)}, u32[]{:S(2)}) collective-permute-start(bf16[128,128]{1,0:T(8,128)(2,1)S(1)} %sum_shares.1.refs_2_), channel_id=1, source_target_pairs={{8,0},{12,4},{0,8},{4,12},{9,1},{13,5},{1,9},{5,13},{10,2},{14,6},... | collective-permute-start | bytes 98312 | tf_op jit(solution)/shard_map/ppermute | solution.py:438
  29.3 2.5 %collective-permute-start.10 = (bf16[128,128]{1,0:T(8,128)(2,1)S(1)}, bf16[128,128]{1,0:T(8,128)(2,1)S(1)}, u32[]{:S(2)}, u32[]{:S(2)}) collective-permute-start(bf16[128,128]{1,0:T(8,128)(2,1)S(1)} %sum_shares.1.refs_2_), channel_id=1, source_target_pairs={{12,0},{8,4},{4,8},{0,12},{13,1},{9,5},{5,9},{1,13},{14,2},{10,6},... | collective-permute-start | bytes 98312 | tf_op jit(solution)/shard_map/ppermute | solution.py:438
  31.8 1.5 %collective-permute-start.11 = (bf16[128,128]{1,0:T(8,128)(2,1)S(1)}, bf16[128,128]{1,0:T(8,128)(2,1)S(1)}, u32[]{:S(2)}, u32[]{:S(2)}) collective-permute-start(bf16[128,128]{1,0:T(8,128)(2,1)S(1)} %sum_shares.1.refs_2_), channel_id=1, source_target_pairs={{16,0},{0,16},{17,1},{1,17},{18,2},{2,18},{19,3},{3,19},{20,4},{4,... | collective-permute-start | bytes 98312 | tf_op jit(solution)/shard_map/ppermute | solution.py:433
  33.3 0.0 collective-permute-done.8.refs_3_
  33.3 0.5 %collective-permute-start.12 = (bf16[128,128]{1,0:T(8,128)(2,1)S(1)}, bf16[128,128]{1,0:T(8,128)(2,1)S(1)}, u32[]{:S(2)}, u32[]{:S(2)}) collective-permute-start(bf16[128,128]{1,0:T(8,128)(2,1)S(1)} %collective-permute-done.8.refs_3_), channel_id=1, source_target_pairs={{16,0},{0,16},{17,1},{1,17},{18,2},{2,18},{19,3},{3,19},{20,4},{4,... | collective-permute-start | bytes 98312 | tf_op jit(solution)/shard_map/ppermute | solution.py:433
  33.8 0.0 collective-permute-done.9.refs_4_
  33.8 1.5 %collective-permute-start.13 = (bf16[128,128]{1,0:T(8,128)(2,1)S(1)}, bf16[128,128]{1,0:T(8,128)(2,1)S(1)}, u32[]{:S(2)}, u32[]{:S(2)}) collective-permute-start(bf16[128,128]{1,0:T(8,128)(2,1)S(1)} %collective-permute-done.9.refs_4_), channel_id=1, source_target_pairs={{16,0},{0,16},{17,1},{1,17},{18,2},{2,18},{19,3},{3,19},{20,4},{4,... | collective-permute-start | bytes 98312 | tf_op jit(solution)/shard_map/ppermute | solution.py:433
  35.3 0.0 collective-permute-done.10.refs_5_
  35.3 1.2 %collective-permute-start.14 = (bf16[128,128]{1,0:T(8,128)(2,1)S(1)}, bf16[128,128]{1,0:T(8,128)(2,1)S(1)}, u32[]{:S(2)}, u32[]{:S(2)}) collective-permute-start(bf16[128,128]{1,0:T(8,128)(2,1)S(1)} %collective-permute-done.10.refs_5_), channel_id=1, source_target_pairs={{16,0},{0,16},{17,1},{1,17},{18,2},{2,18},{19,3},{3,19},{20,4},{4,... | collective-permute-start | bytes 98312 | tf_op jit(solution)/shard_map/ppermute | solution.py:433
  37.1 0.0 collective-permute-done.11.refs_6_
  37.1 0.1 collective-permute-done.12.refs_7_
  37.2 0.5 %collective-permute-done.13.refs_8_ = bf16[128,128]{1,0:T(8,128)(2,1)S(1)} collective-permute-done((bf16[128,128]{1,0:T(8,128)(2,1)S(1)}, bf16[128,128]{1,0:T(8,128)(2,1)S(1)}, u32[]{:S(2)}, u32[]{:S(2)}) %collective-permute-start.13) | collective-permute-done | bytes 32800 | tf_op jit(solution)/shard_map/ppermute | solution.py:433
  37.7 1.5 %collective-permute-done.14.refs_9_ = bf16[128,128]{1,0:T(8,128)(2,1)S(1)} collective-permute-done((bf16[128,128]{1,0:T(8,128)(2,1)S(1)}, bf16[128,128]{1,0:T(8,128)(2,1)S(1)}, u32[]{:S(2)}, u32[]{:S(2)}) %collective-permute-start.14) | collective-permute-done | bytes 32800 | tf_op jit(solution)/shard_map/ppermute | solution.py:433
  39.2 0.0 copy-done
  39.2 2.7 %contraction.1 = (f32[1,2,2,128,128]{4,3,2,1,0:T(8,128)}, f32[1,2,2]{2,1,0:T(2,128)}) custom-call(s32[1,2]{1,0:T(1,128)} %refs_0_.1, s32[1]{0:T(128)S(6)} %copy.10.refs_1_, bf16[128,128]{1,0:T(8,128)(2,1)S(1)} %sum_shares.1.refs_2_, bf16[128,128]{1,0:T(8,128)(2,1)S(1)} %collective-permute-done.8.refs_3_, ...), custom_call_target="tpu_custom_call" | custom-call | tf_op jit(solution)/shard_map/contraction/pallas_call | solution.py:548
  (1 shorter events, 0.0 us)
Async XLA Ops:
  0.6 8.0 %collective-permute-start = (bf16[1,2,144,128]{3,2,1,0:T(8,128)(2,1)}, bf16[1,2,144,128]{3,2,1,0:T(8,128)(2,1)S(1)}, u32[]{:S(2)}, u32[]{:S(2)}) collective-permute-start(bf16[1,2,144,128]{3,2,1,0:T(8,128)(2,1)} %bitcast.8), channel_id=1, source_target_pairs={{4,0},{8,4},{12,8},{0,12},{5,1},{9,5},{13,9},{1,13},{6,2},{10,6},{... | collective-permute-start | bytes 221192 | tf_op jit(solution)/shard_map/ppermute | solution.py:433
  5.7 3.0 %collective-permute-start.1 = (bf16[1,2,144,128]{3,2,1,0:T(8,128)(2,1)}, bf16[1,2,144,128]{3,2,1,0:T(8,128)(2,1)S(1)}, u32[]{:S(2)}, u32[]{:S(2)}) collective-permute-start(bf16[1,2,144,128]{3,2,1,0:T(8,128)(2,1)} %bitcast.9), channel_id=1, source_target_pairs={{1,0},{2,1},{3,2},{0,3},{5,4},{6,5},{7,6},{4,7},{9,8},{10,9},{11,1... | collective-permute-start | bytes 221192 | tf_op jit(solution)/shard_map/ppermute | solution.py:433
  10.0 2.2 %collective-permute-start.3 = (f32[1,512,128]{2,1,0:T(8,128)S(1)}, f32[1,512,128]{2,1,0:T(8,128)S(1)}, u32[]{:S(2)}, u32[]{:S(2)}) collective-permute-start(f32[1,512,128]{2,1,0:T(8,128)S(1)} %get-tuple-element.25), channel_id=1, source_target_pairs={{1,0},{0,1},{3,2},{2,3},{5,4},{4,5},{7,6},{6,7},{9,8},{8,9},{11,10... | collective-permute-start | bytes 786440 | tf_op jit(solution)/shard_map/ppermute | solution.py:438
  12.0 27.2 %copy-start = (bf16[1,2,512,512]{3,2,1,0:T(8,128)(2,1)S(1)}, bf16[1,2,512,512]{3,2,1,0:T(8,128)(2,1)}, u32[]{:S(2)}) copy-start(bf16[1,2,512,512]{3,2,1,0:T(8,128)(2,1)} %param.12) | copy-start | bytes 3145732
  12.0 1.6 %collective-permute-start.2 = (f32[1,512,128]{2,1,0:T(8,128)S(1)}, f32[1,512,128]{2,1,0:T(8,128)S(1)}, u32[]{:S(2)}, u32[]{:S(2)}) collective-permute-start(f32[1,512,128]{2,1,0:T(8,128)S(1)} %get-tuple-element.23), channel_id=1, source_target_pairs={{1,0},{0,1},{3,2},{2,3},{5,4},{4,5},{7,6},{6,7},{9,8},{8,9},{11,10... | collective-permute-start | bytes 786440 | tf_op jit(solution)/shard_map/ppermute | solution.py:438
  12.3 6.0 %collective-permute-start.4 = (s16[1,528,128]{2,1,0:T(8,128)(2,1)S(1)}, s16[1,528,128]{2,1,0:T(8,128)(2,1)S(1)}, u32[]{:S(2)}, u32[]{:S(2)}) collective-permute-start(s16[1,528,128]{2,1,0:T(8,128)(2,1)S(1)} %fold_groups.1), channel_id=1, source_target_pairs={{2,0},{3,1},{0,2},{1,3},{6,4},{7,5},{4,6},{5,7},{10,8},{11,9},{8,1... | collective-permute-start | bytes 405512 | tf_op jit(solution)/shard_map/ppermute | solution.py:438
  18.4 4.5 %collective-permute-start.5 = (s16[144,128]{1,0:T(8,128)(2,1)S(1)}, s16[144,128]{1,0:T(8,128)(2,1)S(1)}, u32[]{:S(2)}, u32[]{:S(2)}) collective-permute-start(s16[144,128]{1,0:T(8,128)(2,1)S(1)} %get-tuple-element.27), channel_id=1, source_target_pairs={{0,4},{4,0},{8,12},{12,8},{1,5},{5,1},{9,13},{13,9},{2,6},{6,2},{1... | collective-permute-start | bytes 110600 | tf_op jit(solution)/shard_map/ppermute | solution.py:443
  18.5 5.3 %collective-permute-start.6 = (s16[144,128]{1,0:T(8,128)(2,1)S(1)}, s16[144,128]{1,0:T(8,128)(2,1)S(1)}, u32[]{:S(2)}, u32[]{:S(2)}) collective-permute-start(s16[144,128]{1,0:T(8,128)(2,1)S(1)} %get-tuple-element.28), channel_id=1, source_target_pairs={{0,8},{4,12},{8,0},{12,4},{1,9},{5,13},{9,1},{13,5},{2,10},{6,14},... | collective-permute-start | bytes 110600 | tf_op jit(solution)/shard_map/ppermute | solution.py:443
  21.5 5.8 %collective-permute-start.7 = (s16[144,128]{1,0:T(8,128)(2,1)S(1)}, s16[144,128]{1,0:T(8,128)(2,1)S(1)}, u32[]{:S(2)}, u32[]{:S(2)}) collective-permute-start(s16[144,128]{1,0:T(8,128)(2,1)S(1)} %get-tuple-element.29), channel_id=1, source_target_pairs={{0,12},{4,8},{8,4},{12,0},{1,13},{5,9},{9,5},{13,1},{2,14},{6,10},... | collective-permute-start | bytes 110600 | tf_op jit(solution)/shard_map/ppermute | solution.py:443
  27.3 5.9 %collective-permute-start.8 = (bf16[128,128]{1,0:T(8,128)(2,1)S(1)}, bf16[128,128]{1,0:T(8,128)(2,1)S(1)}, u32[]{:S(2)}, u32[]{:S(2)}) collective-permute-start(bf16[128,128]{1,0:T(8,128)(2,1)S(1)} %sum_shares.1.refs_2_), channel_id=1, source_target_pairs={{4,0},{0,4},{12,8},{8,12},{5,1},{1,5},{13,9},{9,13},{6,2},{2,6},{1... | collective-permute-start | bytes 98312 | tf_op jit(solution)/shard_map/ppermute | solution.py:438
  27.4 6.4 %collective-permute-start.9 = (bf16[128,128]{1,0:T(8,128)(2,1)S(1)}, bf16[128,128]{1,0:T(8,128)(2,1)S(1)}, u32[]{:S(2)}, u32[]{:S(2)}) collective-permute-start(bf16[128,128]{1,0:T(8,128)(2,1)S(1)} %sum_shares.1.refs_2_), channel_id=1, source_target_pairs={{8,0},{12,4},{0,8},{4,12},{9,1},{13,5},{1,9},{5,13},{10,2},{14,6},... | collective-permute-start | bytes 98312 | tf_op jit(solution)/shard_map/ppermute | solution.py:438
  29.3 6.1 %collective-permute-start.10 = (bf16[128,128]{1,0:T(8,128)(2,1)S(1)}, bf16[128,128]{1,0:T(8,128)(2,1)S(1)}, u32[]{:S(2)}, u32[]{:S(2)}) collective-permute-start(bf16[128,128]{1,0:T(8,128)(2,1)S(1)} %sum_shares.1.refs_2_), channel_id=1, source_target_pairs={{12,0},{8,4},{4,8},{0,12},{13,1},{9,5},{5,9},{1,13},{14,2},{10,6},... | collective-permute-start | bytes 98312 | tf_op jit(solution)/shard_map/ppermute | solution.py:438
  31.8 5.3 %collective-permute-start.11 = (bf16[128,128]{1,0:T(8,128)(2,1)S(1)}, bf16[128,128]{1,0:T(8,128)(2,1)S(1)}, u32[]{:S(2)}, u32[]{:S(2)}) collective-permute-start(bf16[128,128]{1,0:T(8,128)(2,1)S(1)} %sum_shares.1.refs_2_), channel_id=1, source_target_pairs={{16,0},{0,16},{17,1},{1,17},{18,2},{2,18},{19,3},{3,19},{20,4},{4,... | collective-permute-start | bytes 98312 | tf_op jit(solution)/shard_map/ppermute | solution.py:433
  33.3 3.9 %collective-permute-start.12 = (bf16[128,128]{1,0:T(8,128)(2,1)S(1)}, bf16[128,128]{1,0:T(8,128)(2,1)S(1)}, u32[]{:S(2)}, u32[]{:S(2)}) collective-permute-start(bf16[128,128]{1,0:T(8,128)(2,1)S(1)} %collective-permute-done.8.refs_3_), channel_id=1, source_target_pairs={{16,0},{0,16},{17,1},{1,17},{18,2},{2,18},{19,3},{3,19},{20,4},{4,... | collective-permute-start | bytes 98312 | tf_op jit(solution)/shard_map/ppermute | solution.py:433
  33.8 3.9 %collective-permute-start.13 = (bf16[128,128]{1,0:T(8,128)(2,1)S(1)}, bf16[128,128]{1,0:T(8,128)(2,1)S(1)}, u32[]{:S(2)}, u32[]{:S(2)}) collective-permute-start(bf16[128,128]{1,0:T(8,128)(2,1)S(1)} %collective-permute-done.9.refs_4_), channel_id=1, source_target_pairs={{16,0},{0,16},{17,1},{1,17},{18,2},{2,18},{19,3},{3,19},{20,4},{4,... | collective-permute-start | bytes 98312 | tf_op jit(solution)/shard_map/ppermute | solution.py:433
  35.3 3.9 %collective-permute-start.14 = (bf16[128,128]{1,0:T(8,128)(2,1)S(1)}, bf16[128,128]{1,0:T(8,128)(2,1)S(1)}, u32[]{:S(2)}, u32[]{:S(2)}) collective-permute-start(bf16[128,128]{1,0:T(8,128)(2,1)S(1)} %collective-permute-done.10.refs_5_), channel_id=1, source_target_pairs={{16,0},{0,16},{17,1},{1,17},{18,2},{2,18},{19,3},{3,19},{20,4},{4,... | collective-permute-start | bytes 98312 | tf_op jit(solution)/shard_map/ppermute | solution.py:433

commit v6 on v5

--- a/solution.py
+++ b/solution.py
@@ -14,7 +14,6 @@
 LINK_COLS = 54
 TAIL = 16
 FIXED_BITS = 14.0
-DIRECT_LIMIT = 8
 
 
 def wave_constants(cells_z):
@@ -84,20 +83,21 @@
 
 
 def prepare_kernel(cells_x, cells_y, *refs):
-    inputs, refs = refs[:5], refs[5:]
-    matrix_ref, local_ref, left_ref, phase_ref = refs[:4]
-    held, link_rows_ref, sems = refs[4:9], refs[9], refs[10]
+    inputs, live_ref, refs = refs[:6], refs[6], refs[7:]
+    matrix_ref, local_ref, left_ref, phase_ref, weight_ref = refs[:5]
+    held, link_rows_ref, sems = refs[5:11], refs[11], refs[12]
     copies = [
         pltpu.make_async_copy(src, dst, sems.at[k])
         for k, (src, dst) in enumerate(zip(inputs, held))
     ]
     for copy in copies:
         copy.start()
-    v_ref, link_ref, dirs_ref, moms_ref, waves_ref = held
+    v_ref, link_ref, dirs_ref, moms_ref, waves_ref, pair_ref = held
     f32, bf16 = jnp.float32, jnp.bfloat16
     order, vectors = v_ref.shape[2], v_ref.shape[3]
     half, cells_z = order // 2, order // 6
     lines = cells_x * cells_y
+    times = weight_ref.shape[1]
     spread = one_hot(third(iota((half, cells_z), 0)) == iota((half, cells_z), 1))
     row, col = iota((half, LINK_COLS), 0), iota((half, LINK_COLS), 1)
     row_color = row - 3 * third(row)
@@ -117,6 +117,11 @@
     planar = planar_order(order)
     for copy in copies:
         copy.wait()
+    for t in range(times):
+        sink = (pair_ref[0, 0] == t) & (live_ref[0] > 0)
+        source = pair_ref[0, 1] == t
+        weight_ref[0, t] = jnp.full(weight_ref.shape[2:], jnp.where(sink, 1.0, 0.0), f32)
+        weight_ref[1, t] = jnp.full(weight_ref.shape[2:], jnp.where(source, 1.0, 0.0), f32)
     for line in range(lines):
         for k in range(LINK_COLS // 2):
             link_rows_ref[line, 2 * k : 2 * k + 2] = link_ref[line, k].astype(f32)
@@ -178,46 +183,35 @@
         )
 
 
-def write_margins(slots, own_ops, field_ref, side_ref, phase_ref, dirs_ref, lines):
-    f32, bf16 = jnp.float32, jnp.bfloat16
-    order, vectors = field_ref.shape[2], field_ref.shape[3]
-    half = order // 2
-    me = lax.axis_index("gy")
-    for j, out_ref, place in slots:
-        for i in range(own_ops):
-            o = (me ^ j) * own_ops + i
-            code = dirs_ref[o]
-            side = jnp.where((code >= 3) & (code < 6), code - 2, 0)
-            cosine = phase_ref[o, :, 0:vectors]
-            sine = phase_ref[o, :, vectors : 2 * vectors]
-            pairs = []
-            for line in range(lines):
-                real, imag = field_ref[code, line, 0:half], field_ref[code, line, half:order]
-                turned_r, turned_i = cosine * real - sine * imag, sine * real + cosine * imag
-                pairs.append(jnp.concatenate([turned_r, turned_i], axis=1))
-                pairs.append(jnp.concatenate([turned_i, -turned_r], axis=1))
-            product = jnp.dot(
-                side_ref[side],
-                jnp.concatenate(pairs, axis=0).astype(bf16),
-                preferred_element_type=f32,
-            )
-            first = 2 * i * vectors
-            out_ref[place, first : first + vectors] = product[:, :vectors]
-            out_ref[place, first + vectors : first + 2 * vectors] = product[:, vectors:]
-
-
 def low_bit(j):
     return (j & -j).bit_length() - 1
 
 
+def put_product(out_ref, place, i, side, pair):
+    vectors = pair.shape[1] // 2
+    product = jnp.dot(side, pair, preferred_element_type=jnp.float32)
+    first = 2 * i * vectors
+    out_ref[place, first : first + vectors] = product[:, :vectors]
+    out_ref[place, first + vectors : first + 2 * vectors] = product[:, vectors:]
+
+
+def first_groups(groups):
+    return sorted((j for j in range(groups) if j & 2), key=lambda j: -(j & 1))
+
+
+def second_groups(groups):
+    return sorted((j for j in range(groups) if not j & 2), key=lambda j: -(j & 1))
+
+
 def first_margin_kernel(cells_x, cells_y, groups, own_ops, *refs):
     matrix_ref, local_ref, left_ref, phase_ref, halo_x_ref, halo_y_ref, dirs_hbm = refs[:7]
-    swap_ref, hold_ref, field_ref, side_ref, dirs_ref, sem = refs[7:]
+    swap_ref, hold_ref, later_side_ref, later_pair_ref = refs[7:11]
+    field_ref, side_ref, dirs_ref, sem = refs[11:]
     f32, bf16 = jnp.float32, jnp.bfloat16
     copy = pltpu.make_async_copy(dirs_hbm, dirs_ref, sem)
     copy.start()
     lines = cells_x * cells_y
-    order = halo_x_ref.shape[2]
+    order, vectors = halo_x_ref.shape[2], halo_x_ref.shape[3]
     half = order // 2
     planar = planar_order(order)
     side_ref[0] = left_ref[0]
@@ -239,22 +233,38 @@
     for k, (code, line) in enumerate(local_fields(cells_x, cells_y)):
         field_ref[code, line] = local_ref[k]
     copy.wait()
-    slots = [(j, swap_ref if j & 1 else hold_ref, j >> 2) for j in range(groups) if j & 2]
-    slots.sort(key=lambda slot: -(slot[0] & 1))
-    write_margins(slots, own_ops, field_ref, side_ref, phase_ref, dirs_ref, lines)
-
-
-def second_margin_kernel(lines, groups, own_ops, *refs):
-    field_ref, side_ref, phase_ref, dirs_hbm, swap_ref = refs[:5]
-    hold_refs, dirs_ref, sem = refs[5:-2], refs[-2], refs[-1]
-    copy = pltpu.make_async_copy(dirs_hbm, dirs_ref, sem)
-    copy.start()
-    copy.wait()
-    slots = [(j, swap_ref, j >> 2) for j in range(groups) if j & 3 == 1]
-    for j in range(0, groups, 4):
+    me = lax.axis_index("gy")
+    later = 0
+    for j in first_groups(groups) + second_groups(groups):
+        for i in range(own_ops):
+            o = (me ^ j) * own_ops + i
+            code = dirs_ref[o]
+            side = jnp.where((code >= 3) & (code < 6), code - 2, 0)
+            cosine = phase_ref[o, :, 0:vectors]
+            sine = phase_ref[o, :, vectors : 2 * vectors]
+            pairs = []
+            for line in range(lines):
+                real, imag = field_ref[code, line, 0:half], field_ref[code, line, half:order]
+                turned_r, turned_i = cosine * real - sine * imag, sine * real + cosine * imag
+                pairs.append(jnp.concatenate([turned_r, turned_i], axis=1))
+                pairs.append(jnp.concatenate([turned_i, -turned_r], axis=1))
+            pair = jnp.concatenate(pairs, axis=0).astype(bf16)
+            if j & 2:
+                put_product(swap_ref if j & 1 else hold_ref, j >> 2, i, side_ref[side], pair)
+            else:
+                later_side_ref[later] = side_ref[side]
+                later_pair_ref[later] = pair
+                later += 1
+
+
+def second_margin_kernel(groups, own_ops, side_ref, pair_ref, swap_ref, *hold_refs):
+    later = 0
+    for j in second_groups(groups):
         level = low_bit(j) if j else groups.bit_length() - 1
-        slots.append((j, hold_refs[level - 2], j >> (level + 1)))
-    write_margins(slots, own_ops, field_ref, side_ref, phase_ref, dirs_ref, lines)
+        for i in range(own_ops):
+            out_ref, place = (swap_ref, j >> 2) if j & 1 else (hold_refs[level - 2], j >> (level + 1))
+            put_product(out_ref, place, i, side_ref[later], pair_ref[later])
+            later += 1
 
 
 def scale_of(block):
@@ -280,85 +290,93 @@
     return block * jnp.exp2(scales[k : k + 1] - FIXED_BITS)
 
 
-def arrived_block(received, j, rows, p):
-    total = received[0][j >> 2, p * rows : (p + 1) * rows]
+def group_block(held_ref, received, k, j, start, rows):
+    span = pl.ds(start, rows)
+    total = held_ref[k, span] + received[0][j >> 2, span]
     for b, ref in enumerate(received[1:], 1):
-        total = total + from_fixed(ref.at[j >> (b + 1)], rows, p)
+        total = total + fixed_at(ref.at[j >> (b + 1)], start, rows)
     return total
 
 
-def fold_kernel(level, count_blocks, *refs):
+def fixed_at(ref, start, rows):
+    tail = ref[ref.shape[0] - TAIL :].astype(jnp.int32).astype(jnp.float32)
+    scale = jnp.max(
+        jnp.where(iota(tail.shape, 0) == start // rows, tail, -1000.0), axis=0, keepdims=True
+    )
+    block = ref[pl.ds(start, rows)].astype(jnp.int32).astype(jnp.float32)
+    return block * jnp.exp2(scale - FIXED_BITS)
+
+
+def fold_kernel(level, vectors, *refs):
     held_ref, received, out_ref = refs[0], refs[1:-1], refs[-1]
-    rows = held_ref.shape[1] // count_blocks
     for k in range(held_ref.shape[0]):
         j = (2 * k + 1) << level
         blocks = [
-            held_ref[k, p * rows : (p + 1) * rows] + arrived_block(received, j, rows, p)
-            for p in range(count_blocks)
+            group_block(held_ref, received, k, j, start, vectors)
+            for start in range(0, held_ref.shape[1], vectors)
         ]
         put_fixed(out_ref.at[k], blocks)
 
 
-def share_kernel(levels, count_blocks, *refs):
-    held_ref, received, refs = refs[0], refs[1 : 1 + levels], refs[1 + levels :]
-    outs, total_ref = refs[:-1], refs[-1]
-    span = held_ref.shape[1] // count_blocks
-    for p in range(count_blocks):
-        here = slice(p * span, (p + 1) * span)
-        total_ref[here] = held_ref[0, here] + arrived_block(received, 0, span, p)
-    rows = outs[0].shape[0]
-    me = lax.axis_index("gx")
-    for step, out_ref in enumerate(outs):
-        chunk = partner_of(me, step, len(outs))
-        total = total_ref[pl.ds(pl.multiple_of(chunk * rows, rows), rows)]
-        if step:
-            put_fixed(out_ref, [total])
-        else:
-            out_ref[...] = total
-
-
-def partner_of(me, step, count):
-    if count & (count - 1) == 0:
-        return me ^ step
-    return (me + step) % count
-
-
-def sum_kernel(norm_factor, *refs):
-    own_ref, received, out_ref = refs[0], refs[1:-1], refs[-1]
-    total = own_ref[...]
-    for ref in received:
-        total = total + from_fixed(ref, total.shape[0], 0)
-    out_ref[...] = (total * norm_factor).astype(out_ref.dtype)
-
-
-def contract_kernel(times, steps, *refs):
-    pair_hbm, live_ref = refs[:2]
-    chunks, refs = refs[2 : 2 + times * steps], refs[2 + times * steps :]
-    tau_ref, margin_ref, corr_ref = refs[:3]
-    every_ref, left_ref, right_ref, pair_ref, sem = refs[3:]
-    f32 = jnp.float32
-    copy = pltpu.make_async_copy(pair_hbm, pair_ref, sem)
-    copy.start()
-    vectors = every_ref.shape[2]
-    count_ops = margin_ref.shape[1]
+def half_rows(held_ref, vectors, kept):
+    me = lax.axis_index("gx") & 1
+    half = held_ref.shape[1] // 2
+    base = pl.multiple_of((me if kept else 1 - me) * half, half)
+    return [base + step for step in range(0, half, vectors)]
+
+
+def fold_halves_kernel(vectors, *refs):
+    held_ref, received, outs = refs[0], refs[1:-2], refs[-2:]
+    for kept, out_ref in enumerate(outs):
+        starts = half_rows(held_ref, vectors, kept)
+        blocks = [group_block(held_ref, received, 0, held_ref.shape[0], s, vectors) for s in starts]
+        put_fixed(out_ref, blocks)
+
+
+def half_kernel(vectors, kept, *refs):
+    count = 3 if kept else 2
+    held_ref, received, last, out_ref = refs[0], refs[1:-count], refs[-count:-1], refs[-1]
+    blocks = []
+    for p, start in enumerate(half_rows(held_ref, vectors, kept)):
+        total = group_block(held_ref, received, 0, 0, start, vectors)
+        for ref in last:
+            total = total + from_fixed(ref, vectors, p)
+        blocks.append(total)
+    put_fixed(out_ref, blocks)
+
+
+def both_kernel(vectors, norm_factor, own_ref, arrived_ref, out_ref):
+    blocks = [
+        from_fixed(own_ref, vectors, p) + from_fixed(arrived_ref, vectors, p)
+        for p in range((own_ref.shape[0] - TAIL) // vectors)
+    ]
+    if norm_factor is None:
+        put_fixed(out_ref, blocks)
+        return
+    for p, block in enumerate(blocks):
+        out_ref[p * vectors : (p + 1) * vectors] = (block * norm_factor).astype(out_ref.dtype)
+
+
+def contract(sums_ref, weight_ref, blocks, tau_ref, left_ref, right_ref):
+    f32, bf16 = jnp.float32, jnp.bfloat16
+    vectors = sums_ref.shape[2]
+    count_ops = sums_ref.shape[0] // 2
     order = tau_ref.shape[2]
     spins = order // vectors
-    me_t, me_x = lax.axis_index("ta"), lax.axis_index("gx")
-    rows = chunks[0].shape[0]
-    for k, ref in enumerate(chunks):
-        at_t = lax.rem(me_t + k // steps, times)
-        place = partner_of(me_x, k % steps, steps)
-        every_ref[at_t, pl.ds(pl.multiple_of(place * rows, rows), rows)] = ref[...]
-    copy.wait()
-    sink, source = pair_ref[0, 0], pair_ref[0, 1]
-    live = live_ref[0] > 0
+    me_t = lax.axis_index("ta")
+    times = len(blocks)
+
+    def chosen(end, k):
+        total = jnp.zeros((vectors // 8, 8, vectors), f32)
+        for t in range(times):
+            weight = weight_ref[end, lax.rem(me_t + t, times)]
+            total = total + blocks[t](k).astype(f32).reshape(total.shape) * weight
+        return total.reshape(vectors, vectors)
+
     for o in range(count_ops):
         first = 2 * o * vectors
-        part = lambda t, k: every_ref[t, first + k * vectors : first + (k + 1) * vectors]
-        margin_ref[0, o, 0] = part(me_t, 0).astype(f32)
-        margin_ref[0, o, 1] = part(me_t, 1).astype(f32)
-        a_r, a_i = part(sink, 0), part(sink, 1)
-        b_r, b_i = part(source, 0).T, part(source, 1).T
+        a_r, a_i = chosen(0, 2 * o).astype(bf16), chosen(0, 2 * o + 1).astype(bf16)
+        b_r, b_i = chosen(1, 2 * o).T.astype(bf16), chosen(1, 2 * o + 1).T.astype(bf16)
         real, imag = slice(first, first + vectors), slice(first + vectors, first + 2 * vectors)
         left_ref[real, 0:vectors] = a_r
         left_ref[real, vectors:] = -a_i
@@ -368,9 +386,9 @@
         right_ref[0:vectors, imag] = -b_i
         right_ref[vectors:, real] = b_i
         right_ref[vectors:, imag] = b_r
-    lanes = 32
+    lanes = sums_ref.shape[1]
     fold = lambda t: jnp.sum(t.reshape(vectors // lanes, lanes, vectors), axis=0)
-    sums = [[jnp.zeros((lanes, vectors), f32) for _ in range(2)] for _ in range(count_ops)]
+    sums = [jnp.zeros((lanes, vectors), f32) for _ in range(2 * count_ops)]
     for s in range(spins):
         rows = slice(s * vectors, (s + 1) * vectors)
         x = jnp.dot(
@@ -391,12 +409,62 @@
                 x_i = x[first + vectors : first + 2 * vectors, cols]
                 y_r = y[:, first : first + vectors]
                 y_i = y[:, first + vectors : first + 2 * vectors]
-                sums[o][0] = sums[o][0] + fold(x_r * y_r + x_i * y_i)
-                sums[o][1] = sums[o][1] + fold(x_i * y_r - x_r * y_i)
+                sums[2 * o] = sums[2 * o] + fold(x_r * y_r + x_i * y_i)
+                sums[2 * o + 1] = sums[2 * o + 1] + fold(x_i * y_r - x_r * y_i)
+    for k, total in enumerate(sums):
+        sums_ref[k] = total
+
+
+def part_of(ref, vectors):
+    return lambda k: ref[k * vectors : (k + 1) * vectors]
+
+
+def first_contract_kernel(times, weight_ref, tau_ref, *refs):
+    blocks, (sums_ref, left_ref, right_ref) = refs[:times], refs[times:]
+    vectors = sums_ref.shape[2]
+    blocks = [part_of(ref, vectors) for ref in blocks]
+    contract(sums_ref, weight_ref, blocks, tau_ref, left_ref, right_ref)
+
+
+def second_contract_kernel(times, split, weight_ref, tau_ref, *refs):
+    kept, other, refs = refs[:times], refs[times : 2 * times], refs[2 * times :]
+    if split:
+        first_sums_ref, refs = refs[0], refs[1:]
+    margin_ref, corr_ref, sums_ref, left_ref, right_ref = refs
+    vectors = sums_ref.shape[2]
+    half = kept[0].shape[0]
+    me = lax.axis_index("gx") & 1
+    places = (me, 1 - me)
+    for place, ref in zip(places, (kept[0], other[0])):
+        span = pl.ds(pl.multiple_of(place * half, half), half)
+        margin_ref[0, span] = ref[...].astype(jnp.float32)
     scale = 1.0 / vectors
-    for o in range(count_ops):
-        for k in range(2):
-            corr_ref[0, o, k] = jnp.where(live, jnp.sum(sums[o][k]) * scale, 0.0)
+
+    def put(sums, first):
+        for k in range(sums.shape[0]):
+            corr_ref[0, first + k // 2, k % 2] = jnp.sum(sums[k]) * scale
+
+    if split:
+        blocks = [part_of(ref, vectors) for ref in other]
+        contract(sums_ref, weight_ref, blocks, tau_ref, left_ref, right_ref)
+        own_ops = sums_ref.shape[0] // 2
+        put(first_sums_ref, places[0] * own_ops)
+        put(sums_ref, places[1] * own_ops)
+        return
+    parts_per_half = half // vectors
+
+    def either(kept_ref, other_ref):
+        def part(k):
+            row = (k % parts_per_half) * vectors
+            own, far = kept_ref[row : row + vectors], other_ref[row : row + vectors]
+            mine = (k // parts_per_half == me).astype(jnp.float32)
+            return own.astype(jnp.float32) * mine + far.astype(jnp.float32) * (1.0 - mine)
+
+        return part
+
+    blocks = [either(a, b) for a, b in zip(kept, other)]
+    contract(sums_ref, weight_ref, blocks, tau_ref, left_ref, right_ref)
+    put(sums_ref, 0)
 
 
 def vmem_spec():
@@ -435,12 +503,7 @@
 
 def from_partner(block, axis, step):
     count = lax.axis_size(axis)
-    return lax.ppermute(block, axis, [(partner_of(i, step, count), i) for i in range(count)])
-
-
-def to_partner(block, axis, step):
-    count = lax.axis_size(axis)
-    return lax.ppermute(block, axis, [(i, partner_of(i, step, count)) for i in range(count)])
+    return lax.ppermute(block, axis, [(i ^ step, i) for i in range(count)])
 
 
 def per_device(eigvecs, links, op_dirs, op_moms, perams, pair_times, slot_counts):
@@ -458,13 +521,13 @@
     halo_y = from_step(field, "gy", 1)
     link_field = links[0].transpose(0, 1, 3, 5, 6, 4, 2).reshape(lines, 27, 2, cells_z)
     outside, inside = halo_fields(cells_x, cells_y), local_fields(cells_x, cells_y)
-    inputs = [field, link_field, op_dirs, op_moms, wave_constants(cells_z)]
+    inputs = [field, link_field, op_dirs, op_moms, wave_constants(cells_z), pair_times]
     inputs = [in_hbm(x) for x in inputs]
     held = [
-        pltpu.SMEM(x.shape, x.dtype) if x.ndim == 1 else pltpu.VMEM(x.shape, x.dtype)
+        pltpu.SMEM(x.shape, x.dtype) if x.dtype == jnp.int32 else pltpu.VMEM(x.shape, x.dtype)
         for x in inputs
     ]
-    matrices, local, left, phases = local_call(
+    matrices, local, left, phases, weights = local_call(
         functools.partial(prepare_kernel, cells_x, cells_y),
         "prepare_lines",
         (
@@ -472,97 +535,117 @@
             jax.ShapeDtypeStruct((len(inside), order, vectors), f32),
             jax.ShapeDtypeStruct((2, vectors, lines * order), bf16),
             jax.ShapeDtypeStruct((count_ops, order // 2, 2 * vectors), f32),
+            jax.ShapeDtypeStruct((2, times, 8, vectors), f32),
         ),
-        [hbm_spec()] * len(inputs),
-        (vmem_spec(),) * 4,
+        [hbm_spec()] * len(inputs) + [smem_spec()],
+        (vmem_spec(),) * 5,
         held
         + [
             pltpu.VMEM((lines, LINK_COLS, cells_z), f32),
             pltpu.SemaphoreType.DMA((len(inputs),)),
         ],
-    )(*inputs)
+    )(*inputs, slot_counts)
     part = lambda count: jax.ShapeDtypeStruct((count, own_rows, vectors), f32)
-    dirs = in_hbm(op_dirs)
-    dirs_scratch = [pltpu.SMEM((count_ops,), jnp.int32), pltpu.SemaphoreType.DMA]
-    swap_a, hold_a, fields, sides = local_call(
+    later = count_ops // 2
+    swap_a, hold_a, later_sides, later_pairs = local_call(
         functools.partial(first_margin_kernel, cells_x, cells_y, groups, own_ops),
         "first_margins",
         (
             part(groups // 4),
             part(groups // 4),
-            jax.ShapeDtypeStruct((7, lines, order, vectors), f32),
-            jax.ShapeDtypeStruct((4, vectors, lines * order), bf16),
+            jax.ShapeDtypeStruct((later, vectors, lines * order), bf16),
+            jax.ShapeDtypeStruct((later, lines * order, 2 * vectors), bf16),
         ),
         [vmem_spec()] * 6 + [hbm_spec()],
         (vmem_spec(),) * 4,
-        dirs_scratch,
-    )(matrices, local, left, phases, halo_x, halo_y, dirs)
+        [
+            pltpu.VMEM((7, lines, order, vectors), f32),
+            pltpu.VMEM((4, vectors, lines * order), bf16),
+            pltpu.SMEM((count_ops,), jnp.int32),
+            pltpu.SemaphoreType.DMA,
+        ],
+    )(matrices, local, left, phases, halo_x, halo_y, in_hbm(op_dirs))
     swapped_a = from_partner(swap_a, "gy", 1)
     held_shapes = [part(groups >> (b + 1)) for b in range(2, levels)] + [part(1)]
     swap_b, *held = local_call(
-        functools.partial(second_margin_kernel, lines, groups, own_ops),
+        functools.partial(second_margin_kernel, groups, own_ops),
         "second_margins",
         (part(groups // 4), *held_shapes),
-        [vmem_spec()] * 3 + [hbm_spec()],
+        [vmem_spec()] * 2,
         (vmem_spec(),) * (1 + len(held_shapes)),
-        dirs_scratch,
-    )(fields, sides, phases, dirs)
+    )(later_sides, later_pairs)
     received = [from_partner(swap_b, "gy", 1)]
+
+    def packed(body, name, *inputs, rows=own_rows, lead=(), count=1):
+        shape = jax.ShapeDtypeStruct((*lead, rows + TAIL, vectors), jnp.int16)
+        outs = shape if count == 1 else (shape,) * count
+        specs = vmem_spec() if count == 1 else (vmem_spec(),) * count
+        return local_call(body, name, outs, [vmem_spec()] * len(inputs), specs)(*inputs)
+
+    half = own_rows // 2
     for b in range(1, levels):
         inputs = (hold_a, swapped_a) if b == 1 else (held[b - 2], *received)
-        sent = local_call(
-            functools.partial(fold_kernel, b, 2 * own_ops),
-            "fold_groups",
-            jax.ShapeDtypeStruct((inputs[0].shape[0], own_rows + TAIL, vectors), jnp.int16),
-            [vmem_spec()] * len(inputs),
-            vmem_spec(),
-        )(*inputs)
-        received.append(from_partner(sent, "gy", 1 << b))
+        if b < levels - 1:
+            body = functools.partial(fold_kernel, b, vectors)
+            sent = packed(body, "fold_groups", *inputs, lead=inputs[0].shape[:1])
+            received.append(from_partner(sent, "gy", 1 << b))
+            continue
+        body = functools.partial(fold_halves_kernel, vectors)
+        away, kept = packed(body, "fold_halves", *inputs, rows=half, count=2)
+        away, kept = from_partner(away, "gy", 1 << b), from_partner(kept, "gy", 1 << b)
+    body = functools.partial(half_kernel, vectors, False)
+    sent = packed(body, "send_half", held[-1], *received, away, rows=half)
+    arrived = from_partner(sent, "gx", 1)
+    body = functools.partial(half_kernel, vectors, True)
+    message = packed(body, "keep_half", held[-1], *received, kept, arrived, rows=half)
     norm_factor = 1.0 / math.sqrt(3.0 * cells_x * shares * cells_y * groups * cells_z)
-    direct = shares <= DIRECT_LIMIT and own_rows % (16 * shares) == 0
-    steps = shares if direct else 1
-    rows = own_rows // steps
-    chunk_shapes = [jax.ShapeDtypeStruct((rows, vectors), f32)]
-    chunk_shapes += [jax.ShapeDtypeStruct((rows + TAIL, vectors), jnp.int16)] * (steps - 1)
-    chunks = local_call(
-        functools.partial(share_kernel, levels, 2 * own_ops),
-        "share_rows",
-        tuple(chunk_shapes),
-        [vmem_spec()] * (1 + levels),
-        (vmem_spec(),) * steps,
-        [pltpu.VMEM((own_rows, vectors), f32)],
-    )(held[-1], *received)
-    if direct:
-        arrived = [to_partner(chunks[k], "gx", k) for k in range(1, shares)]
-        own = local_call(
-            functools.partial(sum_kernel, norm_factor),
-            "sum_shares",
-            jax.ShapeDtypeStruct((rows, vectors), bf16),
-            [vmem_spec()] * shares,
-            vmem_spec(),
-        )(chunks[0], *arrived)
-        every = [own] + [from_partner(own, "gx", k) for k in range(1, shares)]
-    else:
-        every = [(lax.psum(chunks[0], "gx") * norm_factor).astype(bf16)]
-    every += [from_step(every[k], "ta", t) for t in range(1, times) for k in range(steps)]
+    step = 2
+    while step < shares:
+        arrived = from_partner(message, "gx", step)
+        step *= 2
+        if step < shares:
+            body = functools.partial(both_kernel, vectors, None)
+            message = packed(body, "sum_both", message, arrived, rows=half)
+    finished = local_call(
+        functools.partial(both_kernel, vectors, norm_factor),
+        "finish_half",
+        jax.ShapeDtypeStruct((half, vectors), bf16),
+        [vmem_spec()] * 2,
+        vmem_spec(),
+    )(message, arrived)
+    kept = [finished] + [from_step(finished, "ta", t) for t in range(1, times)]
+    other = [from_partner(block, "gx", 1) for block in kept]
+    split = own_ops % 2 == 0
+    now_ops = own_ops // 2 if split else own_ops
+    sums_shape = (2 * now_ops, 32, vectors)
+    scratch = [
+        pltpu.VMEM((2 * now_ops * vectors, 2 * vectors), bf16),
+        pltpu.VMEM((2 * vectors, 2 * now_ops * vectors), bf16),
+    ]
+    sums = []
+    if split:
+        sums = [
+            local_call(
+                functools.partial(first_contract_kernel, times),
+                "first_contraction",
+                jax.ShapeDtypeStruct(sums_shape, f32),
+                [vmem_spec()] * (2 + times),
+                vmem_spec(),
+                scratch,
+            )(weights, perams[0], *kept)
+        ]
     margins, correlators = local_call(
-        functools.partial(contract_kernel, times, steps),
-        "contraction",
+        functools.partial(second_contract_kernel, times, split),
+        "second_contraction",
         (
-            jax.ShapeDtypeStruct((1, own_ops, 2, vectors, vectors), f32),
+            jax.ShapeDtypeStruct((1, own_rows, vectors), f32),
             jax.ShapeDtypeStruct((1, own_ops, 2), f32),
         ),
-        [hbm_spec(), smem_spec()] + [vmem_spec()] * (len(every) + 1),
+        [vmem_spec()] * (2 + 2 * times + len(sums)),
         (vmem_spec(), smem_spec()),
-        [
-            pltpu.VMEM((times, own_rows, vectors), bf16),
-            pltpu.VMEM((own_rows, 2 * vectors), bf16),
-            pltpu.VMEM((2 * vectors, own_rows), bf16),
-            pltpu.SMEM((1, 2), jnp.int32),
-            pltpu.SemaphoreType.DMA,
-        ],
-    )(in_hbm(pair_times), slot_counts, *every, perams[0])
-    return (margins, correlators)
+        [pltpu.VMEM(sums_shape, f32)] + scratch,
+    )(weights, perams[0], *kept, *other, *sums)
+    return (margins.reshape(1, own_ops, 2, vectors, vectors), correlators)
 
 
 def solution(mesh):

time: 42.1 us -> 38.6 us (0.917)
  starting transfers between devices: 21.6 us -> 13.3 us
  waiting for transfers between devices: 11.4 us -> 17.2 us
  Pallas kernels: 7.47 us -> 6.46 us
    ppermute x9 -> x8, waiting for transfers between devices: 9.3 us -> 14.9 us  [from_partner(): return lax.ppermute(block, axis, [(i ^ step, i) for i in range(count)])]
    ppermute x9 -> x8, starting transfers between devices: 11.2 us -> 5.71 us  [from_partner(): return lax.ppermute(block, axis, [(i ^ step, i) for i in range(count)])]
    ppermute x6 -> x3, starting transfers between devices: 10.5 us -> 7.59 us  [from_step(): lax.ppermute(block, axis, [((i + step) % count, i) for i in range(count)])]
    pallas_call x5 -> x7, Pallas kernels: 3.97 us -> 3.07 us  [the longest x1 1.62 us: per_device(): local_call(functools.partial(second_contract_kernel, times, split), 'seco...]
    ppermute x6 -> x3, waiting for transfers between devices: 2.15 us -> 2.36 us  [from_step(): lax.ppermute(block, axis, [((i + step) % count, i) for i in range(count)])]
  transfers between devices with their start and end apart: 15 -> 11, of which waited for: 8 -> 8; matrix products, arithmetic and copies ran while one was open for 0% -> 0% of each run, Pallas kernels for 8% -> 9%
where the time goes in v6:
time: 38.6 us; the launch traced here: 38.4 us
  waiting for transfers between devices  17.2 us (45%)
  starting transfers between devices  13.3 us (34%)
  Pallas kernels  6.46 us (17%)
  between operations  1.38 us (4%)
    ppermute x8, waiting for transfers between devices, from_partner(): return lax.ppermute(block, axis, [(i ^ step, i) for i in range(count)])  14.9 us
    ppermute x3, starting transfers between devices, from_step(): lax.ppermute(block, axis, [((i + step) % count, i) for i in range(count)])  7.59 us
    ppermute x8, starting transfers between devices, from_partner(): return lax.ppermute(block, axis, [(i ^ step, i) for i in range(count)])  5.71 us
    ppermute x3, waiting for transfers between devices, from_step(): lax.ppermute(block, axis, [((i + step) % count, i) for i in range(count)])  2.36 us
    pallas_call x1, Pallas kernels, per_device(): local_call(functools.partial(prepare_kernel, cells_x, cells_y), 'prepare_...  2.23 us
    pallas_call x1, Pallas kernels, per_device(): local_call(functools.partial(second_contract_kernel, times, split), 'seco...  1.62 us
    pallas_call x1, Pallas kernels, per_device(): local_call(functools.partial(first_margin_kernel, cells_x, cells_y, group...  1.15 us
    pallas_call x1, Pallas kernels, per_device(): local_call(functools.partial(first_contract_kernel, times), 'first_contra...  0.83 us
  transfers between devices with their start and end apart: 11, of which 8 were waited for; matrix products, arithmetic and copies ran while one was open for 0% of the time, Pallas kernels for 9%

profile of v6, /device:TPU:0, one launch (start us, length us, event | category | flops | bytes accessed | tf_op | source)
XLA Modules:
  0.0 38.4 jit_solution(10513305476790806315)
XLA Ops:
  0.6 2.5 %collective-permute-start.1 = (bf16[1,2,144,128]{3,2,1,0:T(8,128)(2,1)}, bf16[1,2,144,128]{3,2,1,0:T(8,128)(2,1)S(1)}, u32[]{:S(2)}, u32[]{:S(2)}) collective-permute-start(bf16[1,2,144,128]{3,2,1,0:T(8,128)(2,1)} %bitcast.10), channel_id=1, source_target_pairs={{1,0},{2,1},{3,2},{0,3},{5,4},{6,5},{7,6},{4,7},{9,8},{10,9},{11,1... | collective-permute-start | bytes 221192 | tf_op jit(solution)/shard_map/ppermute | solution.py:501
  3.1 3.6 %collective-permute-start = (bf16[1,2,144,128]{3,2,1,0:T(8,128)(2,1)}, bf16[1,2,144,128]{3,2,1,0:T(8,128)(2,1)S(1)}, u32[]{:S(2)}, u32[]{:S(2)}) collective-permute-start(bf16[1,2,144,128]{3,2,1,0:T(8,128)(2,1)} %bitcast.11), channel_id=1, source_target_pairs={{4,0},{8,4},{12,8},{0,12},{5,1},{9,5},{13,9},{1,13},{6,2},{10,6},{... | collective-permute-start | bytes 221192 | tf_op jit(solution)/shard_map/ppermute | solution.py:501
  7.3 2.2 %prepare_lines.1 = (bf16[3,144,128]{2,1,0:T(8,128)(2,1)S(1)}, f32[11,144,128]{2,1,0:T(8,128)S(1)}, bf16[2,128,288]{2,1,0:T(8,128)(2,1)S(1)}, f32[8,72,256]{2,1,0:T(8,128)S(1)}, f32[2,2,8,128]{3,2,1,0:T(8,128)S(1)}) custom-call(bf16[1,2,144,128]{3,2,1,0:T(8,128)(2,1)} %bitcast.12, bf16[2,27,2,24]{3,2,1,0:T(2,128)(2,1)} %bitcast.13, s32[8]{0:T(128)} %refs_6_.2, ...), custom_call_target="tpu_custom_call" | custom-call | tf_op jit(solution)/shard_map/prepare_lines/pallas_call | solution.py:530
  9.6 0.0 collective-permute-done.1.refs_5_
  9.6 0.0 collective-permute-done.refs_4_
  9.6 1.2 %first_margins.1 = (f32[1,512,128]{2,1,0:T(8,128)S(1)}, f32[1,512,128]{2,1,0:T(8,128)S(1)}, bf16[4,128,288]{2,1,0:T(8,128)(2,1)S(1)}, bf16[4,288,256]{2,1,0:T(8,128)(2,1)S(1)}) custom-call(bf16[3,144,128]{2,1,0:T(8,128)(2,1)S(1)} %get-tuple-element.18.refs_0_, f32[11,144,128]{2,1,0:T(8,128)S(1)} %get-tuple-element.19.refs_1_, ...), custom_call_target="tpu_custom_call" | custom-call | tf_op jit(solution)/shard_map/first_margins/pallas_call | solution.py:550
  10.8 0.1 collective-permute-start.3
  10.8 0.3 second_margins.1
  11.1 0.6 %collective-permute-start.2 = (f32[1,512,128]{2,1,0:T(8,128)S(1)}, f32[1,512,128]{2,1,0:T(8,128)S(1)}, u32[]{:S(2)}, u32[]{:S(2)}) collective-permute-start(f32[1,512,128]{2,1,0:T(8,128)S(1)} %get-tuple-element.25), channel_id=1, source_target_pairs={{1,0},{0,1},{3,2},{2,3},{5,4},{4,5},{7,6},{6,7},{9,8},{8,9},{11,10... | collective-permute-start | bytes 786440 | tf_op jit(solution)/shard_map/ppermute | solution.py:506
  11.7 0.7 %collective-permute-done.3.refs_1_ = f32[1,512,128]{2,1,0:T(8,128)S(1)} collective-permute-done((f32[1,512,128]{2,1,0:T(8,128)S(1)}, f32[1,512,128]{2,1,0:T(8,128)S(1)}, u32[]{:S(2)}, u32[]{:S(2)}) %collective-permute-start.3) | collective-permute-done | bytes 262176 | tf_op jit(solution)/shard_map/ppermute | solution.py:506
  12.4 0.0 copy-start
  12.4 0.1 fold_halves.1
  12.5 0.7 %collective-permute-start.5 = (s16[272,128]{1,0:T(8,128)(2,1)S(1)}, s16[272,128]{1,0:T(8,128)(2,1)S(1)}, u32[]{:S(2)}, u32[]{:S(2)}) collective-permute-start(s16[272,128]{1,0:T(8,128)(2,1)S(1)} %get-tuple-element.29), channel_id=1, source_target_pairs={{2,0},{3,1},{0,2},{1,3},{6,4},{7,5},{4,6},{5,7},{10,8},{11,9},{8,1... | collective-permute-start | bytes 208904 | tf_op jit(solution)/shard_map/ppermute | solution.py:506
  13.2 1.4 %collective-permute-start.4 = (s16[272,128]{1,0:T(8,128)(2,1)S(1)}, s16[272,128]{1,0:T(8,128)(2,1)S(1)}, u32[]{:S(2)}, u32[]{:S(2)}) collective-permute-start(s16[272,128]{1,0:T(8,128)(2,1)S(1)} %get-tuple-element.28), channel_id=1, source_target_pairs={{2,0},{3,1},{0,2},{1,3},{6,4},{7,5},{4,6},{5,7},{10,8},{11,9},{8,1... | collective-permute-start | bytes 208904 | tf_op jit(solution)/shard_map/ppermute | solution.py:506
  14.6 0.0 collective-permute-done.2.refs_1_
  14.6 2.9 %collective-permute-done.5.refs_2_ = s16[272,128]{1,0:T(8,128)(2,1)S(1)} collective-permute-done((s16[272,128]{1,0:T(8,128)(2,1)S(1)}, s16[272,128]{1,0:T(8,128)(2,1)S(1)}, u32[]{:S(2)}, u32[]{:S(2)}) %collective-permute-start.5) | collective-permute-done | bytes 69664 | tf_op jit(solution)/shard_map/ppermute | solution.py:506
  17.5 0.1 send_half.1
  17.6 0.1 collective-permute-start.6
  17.7 0.6 %collective-permute-done.4.refs_2_ = s16[272,128]{1,0:T(8,128)(2,1)S(1)} collective-permute-done((s16[272,128]{1,0:T(8,128)(2,1)S(1)}, s16[272,128]{1,0:T(8,128)(2,1)S(1)}, u32[]{:S(2)}, u32[]{:S(2)}) %collective-permute-start.4) | collective-permute-done | bytes 69664 | tf_op jit(solution)/shard_map/ppermute | solution.py:506
  18.3 3.7 %collective-permute-done.6.refs_3_ = s16[272,128]{1,0:T(8,128)(2,1)S(1)} collective-permute-done((s16[272,128]{1,0:T(8,128)(2,1)S(1)}, s16[272,128]{1,0:T(8,128)(2,1)S(1)}, u32[]{:S(2)}, u32[]{:S(2)}) %collective-permute-start.6) | collective-permute-done | bytes 69664 | tf_op jit(solution)/shard_map/ppermute | solution.py:506
  22.0 0.1 keep_half.1.own_ref
  22.1 2.0 %collective-permute-start.7 = (s16[272,128]{1,0:T(8,128)(2,1)S(1)}, s16[272,128]{1,0:T(8,128)(2,1)S(1)}, u32[]{:S(2)}, u32[]{:S(2)}) collective-permute-start(s16[272,128]{1,0:T(8,128)(2,1)S(1)} %keep_half.1.own_ref), channel_id=1, source_target_pairs={{8,0},{12,4},{0,8},{4,12},{9,1},{13,5},{1,9},{5,13},{10,2},{14,6},... | collective-permute-start | bytes 208904 | tf_op jit(solution)/shard_map/ppermute | solution.py:506
  24.1 4.0 %collective-permute-done.7.arrived_ref = s16[272,128]{1,0:T(8,128)(2,1)S(1)} collective-permute-done((s16[272,128]{1,0:T(8,128)(2,1)S(1)}, s16[272,128]{1,0:T(8,128)(2,1)S(1)}, u32[]{:S(2)}, u32[]{:S(2)}) %collective-permute-start.7) | collective-permute-done | bytes 69664 | tf_op jit(solution)/shard_map/ppermute | solution.py:506
  28.2 1.5 %collective-permute-start.8 = (bf16[256,128]{1,0:T(8,128)(2,1)S(1)}, bf16[256,128]{1,0:T(8,128)(2,1)S(1)}, u32[]{:S(2)}, u32[]{:S(2)}) collective-permute-start(bf16[256,128]{1,0:T(8,128)(2,1)S(1)} %finish_half.1.refs_0_), channel_id=1, source_target_pairs={{16,0},{0,16},{17,1},{1,17},{18,2},{2,18},{19,3},{3,19},{20,4},{4,... | collective-permute-start | bytes 196616 | tf_op jit(solution)/shard_map/ppermute | solution.py:501
  29.7 0.4 %collective-permute-start.9 = (bf16[256,128]{1,0:T(8,128)(2,1)S(1)}, bf16[256,128]{1,0:T(8,128)(2,1)S(1)}, u32[]{:S(2)}, u32[]{:S(2)}) collective-permute-start(bf16[256,128]{1,0:T(8,128)(2,1)S(1)} %finish_half.1.refs_0_), channel_id=1, source_target_pairs={{4,0},{0,4},{12,8},{8,12},{5,1},{1,5},{13,9},{9,13},{6,2},{2,6},{1... | collective-permute-start | bytes 196616 | tf_op jit(solution)/shard_map/ppermute | solution.py:506
  30.2 2.4 %collective-permute-done.8.refs_1_ = bf16[256,128]{1,0:T(8,128)(2,1)S(1)} collective-permute-done((bf16[256,128]{1,0:T(8,128)(2,1)S(1)}, bf16[256,128]{1,0:T(8,128)(2,1)S(1)}, u32[]{:S(2)}, u32[]{:S(2)}) %collective-permute-start.8) | collective-permute-done | bytes 65568 | tf_op jit(solution)/shard_map/ppermute | solution.py:501
  32.5 0.4 %collective-permute-start.10 = (bf16[256,128]{1,0:T(8,128)(2,1)S(1)}, bf16[256,128]{1,0:T(8,128)(2,1)S(1)}, u32[]{:S(2)}, u32[]{:S(2)}) collective-permute-start(bf16[256,128]{1,0:T(8,128)(2,1)S(1)} %collective-permute-done.8.refs_1_), channel_id=1, source_target_pairs={{4,0},{0,4},{12,8},{8,12},{5,1},{1,5},{13,9},{9,13},{6,2},{2,6},{1... | collective-permute-start | bytes 196616 | tf_op jit(solution)/shard_map/ppermute | solution.py:506
  32.9 0.0 copy-done
  32.9 0.8 %first_contraction.1.refs_4_ = f32[2,32,128]{2,1,0:T(8,128)S(1)} custom-call(f32[2,2,8,128]{3,2,1,0:T(8,128)S(1)} %get-tuple-element.17.weight_ref, bf16[2,512,512]{2,1,0:T(8,128)(2,1)S(1)} %bitcast.8, bf16[256,128]{1,0:T(8,128)(2,1)S(1)} %finish_half.1.refs_0_, bf16[256,128]{1,0:T(8,128)(2,1)S(1)} %collective-permute-done.8.refs_1_), custom_call_target="tpu_custom_call" | custom-call | tf_op jit(solution)/shard_map/first_contraction/pallas_call | solution.py:628
  33.8 0.2 collective-permute-done.9.refs_2_
  34.0 2.8 %collective-permute-done.10.refs_3_ = bf16[256,128]{1,0:T(8,128)(2,1)S(1)} collective-permute-done((bf16[256,128]{1,0:T(8,128)(2,1)S(1)}, bf16[256,128]{1,0:T(8,128)(2,1)S(1)}, u32[]{:S(2)}, u32[]{:S(2)}) %collective-permute-start.10) | collective-permute-done | bytes 65568 | tf_op jit(solution)/shard_map/ppermute | solution.py:506
  36.8 1.6 %second_contraction.1 = (f32[1,512,128]{2,1,0:T(8,128)}, f32[1,2,2]{2,1,0:T(2,128)}) custom-call(f32[2,2,8,128]{3,2,1,0:T(8,128)S(1)} %get-tuple-element.17.weight_ref, bf16[2,512,512]{2,1,0:T(8,128)(2,1)S(1)} %bitcast.9, bf16[256,128]{1,0:T(8,128)(2,1)S(1)} %finish_half.1.refs_0_, bf16[256,128]{1,0:T(8,128)(2,1)S(1)} %collective-permute-done.8.refs_1_, ...), custom_call_target="tpu_custom_call" | custom-call | tf_op jit(solution)/shard_map/second_contraction/pallas_call | solution.py:637
  (1 shorter events, 0.0 us)
Async XLA Ops:
  0.6 9.0 %collective-permute-start.1 = (bf16[1,2,144,128]{3,2,1,0:T(8,128)(2,1)}, bf16[1,2,144,128]{3,2,1,0:T(8,128)(2,1)S(1)}, u32[]{:S(2)}, u32[]{:S(2)}) collective-permute-start(bf16[1,2,144,128]{3,2,1,0:T(8,128)(2,1)} %bitcast.10), channel_id=1, source_target_pairs={{1,0},{2,1},{3,2},{0,3},{5,4},{6,5},{7,6},{4,7},{9,8},{10,9},{11,1... | collective-permute-start | bytes 221192 | tf_op jit(solution)/shard_map/ppermute | solution.py:501
  3.1 6.5 %collective-permute-start = (bf16[1,2,144,128]{3,2,1,0:T(8,128)(2,1)}, bf16[1,2,144,128]{3,2,1,0:T(8,128)(2,1)S(1)}, u32[]{:S(2)}, u32[]{:S(2)}) collective-permute-start(bf16[1,2,144,128]{3,2,1,0:T(8,128)(2,1)} %bitcast.11), channel_id=1, source_target_pairs={{4,0},{8,4},{12,8},{0,12},{5,1},{9,5},{13,9},{1,13},{6,2},{10,6},{... | collective-permute-start | bytes 221192 | tf_op jit(solution)/shard_map/ppermute | solution.py:501
  10.8 1.6 %collective-permute-start.3 = (f32[1,512,128]{2,1,0:T(8,128)S(1)}, f32[1,512,128]{2,1,0:T(8,128)S(1)}, u32[]{:S(2)}, u32[]{:S(2)}) collective-permute-start(f32[1,512,128]{2,1,0:T(8,128)S(1)} %get-tuple-element.27), channel_id=1, source_target_pairs={{1,0},{0,1},{3,2},{2,3},{5,4},{4,5},{7,6},{6,7},{9,8},{8,9},{11,10... | collective-permute-start | bytes 786440 | tf_op jit(solution)/shard_map/ppermute | solution.py:506
  11.1 3.4 %collective-permute-start.2 = (f32[1,512,128]{2,1,0:T(8,128)S(1)}, f32[1,512,128]{2,1,0:T(8,128)S(1)}, u32[]{:S(2)}, u32[]{:S(2)}) collective-permute-start(f32[1,512,128]{2,1,0:T(8,128)S(1)} %get-tuple-element.25), channel_id=1, source_target_pairs={{1,0},{0,1},{3,2},{2,3},{5,4},{4,5},{7,6},{6,7},{9,8},{8,9},{11,10... | collective-permute-start | bytes 786440 | tf_op jit(solution)/shard_map/ppermute | solution.py:506
  12.4 20.6 %copy-start = (bf16[1,2,512,512]{3,2,1,0:T(8,128)(2,1)S(1)}, bf16[1,2,512,512]{3,2,1,0:T(8,128)(2,1)}, u32[]{:S(2)}) copy-start(bf16[1,2,512,512]{3,2,1,0:T(8,128)(2,1)} %param.12) | copy-start | bytes 3145732
  12.5 5.0 %collective-permute-start.5 = (s16[272,128]{1,0:T(8,128)(2,1)S(1)}, s16[272,128]{1,0:T(8,128)(2,1)S(1)}, u32[]{:S(2)}, u32[]{:S(2)}) collective-permute-start(s16[272,128]{1,0:T(8,128)(2,1)S(1)} %get-tuple-element.29), channel_id=1, source_target_pairs={{2,0},{3,1},{0,2},{1,3},{6,4},{7,5},{4,6},{5,7},{10,8},{11,9},{8,1... | collective-permute-start | bytes 208904 | tf_op jit(solution)/shard_map/ppermute | solution.py:506
  13.2 5.1 %collective-permute-start.4 = (s16[272,128]{1,0:T(8,128)(2,1)S(1)}, s16[272,128]{1,0:T(8,128)(2,1)S(1)}, u32[]{:S(2)}, u32[]{:S(2)}) collective-permute-start(s16[272,128]{1,0:T(8,128)(2,1)S(1)} %get-tuple-element.28), channel_id=1, source_target_pairs={{2,0},{3,1},{0,2},{1,3},{6,4},{7,5},{4,6},{5,7},{10,8},{11,9},{8,1... | collective-permute-start | bytes 208904 | tf_op jit(solution)/shard_map/ppermute | solution.py:506
  17.6 4.4 %collective-permute-start.6 = (s16[272,128]{1,0:T(8,128)(2,1)S(1)}, s16[272,128]{1,0:T(8,128)(2,1)S(1)}, u32[]{:S(2)}, u32[]{:S(2)}) collective-permute-start(s16[272,128]{1,0:T(8,128)(2,1)S(1)} %send_half.1), channel_id=1, source_target_pairs={{4,0},{0,4},{12,8},{8,12},{5,1},{1,5},{13,9},{9,13},{6,2},{2,6},{1... | collective-permute-start | bytes 208904 | tf_op jit(solution)/shard_map/ppermute | solution.py:506
  22.1 6.0 %collective-permute-start.7 = (s16[272,128]{1,0:T(8,128)(2,1)S(1)}, s16[272,128]{1,0:T(8,128)(2,1)S(1)}, u32[]{:S(2)}, u32[]{:S(2)}) collective-permute-start(s16[272,128]{1,0:T(8,128)(2,1)S(1)} %keep_half.1.own_ref), channel_id=1, source_target_pairs={{8,0},{12,4},{0,8},{4,12},{9,1},{13,5},{1,9},{5,13},{10,2},{14,6},... | collective-permute-start | bytes 208904 | tf_op jit(solution)/shard_map/ppermute | solution.py:506
  28.2 4.3 %collective-permute-start.8 = (bf16[256,128]{1,0:T(8,128)(2,1)S(1)}, bf16[256,128]{1,0:T(8,128)(2,1)S(1)}, u32[]{:S(2)}, u32[]{:S(2)}) collective-permute-start(bf16[256,128]{1,0:T(8,128)(2,1)S(1)} %finish_half.1.refs_0_), channel_id=1, source_target_pairs={{16,0},{0,16},{17,1},{1,17},{18,2},{2,18},{19,3},{3,19},{20,4},{4,... | collective-permute-start | bytes 196616 | tf_op jit(solution)/shard_map/ppermute | solution.py:501
  29.7 4.3 %collective-permute-start.9 = (bf16[256,128]{1,0:T(8,128)(2,1)S(1)}, bf16[256,128]{1,0:T(8,128)(2,1)S(1)}, u32[]{:S(2)}, u32[]{:S(2)}) collective-permute-start(bf16[256,128]{1,0:T(8,128)(2,1)S(1)} %finish_half.1.refs_0_), channel_id=1, source_target_pairs={{4,0},{0,4},{12,8},{8,12},{5,1},{1,5},{13,9},{9,13},{6,2},{2,6},{1... | collective-permute-start | bytes 196616 | tf_op jit(solution)/shard_map/ppermute | solution.py:506
  32.5 4.3 %collective-permute-start.10 = (bf16[256,128]{1,0:T(8,128)(2,1)S(1)}, bf16[256,128]{1,0:T(8,128)(2,1)S(1)}, u32[]{:S(2)}, u32[]{:S(2)}) collective-permute-start(bf16[256,128]{1,0:T(8,128)(2,1)S(1)} %collective-permute-done.8.refs_1_), channel_id=1, source_target_pairs={{4,0},{0,4},{12,8},{8,12},{5,1},{1,5},{13,9},{9,13},{6,2},{2,6},{1... | collective-permute-start | bytes 196616 | tf_op jit(solution)/shard_map/ppermute | solution.py:506

commit v7 on v6

--- a/solution.py
+++ b/solution.py
@@ -70,16 +70,58 @@
     )
 
 
-def halo_fields(cells_x, cells_y):
-    pairs = [(0, (cells_x - 1) * cells_y + y) for y in range(cells_y)]
-    return pairs + [(1, x * cells_y + cells_y - 1) for x in range(cells_x)]
+def leaves(cells_x, cells_y, code, line):
+    if code in (0, 3):
+        return line // cells_y == 0
+    return code == 1 and line % cells_y == cells_y - 1
 
 
 def local_fields(cells_x, cells_y):
-    lines = cells_x * cells_y
-    outside = halo_fields(cells_x, cells_y)
-    every = [(code, line) for code in range(7) for line in range(lines)]
-    return [pair for pair in every if pair not in outside]
+    every = [(code, line) for code in range(7) for line in range(cells_x * cells_y)]
+    return [pair for pair in every if not leaves(cells_x, cells_y, *pair)]
+
+
+class LinkForms:
+    def __init__(self, half):
+        cells_z = half // 3
+        self.half = half
+        self.spread = one_hot(third(iota((half, cells_z), 0)) == iota((half, cells_z), 1))
+        row, col = iota((half, LINK_COLS), 0), iota((half, LINK_COLS), 1)
+        row_color = row - 3 * third(row)
+        pair_at = third(col >> 1)
+        col_in, col_out = (col >> 1) - 3 * pair_at, pair_at - 3 * third(pair_at)
+        self.pick = [(row_color == c).astype(jnp.float32) for c in (col_out, col_in)]
+        row, col = iota((LINK_COLS, 6 * 128), 0), iota((LINK_COLS, 6 * 128), 1)
+        block, place = col >> 7, col & 127
+        color = place - 3 * third(place)
+        pair_at = third(row >> 1)
+        row_in, row_out = (row >> 1) - 3 * pair_at, pair_at - 3 * third(pair_at)
+        fits = 2 * third(pair_at) + (row & 1) == block
+        self.expand = [one_hot(fits & (c == color)) for c in (row_in, row_out)]
+        row, col = iota((half, 128), 0), iota((half, 128), 1)
+        self.near = ((third(row) == third(col)) & (col < half)).astype(jnp.float32)
+
+    def seen(self, link_ref, rows_ref):
+        for k in range(LINK_COLS // 2):
+            rows_ref[2 * k : 2 * k + 2] = link_ref[k].astype(jnp.float32)
+        return lax.dot_general(
+            self.spread,
+            rows_ref[...].astype(jnp.bfloat16),
+            (((1,), (1,)), ((), ())),
+            preferred_element_type=jnp.float32,
+        )
+
+    def matrices(self, seen, way, directions):
+        blocks = jnp.dot(
+            (seen * self.pick[way]).astype(jnp.bfloat16),
+            self.expand[way][:, : 256 * directions],
+            preferred_element_type=jnp.float32,
+        )
+        cut = lambda k: blocks[:, 128 * k : 128 * k + 128] * self.near
+        return [
+            jnp.concatenate([cut(2 * d), cut(2 * d + 1)], axis=0).astype(jnp.bfloat16)
+            for d in range(directions)
+        ]
 
 
 def prepare_kernel(cells_x, cells_y, *refs):
@@ -95,25 +137,10 @@
     v_ref, link_ref, dirs_ref, moms_ref, waves_ref, pair_ref = held
     f32, bf16 = jnp.float32, jnp.bfloat16
     order, vectors = v_ref.shape[2], v_ref.shape[3]
-    half, cells_z = order // 2, order // 6
+    half = order // 2
     lines = cells_x * cells_y
     times = weight_ref.shape[1]
-    spread = one_hot(third(iota((half, cells_z), 0)) == iota((half, cells_z), 1))
-    row, col = iota((half, LINK_COLS), 0), iota((half, LINK_COLS), 1)
-    row_color = row - 3 * third(row)
-    pair_at = third(col >> 1)
-    col_in, col_out = (col >> 1) - 3 * pair_at, pair_at - 3 * third(pair_at)
-    pick = [(row_color == col_out).astype(f32), (row_color == col_in).astype(f32)]
-    wide = (LINK_COLS, 6 * 128)
-    row, col = iota(wide, 0), iota(wide, 1)
-    block, place = col >> 7, col & 127
-    color = place - 3 * third(place)
-    pair_at = third(row >> 1)
-    row_in, row_out = (row >> 1) - 3 * pair_at, pair_at - 3 * third(pair_at)
-    fits = 2 * third(pair_at) + (row & 1) == block
-    expand = [one_hot(fits & (row_in == color)), one_hot(fits & (row_out == color))]
-    row, col = iota((half, 128), 0), iota((half, 128), 1)
-    near = ((third(row) == third(col)) & (col < half)).astype(f32)
+    forms = LinkForms(half)
     planar = planar_order(order)
     for copy in copies:
         copy.wait()
@@ -122,10 +149,6 @@
         source = pair_ref[0, 1] == t
         weight_ref[0, t] = jnp.full(weight_ref.shape[2:], jnp.where(sink, 1.0, 0.0), f32)
         weight_ref[1, t] = jnp.full(weight_ref.shape[2:], jnp.where(source, 1.0, 0.0), f32)
-    for line in range(lines):
-        for k in range(LINK_COLS // 2):
-            link_rows_ref[line, 2 * k : 2 * k + 2] = link_ref[line, k].astype(f32)
-    outside = halo_fields(cells_x, cells_y)
     inside = local_fields(cells_x, cells_y)
     ordered = []
     for line in range(lines):
@@ -142,35 +165,24 @@
         columns = slice(line * order, (line + 1) * order)
         left_ref[0, :, columns] = here.T.astype(bf16)
         left_ref[1, :, columns] = ahead_z.T.astype(bf16)
-        seen = lax.dot_general(
-            spread,
-            link_rows_ref[line].astype(bf16),
-            (((1,), (1,)), ((), ())),
-            preferred_element_type=f32,
-        )
+        seen = forms.seen(link_ref.at[line], link_rows_ref.at[line])
         pair = side_by_side(here)
-        for way in range(2):
-            blocks = jnp.dot(
-                (seen * pick[way]).astype(bf16), expand[way], preferred_element_type=f32
+        on_x = line + cells_y if line + cells_y < lines else None
+        for d, matrix in enumerate(forms.matrices(seen, 0, 3)):
+            if d == 0 and on_x is None:
+                continue
+            if d == 1 and leaves(cells_x, cells_y, 1, line):
+                matrix_ref[line // cells_y] = matrix
+                continue
+            ahead = (ordered[on_x] if d == 0 else ordered[line + 1]) if d < 2 else ahead_z
+            local_ref[inside.index((d, on_x if d == 0 else line))] = transport(
+                matrix[:, :half], side_by_side(ahead), 1
             )
-            for d in range(3):
-                matrix = jnp.concatenate(
-                    [
-                        blocks[:, 256 * d : 256 * d + 128] * near,
-                        blocks[:, 256 * d + 128 : 256 * d + 256] * near,
-                    ],
-                    axis=0,
-                ).astype(bf16)
-                if way == 1:
-                    carried = transport(matrix[:, :half], pair, -1)
-                    local_ref[inside.index((3 + d, line))] = carried.astype(bf16).astype(f32)
-                elif (d, line) in outside:
-                    matrix_ref[outside.index((d, line))] = matrix
-                else:
-                    ahead = ahead_z if d == 2 else ordered[line + (cells_y if d == 0 else 1)]
-                    local_ref[inside.index((d, line))] = transport(
-                        matrix[:, :half], side_by_side(ahead), 1
-                    )
+        for d, matrix in enumerate(forms.matrices(seen, 1, 3)):
+            if d == 0 and on_x is None:
+                continue
+            carried = transport(matrix[:, :half], pair, -1).astype(bf16).astype(f32)
+            local_ref[inside.index((3 + d, on_x if d == 0 else line))] = carried
     wave_cols = waves_ref.shape[1]
     per_term = wave_cols // 3
     row, col = iota((wave_cols, 2 * vectors), 0), iota((wave_cols, 2 * vectors), 1)
@@ -183,6 +195,17 @@
         )
 
 
+def behind_kernel(cells_x, cells_y, link_ref, local_ref, field_ref, matrix_ref, rows_ref):
+    half = local_ref.shape[1] // 2
+    forms = LinkForms(half)
+    inside = local_fields(cells_x, cells_y)
+    for y in range(cells_y):
+        seen = forms.seen(link_ref.at[y], rows_ref.at[y])
+        pair = side_by_side(local_ref[inside.index((6, y))])
+        field_ref[y] = transport(forms.matrices(seen, 0, 1)[0][:, :half], pair, 1)
+        matrix_ref[y] = forms.matrices(seen, 1, 1)[0]
+
+
 def low_bit(j):
     return (j & -j).bit_length() - 1
 
@@ -204,9 +227,10 @@
 
 
 def first_margin_kernel(cells_x, cells_y, groups, own_ops, *refs):
-    matrix_ref, local_ref, left_ref, phase_ref, halo_x_ref, halo_y_ref, dirs_hbm = refs[:7]
-    swap_ref, hold_ref, later_side_ref, later_pair_ref = refs[7:11]
-    field_ref, side_ref, dirs_ref, sem = refs[11:]
+    matrix_ref, local_ref, left_ref, phase_ref, behind_ref, adjoint_ref = refs[:6]
+    halo_x_ref, halo_y_ref, dirs_hbm = refs[6:9]
+    swap_ref, hold_ref, later_side_ref, later_pair_ref = refs[9:13]
+    field_ref, side_ref, dirs_ref, sem = refs[13:]
     f32, bf16 = jnp.float32, jnp.bfloat16
     copy = pltpu.make_async_copy(dirs_hbm, dirs_ref, sem)
     copy.start()
@@ -216,20 +240,24 @@
     planar = planar_order(order)
     side_ref[0] = left_ref[0]
     side_ref[3] = left_ref[1]
-    outside = halo_fields(cells_x, cells_y)
-    for d in range(2):
-        for line in range(lines):
-            x, y = line // cells_y, line % cells_y
-            columns = slice(line * order, (line + 1) * order)
-            if (d, line) not in outside:
-                ahead = line + (cells_y if d == 0 else 1)
-                side_ref[1 + d, :, columns] = left_ref[0, :, ahead * order : (ahead + 1) * order]
-                continue
-            halo = halo_x_ref[0, y] if d == 0 else halo_y_ref[x, 0]
-            ahead = jnp.dot(planar, halo, preferred_element_type=f32)
-            side_ref[1 + d, :, columns] = ahead.T.astype(bf16)
-            matrix = matrix_ref[outside.index((d, line))]
-            field_ref[d, line] = transport(matrix[:, :half], side_by_side(ahead), 1)
+    for line in range(lines):
+        x, y = line // cells_y, line % cells_y
+        columns = slice(line * order, (line + 1) * order)
+        if x:
+            back = line - cells_y
+            side_ref[1, :, columns] = left_ref[0, :, back * order : (back + 1) * order]
+        else:
+            back = jnp.dot(planar, halo_x_ref[0, y], preferred_element_type=f32)
+            side_ref[1, :, columns] = back.T.astype(bf16)
+            field_ref[0, line] = behind_ref[y]
+            carried = transport(adjoint_ref[y, :, :half], side_by_side(back), -1)
+            field_ref[3, line] = carried.astype(bf16).astype(f32)
+        if y + 1 < cells_y:
+            side_ref[2, :, columns] = left_ref[0, :, (line + 1) * order : (line + 2) * order]
+        else:
+            ahead = jnp.dot(planar, halo_y_ref[x, 0], preferred_element_type=f32)
+            side_ref[2, :, columns] = ahead.T.astype(bf16)
+            field_ref[1, line] = transport(matrix_ref[x, :, :half], side_by_side(ahead), 1)
     for k, (code, line) in enumerate(local_fields(cells_x, cells_y)):
         field_ref[code, line] = local_ref[k]
     copy.wait()
@@ -239,7 +267,7 @@
         for i in range(own_ops):
             o = (me ^ j) * own_ops + i
             code = dirs_ref[o]
-            side = jnp.where((code >= 3) & (code < 6), code - 2, 0)
+            side = jnp.where(code == 0, 1, jnp.where((code == 4) | (code == 5), code - 2, 0))
             cosine = phase_ref[o, :, 0:vectors]
             sine = phase_ref[o, :, vectors : 2 * vectors]
             pairs = []
@@ -419,52 +447,63 @@
     return lambda k: ref[k * vectors : (k + 1) * vectors]
 
 
-def first_contract_kernel(times, weight_ref, tau_ref, *refs):
-    blocks, (sums_ref, left_ref, right_ref) = refs[:times], refs[times:]
-    vectors = sums_ref.shape[2]
-    blocks = [part_of(ref, vectors) for ref in blocks]
-    contract(sums_ref, weight_ref, blocks, tau_ref, left_ref, right_ref)
+def half_copy(block_ref, wide_ref, margin_hbm, sem, place):
+    half = block_ref.shape[0]
+    wide_ref[...] = block_ref[...].astype(jnp.float32)
+    rows = pl.ds(pl.multiple_of(place * half, half), half)
+    copy = pltpu.make_async_copy(wide_ref, margin_hbm.at[0, rows], sem)
+    copy.start()
+    return copy
+
+
+def first_contract_kernel(times, split, weight_ref, tau_ref, *refs):
+    blocks, (margin_hbm, sums_ref, left_ref, right_ref, wide_ref, sem) = refs[:times], refs[times:]
+    me = lax.axis_index("gx") & 1
+    copy = half_copy(blocks[0], wide_ref, margin_hbm, sem, me)
+    if split:
+        vectors = sums_ref.shape[2]
+        blocks = [part_of(ref, vectors) for ref in blocks]
+        contract(sums_ref, weight_ref, blocks, tau_ref, left_ref, right_ref)
+    else:
+        sums_ref[...] = jnp.zeros_like(sums_ref)
+    copy.wait()
 
 
 def second_contract_kernel(times, split, weight_ref, tau_ref, *refs):
     kept, other, refs = refs[:times], refs[times : 2 * times], refs[2 * times :]
-    if split:
-        first_sums_ref, refs = refs[0], refs[1:]
-    margin_ref, corr_ref, sums_ref, left_ref, right_ref = refs
+    first_sums_ref, _, margin_hbm, corr_ref, sums_ref, left_ref, right_ref, wide_ref, sem = refs
     vectors = sums_ref.shape[2]
     half = kept[0].shape[0]
     me = lax.axis_index("gx") & 1
-    places = (me, 1 - me)
-    for place, ref in zip(places, (kept[0], other[0])):
-        span = pl.ds(pl.multiple_of(place * half, half), half)
-        margin_ref[0, span] = ref[...].astype(jnp.float32)
-    scale = 1.0 / vectors
-
-    def put(sums, first):
-        for k in range(sums.shape[0]):
-            corr_ref[0, first + k // 2, k % 2] = jnp.sum(sums[k]) * scale
-
+    copy = half_copy(other[0], wide_ref, margin_hbm, sem, 1 - me)
     if split:
         blocks = [part_of(ref, vectors) for ref in other]
-        contract(sums_ref, weight_ref, blocks, tau_ref, left_ref, right_ref)
-        own_ops = sums_ref.shape[0] // 2
-        put(first_sums_ref, places[0] * own_ops)
-        put(sums_ref, places[1] * own_ops)
-        return
-    parts_per_half = half // vectors
-
-    def either(kept_ref, other_ref):
-        def part(k):
-            row = (k % parts_per_half) * vectors
-            own, far = kept_ref[row : row + vectors], other_ref[row : row + vectors]
-            mine = (k // parts_per_half == me).astype(jnp.float32)
-            return own.astype(jnp.float32) * mine + far.astype(jnp.float32) * (1.0 - mine)
-
-        return part
-
-    blocks = [either(a, b) for a, b in zip(kept, other)]
+    else:
+        parts_per_half = half // vectors
+
+        def either(kept_ref, other_ref):
+            def part(k):
+                row = (k % parts_per_half) * vectors
+                own, far = kept_ref[row : row + vectors], other_ref[row : row + vectors]
+                mine = (k // parts_per_half == me).astype(jnp.float32)
+                return own.astype(jnp.float32) * mine + far.astype(jnp.float32) * (1.0 - mine)
+
+            return part
+
+        blocks = [either(a, b) for a, b in zip(kept, other)]
     contract(sums_ref, weight_ref, blocks, tau_ref, left_ref, right_ref)
-    put(sums_ref, 0)
+    shape = corr_ref.shape[1:]
+    row, col = iota(shape, 0), iota(shape, 1)
+    result = jnp.zeros(shape, jnp.float32)
+    now_ops = sums_ref.shape[0] // 2
+    for ref, place in ((first_sums_ref, me), (sums_ref, 1 - me)):
+        first = place * now_ops if split else 0
+        for k in range(2 * now_ops if split or ref is sums_ref else 0):
+            total = jnp.sum(jnp.sum(ref[k], axis=0, keepdims=True), axis=1, keepdims=True)
+            here = (row == first + k // 2) & (col == k % 2)
+            result = jnp.where(here, total * (1.0 / vectors), result)
+    corr_ref[0] = result
+    copy.wait()
 
 
 def vmem_spec():
@@ -483,7 +522,7 @@
     return pltpu.with_memory_space_constraint(x, pltpu.HBM)
 
 
-def local_call(body, name, outs, in_specs, out_specs, scratch=(), cost=None):
+def local_call(body, name, outs, in_specs, out_specs, scratch=(), aliases=None):
     return pl.pallas_call(
         body,
         out_shape=outs,
@@ -491,7 +530,7 @@
         out_specs=out_specs,
         scratch_shapes=list(scratch),
         compiler_params=pltpu.CompilerParams(vmem_limit_bytes=VMEM_LIMIT),
-        cost_estimate=cost,
+        input_output_aliases=aliases or {},
         name=name,
     )
 
@@ -517,10 +556,11 @@
     own_ops = count_ops // groups
     own_rows = own_ops * 2 * vectors
     field = eigvecs.reshape(cells_x, cells_y, order, vectors)
-    halo_x = from_step(field[0:1], "gx", 1)
+    link_field = links[0].transpose(0, 1, 3, 5, 6, 4, 2).reshape(lines, 27, 2, cells_z)
+    links_x = from_step(link_field[lines - cells_y :], "gx", -1)
+    halo_x = from_step(field[cells_x - 1 :], "gx", -1)
     halo_y = from_step(field, "gy", 1)
-    link_field = links[0].transpose(0, 1, 3, 5, 6, 4, 2).reshape(lines, 27, 2, cells_z)
-    outside, inside = halo_fields(cells_x, cells_y), local_fields(cells_x, cells_y)
+    inside = local_fields(cells_x, cells_y)
     inputs = [field, link_field, op_dirs, op_moms, wave_constants(cells_z), pair_times]
     inputs = [in_hbm(x) for x in inputs]
     held = [
@@ -531,7 +571,7 @@
         functools.partial(prepare_kernel, cells_x, cells_y),
         "prepare_lines",
         (
-            jax.ShapeDtypeStruct((len(outside), order, 128), bf16),
+            jax.ShapeDtypeStruct((cells_x, order, 128), bf16),
             jax.ShapeDtypeStruct((len(inside), order, vectors), f32),
             jax.ShapeDtypeStruct((2, vectors, lines * order), bf16),
             jax.ShapeDtypeStruct((count_ops, order // 2, 2 * vectors), f32),
@@ -545,6 +585,17 @@
             pltpu.SemaphoreType.DMA((len(inputs),)),
         ],
     )(*inputs, slot_counts)
+    behind, adjoint = local_call(
+        functools.partial(behind_kernel, cells_x, cells_y),
+        "behind_lines",
+        (
+            jax.ShapeDtypeStruct((cells_y, order, vectors), f32),
+            jax.ShapeDtypeStruct((cells_y, order, 128), bf16),
+        ),
+        [vmem_spec()] * 2,
+        (vmem_spec(),) * 2,
+        [pltpu.VMEM((cells_y, LINK_COLS, cells_z), f32)],
+    )(links_x, local)
     part = lambda count: jax.ShapeDtypeStruct((count, own_rows, vectors), f32)
     later = count_ops // 2
     swap_a, hold_a, later_sides, later_pairs = local_call(
@@ -556,7 +607,7 @@
             jax.ShapeDtypeStruct((later, vectors, lines * order), bf16),
             jax.ShapeDtypeStruct((later, lines * order, 2 * vectors), bf16),
         ),
-        [vmem_spec()] * 6 + [hbm_spec()],
+        [vmem_spec()] * 8 + [hbm_spec()],
         (vmem_spec(),) * 4,
         [
             pltpu.VMEM((7, lines, order, vectors), f32),
@@ -564,7 +615,7 @@
             pltpu.SMEM((count_ops,), jnp.int32),
             pltpu.SemaphoreType.DMA,
         ],
-    )(matrices, local, left, phases, halo_x, halo_y, in_hbm(op_dirs))
+    )(matrices, local, left, phases, behind, adjoint, halo_x, halo_y, in_hbm(op_dirs))
     swapped_a = from_partner(swap_a, "gy", 1)
     held_shapes = [part(groups >> (b + 1)) for b in range(2, levels)] + [part(1)]
     swap_b, *held = local_call(
@@ -592,9 +643,11 @@
             continue
         body = functools.partial(fold_halves_kernel, vectors)
         away, kept = packed(body, "fold_halves", *inputs, rows=half, count=2)
-        away, kept = from_partner(away, "gy", 1 << b), from_partner(kept, "gy", 1 << b)
+        away = from_partner(away, "gy", 1 << b)
     body = functools.partial(half_kernel, vectors, False)
     sent = packed(body, "send_half", held[-1], *received, away, rows=half)
+    sent, kept = lax.optimization_barrier((sent, kept))
+    kept = from_partner(kept, "gy", 1 << (levels - 1))
     arrived = from_partner(sent, "gx", 1)
     body = functools.partial(half_kernel, vectors, True)
     message = packed(body, "keep_half", held[-1], *received, kept, arrived, rows=half)
@@ -622,29 +675,25 @@
         pltpu.VMEM((2 * now_ops * vectors, 2 * vectors), bf16),
         pltpu.VMEM((2 * vectors, 2 * now_ops * vectors), bf16),
     ]
-    sums = []
-    if split:
-        sums = [
-            local_call(
-                functools.partial(first_contract_kernel, times),
-                "first_contraction",
-                jax.ShapeDtypeStruct(sums_shape, f32),
-                [vmem_spec()] * (2 + times),
-                vmem_spec(),
-                scratch,
-            )(weights, perams[0], *kept)
-        ]
+    scratch += [pltpu.VMEM((half, vectors), f32), pltpu.SemaphoreType.DMA]
+    margin_shape = jax.ShapeDtypeStruct((1, own_rows, vectors), f32)
+    margins, sums = local_call(
+        functools.partial(first_contract_kernel, times, split),
+        "first_contraction",
+        (margin_shape, jax.ShapeDtypeStruct(sums_shape, f32)),
+        [vmem_spec()] * (2 + times),
+        (hbm_spec(), vmem_spec()),
+        scratch,
+    )(weights, perams[0], *kept)
     margins, correlators = local_call(
         functools.partial(second_contract_kernel, times, split),
         "second_contraction",
-        (
-            jax.ShapeDtypeStruct((1, own_rows, vectors), f32),
-            jax.ShapeDtypeStruct((1, own_ops, 2), f32),
-        ),
-        [vmem_spec()] * (2 + 2 * times + len(sums)),
-        (vmem_spec(), smem_spec()),
+        (margin_shape, jax.ShapeDtypeStruct((1, own_ops, 2), f32)),
+        [vmem_spec()] * (3 + 2 * times) + [hbm_spec()],
+        (hbm_spec(), vmem_spec()),
         [pltpu.VMEM(sums_shape, f32)] + scratch,
-    )(weights, perams[0], *kept, *other, *sums)
+        {3 + 2 * times: 0},
+    )(weights, perams[0], *kept, *other, sums, margins)
     return (margins.reshape(1, own_ops, 2, vectors, vectors), correlators)
 
 

time: 38.6 us -> 40.1 us (1.039)
  starting transfers between devices: 13.3 us -> 10.1 us
  waiting for transfers between devices: 17.2 us -> 20.4 us
  Pallas kernels: 6.46 us -> 8.12 us
    ppermute x8, starting transfers between devices: 5.71 us -> 2.87 us  [from_partner(): return lax.ppermute(block, axis, [(i ^ step, i) for i in range(count)])]
    ppermute x3 -> x4, waiting for transfers between devices: 2.36 us -> 4.35 us  [from_step(): lax.ppermute(block, axis, [((i + step) % count, i) for i in range(count)])]
    pallas_call x1 -> x2, Pallas kernels: 0.83 us -> 2.06 us  [the longest x1 1.48 us: per_device(): local_call(functools.partial(first_contract_kernel, times, split), 'first...]
    ppermute x8, waiting for transfers between devices: 14.9 us -> 16 us  [from_partner(): return lax.ppermute(block, axis, [(i ^ step, i) for i in range(count)])]
    pallas_call x1, Pallas kernels: 1.62 us -> 2.07 us  [per_device(): local_call(functools.partial(second_contract_kernel, times, split), 'seco...]
    ppermute x3 -> x4, starting transfers between devices: 7.59 us -> 7.19 us  [from_step(): lax.ppermute(block, axis, [((i + step) % count, i) for i in range(count)])]
  transfers between devices with their start and end apart: 11 -> 12, of which waited for: 8 -> 8; matrix products, arithmetic and copies ran while one was open for 0% -> 0% of each run, Pallas kernels for 9% -> 11%
where the time goes in v7:
time: 40.1 us; the launch traced here: 39.9 us
  waiting for transfers between devices  20.4 us (51%)
  starting transfers between devices  10.1 us (25%)
  Pallas kernels  8.12 us (20%)
  between operations  1.38 us (3%)
    ppermute x8, waiting for transfers between devices, from_partner(): return lax.ppermute(block, axis, [(i ^ step, i) for i in range(count)])  16 us
    ppermute x4, starting transfers between devices, from_step(): lax.ppermute(block, axis, [((i + step) % count, i) for i in range(count)])  7.19 us
    ppermute x4, waiting for transfers between devices, from_step(): lax.ppermute(block, axis, [((i + step) % count, i) for i in range(count)])  4.35 us
    ppermute x8, starting transfers between devices, from_partner(): return lax.ppermute(block, axis, [(i ^ step, i) for i in range(count)])  2.87 us
    pallas_call x1, Pallas kernels, per_device(): local_call(functools.partial(second_contract_kernel, times, split), 'seco...  2.07 us
    pallas_call x1, Pallas kernels, per_device(): local_call(functools.partial(prepare_kernel, cells_x, cells_y), 'prepare_...  2.03 us
    pallas_call x1, Pallas kernels, per_device(): local_call(functools.partial(first_contract_kernel, times, split), 'first...  1.48 us
    pallas_call x1, Pallas kernels, per_device(): local_call(functools.partial(first_margin_kernel, cells_x, cells_y, group...  1.32 us
  transfers between devices with their start and end apart: 12, of which 8 were waited for; matrix products, arithmetic and copies ran while one was open for 0% of the time, Pallas kernels for 11%

profile of v7, /device:TPU:0, one launch (start us, length us, event | category | flops | bytes accessed | tf_op | source)
XLA Modules:
  0.0 39.9 jit_solution(15094324841029972386)
XLA Ops:
  0.6 2.5 %collective-permute-start.2 = (bf16[1,2,144,128]{3,2,1,0:T(8,128)(2,1)}, bf16[1,2,144,128]{3,2,1,0:T(8,128)(2,1)S(1)}, u32[]{:S(2)}, u32[]{:S(2)}) collective-permute-start(bf16[1,2,144,128]{3,2,1,0:T(8,128)(2,1)} %bitcast.11), channel_id=1, source_target_pairs={{1,0},{2,1},{3,2},{0,3},{5,4},{6,5},{7,6},{4,7},{9,8},{10,9},{11,1... | collective-permute-start | bytes 221192 | tf_op jit(solution)/shard_map/ppermute | solution.py:540
  3.1 1.6 %collective-permute-start.1 = (bf16[1,2,144,128]{3,2,1,0:T(8,128)(2,1)}, bf16[1,2,144,128]{3,2,1,0:T(8,128)(2,1)S(1)}, u32[]{:S(2)}, u32[]{:S(2)}) collective-permute-start(bf16[1,2,144,128]{3,2,1,0:T(8,128)(2,1)} %bitcast.12), channel_id=1, source_target_pairs={{12,0},{0,4},{4,8},{8,12},{13,1},{1,5},{5,9},{9,13},{14,2},{2,6},{... | collective-permute-start | bytes 221192 | tf_op jit(solution)/shard_map/ppermute | solution.py:540
  4.7 1.6 %collective-permute-start = (bf16[2,27,2,24]{3,2,1,0:T(2,128)(2,1)}, bf16[2,27,2,24]{3,2,1,0:T(2,128)(2,1)S(1)}, u32[]{:S(2)}, u32[]{:S(2)}) collective-permute-start(bf16[2,27,2,24]{3,2,1,0:T(2,128)(2,1)} %bitcast.14), channel_id=1, source_target_pairs={{12,0},{0,4},{4,8},{8,12},{13,1},{1,5},{5,9},{9,13},{14,2},{2,6},{... | collective-permute-start | bytes 15560 | tf_op jit(solution)/shard_map/ppermute | solution.py:540
  6.9 2.0 %prepare_lines.1 = (bf16[1,144,128]{2,1,0:T(8,128)(2,1)S(1)}, f32[9,144,128]{2,1,0:T(8,128)S(1)}, bf16[2,128,288]{2,1,0:T(8,128)(2,1)S(1)}, f32[8,72,256]{2,1,0:T(8,128)S(1)}, f32[2,2,8,128]{3,2,1,0:T(8,128)S(1)}) custom-call(bf16[1,2,144,128]{3,2,1,0:T(8,128)(2,1)} %bitcast.13, bf16[2,27,2,24]{3,2,1,0:T(2,128)(2,1)} %bitcast.15, s32[8]{0:T(128)} %refs_8_.1, ...), custom_call_target="tpu_custom_call" | custom-call | tf_op jit(solution)/shard_map/prepare_lines/pallas_call | solution.py:570
  8.9 1.6 %collective-permute-done.link_ref = bf16[2,27,2,24]{3,2,1,0:T(2,128)(2,1)S(1)} collective-permute-done((bf16[2,27,2,24]{3,2,1,0:T(2,128)(2,1)}, bf16[2,27,2,24]{3,2,1,0:T(2,128)(2,1)S(1)}, u32[]{:S(2)}, u32[]{:S(2)}) %collective-permute-start) | collective-permute-done | bytes 5216 | tf_op jit(solution)/shard_map/ppermute | solution.py:540
  10.5 0.6 %behind_lines.1 = (f32[2,144,128]{2,1,0:T(8,128)S(1)}, bf16[2,144,128]{2,1,0:T(8,128)(2,1)S(1)}) custom-call(bf16[2,27,2,24]{3,2,1,0:T(2,128)(2,1)S(1)} %collective-permute-done.link_ref, f32[9,144,128]{2,1,0:T(8,128)S(1)} %get-tuple-element.25.local_ref.refs_1_), custom_call_target="tpu_custom_call" | custom-call | tf_op jit(solution)/shard_map/behind_lines/pallas_call | solution.py:588
  11.1 0.0 collective-permute-done.2.refs_7_
  11.1 0.0 collective-permute-done.1.refs_6_
  11.1 1.3 %first_margins.1 = (f32[1,512,128]{2,1,0:T(8,128)S(1)}, f32[1,512,128]{2,1,0:T(8,128)S(1)}, bf16[4,128,288]{2,1,0:T(8,128)(2,1)S(1)}, bf16[4,288,256]{2,1,0:T(8,128)(2,1)S(1)}) custom-call(bf16[1,144,128]{2,1,0:T(8,128)(2,1)S(1)} %get-tuple-element.24.refs_0_, f32[9,144,128]{2,1,0:T(8,128)S(1)} %get-tuple-element.25.local_ref.refs_1_, ...), custom_call_target="tpu_custom_call" | custom-call | tf_op jit(solution)/shard_map/first_margins/pallas_call | solution.py:601
  12.5 0.1 collective-permute-start.4
  12.5 0.3 second_margins.1
  12.9 0.6 %collective-permute-start.3 = (f32[1,512,128]{2,1,0:T(8,128)S(1)}, f32[1,512,128]{2,1,0:T(8,128)S(1)}, u32[]{:S(2)}, u32[]{:S(2)}) collective-permute-start(f32[1,512,128]{2,1,0:T(8,128)S(1)} %get-tuple-element.33), channel_id=1, source_target_pairs={{1,0},{0,1},{3,2},{2,3},{5,4},{4,5},{7,6},{6,7},{9,8},{8,9},{11,10... | collective-permute-start | bytes 786440 | tf_op jit(solution)/shard_map/ppermute | solution.py:545
  13.4 0.6 %collective-permute-done.4.refs_1_ = f32[1,512,128]{2,1,0:T(8,128)S(1)} collective-permute-done((f32[1,512,128]{2,1,0:T(8,128)S(1)}, f32[1,512,128]{2,1,0:T(8,128)S(1)}, u32[]{:S(2)}, u32[]{:S(2)}) %collective-permute-start.4) | collective-permute-done | bytes 262176 | tf_op jit(solution)/shard_map/ppermute | solution.py:545
  14.1 0.0 copy-start
  14.1 0.1 fold_halves.1
  14.2 0.7 %collective-permute-start.5 = (s16[272,128]{1,0:T(8,128)(2,1)S(1)}, s16[272,128]{1,0:T(8,128)(2,1)S(1)}, u32[]{:S(2)}, u32[]{:S(2)}) collective-permute-start(s16[272,128]{1,0:T(8,128)(2,1)S(1)} %get-tuple-element.36), channel_id=1, source_target_pairs={{2,0},{3,1},{0,2},{1,3},{6,4},{7,5},{4,6},{5,7},{10,8},{11,9},{8,1... | collective-permute-start | bytes 208904 | tf_op jit(solution)/shard_map/ppermute | solution.py:545
  14.9 0.0 collective-permute-done.3.refs_1_
  14.9 3.7 %collective-permute-done.5.refs_2_ = s16[272,128]{1,0:T(8,128)(2,1)S(1)} collective-permute-done((s16[272,128]{1,0:T(8,128)(2,1)S(1)}, s16[272,128]{1,0:T(8,128)(2,1)S(1)}, u32[]{:S(2)}, u32[]{:S(2)}) %collective-permute-start.5) | collective-permute-done | bytes 69664 | tf_op jit(solution)/shard_map/ppermute | solution.py:545
  18.6 0.1 send_half.1
  18.7 0.7 %collective-permute-start.6 = (s16[272,128]{1,0:T(8,128)(2,1)S(1)}, s16[272,128]{1,0:T(8,128)(2,1)S(1)}, u32[]{:S(2)}, u32[]{:S(2)}) collective-permute-start(s16[272,128]{1,0:T(8,128)(2,1)S(1)} %get-tuple-element.38), channel_id=1, source_target_pairs={{2,0},{3,1},{0,2},{1,3},{6,4},{7,5},{4,6},{5,7},{10,8},{11,9},{8,1... | collective-permute-start | bytes 208904 | tf_op jit(solution)/shard_map/ppermute | solution.py:545
  19.3 0.0 collective-permute-start.7
  19.3 3.7 %collective-permute-done.6.refs_2_ = s16[272,128]{1,0:T(8,128)(2,1)S(1)} collective-permute-done((s16[272,128]{1,0:T(8,128)(2,1)S(1)}, s16[272,128]{1,0:T(8,128)(2,1)S(1)}, u32[]{:S(2)}, u32[]{:S(2)}) %collective-permute-start.6) | collective-permute-done | bytes 69664 | tf_op jit(solution)/shard_map/ppermute | solution.py:545
  23.0 0.6 %collective-permute-done.7.refs_3_ = s16[272,128]{1,0:T(8,128)(2,1)S(1)} collective-permute-done((s16[272,128]{1,0:T(8,128)(2,1)S(1)}, s16[272,128]{1,0:T(8,128)(2,1)S(1)}, u32[]{:S(2)}, u32[]{:S(2)}) %collective-permute-start.7) | collective-permute-done | bytes 69664 | tf_op jit(solution)/shard_map/ppermute | solution.py:545
  23.7 0.1 keep_half.1.own_ref
  23.8 0.9 %collective-permute-start.8 = (s16[272,128]{1,0:T(8,128)(2,1)S(1)}, s16[272,128]{1,0:T(8,128)(2,1)S(1)}, u32[]{:S(2)}, u32[]{:S(2)}) collective-permute-start(s16[272,128]{1,0:T(8,128)(2,1)S(1)} %keep_half.1.own_ref), channel_id=1, source_target_pairs={{8,0},{12,4},{0,8},{4,12},{9,1},{13,5},{1,9},{5,13},{10,2},{14,6},... | collective-permute-start | bytes 208904 | tf_op jit(solution)/shard_map/ppermute | solution.py:545
  24.6 4.6 %collective-permute-done.8.arrived_ref = s16[272,128]{1,0:T(8,128)(2,1)S(1)} collective-permute-done((s16[272,128]{1,0:T(8,128)(2,1)S(1)}, s16[272,128]{1,0:T(8,128)(2,1)S(1)}, u32[]{:S(2)}, u32[]{:S(2)}) %collective-permute-start.8) | collective-permute-done | bytes 69664 | tf_op jit(solution)/shard_map/ppermute | solution.py:545
  29.3 1.6 %collective-permute-start.9 = (bf16[256,128]{1,0:T(8,128)(2,1)S(1)}, bf16[256,128]{1,0:T(8,128)(2,1)S(1)}, u32[]{:S(2)}, u32[]{:S(2)}) collective-permute-start(bf16[256,128]{1,0:T(8,128)(2,1)S(1)} %finish_half.1.refs_0_), channel_id=1, source_target_pairs={{16,0},{0,16},{17,1},{1,17},{18,2},{2,18},{19,3},{3,19},{20,4},{4,... | collective-permute-start | bytes 196616 | tf_op jit(solution)/shard_map/ppermute | solution.py:540
  30.8 0.0 collective-permute-start.10
  30.9 2.7 %collective-permute-done.9.refs_1_ = bf16[256,128]{1,0:T(8,128)(2,1)S(1)} collective-permute-done((bf16[256,128]{1,0:T(8,128)(2,1)S(1)}, bf16[256,128]{1,0:T(8,128)(2,1)S(1)}, u32[]{:S(2)}, u32[]{:S(2)}) %collective-permute-start.9) | collective-permute-done | bytes 65568 | tf_op jit(solution)/shard_map/ppermute | solution.py:540
  33.6 0.0 collective-permute-start.11
  33.6 0.0 copy-done
  33.6 1.5 %first_contraction.1 = (f32[1,512,128]{2,1,0:T(8,128)}, f32[2,32,128]{2,1,0:T(8,128)S(1)}) custom-call(f32[2,2,8,128]{3,2,1,0:T(8,128)S(1)} %get-tuple-element.23.weight_ref, bf16[2,512,512]{2,1,0:T(8,128)(2,1)S(1)} %bitcast.8, bf16[256,128]{1,0:T(8,128)(2,1)S(1)} %finish_half.1.refs_0_, bf16[256,128]{1,0:T(8,128)(2,1)S(1)} %collective-permute-done.9.refs_1_), custom_call_target="tpu_custom_call" | custom-call | tf_op jit(solution)/shard_map/first_contraction/pallas_call | solution.py:680
  35.1 0.0 collective-permute-done.10.refs_2_
  35.1 2.7 %collective-permute-done.11.refs_3_ = bf16[256,128]{1,0:T(8,128)(2,1)S(1)} collective-permute-done((bf16[256,128]{1,0:T(8,128)(2,1)S(1)}, bf16[256,128]{1,0:T(8,128)(2,1)S(1)}, u32[]{:S(2)}, u32[]{:S(2)}) %collective-permute-start.11) | collective-permute-done | bytes 65568 | tf_op jit(solution)/shard_map/ppermute | solution.py:545
  37.9 2.1 %second_contraction.1 = (f32[1,512,128]{2,1,0:T(8,128)}, f32[1,2,2]{2,1,0:T(2,128)}) custom-call(f32[2,2,8,128]{3,2,1,0:T(8,128)S(1)} %get-tuple-element.23.weight_ref, bf16[2,512,512]{2,1,0:T(8,128)(2,1)S(1)} %bitcast.9, bf16[256,128]{1,0:T(8,128)(2,1)S(1)} %finish_half.1.refs_0_, ...), custom_call_target="tpu_custom_call", output_to_operand_aliasing={{0}: (7, {})} | custom-call | tf_op jit(solution)/shard_map/second_contraction/pallas_call | solution.py:688
  (1 shorter events, 0.0 us)
Async XLA Ops:
  0.6 10.5 %collective-permute-start.2 = (bf16[1,2,144,128]{3,2,1,0:T(8,128)(2,1)}, bf16[1,2,144,128]{3,2,1,0:T(8,128)(2,1)S(1)}, u32[]{:S(2)}, u32[]{:S(2)}) collective-permute-start(bf16[1,2,144,128]{3,2,1,0:T(8,128)(2,1)} %bitcast.11), channel_id=1, source_target_pairs={{1,0},{2,1},{3,2},{0,3},{5,4},{6,5},{7,6},{4,7},{9,8},{10,9},{11,1... | collective-permute-start | bytes 221192 | tf_op jit(solution)/shard_map/ppermute | solution.py:540
  3.1 8.0 %collective-permute-start.1 = (bf16[1,2,144,128]{3,2,1,0:T(8,128)(2,1)}, bf16[1,2,144,128]{3,2,1,0:T(8,128)(2,1)S(1)}, u32[]{:S(2)}, u32[]{:S(2)}) collective-permute-start(bf16[1,2,144,128]{3,2,1,0:T(8,128)(2,1)} %bitcast.12), channel_id=1, source_target_pairs={{12,0},{0,4},{4,8},{8,12},{13,1},{1,5},{5,9},{9,13},{14,2},{2,6},{... | collective-permute-start | bytes 221192 | tf_op jit(solution)/shard_map/ppermute | solution.py:540
  4.7 5.9 %collective-permute-start = (bf16[2,27,2,24]{3,2,1,0:T(2,128)(2,1)}, bf16[2,27,2,24]{3,2,1,0:T(2,128)(2,1)S(1)}, u32[]{:S(2)}, u32[]{:S(2)}) collective-permute-start(bf16[2,27,2,24]{3,2,1,0:T(2,128)(2,1)} %bitcast.14), channel_id=1, source_target_pairs={{12,0},{0,4},{4,8},{8,12},{13,1},{1,5},{5,9},{9,13},{14,2},{2,6},{... | collective-permute-start | bytes 15560 | tf_op jit(solution)/shard_map/ppermute | solution.py:540
  12.5 1.6 %collective-permute-start.4 = (f32[1,512,128]{2,1,0:T(8,128)S(1)}, f32[1,512,128]{2,1,0:T(8,128)S(1)}, u32[]{:S(2)}, u32[]{:S(2)}) collective-permute-start(f32[1,512,128]{2,1,0:T(8,128)S(1)} %get-tuple-element.35), channel_id=1, source_target_pairs={{1,0},{0,1},{3,2},{2,3},{5,4},{4,5},{7,6},{6,7},{9,8},{8,9},{11,10... | collective-permute-start | bytes 786440 | tf_op jit(solution)/shard_map/ppermute | solution.py:545
  12.9 2.0 %collective-permute-start.3 = (f32[1,512,128]{2,1,0:T(8,128)S(1)}, f32[1,512,128]{2,1,0:T(8,128)S(1)}, u32[]{:S(2)}, u32[]{:S(2)}) collective-permute-start(f32[1,512,128]{2,1,0:T(8,128)S(1)} %get-tuple-element.33), channel_id=1, source_target_pairs={{1,0},{0,1},{3,2},{2,3},{5,4},{4,5},{7,6},{6,7},{9,8},{8,9},{11,10... | collective-permute-start | bytes 786440 | tf_op jit(solution)/shard_map/ppermute | solution.py:545
  14.1 19.5 %copy-start = (bf16[1,2,512,512]{3,2,1,0:T(8,128)(2,1)S(1)}, bf16[1,2,512,512]{3,2,1,0:T(8,128)(2,1)}, u32[]{:S(2)}) copy-start(bf16[1,2,512,512]{3,2,1,0:T(8,128)(2,1)} %param.12) | copy-start | bytes 3145732
  14.2 4.4 %collective-permute-start.5 = (s16[272,128]{1,0:T(8,128)(2,1)S(1)}, s16[272,128]{1,0:T(8,128)(2,1)S(1)}, u32[]{:S(2)}, u32[]{:S(2)}) collective-permute-start(s16[272,128]{1,0:T(8,128)(2,1)S(1)} %get-tuple-element.36), channel_id=1, source_target_pairs={{2,0},{3,1},{0,2},{1,3},{6,4},{7,5},{4,6},{5,7},{10,8},{11,9},{8,1... | collective-permute-start | bytes 208904 | tf_op jit(solution)/shard_map/ppermute | solution.py:545
  18.7 4.4 %collective-permute-start.6 = (s16[272,128]{1,0:T(8,128)(2,1)S(1)}, s16[272,128]{1,0:T(8,128)(2,1)S(1)}, u32[]{:S(2)}, u32[]{:S(2)}) collective-permute-start(s16[272,128]{1,0:T(8,128)(2,1)S(1)} %get-tuple-element.38), channel_id=1, source_target_pairs={{2,0},{3,1},{0,2},{1,3},{6,4},{7,5},{4,6},{5,7},{10,8},{11,9},{8,1... | collective-permute-start | bytes 208904 | tf_op jit(solution)/shard_map/ppermute | solution.py:545
  19.3 4.3 %collective-permute-start.7 = (s16[272,128]{1,0:T(8,128)(2,1)S(1)}, s16[272,128]{1,0:T(8,128)(2,1)S(1)}, u32[]{:S(2)}, u32[]{:S(2)}) collective-permute-start(s16[272,128]{1,0:T(8,128)(2,1)S(1)} %send_half.1), channel_id=1, source_target_pairs={{4,0},{0,4},{12,8},{8,12},{5,1},{1,5},{13,9},{9,13},{6,2},{2,6},{1... | collective-permute-start | bytes 208904 | tf_op jit(solution)/shard_map/ppermute | solution.py:545
  23.8 5.5 %collective-permute-start.8 = (s16[272,128]{1,0:T(8,128)(2,1)S(1)}, s16[272,128]{1,0:T(8,128)(2,1)S(1)}, u32[]{:S(2)}, u32[]{:S(2)}) collective-permute-start(s16[272,128]{1,0:T(8,128)(2,1)S(1)} %keep_half.1.own_ref), channel_id=1, source_target_pairs={{8,0},{12,4},{0,8},{4,12},{9,1},{13,5},{1,9},{5,13},{10,2},{14,6},... | collective-permute-start | bytes 208904 | tf_op jit(solution)/shard_map/ppermute | solution.py:545
  29.3 4.3 %collective-permute-start.9 = (bf16[256,128]{1,0:T(8,128)(2,1)S(1)}, bf16[256,128]{1,0:T(8,128)(2,1)S(1)}, u32[]{:S(2)}, u32[]{:S(2)}) collective-permute-start(bf16[256,128]{1,0:T(8,128)(2,1)S(1)} %finish_half.1.refs_0_), channel_id=1, source_target_pairs={{16,0},{0,16},{17,1},{1,17},{18,2},{2,18},{19,3},{3,19},{20,4},{4,... | collective-permute-start | bytes 196616 | tf_op jit(solution)/shard_map/ppermute | solution.py:540
  30.8 4.3 %collective-permute-start.10 = (bf16[256,128]{1,0:T(8,128)(2,1)S(1)}, bf16[256,128]{1,0:T(8,128)(2,1)S(1)}, u32[]{:S(2)}, u32[]{:S(2)}) collective-permute-start(bf16[256,128]{1,0:T(8,128)(2,1)S(1)} %finish_half.1.refs_0_), channel_id=1, source_target_pairs={{4,0},{0,4},{12,8},{8,12},{5,1},{1,5},{13,9},{9,13},{6,2},{2,6},{1... | collective-permute-start | bytes 196616 | tf_op jit(solution)/shard_map/ppermute | solution.py:545
  33.6 4.3 %collective-permute-start.11 = (bf16[256,128]{1,0:T(8,128)(2,1)S(1)}, bf16[256,128]{1,0:T(8,128)(2,1)S(1)}, u32[]{:S(2)}, u32[]{:S(2)}) collective-permute-start(bf16[256,128]{1,0:T(8,128)(2,1)S(1)} %collective-permute-done.9.refs_1_), channel_id=1, source_target_pairs={{4,0},{0,4},{12,8},{8,12},{5,1},{1,5},{13,9},{9,13},{6,2},{2,6},{1... | collective-permute-start | bytes 196616 | tf_op jit(solution)/shard_map/ppermute | solution.py:545

commit v8 on v6

--- a/solution.py
+++ b/solution.py
@@ -10,6 +10,7 @@
 from jax.sharding import PartitionSpec as P
 
 VMEM_LIMIT = 24 * 1024 * 1024
+AXES = ("ta", "gx", "gy")
 MOMENTA = 3
 LINK_COLS = 54
 TAIL = 16
@@ -84,8 +85,8 @@
 
 def prepare_kernel(cells_x, cells_y, *refs):
     inputs, live_ref, refs = refs[:6], refs[6], refs[7:]
-    matrix_ref, local_ref, left_ref, phase_ref, weight_ref = refs[:5]
-    held, link_rows_ref, sems = refs[5:11], refs[11], refs[12]
+    edge_ref, matrix_ref, local_ref, left_ref, phase_ref, weight_ref = refs[:6]
+    held, link_rows_ref, sems = refs[6:12], refs[12], refs[13]
     copies = [
         pltpu.make_async_copy(src, dst, sems.at[k])
         for k, (src, dst) in enumerate(zip(inputs, held))
@@ -117,6 +118,7 @@
     planar = planar_order(order)
     for copy in copies:
         copy.wait()
+    edge_ref[...] = v_ref[:, 0:1]
     for t in range(times):
         sink = (pair_ref[0, 0] == t) & (live_ref[0] > 0)
         source = pair_ref[0, 1] == t
@@ -183,30 +185,30 @@
         )
 
 
-def low_bit(j):
-    return (j & -j).bit_length() - 1
-
-
-def put_product(out_ref, place, i, side, pair):
+def put_product(out_ref, place, core, i, side, pair):
     vectors = pair.shape[1] // 2
     product = jnp.dot(side, pair, preferred_element_type=jnp.float32)
-    first = 2 * i * vectors
-    out_ref[place, first : first + vectors] = product[:, :vectors]
-    out_ref[place, first + vectors : first + 2 * vectors] = product[:, vectors:]
-
-
-def first_groups(groups):
-    return sorted((j for j in range(groups) if j & 2), key=lambda j: -(j & 1))
-
-
-def second_groups(groups):
-    return sorted((j for j in range(groups) if not j & 2), key=lambda j: -(j & 1))
-
-
-def first_margin_kernel(cells_x, cells_y, groups, own_ops, *refs):
+    own_ops = out_ref.shape[1] // (4 * vectors)
+    for part in range(2):
+        flat = 2 * i + part
+        block = (flat // own_ops) * 2 * own_ops + core * own_ops + flat % own_ops
+        out_ref[place, block * vectors : (block + 1) * vectors] = product[
+            :, part * vectors : (part + 1) * vectors
+        ]
+
+
+def operators(pairs, own_ops, odd):
+    mine = lax.axis_index("gy") >> 1
+    for j in range(1 if odd else 0, pairs, 2):
+        for core in range(2):
+            for i in range(own_ops):
+                yield j >> 1, core, i, (mine ^ j) * 2 * own_ops + core * own_ops + i
+
+
+def first_margin_kernel(cells_x, cells_y, pairs, own_ops, *refs):
     matrix_ref, local_ref, left_ref, phase_ref, halo_x_ref, halo_y_ref, dirs_hbm = refs[:7]
-    swap_ref, hold_ref, later_side_ref, later_pair_ref = refs[7:11]
-    field_ref, side_ref, dirs_ref, sem = refs[11:]
+    out_ref, later_side_ref, later_pair_ref = refs[7:10]
+    field_ref, side_ref, dirs_ref, sem = refs[10:]
     f32, bf16 = jnp.float32, jnp.bfloat16
     copy = pltpu.make_async_copy(dirs_hbm, dirs_ref, sem)
     copy.start()
@@ -233,38 +235,29 @@
     for k, (code, line) in enumerate(local_fields(cells_x, cells_y)):
         field_ref[code, line] = local_ref[k]
     copy.wait()
-    me = lax.axis_index("gy")
-    later = 0
-    for j in first_groups(groups) + second_groups(groups):
-        for i in range(own_ops):
-            o = (me ^ j) * own_ops + i
-            code = dirs_ref[o]
-            side = jnp.where((code >= 3) & (code < 6), code - 2, 0)
-            cosine = phase_ref[o, :, 0:vectors]
-            sine = phase_ref[o, :, vectors : 2 * vectors]
-            pairs = []
-            for line in range(lines):
-                real, imag = field_ref[code, line, 0:half], field_ref[code, line, half:order]
-                turned_r, turned_i = cosine * real - sine * imag, sine * real + cosine * imag
-                pairs.append(jnp.concatenate([turned_r, turned_i], axis=1))
-                pairs.append(jnp.concatenate([turned_i, -turned_r], axis=1))
-            pair = jnp.concatenate(pairs, axis=0).astype(bf16)
-            if j & 2:
-                put_product(swap_ref if j & 1 else hold_ref, j >> 2, i, side_ref[side], pair)
-            else:
-                later_side_ref[later] = side_ref[side]
-                later_pair_ref[later] = pair
-                later += 1
-
-
-def second_margin_kernel(groups, own_ops, side_ref, pair_ref, swap_ref, *hold_refs):
-    later = 0
-    for j in second_groups(groups):
-        level = low_bit(j) if j else groups.bit_length() - 1
-        for i in range(own_ops):
-            out_ref, place = (swap_ref, j >> 2) if j & 1 else (hold_refs[level - 2], j >> (level + 1))
-            put_product(out_ref, place, i, side_ref[later], pair_ref[later])
-            later += 1
+
+    def factors(o):
+        code = dirs_ref[o]
+        side = jnp.where((code >= 3) & (code < 6), code - 2, 0)
+        cosine = phase_ref[o, :, 0:vectors]
+        sine = phase_ref[o, :, vectors : 2 * vectors]
+        rows = []
+        for line in range(lines):
+            real, imag = field_ref[code, line, 0:half], field_ref[code, line, half:order]
+            turned_r, turned_i = cosine * real - sine * imag, sine * real + cosine * imag
+            rows.append(jnp.concatenate([turned_r, turned_i], axis=1))
+            rows.append(jnp.concatenate([turned_i, -turned_r], axis=1))
+        return side_ref[side], jnp.concatenate(rows, axis=0).astype(bf16)
+
+    for place, core, i, o in operators(pairs, own_ops, True):
+        put_product(out_ref, place, core, i, *factors(o))
+    for k, (_, _, _, o) in enumerate(operators(pairs, own_ops, False)):
+        later_side_ref[k], later_pair_ref[k] = factors(o)
+
+
+def second_margin_kernel(pairs, own_ops, side_ref, pair_ref, out_ref):
+    for k, (place, core, i, _) in enumerate(operators(pairs, own_ops, False)):
+        put_product(out_ref, place, core, i, side_ref[k], pair_ref[k])
 
 
 def scale_of(block):
@@ -290,10 +283,9 @@
     return block * jnp.exp2(scales[k : k + 1] - FIXED_BITS)
 
 
-def group_block(held_ref, received, k, j, start, rows):
-    span = pl.ds(start, rows)
-    total = held_ref[k, span] + received[0][j >> 2, span]
-    for b, ref in enumerate(received[1:], 1):
+def group_block(bases, messages, j, start, rows):
+    total = bases[0][j >> 1, pl.ds(start, rows)] + bases[1][j >> 1, pl.ds(start, rows)]
+    for b, ref in enumerate(messages):
         total = total + fixed_at(ref.at[j >> (b + 1)], start, rows)
     return total
 
@@ -307,38 +299,35 @@
     return block * jnp.exp2(scale - FIXED_BITS)
 
 
-def fold_kernel(level, vectors, *refs):
-    held_ref, received, out_ref = refs[0], refs[1:-1], refs[-1]
-    for k in range(held_ref.shape[0]):
-        j = (2 * k + 1) << level
+def fold_kernel(level, vectors, own_ref, other_ref, *refs):
+    messages, out_ref = refs[:-1], refs[-1]
+    for k in range(out_ref.shape[0]):
         blocks = [
-            group_block(held_ref, received, k, j, start, vectors)
-            for start in range(0, held_ref.shape[1], vectors)
+            group_block((own_ref, other_ref), messages, (2 * k + 1) << level, start, vectors)
+            for start in range(0, own_ref.shape[1], vectors)
         ]
         put_fixed(out_ref.at[k], blocks)
 
 
-def half_rows(held_ref, vectors, kept):
+def half_rows(half, vectors, kept):
     me = lax.axis_index("gx") & 1
-    half = held_ref.shape[1] // 2
     base = pl.multiple_of((me if kept else 1 - me) * half, half)
     return [base + step for step in range(0, half, vectors)]
 
 
-def fold_halves_kernel(vectors, *refs):
-    held_ref, received, outs = refs[0], refs[1:-2], refs[-2:]
+def fold_halves_kernel(level, vectors, own_ref, other_ref, *refs):
+    messages, outs = refs[:-2], refs[-2:]
     for kept, out_ref in enumerate(outs):
-        starts = half_rows(held_ref, vectors, kept)
-        blocks = [group_block(held_ref, received, 0, held_ref.shape[0], s, vectors) for s in starts]
-        put_fixed(out_ref, blocks)
-
-
-def half_kernel(vectors, kept, *refs):
-    count = 3 if kept else 2
-    held_ref, received, last, out_ref = refs[0], refs[1:-count], refs[-count:-1], refs[-1]
+        starts = half_rows(own_ref.shape[1] // 2, vectors, kept)
+        bases = (own_ref, other_ref)
+        put_fixed(out_ref, [group_block(bases, messages, 1 << level, s, vectors) for s in starts])
+
+
+def half_kernel(levels, vectors, kept, own_ref, other_ref, *refs):
+    messages, last, out_ref = refs[: levels - 1], refs[levels - 1 : -1], refs[-1]
     blocks = []
-    for p, start in enumerate(half_rows(held_ref, vectors, kept)):
-        total = group_block(held_ref, received, 0, 0, start, vectors)
+    for p, start in enumerate(half_rows(own_ref.shape[1] // 2, vectors, kept)):
+        total = group_block((own_ref, other_ref), messages, 0, start, vectors)
         for ref in last:
             total = total + from_fixed(ref, vectors, p)
         blocks.append(total)
@@ -415,56 +404,72 @@
         sums_ref[k] = total
 
 
-def part_of(ref, vectors):
-    return lambda k: ref[k * vectors : (k + 1) * vectors]
-
-
-def first_contract_kernel(times, weight_ref, tau_ref, *refs):
-    blocks, (sums_ref, left_ref, right_ref) = refs[:times], refs[times:]
+def hand_kernel(*refs):
+    blocks, out_ref = refs[:-1], refs[-1]
+    rows = blocks[0].shape[0] // 2
+    for t, ref in enumerate(blocks):
+        out_ref[t * rows : (t + 1) * rows] = ref[:rows]
+
+
+def own_part(handed_ref, carried_ref, t, vectors):
+    rows = carried_ref.shape[0] // 2
+    second = (lax.axis_index("gy") & 1).astype(jnp.float32)
+
+    def part(k):
+        first = handed_ref[t * rows + k * vectors : t * rows + (k + 1) * vectors]
+        mine = carried_ref[rows + k * vectors : rows + (k + 1) * vectors]
+        return first.astype(jnp.float32) * (1.0 - second) + mine.astype(jnp.float32) * second
+
+    return part
+
+
+def first_contract_kernel(times, weight_ref, tau_ref, handed_ref, *refs):
+    carried, (sums_ref, left_ref, right_ref) = refs[:times], refs[times:]
     vectors = sums_ref.shape[2]
-    blocks = [part_of(ref, vectors) for ref in blocks]
+    blocks = [own_part(handed_ref, ref, t, vectors) for t, ref in enumerate(carried)]
     contract(sums_ref, weight_ref, blocks, tau_ref, left_ref, right_ref)
 
 
 def second_contract_kernel(times, split, weight_ref, tau_ref, *refs):
+    handed, refs = refs[:2], refs[2:]
     kept, other, refs = refs[:times], refs[times : 2 * times], refs[2 * times :]
     if split:
         first_sums_ref, refs = refs[0], refs[1:]
     margin_ref, corr_ref, sums_ref, left_ref, right_ref = refs
     vectors = sums_ref.shape[2]
-    half = kept[0].shape[0]
+    half = kept[0].shape[0] // 2
     me = lax.axis_index("gx") & 1
-    places = (me, 1 - me)
-    for place, ref in zip(places, (kept[0], other[0])):
-        span = pl.ds(pl.multiple_of(place * half, half), half)
-        margin_ref[0, span] = ref[...].astype(jnp.float32)
-    scale = 1.0 / vectors
-
-    def put(sums, first):
-        for k in range(sums.shape[0]):
-            corr_ref[0, first + k // 2, k % 2] = jnp.sum(sums[k]) * scale
-
+    kept = [own_part(handed[0], ref, t, vectors) for t, ref in enumerate(kept)]
+    other = [own_part(handed[1], ref, t, vectors) for t, ref in enumerate(other)]
+    count_parts = half // vectors
+    for place, part in ((me, kept[0]), (1 - me, other[0])):
+        for k in range(count_parts):
+            start = pl.multiple_of(place * half + k * vectors, vectors)
+            margin_ref[0, pl.ds(start, vectors)] = part(k)
+
+    def either(kept_part, other_part):
+        def part(k):
+            mine = (k // count_parts == me).astype(jnp.float32)
+            k = k % count_parts
+            return kept_part(k) * mine + other_part(k) * (1.0 - mine)
+
+        return part
+
+    blocks = other if split else [either(a, b) for a, b in zip(kept, other)]
+    contract(sums_ref, weight_ref, blocks, tau_ref, left_ref, right_ref)
+    now_ops = sums_ref.shape[0] // 2
+    known = [(sums_ref, (1 - me) * now_ops)] if split else [(sums_ref, 0)]
     if split:
-        blocks = [part_of(ref, vectors) for ref in other]
-        contract(sums_ref, weight_ref, blocks, tau_ref, left_ref, right_ref)
-        own_ops = sums_ref.shape[0] // 2
-        put(first_sums_ref, places[0] * own_ops)
-        put(sums_ref, places[1] * own_ops)
-        return
-    parts_per_half = half // vectors
-
-    def either(kept_ref, other_ref):
-        def part(k):
-            row = (k % parts_per_half) * vectors
-            own, far = kept_ref[row : row + vectors], other_ref[row : row + vectors]
-            mine = (k // parts_per_half == me).astype(jnp.float32)
-            return own.astype(jnp.float32) * mine + far.astype(jnp.float32) * (1.0 - mine)
-
-        return part
-
-    blocks = [either(a, b) for a, b in zip(kept, other)]
-    contract(sums_ref, weight_ref, blocks, tau_ref, left_ref, right_ref)
-    put(sums_ref, 0)
+        known.append((first_sums_ref, me * now_ops))
+    shape = corr_ref.shape[1:]
+    row, col = iota(shape, 0), iota(shape, 1)
+    result = jnp.zeros(shape, jnp.float32)
+    for ref, first in known:
+        for k in range(2 * now_ops):
+            total = jnp.sum(jnp.sum(ref[k], axis=0, keepdims=True), axis=1, keepdims=True)
+            here = (row == first + k // 2) & (col == k % 2)
+            result = jnp.where(here, total * (1.0 / vectors), result)
+    corr_ref[0] = result
 
 
 def vmem_spec():
@@ -501,9 +506,29 @@
     return lax.ppermute(block, axis, [((i + step) % count, i) for i in range(count)])
 
 
-def from_partner(block, axis, step):
-    count = lax.axis_size(axis)
-    return lax.ppermute(block, axis, [(i ^ step, i) for i in range(count)])
+def moved(block, place):
+    sizes = [lax.axis_size(axis) for axis in AXES]
+    flat = lambda t, x, y: (t * sizes[1] + x) * sizes[2] + y
+    perm = []
+    for member in np.ndindex(*sizes):
+        target = place(*member)
+        if target is not None:
+            perm.append((flat(*member), flat(*target)))
+    return lax.ppermute(block, AXES, perm)
+
+
+def to_carrier(block):
+    return moved(block, lambda t, x, y: None if y & 1 else (t, x, y + 1))
+
+
+def from_carrier(block):
+    return moved(block, lambda t, x, y: (t, x, y - 1) if y & 1 else None)
+
+
+def between(block, t_step=0, x_bits=0, y_bits=0):
+    times = lax.axis_size("ta")
+    target = lambda t, x, y: ((t + t_step) % times, x ^ x_bits, y ^ y_bits)
+    return moved(block, lambda t, x, y: target(t, x, y) if y & 1 else None)
 
 
 def per_device(eigvecs, links, op_dirs, op_moms, perams, pair_times, slot_counts):
@@ -513,12 +538,12 @@
     lines = cells_x * cells_y
     count_ops = op_dirs.shape[0]
     times, shares, groups = lax.axis_size("ta"), lax.axis_size("gx"), lax.axis_size("gy")
-    levels = groups.bit_length() - 1
+    pairs = groups // 2
+    levels = pairs.bit_length() - 1
     own_ops = count_ops // groups
     own_rows = own_ops * 2 * vectors
     field = eigvecs.reshape(cells_x, cells_y, order, vectors)
     halo_x = from_step(field[0:1], "gx", 1)
-    halo_y = from_step(field, "gy", 1)
     link_field = links[0].transpose(0, 1, 3, 5, 6, 4, 2).reshape(lines, 27, 2, cells_z)
     outside, inside = halo_fields(cells_x, cells_y), local_fields(cells_x, cells_y)
     inputs = [field, link_field, op_dirs, op_moms, wave_constants(cells_z), pair_times]
@@ -527,10 +552,11 @@
         pltpu.SMEM(x.shape, x.dtype) if x.dtype == jnp.int32 else pltpu.VMEM(x.shape, x.dtype)
         for x in inputs
     ]
-    matrices, local, left, phases, weights = local_call(
+    edge, matrices, local, left, phases, weights = local_call(
         functools.partial(prepare_kernel, cells_x, cells_y),
         "prepare_lines",
         (
+            jax.ShapeDtypeStruct((cells_x, 1, order, vectors), bf16),
             jax.ShapeDtypeStruct((len(outside), order, 128), bf16),
             jax.ShapeDtypeStruct((len(inside), order, vectors), f32),
             jax.ShapeDtypeStruct((2, vectors, lines * order), bf16),
@@ -538,26 +564,27 @@
             jax.ShapeDtypeStruct((2, times, 8, vectors), f32),
         ),
         [hbm_spec()] * len(inputs) + [smem_spec()],
-        (vmem_spec(),) * 5,
+        (vmem_spec(),) * 6,
         held
         + [
             pltpu.VMEM((lines, LINK_COLS, cells_z), f32),
             pltpu.SemaphoreType.DMA((len(inputs),)),
         ],
     )(*inputs, slot_counts)
-    part = lambda count: jax.ShapeDtypeStruct((count, own_rows, vectors), f32)
+    halo_y = from_step(edge, "gy", 1)
+    pair_rows = 2 * own_rows
+    part = jax.ShapeDtypeStruct((pairs // 2, pair_rows, vectors), f32)
     later = count_ops // 2
-    swap_a, hold_a, later_sides, later_pairs = local_call(
-        functools.partial(first_margin_kernel, cells_x, cells_y, groups, own_ops),
+    part_a, later_sides, later_pairs = local_call(
+        functools.partial(first_margin_kernel, cells_x, cells_y, pairs, own_ops),
         "first_margins",
         (
-            part(groups // 4),
-            part(groups // 4),
+            part,
             jax.ShapeDtypeStruct((later, vectors, lines * order), bf16),
             jax.ShapeDtypeStruct((later, lines * order, 2 * vectors), bf16),
         ),
         [vmem_spec()] * 6 + [hbm_spec()],
-        (vmem_spec(),) * 4,
+        (vmem_spec(),) * 3,
         [
             pltpu.VMEM((7, lines, order, vectors), f32),
             pltpu.VMEM((4, vectors, lines * order), bf16),
@@ -565,43 +592,43 @@
             pltpu.SemaphoreType.DMA,
         ],
     )(matrices, local, left, phases, halo_x, halo_y, in_hbm(op_dirs))
-    swapped_a = from_partner(swap_a, "gy", 1)
-    held_shapes = [part(groups >> (b + 1)) for b in range(2, levels)] + [part(1)]
-    swap_b, *held = local_call(
-        functools.partial(second_margin_kernel, groups, own_ops),
+    bases_a = (part_a, to_carrier(part_a))
+    part_b = local_call(
+        functools.partial(second_margin_kernel, pairs, own_ops),
         "second_margins",
-        (part(groups // 4), *held_shapes),
+        part,
         [vmem_spec()] * 2,
-        (vmem_spec(),) * (1 + len(held_shapes)),
+        vmem_spec(),
     )(later_sides, later_pairs)
-    received = [from_partner(swap_b, "gy", 1)]
-
-    def packed(body, name, *inputs, rows=own_rows, lead=(), count=1):
+    bases_b = (part_b, to_carrier(part_b))
+
+    def packed(body, name, *inputs, rows=pair_rows, lead=(), count=1):
         shape = jax.ShapeDtypeStruct((*lead, rows + TAIL, vectors), jnp.int16)
         outs = shape if count == 1 else (shape,) * count
         specs = vmem_spec() if count == 1 else (vmem_spec(),) * count
         return local_call(body, name, outs, [vmem_spec()] * len(inputs), specs)(*inputs)
 
-    half = own_rows // 2
-    for b in range(1, levels):
-        inputs = (hold_a, swapped_a) if b == 1 else (held[b - 2], *received)
+    half = pair_rows // 2
+    messages = []
+    for b in range(levels):
+        inputs = bases_b + tuple(messages) if b else bases_a
         if b < levels - 1:
             body = functools.partial(fold_kernel, b, vectors)
-            sent = packed(body, "fold_groups", *inputs, lead=inputs[0].shape[:1])
-            received.append(from_partner(sent, "gy", 1 << b))
+            sent = packed(body, "fold_pairs", *inputs, lead=(pairs >> (b + 1),))
+            messages.append(between(sent, y_bits=2 << b))
             continue
-        body = functools.partial(fold_halves_kernel, vectors)
+        body = functools.partial(fold_halves_kernel, b, vectors)
         away, kept = packed(body, "fold_halves", *inputs, rows=half, count=2)
-        away, kept = from_partner(away, "gy", 1 << b), from_partner(kept, "gy", 1 << b)
-    body = functools.partial(half_kernel, vectors, False)
-    sent = packed(body, "send_half", held[-1], *received, away, rows=half)
-    arrived = from_partner(sent, "gx", 1)
-    body = functools.partial(half_kernel, vectors, True)
-    message = packed(body, "keep_half", held[-1], *received, kept, arrived, rows=half)
+        away, kept = between(away, y_bits=2 << b), between(kept, y_bits=2 << b)
+    body = functools.partial(half_kernel, levels, vectors, False)
+    sent = packed(body, "send_half", *bases_b, *messages, away, rows=half)
+    arrived = between(sent, x_bits=1)
+    body = functools.partial(half_kernel, levels, vectors, True)
+    message = packed(body, "keep_half", *bases_b, *messages, kept, arrived, rows=half)
     norm_factor = 1.0 / math.sqrt(3.0 * cells_x * shares * cells_y * groups * cells_z)
     step = 2
     while step < shares:
-        arrived = from_partner(message, "gx", step)
+        arrived = between(message, x_bits=step)
         step *= 2
         if step < shares:
             body = functools.partial(both_kernel, vectors, None)
@@ -613,8 +640,15 @@
         [vmem_spec()] * 2,
         vmem_spec(),
     )(message, arrived)
-    kept = [finished] + [from_step(finished, "ta", t) for t in range(1, times)]
-    other = [from_partner(block, "gx", 1) for block in kept]
+    kept = [finished] + [between(finished, t_step=-t) for t in range(1, times)]
+    other = [between(block, x_bits=1) for block in kept]
+
+    def handed(blocks, name):
+        shape = jax.ShapeDtypeStruct((times * half // 2, vectors), bf16)
+        specs = [vmem_spec()] * times
+        return from_carrier(local_call(hand_kernel, name, shape, specs, vmem_spec())(*blocks))
+
+    hands = [handed(kept, "hand_kept"), handed(other, "hand_other")]
     split = own_ops % 2 == 0
     now_ops = own_ops // 2 if split else own_ops
     sums_shape = (2 * now_ops, 32, vectors)
@@ -629,10 +663,10 @@
                 functools.partial(first_contract_kernel, times),
                 "first_contraction",
                 jax.ShapeDtypeStruct(sums_shape, f32),
-                [vmem_spec()] * (2 + times),
+                [vmem_spec()] * (3 + times),
                 vmem_spec(),
                 scratch,
-            )(weights, perams[0], *kept)
+            )(weights, perams[0], hands[0], *kept)
         ]
     margins, correlators = local_call(
         functools.partial(second_contract_kernel, times, split),
@@ -641,10 +675,10 @@
             jax.ShapeDtypeStruct((1, own_rows, vectors), f32),
             jax.ShapeDtypeStruct((1, own_ops, 2), f32),
         ),
-        [vmem_spec()] * (2 + 2 * times + len(sums)),
-        (vmem_spec(), smem_spec()),
+        [vmem_spec()] * (4 + 2 * times + len(sums)),
+        (vmem_spec(), vmem_spec()),
         [pltpu.VMEM(sums_shape, f32)] + scratch,
-    )(weights, perams[0], *kept, *other, *sums)
+    )(weights, perams[0], *hands, *kept, *other, *sums)
     return (margins.reshape(1, own_ops, 2, vectors, vectors), correlators)
 
 

time: 38.6 us -> 52.7 us (1.37)
  waiting for transfers between devices: 17.2 us -> 26.4 us
  starting transfers between devices: 13.3 us -> 17.4 us
    ppermute x8 -> x11, waiting for transfers between devices: 14.9 us -> 24.7 us  [moved(): return lax.ppermute(block, AXES, perm)]
    ppermute x8 -> x11, starting transfers between devices: 5.71 us -> 11.6 us  [moved(): return lax.ppermute(block, AXES, perm)]
    ppermute x3 -> x2, starting transfers between devices: 7.59 us -> 5.84 us  [from_step(): lax.ppermute(block, axis, [((i + step) % count, i) for i in range(count)])]
    ppermute x3 -> x2, waiting for transfers between devices: 2.36 us -> 1.64 us  [from_step(): lax.ppermute(block, axis, [((i + step) % count, i) for i in range(count)])]
    pallas_call x2 -> x4, Pallas kernels: 1.45 us -> 1.61 us  [the longest x1 1.3 us: per_device(): local_call(functools.partial(first_margin_kernel, cells_x, cells_y, pairs...]
  transfers between devices with their start and end apart: 11 -> 13, of which waited for: 8 -> 3; matrix products, arithmetic and copies ran while one was open for 0% -> 0% of each run, Pallas kernels for 9% -> 7%
where the time goes in v8:
time: 52.7 us; the launch traced here: 52.3 us
  waiting for transfers between devices  26.4 us (50%)
  starting transfers between devices  17.4 us (33%)
  Pallas kernels  6.96 us (13%)
  between operations  1.52 us (3%)
    ppermute x11, waiting for transfers between devices, moved(): return lax.ppermute(block, AXES, perm)  24.7 us
    ppermute x11, starting transfers between devices, moved(): return lax.ppermute(block, AXES, perm)  11.6 us
    ppermute x2, starting transfers between devices, from_step(): lax.ppermute(block, axis, [((i + step) % count, i) for i in range(count)])  5.84 us
    pallas_call x1, Pallas kernels, per_device(): local_call(functools.partial(prepare_kernel, cells_x, cells_y), 'prepare_...  2.24 us
    ppermute x2, waiting for transfers between devices, from_step(): lax.ppermute(block, axis, [((i + step) % count, i) for i in range(count)])  1.64 us
    pallas_call x1, Pallas kernels, per_device(): local_call(functools.partial(second_contract_kernel, times, split), 'seco...  1.62 us
    pallas_call x1, Pallas kernels, per_device(): local_call(functools.partial(first_margin_kernel, cells_x, cells_y, pairs...  1.3 us
  transfers between devices with their start and end apart: 13, of which 3 were waited for; matrix products, arithmetic and copies ran while one was open for 0% of the time, Pallas kernels for 7%

profile of v8, /device:TPU:0, one launch (start us, length us, event | category | flops | bytes accessed | tf_op | source)
XLA Modules:
  0.0 52.3 jit_solution(17726646609878303028)
XLA Ops:
  0.6 5.1 %collective-permute-start = (bf16[1,2,144,128]{3,2,1,0:T(8,128)(2,1)}, bf16[1,2,144,128]{3,2,1,0:T(8,128)(2,1)S(1)}, u32[]{:S(2)}, u32[]{:S(2)}) collective-permute-start(bf16[1,2,144,128]{3,2,1,0:T(8,128)(2,1)} %bitcast.10), channel_id=1, source_target_pairs={{4,0},{8,4},{12,8},{0,12},{5,1},{9,5},{13,9},{1,13},{6,2},{10,6},{... | collective-permute-start | bytes 221192 | tf_op jit(solution)/shard_map/ppermute | solution.py:506
  6.4 2.2 %prepare_lines.1 = (bf16[1,1,144,128]{3,2,1,0:T(8,128)(2,1)S(1)}, bf16[3,144,128]{2,1,0:T(8,128)(2,1)S(1)}, f32[11,144,128]{2,1,0:T(8,128)S(1)}, bf16[2,128,288]...) custom-call(bf16[1,2,144,128]{3,2,1,0:T(8,128)(2,1)} %bitcast.11, ...), custom_call_target="tpu_custom_call" | custom-call | tf_op jit(solution)/shard_map/prepare_lines/pallas_call | solution.py:555
  8.6 0.7 %collective-permute-start.1 = (bf16[1,1,144,128]{3,2,1,0:T(8,128)(2,1)S(1)}, bf16[1,1,144,128]{3,2,1,0:T(8,128)(2,1)S(1)}, u32[]{:S(2)}, u32[]{:S(2)}) collective-permute-start(bf16[1,1,144,128]{3,2,1,0:T(8,128)(2,1)S(1)} %get-tuple-element.20), channel_id=1, source_target_pairs={{1,0},{2,1},{3,2},{0,3},{5,4},{6,5},{7,6},{4,7},{9,8},{10,9},{11,1... | collective-permute-start | bytes 110600 | tf_op jit(solution)/shard_map/ppermute | solution.py:506
  9.4 1.6 %collective-permute-done.1.refs_5_ = bf16[1,1,144,128]{3,2,1,0:T(8,128)(2,1)S(1)} collective-permute-done((bf16[1,1,144,128]{3,2,1,0:T(8,128)(2,1)S(1)}, bf16[1,1,144,128]{3,2,1,0:T(8,128)(2,1)S(1)}, u32[]{:S(2)}, u32[]{:S(2)}) %collective-permute-start.1) | collective-permute-done | bytes 36896 | tf_op jit(solution)/shard_map/ppermute | solution.py:506
  11.0 0.0 collective-permute-done.refs_4_
  11.0 1.3 %first_margins.1 = (f32[1,1024,128]{2,1,0:T(8,128)S(1)}, bf16[4,128,288]{2,1,0:T(8,128)(2,1)S(1)}, bf16[4,288,256]{2,1,0:T(8,128)(2,1)S(1)}) custom-call(bf16[3,144,128]{2,1,0:T(8,128)(2,1)S(1)} %get-tuple-element.16.refs_0_, f32[11,144,128]{2,1,0:T(8,128)S(1)} %get-tuple-element.17.refs_1_, bf16[2,128,288]{2,1,0:T(8,128)(2,1)S(1)} %get-tuple-element.18.refs_2_, ...), custom_call_target="tpu_custom_call" | custom-call | tf_op jit(solution)/shard_map/first_margins/pallas_call | solution.py:578
  12.3 2.9 %collective-permute-start.3 = (f32[1,1024,128]{2,1,0:T(8,128)S(1)}, f32[1,1024,128]{2,1,0:T(8,128)S(1)}, u32[]{:S(2)}, u32[]{:S(2)}) collective-permute-start(f32[1,1024,128]{2,1,0:T(8,128)S(1)} %get-tuple-element.23.own_ref), channel_id=1, source_target_pairs={{0,1},{2,3},{4,5},{6,7},{8,9},{10,11},{12,13},{14,15},{16,17},{18,... | collective-permute-start | bytes 1572872 | tf_op jit(solution)/shard_map/ppermute | solution.py:517
  15.2 0.3 second_margins.1.own_ref
  15.5 1.3 %collective-permute-start.2 = (f32[1,1024,128]{2,1,0:T(8,128)S(1)}, f32[1,1024,128]{2,1,0:T(8,128)S(1)}, u32[]{:S(2)}, u32[]{:S(2)}) collective-permute-start(f32[1,1024,128]{2,1,0:T(8,128)S(1)} %second_margins.1.own_ref), channel_id=1, source_target_pairs={{0,1},{2,3},{4,5},{6,7},{8,9},{10,11},{12,13},{14,15},{16,17},{18,... | collective-permute-start | bytes 1572872 | tf_op jit(solution)/shard_map/ppermute | solution.py:517
  16.8 0.0 collective-permute-done.3.other_ref
  16.8 0.2 fold_halves.1
  17.1 0.7 %collective-permute-start.5 = (s16[528,128]{1,0:T(8,128)(2,1)S(1)}, s16[528,128]{1,0:T(8,128)(2,1)S(1)}, u32[]{:S(2)}, u32[]{:S(2)}) collective-permute-start(s16[528,128]{1,0:T(8,128)(2,1)S(1)} %get-tuple-element.25), channel_id=1, source_target_pairs={{1,3},{3,1},{5,7},{7,5},{9,11},{11,9},{13,15},{15,13},{17,19},{19,... | collective-permute-start | bytes 405512 | tf_op jit(solution)/shard_map/ppermute | solution.py:517
  17.7 0.7 %collective-permute-start.4 = (s16[528,128]{1,0:T(8,128)(2,1)S(1)}, s16[528,128]{1,0:T(8,128)(2,1)S(1)}, u32[]{:S(2)}, u32[]{:S(2)}) collective-permute-start(s16[528,128]{1,0:T(8,128)(2,1)S(1)} %get-tuple-element.24), channel_id=1, source_target_pairs={{1,3},{3,1},{5,7},{7,5},{9,11},{11,9},{13,15},{15,13},{17,19},{19,... | collective-permute-start | bytes 405512 | tf_op jit(solution)/shard_map/ppermute | solution.py:517
  18.4 0.0 collective-permute-done.2.other_ref
  18.4 0.0 collective-permute-done.5.refs_0_
  18.4 0.1 send_half.1
  18.6 0.0 copy-start
  18.6 0.8 %collective-permute-start.6 = (s16[528,128]{1,0:T(8,128)(2,1)S(1)}, s16[528,128]{1,0:T(8,128)(2,1)S(1)}, u32[]{:S(2)}, u32[]{:S(2)}) collective-permute-start(s16[528,128]{1,0:T(8,128)(2,1)S(1)} %send_half.1), channel_id=1, source_target_pairs={{1,5},{3,7},{5,1},{7,3},{9,13},{11,15},{13,9},{15,11},{17,21},{19,... | collective-permute-start | bytes 405512 | tf_op jit(solution)/shard_map/ppermute | solution.py:517
  19.4 0.0 collective-permute-done.4.refs_0_
  19.4 0.0 collective-permute-done.6.refs_1_
  19.4 0.2 keep_half.1.own_ref
  19.6 0.7 %collective-permute-start.7 = (s16[528,128]{1,0:T(8,128)(2,1)S(1)}, s16[528,128]{1,0:T(8,128)(2,1)S(1)}, u32[]{:S(2)}, u32[]{:S(2)}) collective-permute-start(s16[528,128]{1,0:T(8,128)(2,1)S(1)} %keep_half.1.own_ref), channel_id=1, source_target_pairs={{1,9},{3,11},{5,13},{7,15},{9,1},{11,3},{13,5},{15,7},{17,25},{19,... | collective-permute-start | bytes 405512 | tf_op jit(solution)/shard_map/ppermute | solution.py:517
  20.3 0.0 collective-permute-done.7.arrived_ref
  20.3 0.1 finish_half.1.refs_0_.refs_2_
  20.4 0.7 %collective-permute-start.8 = (bf16[512,128]{1,0:T(8,128)(2,1)S(1)}, bf16[512,128]{1,0:T(8,128)(2,1)S(1)}, u32[]{:S(2)}, u32[]{:S(2)}) collective-permute-start(bf16[512,128]{1,0:T(8,128)(2,1)S(1)} %finish_half.1.refs_0_.refs_2_), channel_id=1, source_target_pairs={{1,17},{3,19},{5,21},{7,23},{9,25},{11,27},{13,29},{15,31},{17,1},... | collective-permute-start | bytes 393224 | tf_op jit(solution)/shard_map/ppermute | solution.py:517
  21.0 0.7 %collective-permute-start.10 = (bf16[512,128]{1,0:T(8,128)(2,1)S(1)}, bf16[512,128]{1,0:T(8,128)(2,1)S(1)}, u32[]{:S(2)}, u32[]{:S(2)}) collective-permute-start(bf16[512,128]{1,0:T(8,128)(2,1)S(1)} %finish_half.1.refs_0_.refs_2_), channel_id=1, source_target_pairs={{1,5},{3,7},{5,1},{7,3},{9,13},{11,15},{13,9},{15,11},{17,21},{19,... | collective-permute-start | bytes 393224 | tf_op jit(solution)/shard_map/ppermute | solution.py:517
  21.7 0.0 collective-permute-done.8.refs_1_.refs_3_
  21.7 0.7 %collective-permute-start.11 = (bf16[512,128]{1,0:T(8,128)(2,1)S(1)}, bf16[512,128]{1,0:T(8,128)(2,1)S(1)}, u32[]{:S(2)}, u32[]{:S(2)}) collective-permute-start(bf16[512,128]{1,0:T(8,128)(2,1)S(1)} %collective-permute-done.8.refs_1_.refs_3_), channel_id=1, source_target_pairs={{1,5},{3,7},{5,1},{7,3},{9,13},{11,15},{13,9},{15,11},{17,21},{19,... | collective-permute-start | bytes 393224 | tf_op jit(solution)/shard_map/ppermute | solution.py:517
  22.4 1.3 %collective-permute-start.9 = (bf16[512,128]{1,0:T(8,128)(2,1)S(1)}, bf16[512,128]{1,0:T(8,128)(2,1)S(1)}, u32[]{:S(2)}, u32[]{:S(2)}) collective-permute-start(bf16[512,128]{1,0:T(8,128)(2,1)S(1)} %hand_kept.1), channel_id=1, source_target_pairs={{1,0},{3,2},{5,4},{7,6},{9,8},{11,10},{13,12},{15,14},{17,16},{19,... | collective-permute-start | bytes 393224 | tf_op jit(solution)/shard_map/ppermute | solution.py:517
  23.7 0.0 collective-permute-done.10.refs_0_.refs_4_
  23.7 0.0 collective-permute-done.11.refs_1_.refs_5_
  23.8 1.3 %collective-permute-start.12 = (bf16[512,128]{1,0:T(8,128)(2,1)S(1)}, bf16[512,128]{1,0:T(8,128)(2,1)S(1)}, u32[]{:S(2)}, u32[]{:S(2)}) collective-permute-start(bf16[512,128]{1,0:T(8,128)(2,1)S(1)} %hand_other.1), channel_id=1, source_target_pairs={{1,0},{3,2},{5,4},{7,6},{9,8},{11,10},{13,12},{15,14},{17,16},{19,... | collective-permute-start | bytes 393224 | tf_op jit(solution)/shard_map/ppermute | solution.py:517
  25.1 22.7 %collective-permute-done.9.handed_ref.refs_0_ = bf16[512,128]{1,0:T(8,128)(2,1)S(1)} collective-permute-done((bf16[512,128]{1,0:T(8,128)(2,1)S(1)}, bf16[512,128]{1,0:T(8,128)(2,1)S(1)}, u32[]{:S(2)}, u32[]{:S(2)}) %collective-permute-start.9) | collective-permute-done | bytes 131104 | tf_op jit(solution)/shard_map/ppermute | solution.py:517
  47.7 0.0 copy-done
  47.7 0.9 %first_contraction.1.refs_6_ = f32[2,32,128]{2,1,0:T(8,128)S(1)} custom-call(f32[2,2,8,128]{3,2,1,0:T(8,128)S(1)} %get-tuple-element.15.weight_ref, bf16[2,512,512]{2,1,0:T(8,128)(2,1)S(1)} %bitcast.8, bf16[512,128]{1,0:T(8,128)(2,1)S(1)} %collective-permute-done.9.handed_ref.refs_0_, bf16[512,128]{1,0:T(8,128)(2,1)S(1)} %finish_half.1.refs_0_.refs_2_, ...), custom_call_target="tpu_custom_call" | custom-call | tf_op jit(solution)/shard_map/first_contraction/pallas_call | solution.py:662
  48.6 2.1 %collective-permute-done.12.refs_1_ = bf16[512,128]{1,0:T(8,128)(2,1)S(1)} collective-permute-done((bf16[512,128]{1,0:T(8,128)(2,1)S(1)}, bf16[512,128]{1,0:T(8,128)(2,1)S(1)}, u32[]{:S(2)}, u32[]{:S(2)}) %collective-permute-start.12) | collective-permute-done | bytes 131104 | tf_op jit(solution)/shard_map/ppermute | solution.py:517
  50.7 1.6 %second_contraction.1 = (f32[1,512,128]{2,1,0:T(8,128)}, f32[1,2,2]{2,1,0:T(2,128)}) custom-call(f32[2,2,8,128]{3,2,1,0:T(8,128)S(1)} %get-tuple-element.15.weight_ref, bf16[2,512,512]{2,1,0:T(8,128)(2,1)S(1)} %bitcast.9, bf16[512,128]{1,0:T(8,128)(2,1)S(1)} %collective-permute-done.9.handed_ref.refs_0_, ...), custom_call_target="tpu_custom_call" | custom-call | tf_op jit(solution)/shard_map/second_contraction/pallas_call | solution.py:671
  (2 shorter events, 0.0 us)
Async XLA Ops:
  0.6 10.4 %collective-permute-start = (bf16[1,2,144,128]{3,2,1,0:T(8,128)(2,1)}, bf16[1,2,144,128]{3,2,1,0:T(8,128)(2,1)S(1)}, u32[]{:S(2)}, u32[]{:S(2)}) collective-permute-start(bf16[1,2,144,128]{3,2,1,0:T(8,128)(2,1)} %bitcast.10), channel_id=1, source_target_pairs={{4,0},{8,4},{12,8},{0,12},{5,1},{9,5},{13,9},{1,13},{6,2},{10,6},{... | collective-permute-start | bytes 221192 | tf_op jit(solution)/shard_map/ppermute | solution.py:506
  8.6 2.4 %collective-permute-start.1 = (bf16[1,1,144,128]{3,2,1,0:T(8,128)(2,1)S(1)}, bf16[1,1,144,128]{3,2,1,0:T(8,128)(2,1)S(1)}, u32[]{:S(2)}, u32[]{:S(2)}) collective-permute-start(bf16[1,1,144,128]{3,2,1,0:T(8,128)(2,1)S(1)} %get-tuple-element.20), channel_id=1, source_target_pairs={{1,0},{2,1},{3,2},{0,3},{5,4},{6,5},{7,6},{4,7},{9,8},{10,9},{11,1... | collective-permute-start | bytes 110600 | tf_op jit(solution)/shard_map/ppermute | solution.py:506
  12.3 4.5 %collective-permute-start.3 = (f32[1,1024,128]{2,1,0:T(8,128)S(1)}, f32[1,1024,128]{2,1,0:T(8,128)S(1)}, u32[]{:S(2)}, u32[]{:S(2)}) collective-permute-start(f32[1,1024,128]{2,1,0:T(8,128)S(1)} %get-tuple-element.23.own_ref), channel_id=1, source_target_pairs={{0,1},{2,3},{4,5},{6,7},{8,9},{10,11},{12,13},{14,15},{16,17},{18,... | collective-permute-start | bytes 1572872 | tf_op jit(solution)/shard_map/ppermute | solution.py:517
  15.5 2.9 %collective-permute-start.2 = (f32[1,1024,128]{2,1,0:T(8,128)S(1)}, f32[1,1024,128]{2,1,0:T(8,128)S(1)}, u32[]{:S(2)}, u32[]{:S(2)}) collective-permute-start(f32[1,1024,128]{2,1,0:T(8,128)S(1)} %second_margins.1.own_ref), channel_id=1, source_target_pairs={{0,1},{2,3},{4,5},{6,7},{8,9},{10,11},{12,13},{14,15},{16,17},{18,... | collective-permute-start | bytes 1572872 | tf_op jit(solution)/shard_map/ppermute | solution.py:517
  17.1 1.4 %collective-permute-start.5 = (s16[528,128]{1,0:T(8,128)(2,1)S(1)}, s16[528,128]{1,0:T(8,128)(2,1)S(1)}, u32[]{:S(2)}, u32[]{:S(2)}) collective-permute-start(s16[528,128]{1,0:T(8,128)(2,1)S(1)} %get-tuple-element.25), channel_id=1, source_target_pairs={{1,3},{3,1},{5,7},{7,5},{9,11},{11,9},{13,15},{15,13},{17,19},{19,... | collective-permute-start | bytes 405512 | tf_op jit(solution)/shard_map/ppermute | solution.py:517
  17.7 1.7 %collective-permute-start.4 = (s16[528,128]{1,0:T(8,128)(2,1)S(1)}, s16[528,128]{1,0:T(8,128)(2,1)S(1)}, u32[]{:S(2)}, u32[]{:S(2)}) collective-permute-start(s16[528,128]{1,0:T(8,128)(2,1)S(1)} %get-tuple-element.24), channel_id=1, source_target_pairs={{1,3},{3,1},{5,7},{7,5},{9,11},{11,9},{13,15},{15,13},{17,19},{19,... | collective-permute-start | bytes 405512 | tf_op jit(solution)/shard_map/ppermute | solution.py:517
  18.6 29.2 %copy-start = (bf16[1,2,512,512]{3,2,1,0:T(8,128)(2,1)S(1)}, bf16[1,2,512,512]{3,2,1,0:T(8,128)(2,1)}, u32[]{:S(2)}) copy-start(bf16[1,2,512,512]{3,2,1,0:T(8,128)(2,1)} %param.12) | copy-start | bytes 3145732
  18.6 0.8 %collective-permute-start.6 = (s16[528,128]{1,0:T(8,128)(2,1)S(1)}, s16[528,128]{1,0:T(8,128)(2,1)S(1)}, u32[]{:S(2)}, u32[]{:S(2)}) collective-permute-start(s16[528,128]{1,0:T(8,128)(2,1)S(1)} %send_half.1), channel_id=1, source_target_pairs={{1,5},{3,7},{5,1},{7,3},{9,13},{11,15},{13,9},{15,11},{17,21},{19,... | collective-permute-start | bytes 405512 | tf_op jit(solution)/shard_map/ppermute | solution.py:517
  19.6 0.7 %collective-permute-start.7 = (s16[528,128]{1,0:T(8,128)(2,1)S(1)}, s16[528,128]{1,0:T(8,128)(2,1)S(1)}, u32[]{:S(2)}, u32[]{:S(2)}) collective-permute-start(s16[528,128]{1,0:T(8,128)(2,1)S(1)} %keep_half.1.own_ref), channel_id=1, source_target_pairs={{1,9},{3,11},{5,13},{7,15},{9,1},{11,3},{13,5},{15,7},{17,25},{19,... | collective-permute-start | bytes 405512 | tf_op jit(solution)/shard_map/ppermute | solution.py:517
  20.4 1.4 %collective-permute-start.8 = (bf16[512,128]{1,0:T(8,128)(2,1)S(1)}, bf16[512,128]{1,0:T(8,128)(2,1)S(1)}, u32[]{:S(2)}, u32[]{:S(2)}) collective-permute-start(bf16[512,128]{1,0:T(8,128)(2,1)S(1)} %finish_half.1.refs_0_.refs_2_), channel_id=1, source_target_pairs={{1,17},{3,19},{5,21},{7,23},{9,25},{11,27},{13,29},{15,31},{17,1},... | collective-permute-start | bytes 393224 | tf_op jit(solution)/shard_map/ppermute | solution.py:517
  21.0 2.7 %collective-permute-start.10 = (bf16[512,128]{1,0:T(8,128)(2,1)S(1)}, bf16[512,128]{1,0:T(8,128)(2,1)S(1)}, u32[]{:S(2)}, u32[]{:S(2)}) collective-permute-start(bf16[512,128]{1,0:T(8,128)(2,1)S(1)} %finish_half.1.refs_0_.refs_2_), channel_id=1, source_target_pairs={{1,5},{3,7},{5,1},{7,3},{9,13},{11,15},{13,9},{15,11},{17,21},{19,... | collective-permute-start | bytes 393224 | tf_op jit(solution)/shard_map/ppermute | solution.py:517
  21.7 2.0 %collective-permute-start.11 = (bf16[512,128]{1,0:T(8,128)(2,1)S(1)}, bf16[512,128]{1,0:T(8,128)(2,1)S(1)}, u32[]{:S(2)}, u32[]{:S(2)}) collective-permute-start(bf16[512,128]{1,0:T(8,128)(2,1)S(1)} %collective-permute-done.8.refs_1_.refs_3_), channel_id=1, source_target_pairs={{1,5},{3,7},{5,1},{7,3},{9,13},{11,15},{13,9},{15,11},{17,21},{19,... | collective-permute-start | bytes 393224 | tf_op jit(solution)/shard_map/ppermute | solution.py:517
  22.4 25.3 %collective-permute-start.9 = (bf16[512,128]{1,0:T(8,128)(2,1)S(1)}, bf16[512,128]{1,0:T(8,128)(2,1)S(1)}, u32[]{:S(2)}, u32[]{:S(2)}) collective-permute-start(bf16[512,128]{1,0:T(8,128)(2,1)S(1)} %hand_kept.1), channel_id=1, source_target_pairs={{1,0},{3,2},{5,4},{7,6},{9,8},{11,10},{13,12},{15,14},{17,16},{19,... | collective-permute-start | bytes 393224 | tf_op jit(solution)/shard_map/ppermute | solution.py:517
  23.8 26.9 %collective-permute-start.12 = (bf16[512,128]{1,0:T(8,128)(2,1)S(1)}, bf16[512,128]{1,0:T(8,128)(2,1)S(1)}, u32[]{:S(2)}, u32[]{:S(2)}) collective-permute-start(bf16[512,128]{1,0:T(8,128)(2,1)S(1)} %hand_other.1), channel_id=1, source_target_pairs={{1,0},{3,2},{5,4},{7,6},{9,8},{11,10},{13,12},{15,14},{17,16},{19,... | collective-permute-start | bytes 393224 | tf_op jit(solution)/shard_map/ppermute | solution.py:517

commit v9 on v8

--- a/solution.py
+++ b/solution.py
@@ -511,24 +511,18 @@
     flat = lambda t, x, y: (t * sizes[1] + x) * sizes[2] + y
     perm = []
     for member in np.ndindex(*sizes):
-        target = place(*member)
-        if target is not None:
-            perm.append((flat(*member), flat(*target)))
+        perm.append((flat(*member), flat(*place(*member))))
     return lax.ppermute(block, AXES, perm)
 
 
-def to_carrier(block):
-    return moved(block, lambda t, x, y: None if y & 1 else (t, x, y + 1))
-
-
-def from_carrier(block):
-    return moved(block, lambda t, x, y: (t, x, y - 1) if y & 1 else None)
+def swapped(block):
+    return moved(block, lambda t, x, y: (t, x, y ^ 1))
 
 
 def between(block, t_step=0, x_bits=0, y_bits=0):
     times = lax.axis_size("ta")
     target = lambda t, x, y: ((t + t_step) % times, x ^ x_bits, y ^ y_bits)
-    return moved(block, lambda t, x, y: target(t, x, y) if y & 1 else None)
+    return moved(block, lambda t, x, y: target(t, x, y) if y & 1 else (t, x, y))
 
 
 def per_device(eigvecs, links, op_dirs, op_moms, perams, pair_times, slot_counts):
@@ -592,7 +586,7 @@
             pltpu.SemaphoreType.DMA,
         ],
     )(matrices, local, left, phases, halo_x, halo_y, in_hbm(op_dirs))
-    bases_a = (part_a, to_carrier(part_a))
+    bases_a = (part_a, swapped(part_a))
     part_b = local_call(
         functools.partial(second_margin_kernel, pairs, own_ops),
         "second_margins",
@@ -600,7 +594,7 @@
         [vmem_spec()] * 2,
         vmem_spec(),
     )(later_sides, later_pairs)
-    bases_b = (part_b, to_carrier(part_b))
+    bases_b = (part_b, swapped(part_b))
 
     def packed(body, name, *inputs, rows=pair_rows, lead=(), count=1):
         shape = jax.ShapeDtypeStruct((*lead, rows + TAIL, vectors), jnp.int16)
@@ -646,7 +640,7 @@
     def handed(blocks, name):
         shape = jax.ShapeDtypeStruct((times * half // 2, vectors), bf16)
         specs = [vmem_spec()] * times
-        return from_carrier(local_call(hand_kernel, name, shape, specs, vmem_spec())(*blocks))
+        return swapped(local_call(hand_kernel, name, shape, specs, vmem_spec())(*blocks))
 
     hands = [handed(kept, "hand_kept"), handed(other, "hand_other")]
     split = own_ops % 2 == 0

time: 52.7 us -> 49.8 us (0.945)
  waiting for transfers between devices: 26.4 us -> 2.89 us
  starting transfers between devices: 17.4 us -> 38.1 us
    ppermute x11, waiting for transfers between devices: 24.7 us -> 1.25 us  [moved(): return lax.ppermute(block, AXES, perm)]
    ppermute x11, starting transfers between devices: 11.6 us -> 32.3 us  [moved(): return lax.ppermute(block, AXES, perm)]
  transfers between devices with their start and end apart: 13 -> 13, of which waited for: 3 -> 3; matrix products, arithmetic and copies ran while one was open for 0% -> 0% of each run, Pallas kernels for 7% -> 8%
where the time goes in v9:
time: 49.8 us; the launch traced here: 49.4 us
  starting transfers between devices  38.1 us (77%)
  Pallas kernels  6.95 us (14%)
  waiting for transfers between devices  2.89 us (6%)
  between operations  1.46 us (3%)
    ppermute x11, starting transfers between devices, moved(): return lax.ppermute(block, AXES, perm)  32.3 us
    ppermute x2, starting transfers between devices, from_step(): lax.ppermute(block, axis, [((i + step) % count, i) for i in range(count)])  5.84 us
    pallas_call x1, Pallas kernels, per_device(): local_call(functools.partial(prepare_kernel, cells_x, cells_y), 'prepare_...  2.24 us
    ppermute x2, waiting for transfers between devices, from_step(): lax.ppermute(block, axis, [((i + step) % count, i) for i in range(count)])  1.64 us
    pallas_call x1, Pallas kernels, per_device(): local_call(functools.partial(second_contract_kernel, times, split), 'seco...  1.62 us
    pallas_call x1, Pallas kernels, per_device(): local_call(functools.partial(first_margin_kernel, cells_x, cells_y, pairs...  1.3 us
    ppermute x11, waiting for transfers between devices, moved(): return lax.ppermute(block, AXES, perm)  1.25 us
  transfers between devices with their start and end apart: 13, of which 3 were waited for; matrix products, arithmetic and copies ran while one was open for 0% of the time, Pallas kernels for 8%

profile of v9, /device:TPU:0, one launch (start us, length us, event | category | flops | bytes accessed | tf_op | source)
XLA Modules:
  0.0 49.4 jit_solution(1388703082216606323)
XLA Ops:
  0.6 5.1 %collective-permute-start = (bf16[1,2,144,128]{3,2,1,0:T(8,128)(2,1)}, bf16[1,2,144,128]{3,2,1,0:T(8,128)(2,1)S(1)}, u32[]{:S(2)}, u32[]{:S(2)}) collective-permute-start(bf16[1,2,144,128]{3,2,1,0:T(8,128)(2,1)} %bitcast.10), channel_id=1, source_target_pairs={{4,0},{8,4},{12,8},{0,12},{5,1},{9,5},{13,9},{1,13},{6,2},{10,6},{... | collective-permute-start | bytes 221192 | tf_op jit(solution)/shard_map/ppermute | solution.py:506
  6.4 2.2 %prepare_lines.1 = (bf16[1,1,144,128]{3,2,1,0:T(8,128)(2,1)S(1)}, bf16[3,144,128]{2,1,0:T(8,128)(2,1)S(1)}, f32[11,144,128]{2,1,0:T(8,128)S(1)}, bf16[2,128,288]...) custom-call(bf16[1,2,144,128]{3,2,1,0:T(8,128)(2,1)} %bitcast.11, ...), custom_call_target="tpu_custom_call" | custom-call | tf_op jit(solution)/shard_map/prepare_lines/pallas_call | solution.py:549
  8.6 0.7 %collective-permute-start.1 = (bf16[1,1,144,128]{3,2,1,0:T(8,128)(2,1)S(1)}, bf16[1,1,144,128]{3,2,1,0:T(8,128)(2,1)S(1)}, u32[]{:S(2)}, u32[]{:S(2)}) collective-permute-start(bf16[1,1,144,128]{3,2,1,0:T(8,128)(2,1)S(1)} %get-tuple-element.20), channel_id=1, source_target_pairs={{1,0},{2,1},{3,2},{0,3},{5,4},{6,5},{7,6},{4,7},{9,8},{10,9},{11,1... | collective-permute-start | bytes 110600 | tf_op jit(solution)/shard_map/ppermute | solution.py:506
  9.4 1.6 %collective-permute-done.1.refs_5_ = bf16[1,1,144,128]{3,2,1,0:T(8,128)(2,1)S(1)} collective-permute-done((bf16[1,1,144,128]{3,2,1,0:T(8,128)(2,1)S(1)}, bf16[1,1,144,128]{3,2,1,0:T(8,128)(2,1)S(1)}, u32[]{:S(2)}, u32[]{:S(2)}) %collective-permute-start.1) | collective-permute-done | bytes 36896 | tf_op jit(solution)/shard_map/ppermute | solution.py:506
  11.0 0.0 collective-permute-done.refs_4_
  11.0 1.3 %first_margins.1 = (f32[1,1024,128]{2,1,0:T(8,128)S(1)}, bf16[4,128,288]{2,1,0:T(8,128)(2,1)S(1)}, bf16[4,288,256]{2,1,0:T(8,128)(2,1)S(1)}) custom-call(bf16[3,144,128]{2,1,0:T(8,128)(2,1)S(1)} %get-tuple-element.16.refs_0_, f32[11,144,128]{2,1,0:T(8,128)S(1)} %get-tuple-element.17.refs_1_, bf16[2,128,288]{2,1,0:T(8,128)(2,1)S(1)} %get-tuple-element.18.refs_2_, ...), custom_call_target="tpu_custom_call" | custom-call | tf_op jit(solution)/shard_map/first_margins/pallas_call | solution.py:572
  12.3 1.0 %collective-permute-start.3 = (f32[1,1024,128]{2,1,0:T(8,128)S(1)}, f32[1,1024,128]{2,1,0:T(8,128)S(1)}, u32[]{:S(2)}, u32[]{:S(2)}) collective-permute-start(f32[1,1024,128]{2,1,0:T(8,128)S(1)} %get-tuple-element.23.own_ref), channel_id=1, source_target_pairs={{0,1},{1,0},{2,3},{3,2},{4,5},{5,4},{6,7},{7,6},{8,9},{9,8},{10,11... | collective-permute-start | bytes 1572872 | tf_op jit(solution)/shard_map/ppermute | solution.py:515
  13.3 0.3 second_margins.1.own_ref
  13.6 0.1 collective-permute-start.2
  13.7 1.1 %collective-permute-done.3.other_ref = f32[1,1024,128]{2,1,0:T(8,128)S(1)} collective-permute-done((f32[1,1024,128]{2,1,0:T(8,128)S(1)}, f32[1,1024,128]{2,1,0:T(8,128)S(1)}, u32[]{:S(2)}, u32[]{:S(2)}) %collective-permute-start.3) | collective-permute-done | bytes 524320 | tf_op jit(solution)/shard_map/ppermute | solution.py:515
  14.9 0.2 fold_halves.1
  15.1 0.7 %collective-permute-start.5 = (s16[528,128]{1,0:T(8,128)(2,1)S(1)}, s16[528,128]{1,0:T(8,128)(2,1)S(1)}, u32[]{:S(2)}, u32[]{:S(2)}) collective-permute-start(s16[528,128]{1,0:T(8,128)(2,1)S(1)} %get-tuple-element.25), channel_id=1, source_target_pairs={{0,0},{1,3},{2,2},{3,1},{4,4},{5,7},{6,6},{7,5},{8,8},{9,11},{10,1... | collective-permute-start | bytes 405512 | tf_op jit(solution)/shard_map/ppermute | solution.py:515
  15.7 0.7 %collective-permute-start.4 = (s16[528,128]{1,0:T(8,128)(2,1)S(1)}, s16[528,128]{1,0:T(8,128)(2,1)S(1)}, u32[]{:S(2)}, u32[]{:S(2)}) collective-permute-start(s16[528,128]{1,0:T(8,128)(2,1)S(1)} %get-tuple-element.24), channel_id=1, source_target_pairs={{0,0},{1,3},{2,2},{3,1},{4,4},{5,7},{6,6},{7,5},{8,8},{9,11},{10,1... | collective-permute-start | bytes 405512 | tf_op jit(solution)/shard_map/ppermute | solution.py:515
  16.4 0.0 collective-permute-done.2.other_ref
  16.4 0.0 collective-permute-done.5.refs_0_
  16.4 0.1 send_half.1
  16.6 0.0 copy-start
  16.6 0.8 %collective-permute-start.6 = (s16[528,128]{1,0:T(8,128)(2,1)S(1)}, s16[528,128]{1,0:T(8,128)(2,1)S(1)}, u32[]{:S(2)}, u32[]{:S(2)}) collective-permute-start(s16[528,128]{1,0:T(8,128)(2,1)S(1)} %send_half.1), channel_id=1, source_target_pairs={{0,0},{1,5},{2,2},{3,7},{4,4},{5,1},{6,6},{7,3},{8,8},{9,13},{10,1... | collective-permute-start | bytes 405512 | tf_op jit(solution)/shard_map/ppermute | solution.py:515
  17.4 0.0 collective-permute-done.4.refs_0_
  17.4 0.0 collective-permute-done.6.refs_1_
  17.4 0.2 keep_half.1.own_ref
  17.6 0.7 %collective-permute-start.7 = (s16[528,128]{1,0:T(8,128)(2,1)S(1)}, s16[528,128]{1,0:T(8,128)(2,1)S(1)}, u32[]{:S(2)}, u32[]{:S(2)}) collective-permute-start(s16[528,128]{1,0:T(8,128)(2,1)S(1)} %keep_half.1.own_ref), channel_id=1, source_target_pairs={{0,0},{1,9},{2,2},{3,11},{4,4},{5,13},{6,6},{7,15},{8,8},{9,1},{10... | collective-permute-start | bytes 405512 | tf_op jit(solution)/shard_map/ppermute | solution.py:515
  18.3 0.0 collective-permute-done.7.arrived_ref
  18.3 0.1 finish_half.1.refs_0_.refs_2_
  18.4 0.7 %collective-permute-start.8 = (bf16[512,128]{1,0:T(8,128)(2,1)S(1)}, bf16[512,128]{1,0:T(8,128)(2,1)S(1)}, u32[]{:S(2)}, u32[]{:S(2)}) collective-permute-start(bf16[512,128]{1,0:T(8,128)(2,1)S(1)} %finish_half.1.refs_0_.refs_2_), channel_id=1, source_target_pairs={{0,0},{1,17},{2,2},{3,19},{4,4},{5,21},{6,6},{7,23},{8,8},{9,25},{... | collective-permute-start | bytes 393224 | tf_op jit(solution)/shard_map/ppermute | solution.py:515
  19.1 0.7 %collective-permute-start.10 = (bf16[512,128]{1,0:T(8,128)(2,1)S(1)}, bf16[512,128]{1,0:T(8,128)(2,1)S(1)}, u32[]{:S(2)}, u32[]{:S(2)}) collective-permute-start(bf16[512,128]{1,0:T(8,128)(2,1)S(1)} %finish_half.1.refs_0_.refs_2_), channel_id=1, source_target_pairs={{0,0},{1,5},{2,2},{3,7},{4,4},{5,1},{6,6},{7,3},{8,8},{9,13},{10,1... | collective-permute-start | bytes 393224 | tf_op jit(solution)/shard_map/ppermute | solution.py:515
  19.7 0.0 collective-permute-done.8.refs_1_.refs_3_
  19.7 0.7 %collective-permute-start.11 = (bf16[512,128]{1,0:T(8,128)(2,1)S(1)}, bf16[512,128]{1,0:T(8,128)(2,1)S(1)}, u32[]{:S(2)}, u32[]{:S(2)}) collective-permute-start(bf16[512,128]{1,0:T(8,128)(2,1)S(1)} %collective-permute-done.8.refs_1_.refs_3_), channel_id=1, source_target_pairs={{0,0},{1,5},{2,2},{3,7},{4,4},{5,1},{6,6},{7,3},{8,8},{9,13},{10,1... | collective-permute-start | bytes 393224 | tf_op jit(solution)/shard_map/ppermute | solution.py:515
  20.4 23.4 %collective-permute-start.9 = (bf16[512,128]{1,0:T(8,128)(2,1)S(1)}, bf16[512,128]{1,0:T(8,128)(2,1)S(1)}, u32[]{:S(2)}, u32[]{:S(2)}) collective-permute-start(bf16[512,128]{1,0:T(8,128)(2,1)S(1)} %hand_kept.1), channel_id=1, source_target_pairs={{0,1},{1,0},{2,3},{3,2},{4,5},{5,4},{6,7},{7,6},{8,9},{9,8},{10,11... | collective-permute-start | bytes 393224 | tf_op jit(solution)/shard_map/ppermute | solution.py:515
  43.8 0.0 collective-permute-done.10.refs_0_.refs_4_
  43.9 0.0 collective-permute-done.11.refs_1_.refs_5_
  43.9 2.9 %collective-permute-start.12 = (bf16[512,128]{1,0:T(8,128)(2,1)S(1)}, bf16[512,128]{1,0:T(8,128)(2,1)S(1)}, u32[]{:S(2)}, u32[]{:S(2)}) collective-permute-start(bf16[512,128]{1,0:T(8,128)(2,1)S(1)} %hand_other.1), channel_id=1, source_target_pairs={{0,1},{1,0},{2,3},{3,2},{4,5},{5,4},{6,7},{7,6},{8,9},{9,8},{10,11... | collective-permute-start | bytes 393224 | tf_op jit(solution)/shard_map/ppermute | solution.py:515
  46.8 0.0 collective-permute-done.9.handed_ref.refs_0_
  46.8 0.0 copy-done
  46.8 0.9 %first_contraction.1.refs_6_ = f32[2,32,128]{2,1,0:T(8,128)S(1)} custom-call(f32[2,2,8,128]{3,2,1,0:T(8,128)S(1)} %get-tuple-element.15.weight_ref, bf16[2,512,512]{2,1,0:T(8,128)(2,1)S(1)} %bitcast.8, bf16[512,128]{1,0:T(8,128)(2,1)S(1)} %collective-permute-done.9.handed_ref.refs_0_, bf16[512,128]{1,0:T(8,128)(2,1)S(1)} %finish_half.1.refs_0_.refs_2_, ...), custom_call_target="tpu_custom_call" | custom-call | tf_op jit(solution)/shard_map/first_contraction/pallas_call | solution.py:656
  47.7 0.1 collective-permute-done.12.refs_1_
  47.8 1.6 %second_contraction.1 = (f32[1,512,128]{2,1,0:T(8,128)}, f32[1,2,2]{2,1,0:T(2,128)}) custom-call(f32[2,2,8,128]{3,2,1,0:T(8,128)S(1)} %get-tuple-element.15.weight_ref, bf16[2,512,512]{2,1,0:T(8,128)(2,1)S(1)} %bitcast.9, bf16[512,128]{1,0:T(8,128)(2,1)S(1)} %collective-permute-done.9.handed_ref.refs_0_, ...), custom_call_target="tpu_custom_call" | custom-call | tf_op jit(solution)/shard_map/second_contraction/pallas_call | solution.py:665
  (2 shorter events, 0.0 us)
Async XLA Ops:
  0.6 10.4 %collective-permute-start = (bf16[1,2,144,128]{3,2,1,0:T(8,128)(2,1)}, bf16[1,2,144,128]{3,2,1,0:T(8,128)(2,1)S(1)}, u32[]{:S(2)}, u32[]{:S(2)}) collective-permute-start(bf16[1,2,144,128]{3,2,1,0:T(8,128)(2,1)} %bitcast.10), channel_id=1, source_target_pairs={{4,0},{8,4},{12,8},{0,12},{5,1},{9,5},{13,9},{1,13},{6,2},{10,6},{... | collective-permute-start | bytes 221192 | tf_op jit(solution)/shard_map/ppermute | solution.py:506
  8.6 2.4 %collective-permute-start.1 = (bf16[1,1,144,128]{3,2,1,0:T(8,128)(2,1)S(1)}, bf16[1,1,144,128]{3,2,1,0:T(8,128)(2,1)S(1)}, u32[]{:S(2)}, u32[]{:S(2)}) collective-permute-start(bf16[1,1,144,128]{3,2,1,0:T(8,128)(2,1)S(1)} %get-tuple-element.20), channel_id=1, source_target_pairs={{1,0},{2,1},{3,2},{0,3},{5,4},{6,5},{7,6},{4,7},{9,8},{10,9},{11,1... | collective-permute-start | bytes 110600 | tf_op jit(solution)/shard_map/ppermute | solution.py:506
  12.3 2.6 %collective-permute-start.3 = (f32[1,1024,128]{2,1,0:T(8,128)S(1)}, f32[1,1024,128]{2,1,0:T(8,128)S(1)}, u32[]{:S(2)}, u32[]{:S(2)}) collective-permute-start(f32[1,1024,128]{2,1,0:T(8,128)S(1)} %get-tuple-element.23.own_ref), channel_id=1, source_target_pairs={{0,1},{1,0},{2,3},{3,2},{4,5},{5,4},{6,7},{7,6},{8,9},{9,8},{10,11... | collective-permute-start | bytes 1572872 | tf_op jit(solution)/shard_map/ppermute | solution.py:515
  13.6 2.8 %collective-permute-start.2 = (f32[1,1024,128]{2,1,0:T(8,128)S(1)}, f32[1,1024,128]{2,1,0:T(8,128)S(1)}, u32[]{:S(2)}, u32[]{:S(2)}) collective-permute-start(f32[1,1024,128]{2,1,0:T(8,128)S(1)} %second_margins.1.own_ref), channel_id=1, source_target_pairs={{0,1},{1,0},{2,3},{3,2},{4,5},{5,4},{6,7},{7,6},{8,9},{9,8},{10,11... | collective-permute-start | bytes 1572872 | tf_op jit(solution)/shard_map/ppermute | solution.py:515
  15.1 1.4 %collective-permute-start.5 = (s16[528,128]{1,0:T(8,128)(2,1)S(1)}, s16[528,128]{1,0:T(8,128)(2,1)S(1)}, u32[]{:S(2)}, u32[]{:S(2)}) collective-permute-start(s16[528,128]{1,0:T(8,128)(2,1)S(1)} %get-tuple-element.25), channel_id=1, source_target_pairs={{0,0},{1,3},{2,2},{3,1},{4,4},{5,7},{6,6},{7,5},{8,8},{9,11},{10,1... | collective-permute-start | bytes 405512 | tf_op jit(solution)/shard_map/ppermute | solution.py:515
  15.7 1.7 %collective-permute-start.4 = (s16[528,128]{1,0:T(8,128)(2,1)S(1)}, s16[528,128]{1,0:T(8,128)(2,1)S(1)}, u32[]{:S(2)}, u32[]{:S(2)}) collective-permute-start(s16[528,128]{1,0:T(8,128)(2,1)S(1)} %get-tuple-element.24), channel_id=1, source_target_pairs={{0,0},{1,3},{2,2},{3,1},{4,4},{5,7},{6,6},{7,5},{8,8},{9,11},{10,1... | collective-permute-start | bytes 405512 | tf_op jit(solution)/shard_map/ppermute | solution.py:515
  16.6 30.2 %copy-start = (bf16[1,2,512,512]{3,2,1,0:T(8,128)(2,1)S(1)}, bf16[1,2,512,512]{3,2,1,0:T(8,128)(2,1)}, u32[]{:S(2)}) copy-start(bf16[1,2,512,512]{3,2,1,0:T(8,128)(2,1)} %param.12) | copy-start | bytes 3145732
  16.6 0.8 %collective-permute-start.6 = (s16[528,128]{1,0:T(8,128)(2,1)S(1)}, s16[528,128]{1,0:T(8,128)(2,1)S(1)}, u32[]{:S(2)}, u32[]{:S(2)}) collective-permute-start(s16[528,128]{1,0:T(8,128)(2,1)S(1)} %send_half.1), channel_id=1, source_target_pairs={{0,0},{1,5},{2,2},{3,7},{4,4},{5,1},{6,6},{7,3},{8,8},{9,13},{10,1... | collective-permute-start | bytes 405512 | tf_op jit(solution)/shard_map/ppermute | solution.py:515
  17.6 0.7 %collective-permute-start.7 = (s16[528,128]{1,0:T(8,128)(2,1)S(1)}, s16[528,128]{1,0:T(8,128)(2,1)S(1)}, u32[]{:S(2)}, u32[]{:S(2)}) collective-permute-start(s16[528,128]{1,0:T(8,128)(2,1)S(1)} %keep_half.1.own_ref), channel_id=1, source_target_pairs={{0,0},{1,9},{2,2},{3,11},{4,4},{5,13},{6,6},{7,15},{8,8},{9,1},{10... | collective-permute-start | bytes 405512 | tf_op jit(solution)/shard_map/ppermute | solution.py:515
  18.4 1.4 %collective-permute-start.8 = (bf16[512,128]{1,0:T(8,128)(2,1)S(1)}, bf16[512,128]{1,0:T(8,128)(2,1)S(1)}, u32[]{:S(2)}, u32[]{:S(2)}) collective-permute-start(bf16[512,128]{1,0:T(8,128)(2,1)S(1)} %finish_half.1.refs_0_.refs_2_), channel_id=1, source_target_pairs={{0,0},{1,17},{2,2},{3,19},{4,4},{5,21},{6,6},{7,23},{8,8},{9,25},{... | collective-permute-start | bytes 393224 | tf_op jit(solution)/shard_map/ppermute | solution.py:515
  19.1 24.8 %collective-permute-start.10 = (bf16[512,128]{1,0:T(8,128)(2,1)S(1)}, bf16[512,128]{1,0:T(8,128)(2,1)S(1)}, u32[]{:S(2)}, u32[]{:S(2)}) collective-permute-start(bf16[512,128]{1,0:T(8,128)(2,1)S(1)} %finish_half.1.refs_0_.refs_2_), channel_id=1, source_target_pairs={{0,0},{1,5},{2,2},{3,7},{4,4},{5,1},{6,6},{7,3},{8,8},{9,13},{10,1... | collective-permute-start | bytes 393224 | tf_op jit(solution)/shard_map/ppermute | solution.py:515
  19.7 24.1 %collective-permute-start.11 = (bf16[512,128]{1,0:T(8,128)(2,1)S(1)}, bf16[512,128]{1,0:T(8,128)(2,1)S(1)}, u32[]{:S(2)}, u32[]{:S(2)}) collective-permute-start(bf16[512,128]{1,0:T(8,128)(2,1)S(1)} %collective-permute-done.8.refs_1_.refs_3_), channel_id=1, source_target_pairs={{0,0},{1,5},{2,2},{3,7},{4,4},{5,1},{6,6},{7,3},{8,8},{9,13},{10,1... | collective-permute-start | bytes 393224 | tf_op jit(solution)/shard_map/ppermute | solution.py:515
  20.4 26.4 %collective-permute-start.9 = (bf16[512,128]{1,0:T(8,128)(2,1)S(1)}, bf16[512,128]{1,0:T(8,128)(2,1)S(1)}, u32[]{:S(2)}, u32[]{:S(2)}) collective-permute-start(bf16[512,128]{1,0:T(8,128)(2,1)S(1)} %hand_kept.1), channel_id=1, source_target_pairs={{0,1},{1,0},{2,3},{3,2},{4,5},{5,4},{6,7},{7,6},{8,9},{9,8},{10,11... | collective-permute-start | bytes 393224 | tf_op jit(solution)/shard_map/ppermute | solution.py:515
  43.9 3.9 %collective-permute-start.12 = (bf16[512,128]{1,0:T(8,128)(2,1)S(1)}, bf16[512,128]{1,0:T(8,128)(2,1)S(1)}, u32[]{:S(2)}, u32[]{:S(2)}) collective-permute-start(bf16[512,128]{1,0:T(8,128)(2,1)S(1)} %hand_other.1), channel_id=1, source_target_pairs={{0,1},{1,0},{2,3},{3,2},{4,5},{5,4},{6,7},{7,6},{8,9},{9,8},{10,11... | collective-permute-start | bytes 393224 | tf_op jit(solution)/shard_map/ppermute | solution.py:515

commit v10 on v6

--- a/solution.py
+++ b/solution.py
@@ -204,7 +204,7 @@
 
 
 def first_margin_kernel(cells_x, cells_y, groups, own_ops, *refs):
-    matrix_ref, local_ref, left_ref, phase_ref, halo_x_ref, halo_y_ref, dirs_hbm = refs[:7]
+    matrix_ref, local_ref, left_ref, phase_ref, halo_y_ref, halo_x_ref, dirs_hbm = refs[:7]
     swap_ref, hold_ref, later_side_ref, later_pair_ref = refs[7:11]
     field_ref, side_ref, dirs_ref, sem = refs[11:]
     f32, bf16 = jnp.float32, jnp.bfloat16
@@ -430,27 +430,16 @@
     kept, other, refs = refs[:times], refs[times : 2 * times], refs[2 * times :]
     if split:
         first_sums_ref, refs = refs[0], refs[1:]
-    margin_ref, corr_ref, sums_ref, left_ref, right_ref = refs
+    margin_hbm, corr_ref, sums_ref, left_ref, right_ref, wide_ref, sems = refs
     vectors = sums_ref.shape[2]
     half = kept[0].shape[0]
     me = lax.axis_index("gx") & 1
-    places = (me, 1 - me)
-    for place, ref in zip(places, (kept[0], other[0])):
-        span = pl.ds(pl.multiple_of(place * half, half), half)
-        margin_ref[0, span] = ref[...].astype(jnp.float32)
-    scale = 1.0 / vectors
-
-    def put(sums, first):
-        for k in range(sums.shape[0]):
-            corr_ref[0, first + k // 2, k % 2] = jnp.sum(sums[k]) * scale
-
-    if split:
-        blocks = [part_of(ref, vectors) for ref in other]
-        contract(sums_ref, weight_ref, blocks, tau_ref, left_ref, right_ref)
-        own_ops = sums_ref.shape[0] // 2
-        put(first_sums_ref, places[0] * own_ops)
-        put(sums_ref, places[1] * own_ops)
-        return
+    copies = []
+    for k, (place, ref) in enumerate(((me, kept[0]), (1 - me, other[0]))):
+        wide_ref[k] = ref[...].astype(jnp.float32)
+        rows = pl.ds(pl.multiple_of(place * half, half), half)
+        copies.append(pltpu.make_async_copy(wide_ref.at[k], margin_hbm.at[0, rows], sems.at[k]))
+        copies[k].start()
     parts_per_half = half // vectors
 
     def either(kept_ref, other_ref):
@@ -462,9 +451,25 @@
 
         return part
 
-    blocks = [either(a, b) for a, b in zip(kept, other)]
+    blocks = [part_of(ref, vectors) for ref in other]
+    if not split:
+        blocks = [either(a, b) for a, b in zip(kept, other)]
     contract(sums_ref, weight_ref, blocks, tau_ref, left_ref, right_ref)
-    put(sums_ref, 0)
+    now_ops = sums_ref.shape[0] // 2
+    known = [(sums_ref, (1 - me) * now_ops)] if split else [(sums_ref, 0)]
+    if split:
+        known.append((first_sums_ref, me * now_ops))
+    shape = corr_ref.shape[1:]
+    row, col = iota(shape, 0), iota(shape, 1)
+    result = jnp.zeros(shape, jnp.float32)
+    for ref, first in known:
+        for k in range(2 * now_ops):
+            total = jnp.sum(jnp.sum(ref[k], axis=0, keepdims=True), axis=1, keepdims=True)
+            here = (row == first + k // 2) & (col == k % 2)
+            result = jnp.where(here, total * (1.0 / vectors), result)
+    corr_ref[0] = result
+    for copy in copies:
+        copy.wait()
 
 
 def vmem_spec():
@@ -564,7 +569,7 @@
             pltpu.SMEM((count_ops,), jnp.int32),
             pltpu.SemaphoreType.DMA,
         ],
-    )(matrices, local, left, phases, halo_x, halo_y, in_hbm(op_dirs))
+    )(matrices, local, left, phases, halo_y, halo_x, in_hbm(op_dirs))
     swapped_a = from_partner(swap_a, "gy", 1)
     held_shapes = [part(groups >> (b + 1)) for b in range(2, levels)] + [part(1)]
     swap_b, *held = local_call(
@@ -642,8 +647,10 @@
             jax.ShapeDtypeStruct((1, own_ops, 2), f32),
         ),
         [vmem_spec()] * (2 + 2 * times + len(sums)),
-        (vmem_spec(), smem_spec()),
-        [pltpu.VMEM(sums_shape, f32)] + scratch,
+        (hbm_spec(), vmem_spec()),
+        [pltpu.VMEM(sums_shape, f32)]
+        + scratch
+        + [pltpu.VMEM((2, half, vectors), f32), pltpu.SemaphoreType.DMA((2,))],
     )(weights, perams[0], *kept, *other, *sums)
     return (margins.reshape(1, own_ops, 2, vectors, vectors), correlators)
 

time: 38.6 us -> 38.4 us (level)
  starting transfers between devices: 13.3 us -> 11.3 us
  waiting for transfers between devices: 17.2 us -> 18.6 us
  Pallas kernels: 6.46 us -> 6.97 us
    ppermute x8, starting transfers between devices: 5.71 us -> 3.92 us  [from_partner(): return lax.ppermute(block, axis, [(i ^ step, i) for i in range(count)])]
    ppermute x8, waiting for transfers between devices: 14.9 us -> 15.8 us  [from_partner(): return lax.ppermute(block, axis, [(i ^ step, i) for i in range(count)])]
    pallas_call x1, Pallas kernels: 1.62 us -> 2.12 us  [per_device(): local_call(functools.partial(second_contract_kernel, times, split), 'seco...]
    ppermute x3, waiting for transfers between devices: 2.36 us -> 2.75 us  [from_step(): lax.ppermute(block, axis, [((i + step) % count, i) for i in range(count)])]
where the time goes in v10:
time: 38.4 us; the launch traced here: 38.2 us
  waiting for transfers between devices  18.6 us (48%)
  starting transfers between devices  11.3 us (29%)
  Pallas kernels  6.97 us (18%)
  between operations  1.37 us (4%)
    ppermute x8, waiting for transfers between devices, from_partner(): return lax.ppermute(block, axis, [(i ^ step, i) for i in range(count)])  15.8 us
    ppermute x3, starting transfers between devices, from_step(): lax.ppermute(block, axis, [((i + step) % count, i) for i in range(count)])  7.36 us
    ppermute x8, starting transfers between devices, from_partner(): return lax.ppermute(block, axis, [(i ^ step, i) for i in range(count)])  3.92 us
    ppermute x3, waiting for transfers between devices, from_step(): lax.ppermute(block, axis, [((i + step) % count, i) for i in range(count)])  2.75 us
    pallas_call x1, Pallas kernels, per_device(): local_call(functools.partial(prepare_kernel, cells_x, cells_y), 'prepare_...  2.23 us
    pallas_call x1, Pallas kernels, per_device(): local_call(functools.partial(second_contract_kernel, times, split), 'seco...  2.12 us
    pallas_call x1, Pallas kernels, per_device(): local_call(functools.partial(first_margin_kernel, cells_x, cells_y, group...  1.15 us
    pallas_call x1, Pallas kernels, per_device(): local_call(functools.partial(first_contract_kernel, times), 'first_contra...  0.83 us
  transfers between devices with their start and end apart: 11, of which 8 were waited for; matrix products, arithmetic and copies ran while one was open for 0% of the time, Pallas kernels for 9%

profile of v10, /device:TPU:0, one launch (start us, length us, event | category | flops | bytes accessed | tf_op | source)
XLA Modules:
  0.0 38.2 jit_solution(4547022636310350808)
XLA Ops:
  0.6 5.1 %collective-permute-start.1 = (bf16[1,2,144,128]{3,2,1,0:T(8,128)(2,1)}, bf16[1,2,144,128]{3,2,1,0:T(8,128)(2,1)S(1)}, u32[]{:S(2)}, u32[]{:S(2)}) collective-permute-start(bf16[1,2,144,128]{3,2,1,0:T(8,128)(2,1)} %bitcast.10), channel_id=1, source_target_pairs={{4,0},{8,4},{12,8},{0,12},{5,1},{9,5},{13,9},{1,13},{6,2},{10,6},{... | collective-permute-start | bytes 221192 | tf_op jit(solution)/shard_map/ppermute | solution.py:506
  5.7 0.7 %collective-permute-start = (bf16[1,2,144,128]{3,2,1,0:T(8,128)(2,1)}, bf16[1,2,144,128]{3,2,1,0:T(8,128)(2,1)S(1)}, u32[]{:S(2)}, u32[]{:S(2)}) collective-permute-start(bf16[1,2,144,128]{3,2,1,0:T(8,128)(2,1)} %bitcast.11), channel_id=1, source_target_pairs={{1,0},{2,1},{3,2},{0,3},{5,4},{6,5},{7,6},{4,7},{9,8},{10,9},{11,1... | collective-permute-start | bytes 221192 | tf_op jit(solution)/shard_map/ppermute | solution.py:506
  7.1 2.2 %prepare_lines.1 = (bf16[3,144,128]{2,1,0:T(8,128)(2,1)S(1)}, f32[11,144,128]{2,1,0:T(8,128)S(1)}, bf16[2,128,288]{2,1,0:T(8,128)(2,1)S(1)}, f32[8,72,256]{2,1,0:T(8,128)S(1)}, f32[2,2,8,128]{3,2,1,0:T(8,128)S(1)}) custom-call(bf16[1,2,144,128]{3,2,1,0:T(8,128)(2,1)} %bitcast.12, bf16[2,27,2,24]{3,2,1,0:T(2,128)(2,1)} %bitcast.13, s32[8]{0:T(128)} %refs_6_.2, ...), custom_call_target="tpu_custom_call" | custom-call | tf_op jit(solution)/shard_map/prepare_lines/pallas_call | solution.py:535
  9.3 0.0 collective-permute-done.1.refs_5_
  9.3 0.0 collective-permute-done.refs_4_
  9.3 1.2 %first_margins.1 = (f32[1,512,128]{2,1,0:T(8,128)S(1)}, f32[1,512,128]{2,1,0:T(8,128)S(1)}, bf16[4,128,288]{2,1,0:T(8,128)(2,1)S(1)}, bf16[4,288,256]{2,1,0:T(8,128)(2,1)S(1)}) custom-call(bf16[3,144,128]{2,1,0:T(8,128)(2,1)S(1)} %get-tuple-element.18.refs_0_, f32[11,144,128]{2,1,0:T(8,128)S(1)} %get-tuple-element.19.refs_1_, ...), custom_call_target="tpu_custom_call" | custom-call | tf_op jit(solution)/shard_map/first_margins/pallas_call | solution.py:555
  10.5 0.4 %collective-permute-start.3 = (f32[1,512,128]{2,1,0:T(8,128)S(1)}, f32[1,512,128]{2,1,0:T(8,128)S(1)}, u32[]{:S(2)}, u32[]{:S(2)}) collective-permute-start(f32[1,512,128]{2,1,0:T(8,128)S(1)} %get-tuple-element.27), channel_id=1, source_target_pairs={{1,0},{0,1},{3,2},{2,3},{5,4},{4,5},{7,6},{6,7},{9,8},{8,9},{11,10... | collective-permute-start | bytes 786440 | tf_op jit(solution)/shard_map/ppermute | solution.py:511
  10.9 0.3 second_margins.1
  11.2 0.3 collective-permute-start.2
  11.4 0.7 %collective-permute-done.3.refs_1_ = f32[1,512,128]{2,1,0:T(8,128)S(1)} collective-permute-done((f32[1,512,128]{2,1,0:T(8,128)S(1)}, f32[1,512,128]{2,1,0:T(8,128)S(1)}, u32[]{:S(2)}, u32[]{:S(2)}) %collective-permute-start.3) | collective-permute-done | bytes 262176 | tf_op jit(solution)/shard_map/ppermute | solution.py:511
  12.1 0.0 copy-start
  12.1 0.1 fold_halves.1
  12.2 1.2 %collective-permute-start.5 = (s16[272,128]{1,0:T(8,128)(2,1)S(1)}, s16[272,128]{1,0:T(8,128)(2,1)S(1)}, u32[]{:S(2)}, u32[]{:S(2)}) collective-permute-start(s16[272,128]{1,0:T(8,128)(2,1)S(1)} %get-tuple-element.29), channel_id=1, source_target_pairs={{2,0},{3,1},{0,2},{1,3},{6,4},{7,5},{4,6},{5,7},{10,8},{11,9},{8,1... | collective-permute-start | bytes 208904 | tf_op jit(solution)/shard_map/ppermute | solution.py:511
  13.4 0.9 %collective-permute-start.4 = (s16[272,128]{1,0:T(8,128)(2,1)S(1)}, s16[272,128]{1,0:T(8,128)(2,1)S(1)}, u32[]{:S(2)}, u32[]{:S(2)}) collective-permute-start(s16[272,128]{1,0:T(8,128)(2,1)S(1)} %get-tuple-element.28), channel_id=1, source_target_pairs={{2,0},{3,1},{0,2},{1,3},{6,4},{7,5},{4,6},{5,7},{10,8},{11,9},{8,1... | collective-permute-start | bytes 208904 | tf_op jit(solution)/shard_map/ppermute | solution.py:511
  14.3 0.0 collective-permute-done.2.refs_1_
  14.3 3.0 %collective-permute-done.5.refs_2_ = s16[272,128]{1,0:T(8,128)(2,1)S(1)} collective-permute-done((s16[272,128]{1,0:T(8,128)(2,1)S(1)}, s16[272,128]{1,0:T(8,128)(2,1)S(1)}, u32[]{:S(2)}, u32[]{:S(2)}) %collective-permute-start.5) | collective-permute-done | bytes 69664 | tf_op jit(solution)/shard_map/ppermute | solution.py:511
  17.3 0.1 send_half.1
  17.4 0.1 collective-permute-start.6
  17.4 0.7 %collective-permute-done.4.refs_2_ = s16[272,128]{1,0:T(8,128)(2,1)S(1)} collective-permute-done((s16[272,128]{1,0:T(8,128)(2,1)S(1)}, s16[272,128]{1,0:T(8,128)(2,1)S(1)}, u32[]{:S(2)}, u32[]{:S(2)}) %collective-permute-start.4) | collective-permute-done | bytes 69664 | tf_op jit(solution)/shard_map/ppermute | solution.py:511
  18.2 3.6 %collective-permute-done.6.refs_3_ = s16[272,128]{1,0:T(8,128)(2,1)S(1)} collective-permute-done((s16[272,128]{1,0:T(8,128)(2,1)S(1)}, s16[272,128]{1,0:T(8,128)(2,1)S(1)}, u32[]{:S(2)}, u32[]{:S(2)}) %collective-permute-start.6) | collective-permute-done | bytes 69664 | tf_op jit(solution)/shard_map/ppermute | solution.py:511
  21.7 0.1 keep_half.1.own_ref
  21.8 1.1 %collective-permute-start.7 = (s16[272,128]{1,0:T(8,128)(2,1)S(1)}, s16[272,128]{1,0:T(8,128)(2,1)S(1)}, u32[]{:S(2)}, u32[]{:S(2)}) collective-permute-start(s16[272,128]{1,0:T(8,128)(2,1)S(1)} %keep_half.1.own_ref), channel_id=1, source_target_pairs={{8,0},{12,4},{0,8},{4,12},{9,1},{13,5},{1,9},{5,13},{10,2},{14,6},... | collective-permute-start | bytes 208904 | tf_op jit(solution)/shard_map/ppermute | solution.py:511
  23.0 4.5 %collective-permute-done.7.arrived_ref = s16[272,128]{1,0:T(8,128)(2,1)S(1)} collective-permute-done((s16[272,128]{1,0:T(8,128)(2,1)S(1)}, s16[272,128]{1,0:T(8,128)(2,1)S(1)}, u32[]{:S(2)}, u32[]{:S(2)}) %collective-permute-start.7) | collective-permute-done | bytes 69664 | tf_op jit(solution)/shard_map/ppermute | solution.py:511
  27.5 1.6 %collective-permute-start.8 = (bf16[256,128]{1,0:T(8,128)(2,1)S(1)}, bf16[256,128]{1,0:T(8,128)(2,1)S(1)}, u32[]{:S(2)}, u32[]{:S(2)}) collective-permute-start(bf16[256,128]{1,0:T(8,128)(2,1)S(1)} %finish_half.1.refs_0_), channel_id=1, source_target_pairs={{16,0},{0,16},{17,1},{1,17},{18,2},{2,18},{19,3},{3,19},{20,4},{4,... | collective-permute-start | bytes 196616 | tf_op jit(solution)/shard_map/ppermute | solution.py:506
  29.1 0.0 collective-permute-start.9
  29.1 2.7 %collective-permute-done.8.refs_1_ = bf16[256,128]{1,0:T(8,128)(2,1)S(1)} collective-permute-done((bf16[256,128]{1,0:T(8,128)(2,1)S(1)}, bf16[256,128]{1,0:T(8,128)(2,1)S(1)}, u32[]{:S(2)}, u32[]{:S(2)}) %collective-permute-start.8) | collective-permute-done | bytes 65568 | tf_op jit(solution)/shard_map/ppermute | solution.py:506
  31.8 0.0 collective-permute-start.10
  31.8 0.0 copy-done
  31.8 0.8 %first_contraction.1.refs_4_ = f32[2,32,128]{2,1,0:T(8,128)S(1)} custom-call(f32[2,2,8,128]{3,2,1,0:T(8,128)S(1)} %get-tuple-element.17.weight_ref, bf16[2,512,512]{2,1,0:T(8,128)(2,1)S(1)} %bitcast.8, bf16[256,128]{1,0:T(8,128)(2,1)S(1)} %finish_half.1.refs_0_, bf16[256,128]{1,0:T(8,128)(2,1)S(1)} %collective-permute-done.8.refs_1_), custom_call_target="tpu_custom_call" | custom-call | tf_op jit(solution)/shard_map/first_contraction/pallas_call | solution.py:633
  32.7 0.7 %collective-permute-done.9.refs_2_ = bf16[256,128]{1,0:T(8,128)(2,1)S(1)} collective-permute-done((bf16[256,128]{1,0:T(8,128)(2,1)S(1)}, bf16[256,128]{1,0:T(8,128)(2,1)S(1)}, u32[]{:S(2)}, u32[]{:S(2)}) %collective-permute-start.9) | collective-permute-done | bytes 65568 | tf_op jit(solution)/shard_map/ppermute | solution.py:511
  33.3 2.7 %collective-permute-done.10.refs_3_ = bf16[256,128]{1,0:T(8,128)(2,1)S(1)} collective-permute-done((bf16[256,128]{1,0:T(8,128)(2,1)S(1)}, bf16[256,128]{1,0:T(8,128)(2,1)S(1)}, u32[]{:S(2)}, u32[]{:S(2)}) %collective-permute-start.10) | collective-permute-done | bytes 65568 | tf_op jit(solution)/shard_map/ppermute | solution.py:511
  36.1 2.1 %second_contraction.1 = (f32[1,512,128]{2,1,0:T(8,128)}, f32[1,2,2]{2,1,0:T(2,128)}) custom-call(f32[2,2,8,128]{3,2,1,0:T(8,128)S(1)} %get-tuple-element.17.weight_ref, bf16[2,512,512]{2,1,0:T(8,128)(2,1)S(1)} %bitcast.9, bf16[256,128]{1,0:T(8,128)(2,1)S(1)} %finish_half.1.refs_0_, bf16[256,128]{1,0:T(8,128)(2,1)S(1)} %collective-permute-done.8.refs_1_, ...), custom_call_target="tpu_custom_call" | custom-call | tf_op jit(solution)/shard_map/second_contraction/pallas_call | solution.py:642
  (1 shorter events, 0.0 us)
Async XLA Ops:
  0.6 8.7 %collective-permute-start.1 = (bf16[1,2,144,128]{3,2,1,0:T(8,128)(2,1)}, bf16[1,2,144,128]{3,2,1,0:T(8,128)(2,1)S(1)}, u32[]{:S(2)}, u32[]{:S(2)}) collective-permute-start(bf16[1,2,144,128]{3,2,1,0:T(8,128)(2,1)} %bitcast.10), channel_id=1, source_target_pairs={{4,0},{8,4},{12,8},{0,12},{5,1},{9,5},{13,9},{1,13},{6,2},{10,6},{... | collective-permute-start | bytes 221192 | tf_op jit(solution)/shard_map/ppermute | solution.py:506
  5.7 3.6 %collective-permute-start = (bf16[1,2,144,128]{3,2,1,0:T(8,128)(2,1)}, bf16[1,2,144,128]{3,2,1,0:T(8,128)(2,1)S(1)}, u32[]{:S(2)}, u32[]{:S(2)}) collective-permute-start(bf16[1,2,144,128]{3,2,1,0:T(8,128)(2,1)} %bitcast.11), channel_id=1, source_target_pairs={{1,0},{2,1},{3,2},{0,3},{5,4},{6,5},{7,6},{4,7},{9,8},{10,9},{11,1... | collective-permute-start | bytes 221192 | tf_op jit(solution)/shard_map/ppermute | solution.py:506
  10.5 1.6 %collective-permute-start.3 = (f32[1,512,128]{2,1,0:T(8,128)S(1)}, f32[1,512,128]{2,1,0:T(8,128)S(1)}, u32[]{:S(2)}, u32[]{:S(2)}) collective-permute-start(f32[1,512,128]{2,1,0:T(8,128)S(1)} %get-tuple-element.27), channel_id=1, source_target_pairs={{1,0},{0,1},{3,2},{2,3},{5,4},{4,5},{7,6},{6,7},{9,8},{8,9},{11,10... | collective-permute-start | bytes 786440 | tf_op jit(solution)/shard_map/ppermute | solution.py:511
  11.2 3.1 %collective-permute-start.2 = (f32[1,512,128]{2,1,0:T(8,128)S(1)}, f32[1,512,128]{2,1,0:T(8,128)S(1)}, u32[]{:S(2)}, u32[]{:S(2)}) collective-permute-start(f32[1,512,128]{2,1,0:T(8,128)S(1)} %get-tuple-element.25), channel_id=1, source_target_pairs={{1,0},{0,1},{3,2},{2,3},{5,4},{4,5},{7,6},{6,7},{9,8},{8,9},{11,10... | collective-permute-start | bytes 786440 | tf_op jit(solution)/shard_map/ppermute | solution.py:511
  12.1 19.7 %copy-start = (bf16[1,2,512,512]{3,2,1,0:T(8,128)(2,1)S(1)}, bf16[1,2,512,512]{3,2,1,0:T(8,128)(2,1)}, u32[]{:S(2)}) copy-start(bf16[1,2,512,512]{3,2,1,0:T(8,128)(2,1)} %param.12) | copy-start | bytes 3145732
  12.2 5.1 %collective-permute-start.5 = (s16[272,128]{1,0:T(8,128)(2,1)S(1)}, s16[272,128]{1,0:T(8,128)(2,1)S(1)}, u32[]{:S(2)}, u32[]{:S(2)}) collective-permute-start(s16[272,128]{1,0:T(8,128)(2,1)S(1)} %get-tuple-element.29), channel_id=1, source_target_pairs={{2,0},{3,1},{0,2},{1,3},{6,4},{7,5},{4,6},{5,7},{10,8},{11,9},{8,1... | collective-permute-start | bytes 208904 | tf_op jit(solution)/shard_map/ppermute | solution.py:511
  13.4 4.8 %collective-permute-start.4 = (s16[272,128]{1,0:T(8,128)(2,1)S(1)}, s16[272,128]{1,0:T(8,128)(2,1)S(1)}, u32[]{:S(2)}, u32[]{:S(2)}) collective-permute-start(s16[272,128]{1,0:T(8,128)(2,1)S(1)} %get-tuple-element.28), channel_id=1, source_target_pairs={{2,0},{3,1},{0,2},{1,3},{6,4},{7,5},{4,6},{5,7},{10,8},{11,9},{8,1... | collective-permute-start | bytes 208904 | tf_op jit(solution)/shard_map/ppermute | solution.py:511
  17.4 4.4 %collective-permute-start.6 = (s16[272,128]{1,0:T(8,128)(2,1)S(1)}, s16[272,128]{1,0:T(8,128)(2,1)S(1)}, u32[]{:S(2)}, u32[]{:S(2)}) collective-permute-start(s16[272,128]{1,0:T(8,128)(2,1)S(1)} %send_half.1), channel_id=1, source_target_pairs={{4,0},{0,4},{12,8},{8,12},{5,1},{1,5},{13,9},{9,13},{6,2},{2,6},{1... | collective-permute-start | bytes 208904 | tf_op jit(solution)/shard_map/ppermute | solution.py:511
  21.8 5.6 %collective-permute-start.7 = (s16[272,128]{1,0:T(8,128)(2,1)S(1)}, s16[272,128]{1,0:T(8,128)(2,1)S(1)}, u32[]{:S(2)}, u32[]{:S(2)}) collective-permute-start(s16[272,128]{1,0:T(8,128)(2,1)S(1)} %keep_half.1.own_ref), channel_id=1, source_target_pairs={{8,0},{12,4},{0,8},{4,12},{9,1},{13,5},{1,9},{5,13},{10,2},{14,6},... | collective-permute-start | bytes 208904 | tf_op jit(solution)/shard_map/ppermute | solution.py:511
  27.5 4.3 %collective-permute-start.8 = (bf16[256,128]{1,0:T(8,128)(2,1)S(1)}, bf16[256,128]{1,0:T(8,128)(2,1)S(1)}, u32[]{:S(2)}, u32[]{:S(2)}) collective-permute-start(bf16[256,128]{1,0:T(8,128)(2,1)S(1)} %finish_half.1.refs_0_), channel_id=1, source_target_pairs={{16,0},{0,16},{17,1},{1,17},{18,2},{2,18},{19,3},{3,19},{20,4},{4,... | collective-permute-start | bytes 196616 | tf_op jit(solution)/shard_map/ppermute | solution.py:506
  29.1 4.3 %collective-permute-start.9 = (bf16[256,128]{1,0:T(8,128)(2,1)S(1)}, bf16[256,128]{1,0:T(8,128)(2,1)S(1)}, u32[]{:S(2)}, u32[]{:S(2)}) collective-permute-start(bf16[256,128]{1,0:T(8,128)(2,1)S(1)} %finish_half.1.refs_0_), channel_id=1, source_target_pairs={{4,0},{0,4},{12,8},{8,12},{5,1},{1,5},{13,9},{9,13},{6,2},{2,6},{1... | collective-permute-start | bytes 196616 | tf_op jit(solution)/shard_map/ppermute | solution.py:511
  31.8 4.3 %collective-permute-start.10 = (bf16[256,128]{1,0:T(8,128)(2,1)S(1)}, bf16[256,128]{1,0:T(8,128)(2,1)S(1)}, u32[]{:S(2)}, u32[]{:S(2)}) collective-permute-start(bf16[256,128]{1,0:T(8,128)(2,1)S(1)} %collective-permute-done.8.refs_1_), channel_id=1, source_target_pairs={{4,0},{0,4},{12,8},{8,12},{5,1},{1,5},{13,9},{9,13},{6,2},{2,6},{1... | collective-permute-start | bytes 196616 | tf_op jit(solution)/shard_map/ppermute | solution.py:511

commit v11 on v10

--- a/solution.py
+++ b/solution.py
@@ -83,7 +83,7 @@
 
 
 def prepare_kernel(cells_x, cells_y, *refs):
-    inputs, live_ref, refs = refs[:6], refs[6], refs[7:]
+    inputs, refs = refs[:6], refs[6:]
     matrix_ref, local_ref, left_ref, phase_ref, weight_ref = refs[:5]
     held, link_rows_ref, sems = refs[5:11], refs[11], refs[12]
     copies = [
@@ -118,7 +118,7 @@
     for copy in copies:
         copy.wait()
     for t in range(times):
-        sink = (pair_ref[0, 0] == t) & (live_ref[0] > 0)
+        sink = pair_ref[0, 0] == t
         source = pair_ref[0, 1] == t
         weight_ref[0, t] = jnp.full(weight_ref.shape[2:], jnp.where(sink, 1.0, 0.0), f32)
         weight_ref[1, t] = jnp.full(weight_ref.shape[2:], jnp.where(source, 1.0, 0.0), f32)
@@ -187,12 +187,16 @@
     return (j & -j).bit_length() - 1
 
 
-def put_product(out_ref, place, i, side, pair):
+def parts_of_product(side, pair):
     vectors = pair.shape[1] // 2
     product = jnp.dot(side, pair, preferred_element_type=jnp.float32)
-    first = 2 * i * vectors
-    out_ref[place, first : first + vectors] = product[:, :vectors]
-    out_ref[place, first + vectors : first + 2 * vectors] = product[:, vectors:]
+    return [product[:, :vectors], product[:, vectors:]]
+
+
+def put_product(out_ref, place, i, side, pair):
+    for k, block in enumerate(parts_of_product(side, pair)):
+        rows = block.shape[0]
+        out_ref[place, (2 * i + k) * rows : (2 * i + k + 1) * rows] = block
 
 
 def first_groups(groups):
@@ -204,7 +208,7 @@
 
 
 def first_margin_kernel(cells_x, cells_y, groups, own_ops, *refs):
-    matrix_ref, local_ref, left_ref, phase_ref, halo_y_ref, halo_x_ref, dirs_hbm = refs[:7]
+    matrix_ref, local_ref, left_ref, phase_ref, halo_x_ref, halo_y_ref, dirs_hbm = refs[:7]
     swap_ref, hold_ref, later_side_ref, later_pair_ref = refs[7:11]
     field_ref, side_ref, dirs_ref, sem = refs[11:]
     f32, bf16 = jnp.float32, jnp.bfloat16
@@ -290,10 +294,10 @@
     return block * jnp.exp2(scales[k : k + 1] - FIXED_BITS)
 
 
-def group_block(held_ref, received, k, j, start, rows):
+def group_block(held_ref, swapped_ref, messages, k, j, start, rows):
     span = pl.ds(start, rows)
-    total = held_ref[k, span] + received[0][j >> 2, span]
-    for b, ref in enumerate(received[1:], 1):
+    total = held_ref[k, span] + swapped_ref[j >> 2, span]
+    for b, ref in enumerate(messages, 1):
         total = total + fixed_at(ref.at[j >> (b + 1)], start, rows)
     return total
 
@@ -307,39 +311,40 @@
     return block * jnp.exp2(scale - FIXED_BITS)
 
 
-def fold_kernel(level, vectors, *refs):
-    held_ref, received, out_ref = refs[0], refs[1:-1], refs[-1]
+def fold_kernel(level, vectors, held_ref, swapped_ref, *refs):
+    messages, out_ref = refs[:-1], refs[-1]
     for k in range(held_ref.shape[0]):
-        j = (2 * k + 1) << level
         blocks = [
-            group_block(held_ref, received, k, j, start, vectors)
+            group_block(held_ref, swapped_ref, messages, k, (2 * k + 1) << level, start, vectors)
             for start in range(0, held_ref.shape[1], vectors)
         ]
         put_fixed(out_ref.at[k], blocks)
 
 
-def half_rows(held_ref, vectors, kept):
+def half_rows(rows, vectors, kept):
     me = lax.axis_index("gx") & 1
-    half = held_ref.shape[1] // 2
+    half = rows // 2
     base = pl.multiple_of((me if kept else 1 - me) * half, half)
     return [base + step for step in range(0, half, vectors)]
 
 
-def fold_halves_kernel(vectors, *refs):
-    held_ref, received, outs = refs[0], refs[1:-2], refs[-2:]
+def fold_halves_kernel(level, vectors, held_ref, swapped_ref, *refs):
+    messages, outs = refs[:-2], refs[-2:]
+    group = 1 << level
     for kept, out_ref in enumerate(outs):
-        starts = half_rows(held_ref, vectors, kept)
-        blocks = [group_block(held_ref, received, 0, held_ref.shape[0], s, vectors) for s in starts]
-        put_fixed(out_ref, blocks)
-
-
-def half_kernel(vectors, kept, *refs):
-    count = 3 if kept else 2
-    held_ref, received, last, out_ref = refs[0], refs[1:-count], refs[-count:-1], refs[-1]
+        starts = half_rows(held_ref.shape[1], vectors, kept)
+        put_fixed(
+            out_ref,
+            [group_block(held_ref, swapped_ref, messages, 0, group, s, vectors) for s in starts],
+        )
+
+
+def half_kernel(levels, vectors, kept, own_ref, swapped_ref, *refs):
+    messages, came, out_ref = refs[: levels - 2], refs[levels - 2 : -1], refs[-1]
     blocks = []
-    for p, start in enumerate(half_rows(held_ref, vectors, kept)):
-        total = group_block(held_ref, received, 0, 0, start, vectors)
-        for ref in last:
+    for p, start in enumerate(half_rows(own_ref.shape[1], vectors, kept)):
+        total = group_block(own_ref, swapped_ref, messages, 0, 0, start, vectors)
+        for ref in came:
             total = total + from_fixed(ref, vectors, p)
         blocks.append(total)
     put_fixed(out_ref, blocks)
@@ -419,27 +424,32 @@
     return lambda k: ref[k * vectors : (k + 1) * vectors]
 
 
-def first_contract_kernel(times, weight_ref, tau_ref, *refs):
-    blocks, (sums_ref, left_ref, right_ref) = refs[:times], refs[times:]
-    vectors = sums_ref.shape[2]
-    blocks = [part_of(ref, vectors) for ref in blocks]
-    contract(sums_ref, weight_ref, blocks, tau_ref, left_ref, right_ref)
+def first_contract_kernel(times, split, live_ref, weight_ref, tau_ref, *refs):
+    blocks, (live_out_ref, sums_ref, left_ref, right_ref) = refs[:times], refs[times:]
+    live = jnp.where(live_ref[0] > 0, 1.0, 0.0)
+    live_out_ref[...] = jnp.full(live_out_ref.shape, live, jnp.float32)
+    if split:
+        vectors = sums_ref.shape[2]
+        blocks = [part_of(ref, vectors) for ref in blocks]
+        contract(sums_ref, weight_ref, blocks, tau_ref, left_ref, right_ref)
+    else:
+        sums_ref[...] = jnp.zeros_like(sums_ref)
+
+
+def margins_kernel(kept_ref, other_ref, margin_ref):
+    half = kept_ref.shape[0]
+    me = lax.axis_index("gx") & 1
+    for place, ref in ((me, kept_ref), (1 - me, other_ref)):
+        rows = pl.ds(pl.multiple_of(place * half, half), half)
+        margin_ref[0, rows] = ref[...].astype(jnp.float32)
 
 
 def second_contract_kernel(times, split, weight_ref, tau_ref, *refs):
     kept, other, refs = refs[:times], refs[times : 2 * times], refs[2 * times :]
-    if split:
-        first_sums_ref, refs = refs[0], refs[1:]
-    margin_hbm, corr_ref, sums_ref, left_ref, right_ref, wide_ref, sems = refs
+    live_ref, first_sums_ref, corr_ref, sums_ref, left_ref, right_ref = refs
     vectors = sums_ref.shape[2]
     half = kept[0].shape[0]
     me = lax.axis_index("gx") & 1
-    copies = []
-    for k, (place, ref) in enumerate(((me, kept[0]), (1 - me, other[0]))):
-        wide_ref[k] = ref[...].astype(jnp.float32)
-        rows = pl.ds(pl.multiple_of(place * half, half), half)
-        copies.append(pltpu.make_async_copy(wide_ref.at[k], margin_hbm.at[0, rows], sems.at[k]))
-        copies[k].start()
     parts_per_half = half // vectors
 
     def either(kept_ref, other_ref):
@@ -467,9 +477,7 @@
             total = jnp.sum(jnp.sum(ref[k], axis=0, keepdims=True), axis=1, keepdims=True)
             here = (row == first + k // 2) & (col == k % 2)
             result = jnp.where(here, total * (1.0 / vectors), result)
-    corr_ref[0] = result
-    for copy in copies:
-        copy.wait()
+    corr_ref[0] = result * live_ref[0 : shape[0], 0 : shape[1]]
 
 
 def vmem_spec():
@@ -542,14 +550,14 @@
             jax.ShapeDtypeStruct((count_ops, order // 2, 2 * vectors), f32),
             jax.ShapeDtypeStruct((2, times, 8, vectors), f32),
         ),
-        [hbm_spec()] * len(inputs) + [smem_spec()],
+        [hbm_spec()] * len(inputs),
         (vmem_spec(),) * 5,
         held
         + [
             pltpu.VMEM((lines, LINK_COLS, cells_z), f32),
             pltpu.SemaphoreType.DMA((len(inputs),)),
         ],
-    )(*inputs, slot_counts)
+    )(*inputs)
     part = lambda count: jax.ShapeDtypeStruct((count, own_rows, vectors), f32)
     later = count_ops // 2
     swap_a, hold_a, later_sides, later_pairs = local_call(
@@ -569,7 +577,7 @@
             pltpu.SMEM((count_ops,), jnp.int32),
             pltpu.SemaphoreType.DMA,
         ],
-    )(matrices, local, left, phases, halo_y, halo_x, in_hbm(op_dirs))
+    )(matrices, local, left, phases, halo_x, halo_y, in_hbm(op_dirs))
     swapped_a = from_partner(swap_a, "gy", 1)
     held_shapes = [part(groups >> (b + 1)) for b in range(2, levels)] + [part(1)]
     swap_b, *held = local_call(
@@ -578,8 +586,13 @@
         (part(groups // 4), *held_shapes),
         [vmem_spec()] * 2,
         (vmem_spec(),) * (1 + len(held_shapes)),
+        cost=pl.CostEstimate(
+            flops=later * 4 * lines * order * vectors * vectors,
+            bytes_accessed=later * 6 * lines * order * vectors + later * 8 * vectors * vectors,
+            transcendentals=0,
+        ),
     )(later_sides, later_pairs)
-    received = [from_partner(swap_b, "gy", 1)]
+    swapped_b = from_partner(swap_b, "gy", 1)
 
     def packed(body, name, *inputs, rows=own_rows, lead=(), count=1):
         shape = jax.ShapeDtypeStruct((*lead, rows + TAIL, vectors), jnp.int16)
@@ -588,21 +601,22 @@
         return local_call(body, name, outs, [vmem_spec()] * len(inputs), specs)(*inputs)
 
     half = own_rows // 2
+    messages = []
     for b in range(1, levels):
-        inputs = (hold_a, swapped_a) if b == 1 else (held[b - 2], *received)
+        inputs = (hold_a, swapped_a) if b == 1 else (held[b - 2], swapped_b, *messages)
         if b < levels - 1:
             body = functools.partial(fold_kernel, b, vectors)
             sent = packed(body, "fold_groups", *inputs, lead=inputs[0].shape[:1])
-            received.append(from_partner(sent, "gy", 1 << b))
+            messages.append(from_partner(sent, "gy", 1 << b))
             continue
-        body = functools.partial(fold_halves_kernel, vectors)
+        body = functools.partial(fold_halves_kernel, b, vectors)
         away, kept = packed(body, "fold_halves", *inputs, rows=half, count=2)
         away, kept = from_partner(away, "gy", 1 << b), from_partner(kept, "gy", 1 << b)
-    body = functools.partial(half_kernel, vectors, False)
-    sent = packed(body, "send_half", held[-1], *received, away, rows=half)
-    arrived = from_partner(sent, "gx", 1)
-    body = functools.partial(half_kernel, vectors, True)
-    message = packed(body, "keep_half", held[-1], *received, kept, arrived, rows=half)
+    inputs = (held[-1], swapped_b, *messages)
+    body = functools.partial(half_kernel, levels, vectors, False)
+    arrived = from_partner(packed(body, "send_half", *inputs, away, rows=half), "gx", 1)
+    body = functools.partial(half_kernel, levels, vectors, True)
+    message = packed(body, "keep_half", *inputs, kept, arrived, rows=half)
     norm_factor = 1.0 / math.sqrt(3.0 * cells_x * shares * cells_y * groups * cells_z)
     step = 2
     while step < shares:
@@ -627,31 +641,29 @@
         pltpu.VMEM((2 * now_ops * vectors, 2 * vectors), bf16),
         pltpu.VMEM((2 * vectors, 2 * now_ops * vectors), bf16),
     ]
-    sums = []
-    if split:
-        sums = [
-            local_call(
-                functools.partial(first_contract_kernel, times),
-                "first_contraction",
-                jax.ShapeDtypeStruct(sums_shape, f32),
-                [vmem_spec()] * (2 + times),
-                vmem_spec(),
-                scratch,
-            )(weights, perams[0], *kept)
-        ]
-    margins, correlators = local_call(
+    margins = local_call(
+        margins_kernel,
+        "margins_out",
+        jax.ShapeDtypeStruct((1, own_rows, vectors), f32),
+        [vmem_spec()] * 2,
+        vmem_spec(),
+    )(kept[0], other[0])
+    live, sums = local_call(
+        functools.partial(first_contract_kernel, times, split),
+        "first_contraction",
+        (jax.ShapeDtypeStruct((8, vectors), f32), jax.ShapeDtypeStruct(sums_shape, f32)),
+        [smem_spec()] + [vmem_spec()] * (2 + times),
+        (vmem_spec(),) * 2,
+        scratch,
+    )(slot_counts, weights, perams[0], *kept)
+    correlators = local_call(
         functools.partial(second_contract_kernel, times, split),
         "second_contraction",
-        (
-            jax.ShapeDtypeStruct((1, own_rows, vectors), f32),
-            jax.ShapeDtypeStruct((1, own_ops, 2), f32),
-        ),
-        [vmem_spec()] * (2 + 2 * times + len(sums)),
-        (hbm_spec(), vmem_spec()),
-        [pltpu.VMEM(sums_shape, f32)]
-        + scratch
-        + [pltpu.VMEM((2, half, vectors), f32), pltpu.SemaphoreType.DMA((2,))],
-    )(weights, perams[0], *kept, *other, *sums)
+        jax.ShapeDtypeStruct((1, own_ops, 2), f32),
+        [vmem_spec()] * (4 + 2 * times),
+        vmem_spec(),
+        [pltpu.VMEM(sums_shape, f32)] + scratch,
+    )(weights, perams[0], *kept, *other, live, sums)
     return (margins.reshape(1, own_ops, 2, vectors, vectors), correlators)
 
 

time: 38.4 us -> 37.8 us (0.984)
  waiting for transfers between devices: 18.6 us -> 17.3 us
  starting transfers between devices: 11.3 us -> 11.8 us
    ppermute x8, waiting for transfers between devices: 15.8 us -> 14.5 us  [from_partner(): return lax.ppermute(block, axis, [(i ^ step, i) for i in range(count)])]
    pallas_call x1 -> x2, Pallas kernels: 0.83 us -> 1.59 us  [the longest x1 0.86 us: per_device(): local_call(functools.partial(first_contract_kernel, times, split), 'first...]
    pallas_call x1, Pallas kernels: 2.12 us -> 1.51 us  [per_device(): local_call(functools.partial(second_contract_kernel, times, split), 'seco...]
    ppermute x8, starting transfers between devices: 3.92 us -> 4.41 us  [from_partner(): return lax.ppermute(block, axis, [(i ^ step, i) for i in range(count)])]
  transfers between devices with their start and end apart: 11 -> 11, of which waited for: 8 -> 8; matrix products, arithmetic and copies ran while one was open for 0% -> 0% of each run, Pallas kernels for 9% -> 12%
where the time goes in v11:
time: 37.8 us; the launch traced here: 37.6 us
  waiting for transfers between devices  17.3 us (46%)
  starting transfers between devices  11.8 us (31%)
  Pallas kernels  7.12 us (19%)
  between operations  1.37 us (4%)
    ppermute x8, waiting for transfers between devices, from_partner(): return lax.ppermute(block, axis, [(i ^ step, i) for i in range(count)])  14.5 us
    ppermute x3, starting transfers between devices, from_step(): lax.ppermute(block, axis, [((i + step) % count, i) for i in range(count)])  7.36 us
    ppermute x8, starting transfers between devices, from_partner(): return lax.ppermute(block, axis, [(i ^ step, i) for i in range(count)])  4.41 us
    ppermute x3, waiting for transfers between devices, from_step(): lax.ppermute(block, axis, [((i + step) % count, i) for i in range(count)])  2.78 us
    pallas_call x1, Pallas kernels, per_device(): local_call(functools.partial(prepare_kernel, cells_x, cells_y), 'prepare_...  2.25 us
    pallas_call x1, Pallas kernels, per_device(): local_call(functools.partial(second_contract_kernel, times, split), 'seco...  1.51 us
    pallas_call x1, Pallas kernels, per_device(): local_call(functools.partial(first_margin_kernel, cells_x, cells_y, group...  1.15 us
    pallas_call x1, Pallas kernels, per_device(): local_call(functools.partial(first_contract_kernel, times, split), 'first...  0.86 us
  transfers between devices with their start and end apart: 11, of which 8 were waited for; matrix products, arithmetic and copies ran while one was open for 0% of the time, Pallas kernels for 12%

profile of v11, /device:TPU:0, one launch (start us, length us, event | category | flops | bytes accessed | tf_op | source)
XLA Modules:
  0.0 37.6 jit_solution(10772933489612262061)
XLA Ops:
  0.6 5.1 %collective-permute-start = (bf16[1,2,144,128]{3,2,1,0:T(8,128)(2,1)}, bf16[1,2,144,128]{3,2,1,0:T(8,128)(2,1)S(1)}, u32[]{:S(2)}, u32[]{:S(2)}) collective-permute-start(bf16[1,2,144,128]{3,2,1,0:T(8,128)(2,1)} %bitcast.11), channel_id=1, source_target_pairs={{4,0},{8,4},{12,8},{0,12},{5,1},{9,5},{13,9},{1,13},{6,2},{10,6},{... | collective-permute-start | bytes 221192 | tf_op jit(solution)/shard_map/ppermute | solution.py:514
  5.7 0.7 %collective-permute-start.1 = (bf16[1,2,144,128]{3,2,1,0:T(8,128)(2,1)}, bf16[1,2,144,128]{3,2,1,0:T(8,128)(2,1)S(1)}, u32[]{:S(2)}, u32[]{:S(2)}) collective-permute-start(bf16[1,2,144,128]{3,2,1,0:T(8,128)(2,1)} %bitcast.12), channel_id=1, source_target_pairs={{1,0},{2,1},{3,2},{0,3},{5,4},{6,5},{7,6},{4,7},{9,8},{10,9},{11,1... | collective-permute-start | bytes 221192 | tf_op jit(solution)/shard_map/ppermute | solution.py:514
  6.4 2.3 %prepare_lines.1 = (bf16[3,144,128]{2,1,0:T(8,128)(2,1)S(1)}, f32[11,144,128]{2,1,0:T(8,128)S(1)}, bf16[2,128,288]{2,1,0:T(8,128)(2,1)S(1)}, f32[8,72,256]{2,1,0:T(8,128)S(1)}, f32[2,2,8,128]{3,2,1,0:T(8,128)S(1)}) custom-call(bf16[1,2,144,128]{3,2,1,0:T(8,128)(2,1)} %bitcast.13, bf16[2,27,2,24]{3,2,1,0:T(2,128)(2,1)} %bitcast.14, s32[8]{0:T(128)} %refs_6_.1, ...), custom_call_target="tpu_custom_call" | custom-call | tf_op jit(solution)/shard_map/prepare_lines/pallas_call | solution.py:543
  8.7 0.0 collective-permute-done.refs_4_
  8.7 0.0 collective-permute-done.1.refs_5_
  8.7 1.1 %first_margins.1 = (f32[1,512,128]{2,1,0:T(8,128)S(1)}, f32[1,512,128]{2,1,0:T(8,128)S(1)}, bf16[4,128,288]{2,1,0:T(8,128)(2,1)S(1)}, bf16[4,288,256]{2,1,0:T(8,128)(2,1)S(1)}) custom-call(bf16[3,144,128]{2,1,0:T(8,128)(2,1)S(1)} %get-tuple-element.17.refs_0_, f32[11,144,128]{2,1,0:T(8,128)S(1)} %get-tuple-element.18.refs_1_, ...), custom_call_target="tpu_custom_call" | custom-call | tf_op jit(solution)/shard_map/first_margins/pallas_call | solution.py:563
  9.9 1.0 %collective-permute-start.3 = (f32[1,512,128]{2,1,0:T(8,128)S(1)}, f32[1,512,128]{2,1,0:T(8,128)S(1)}, u32[]{:S(2)}, u32[]{:S(2)}) collective-permute-start(f32[1,512,128]{2,1,0:T(8,128)S(1)} %get-tuple-element.26), channel_id=1, source_target_pairs={{1,0},{0,1},{3,2},{2,3},{5,4},{4,5},{7,6},{6,7},{9,8},{8,9},{11,10... | collective-permute-start | bytes 786440 | tf_op jit(solution)/shard_map/ppermute | solution.py:519
  10.9 0.3 second_margins.1
  11.2 0.1 collective-permute-start.2
  11.2 0.8 %collective-permute-done.3.swapped_ref = f32[1,512,128]{2,1,0:T(8,128)S(1)} collective-permute-done((f32[1,512,128]{2,1,0:T(8,128)S(1)}, f32[1,512,128]{2,1,0:T(8,128)S(1)}, u32[]{:S(2)}, u32[]{:S(2)}) %collective-permute-start.3) | collective-permute-done | bytes 262176 | tf_op jit(solution)/shard_map/ppermute | solution.py:519
  12.0 0.1 fold_halves.1
  12.1 0.0 copy-start
  12.2 1.2 %collective-permute-start.5 = (s16[272,128]{1,0:T(8,128)(2,1)S(1)}, s16[272,128]{1,0:T(8,128)(2,1)S(1)}, u32[]{:S(2)}, u32[]{:S(2)}) collective-permute-start(s16[272,128]{1,0:T(8,128)(2,1)S(1)} %get-tuple-element.28), channel_id=1, source_target_pairs={{2,0},{3,1},{0,2},{1,3},{6,4},{7,5},{4,6},{5,7},{10,8},{11,9},{8,1... | collective-permute-start | bytes 208904 | tf_op jit(solution)/shard_map/ppermute | solution.py:519
  13.4 0.9 %collective-permute-start.4 = (s16[272,128]{1,0:T(8,128)(2,1)S(1)}, s16[272,128]{1,0:T(8,128)(2,1)S(1)}, u32[]{:S(2)}, u32[]{:S(2)}) collective-permute-start(s16[272,128]{1,0:T(8,128)(2,1)S(1)} %get-tuple-element.27), channel_id=1, source_target_pairs={{2,0},{3,1},{0,2},{1,3},{6,4},{7,5},{4,6},{5,7},{10,8},{11,9},{8,1... | collective-permute-start | bytes 208904 | tf_op jit(solution)/shard_map/ppermute | solution.py:519
  14.3 0.0 collective-permute-done.2.swapped_ref
  14.3 3.0 %collective-permute-done.5.refs_0_ = s16[272,128]{1,0:T(8,128)(2,1)S(1)} collective-permute-done((s16[272,128]{1,0:T(8,128)(2,1)S(1)}, s16[272,128]{1,0:T(8,128)(2,1)S(1)}, u32[]{:S(2)}, u32[]{:S(2)}) %collective-permute-start.5) | collective-permute-done | bytes 69664 | tf_op jit(solution)/shard_map/ppermute | solution.py:519
  17.2 0.1 send_half.1
  17.3 0.1 collective-permute-start.6
  17.4 0.8 %collective-permute-done.4.refs_0_ = s16[272,128]{1,0:T(8,128)(2,1)S(1)} collective-permute-done((s16[272,128]{1,0:T(8,128)(2,1)S(1)}, s16[272,128]{1,0:T(8,128)(2,1)S(1)}, u32[]{:S(2)}, u32[]{:S(2)}) %collective-permute-start.4) | collective-permute-done | bytes 69664 | tf_op jit(solution)/shard_map/ppermute | solution.py:519
  18.2 3.5 %collective-permute-done.6.refs_1_ = s16[272,128]{1,0:T(8,128)(2,1)S(1)} collective-permute-done((s16[272,128]{1,0:T(8,128)(2,1)S(1)}, s16[272,128]{1,0:T(8,128)(2,1)S(1)}, u32[]{:S(2)}, u32[]{:S(2)}) %collective-permute-start.6) | collective-permute-done | bytes 69664 | tf_op jit(solution)/shard_map/ppermute | solution.py:519
  21.7 0.1 keep_half.1.own_ref
  21.8 1.2 %collective-permute-start.7 = (s16[272,128]{1,0:T(8,128)(2,1)S(1)}, s16[272,128]{1,0:T(8,128)(2,1)S(1)}, u32[]{:S(2)}, u32[]{:S(2)}) collective-permute-start(s16[272,128]{1,0:T(8,128)(2,1)S(1)} %keep_half.1.own_ref), channel_id=1, source_target_pairs={{8,0},{12,4},{0,8},{4,12},{9,1},{13,5},{1,9},{5,13},{10,2},{14,6},... | collective-permute-start | bytes 208904 | tf_op jit(solution)/shard_map/ppermute | solution.py:519
  23.0 4.5 %collective-permute-done.7.arrived_ref = s16[272,128]{1,0:T(8,128)(2,1)S(1)} collective-permute-done((s16[272,128]{1,0:T(8,128)(2,1)S(1)}, s16[272,128]{1,0:T(8,128)(2,1)S(1)}, u32[]{:S(2)}, u32[]{:S(2)}) %collective-permute-start.7) | collective-permute-done | bytes 69664 | tf_op jit(solution)/shard_map/ppermute | solution.py:519
  27.5 1.6 %collective-permute-start.9 = (bf16[256,128]{1,0:T(8,128)(2,1)S(1)}, bf16[256,128]{1,0:T(8,128)(2,1)S(1)}, u32[]{:S(2)}, u32[]{:S(2)}) collective-permute-start(bf16[256,128]{1,0:T(8,128)(2,1)S(1)} %finish_half.1.kept_ref.refs_0_), channel_id=1, source_target_pairs={{16,0},{0,16},{17,1},{1,17},{18,2},{2,18},{19,3},{3,19},{20,4},{4,... | collective-permute-start | bytes 196616 | tf_op jit(solution)/shard_map/ppermute | solution.py:514
  29.1 0.0 collective-permute-start.8
  29.1 2.8 %collective-permute-done.9.refs_1_ = bf16[256,128]{1,0:T(8,128)(2,1)S(1)} collective-permute-done((bf16[256,128]{1,0:T(8,128)(2,1)S(1)}, bf16[256,128]{1,0:T(8,128)(2,1)S(1)}, u32[]{:S(2)}, u32[]{:S(2)}) %collective-permute-start.9) | collective-permute-done | bytes 65568 | tf_op jit(solution)/shard_map/ppermute | solution.py:514
  31.8 0.0 collective-permute-start.10
  32.5 0.9 %collective-permute-done.8.other_ref.refs_2_ = bf16[256,128]{1,0:T(8,128)(2,1)S(1)} collective-permute-done((bf16[256,128]{1,0:T(8,128)(2,1)S(1)}, bf16[256,128]{1,0:T(8,128)(2,1)S(1)}, u32[]{:S(2)}, u32[]{:S(2)}) %collective-permute-start.8) | collective-permute-done | bytes 65568 | tf_op jit(solution)/shard_map/ppermute | solution.py:519
  33.3 0.7 %margins_out.1 = f32[1,512,128]{2,1,0:T(8,128)} custom-call(bf16[256,128]{1,0:T(8,128)(2,1)S(1)} %finish_half.1.kept_ref.refs_0_, bf16[256,128]{1,0:T(8,128)(2,1)S(1)} %collective-permute-done.8.other_ref.refs_2_), custom_call_target="tpu_custom_call" | custom-call | tf_op jit(solution)/shard_map/margins_out/pallas_call | solution.py:644
  34.1 0.0 copy-done
  34.1 0.9 %first_contraction.1 = (f32[8,128]{1,0:T(8,128)S(1)}, f32[2,32,128]{2,1,0:T(8,128)S(1)}) custom-call(s32[1]{0:T(128)S(6)} %copy.10.live_ref, f32[2,2,8,128]{3,2,1,0:T(8,128)S(1)} %get-tuple-element.29.weight_ref, bf16[2,512,512]{2,1,0:T(8,128)(2,1)S(1)} %bitcast.8, bf16[256,128]{1,0:T(8,128)(2,1)S(1)} %finish_half.1.kept_ref.refs_0_, ...), custom_call_target="tpu_custom_call" | custom-call | tf_op jit(solution)/shard_map/first_contraction/pallas_call | solution.py:651
  34.9 1.2 %collective-permute-done.10.refs_3_ = bf16[256,128]{1,0:T(8,128)(2,1)S(1)} collective-permute-done((bf16[256,128]{1,0:T(8,128)(2,1)S(1)}, bf16[256,128]{1,0:T(8,128)(2,1)S(1)}, u32[]{:S(2)}, u32[]{:S(2)}) %collective-permute-start.10) | collective-permute-done | bytes 65568 | tf_op jit(solution)/shard_map/ppermute | solution.py:519
  36.1 1.5 %second_contraction.1 = f32[1,2,2]{2,1,0:T(2,128)} custom-call(f32[2,2,8,128]{3,2,1,0:T(8,128)S(1)} %get-tuple-element.29.weight_ref, bf16[2,512,512]{2,1,0:T(8,128)(2,1)S(1)} %bitcast.9, bf16[256,128]{1,0:T(8,128)(2,1)S(1)} %finish_half.1.kept_ref.refs_0_, bf16[256,128]{1,0:T(8,128)(2,1)S(1)} %collective-permute-done.9.refs_1_, ...), custom_call_target="tpu_custom_call" | custom-call | tf_op jit(solution)/shard_map/second_contraction/pallas_call | solution.py:659
  (1 shorter events, 0.0 us)
Async XLA Ops:
  0.6 8.0 %collective-permute-start = (bf16[1,2,144,128]{3,2,1,0:T(8,128)(2,1)}, bf16[1,2,144,128]{3,2,1,0:T(8,128)(2,1)S(1)}, u32[]{:S(2)}, u32[]{:S(2)}) collective-permute-start(bf16[1,2,144,128]{3,2,1,0:T(8,128)(2,1)} %bitcast.11), channel_id=1, source_target_pairs={{4,0},{8,4},{12,8},{0,12},{5,1},{9,5},{13,9},{1,13},{6,2},{10,6},{... | collective-permute-start | bytes 221192 | tf_op jit(solution)/shard_map/ppermute | solution.py:514
  5.7 3.0 %collective-permute-start.1 = (bf16[1,2,144,128]{3,2,1,0:T(8,128)(2,1)}, bf16[1,2,144,128]{3,2,1,0:T(8,128)(2,1)S(1)}, u32[]{:S(2)}, u32[]{:S(2)}) collective-permute-start(bf16[1,2,144,128]{3,2,1,0:T(8,128)(2,1)} %bitcast.12), channel_id=1, source_target_pairs={{1,0},{2,1},{3,2},{0,3},{5,4},{6,5},{7,6},{4,7},{9,8},{10,9},{11,1... | collective-permute-start | bytes 221192 | tf_op jit(solution)/shard_map/ppermute | solution.py:514
  9.9 2.2 %collective-permute-start.3 = (f32[1,512,128]{2,1,0:T(8,128)S(1)}, f32[1,512,128]{2,1,0:T(8,128)S(1)}, u32[]{:S(2)}, u32[]{:S(2)}) collective-permute-start(f32[1,512,128]{2,1,0:T(8,128)S(1)} %get-tuple-element.26), channel_id=1, source_target_pairs={{1,0},{0,1},{3,2},{2,3},{5,4},{4,5},{7,6},{6,7},{9,8},{8,9},{11,10... | collective-permute-start | bytes 786440 | tf_op jit(solution)/shard_map/ppermute | solution.py:519
  11.2 3.1 %collective-permute-start.2 = (f32[1,512,128]{2,1,0:T(8,128)S(1)}, f32[1,512,128]{2,1,0:T(8,128)S(1)}, u32[]{:S(2)}, u32[]{:S(2)}) collective-permute-start(f32[1,512,128]{2,1,0:T(8,128)S(1)} %get-tuple-element.24), channel_id=1, source_target_pairs={{1,0},{0,1},{3,2},{2,3},{5,4},{4,5},{7,6},{6,7},{9,8},{8,9},{11,10... | collective-permute-start | bytes 786440 | tf_op jit(solution)/shard_map/ppermute | solution.py:519
  12.1 21.9 %copy-start = (bf16[1,2,512,512]{3,2,1,0:T(8,128)(2,1)S(1)}, bf16[1,2,512,512]{3,2,1,0:T(8,128)(2,1)}, u32[]{:S(2)}) copy-start(bf16[1,2,512,512]{3,2,1,0:T(8,128)(2,1)} %param.12) | copy-start | bytes 3145732
  12.2 5.1 %collective-permute-start.5 = (s16[272,128]{1,0:T(8,128)(2,1)S(1)}, s16[272,128]{1,0:T(8,128)(2,1)S(1)}, u32[]{:S(2)}, u32[]{:S(2)}) collective-permute-start(s16[272,128]{1,0:T(8,128)(2,1)S(1)} %get-tuple-element.28), channel_id=1, source_target_pairs={{2,0},{3,1},{0,2},{1,3},{6,4},{7,5},{4,6},{5,7},{10,8},{11,9},{8,1... | collective-permute-start | bytes 208904 | tf_op jit(solution)/shard_map/ppermute | solution.py:519
  13.4 4.8 %collective-permute-start.4 = (s16[272,128]{1,0:T(8,128)(2,1)S(1)}, s16[272,128]{1,0:T(8,128)(2,1)S(1)}, u32[]{:S(2)}, u32[]{:S(2)}) collective-permute-start(s16[272,128]{1,0:T(8,128)(2,1)S(1)} %get-tuple-element.27), channel_id=1, source_target_pairs={{2,0},{3,1},{0,2},{1,3},{6,4},{7,5},{4,6},{5,7},{10,8},{11,9},{8,1... | collective-permute-start | bytes 208904 | tf_op jit(solution)/shard_map/ppermute | solution.py:519
  17.3 4.4 %collective-permute-start.6 = (s16[272,128]{1,0:T(8,128)(2,1)S(1)}, s16[272,128]{1,0:T(8,128)(2,1)S(1)}, u32[]{:S(2)}, u32[]{:S(2)}) collective-permute-start(s16[272,128]{1,0:T(8,128)(2,1)S(1)} %send_half.1), channel_id=1, source_target_pairs={{4,0},{0,4},{12,8},{8,12},{5,1},{1,5},{13,9},{9,13},{6,2},{2,6},{1... | collective-permute-start | bytes 208904 | tf_op jit(solution)/shard_map/ppermute | solution.py:519
  21.8 5.6 %collective-permute-start.7 = (s16[272,128]{1,0:T(8,128)(2,1)S(1)}, s16[272,128]{1,0:T(8,128)(2,1)S(1)}, u32[]{:S(2)}, u32[]{:S(2)}) collective-permute-start(s16[272,128]{1,0:T(8,128)(2,1)S(1)} %keep_half.1.own_ref), channel_id=1, source_target_pairs={{8,0},{12,4},{0,8},{4,12},{9,1},{13,5},{1,9},{5,13},{10,2},{14,6},... | collective-permute-start | bytes 208904 | tf_op jit(solution)/shard_map/ppermute | solution.py:519
  27.5 4.3 %collective-permute-start.9 = (bf16[256,128]{1,0:T(8,128)(2,1)S(1)}, bf16[256,128]{1,0:T(8,128)(2,1)S(1)}, u32[]{:S(2)}, u32[]{:S(2)}) collective-permute-start(bf16[256,128]{1,0:T(8,128)(2,1)S(1)} %finish_half.1.kept_ref.refs_0_), channel_id=1, source_target_pairs={{16,0},{0,16},{17,1},{1,17},{18,2},{2,18},{19,3},{3,19},{20,4},{4,... | collective-permute-start | bytes 196616 | tf_op jit(solution)/shard_map/ppermute | solution.py:514
  29.1 4.3 %collective-permute-start.8 = (bf16[256,128]{1,0:T(8,128)(2,1)S(1)}, bf16[256,128]{1,0:T(8,128)(2,1)S(1)}, u32[]{:S(2)}, u32[]{:S(2)}) collective-permute-start(bf16[256,128]{1,0:T(8,128)(2,1)S(1)} %finish_half.1.kept_ref.refs_0_), channel_id=1, source_target_pairs={{4,0},{0,4},{12,8},{8,12},{5,1},{1,5},{13,9},{9,13},{6,2},{2,6},{1... | collective-permute-start | bytes 196616 | tf_op jit(solution)/shard_map/ppermute | solution.py:519
  31.8 4.3 %collective-permute-start.10 = (bf16[256,128]{1,0:T(8,128)(2,1)S(1)}, bf16[256,128]{1,0:T(8,128)(2,1)S(1)}, u32[]{:S(2)}, u32[]{:S(2)}) collective-permute-start(bf16[256,128]{1,0:T(8,128)(2,1)S(1)} %collective-permute-done.9.refs_1_), channel_id=1, source_target_pairs={{4,0},{0,4},{12,8},{8,12},{5,1},{1,5},{13,9},{9,13},{6,2},{2,6},{1... | collective-permute-start | bytes 196616 | tf_op jit(solution)/shard_map/ppermute | solution.py:519

commit v12 on v11

--- a/solution.py
+++ b/solution.py
@@ -445,7 +445,7 @@
 
 
 def second_contract_kernel(times, split, weight_ref, tau_ref, *refs):
-    kept, other, refs = refs[:times], refs[times : 2 * times], refs[2 * times :]
+    other, kept, refs = refs[:times], refs[times : 2 * times], refs[2 * times :]
     live_ref, first_sums_ref, corr_ref, sums_ref, left_ref, right_ref = refs
     vectors = sums_ref.shape[2]
     half = kept[0].shape[0]
@@ -517,6 +517,16 @@
 def from_partner(block, axis, step):
     count = lax.axis_size(axis)
     return lax.ppermute(block, axis, [(i ^ step, i) for i in range(count)])
+
+
+def from_diagonal(block, axes, sources):
+    rows, columns = (lax.axis_size(axis) for axis in axes)
+    perm = []
+    for row in range(rows):
+        for column in range(columns):
+            from_row, from_column = sources(row, column)
+            perm.append((from_row * columns + from_column, row * columns + column))
+    return lax.ppermute(block, axes, perm)
 
 
 def per_device(eigvecs, links, op_dirs, op_moms, perams, pair_times, slot_counts):
@@ -611,12 +621,13 @@
             continue
         body = functools.partial(fold_halves_kernel, b, vectors)
         away, kept = packed(body, "fold_halves", *inputs, rows=half, count=2)
-        away, kept = from_partner(away, "gy", 1 << b), from_partner(kept, "gy", 1 << b)
+        away = from_diagonal(away, ("gx", "gy"), lambda x, y: (x ^ 1, y ^ (1 << b)))
+        kept = from_partner(kept, "gy", 1 << b)
     inputs = (held[-1], swapped_b, *messages)
     body = functools.partial(half_kernel, levels, vectors, False)
-    arrived = from_partner(packed(body, "send_half", *inputs, away, rows=half), "gx", 1)
+    arrived = from_partner(packed(body, "send_half", *inputs, rows=half), "gx", 1)
     body = functools.partial(half_kernel, levels, vectors, True)
-    message = packed(body, "keep_half", *inputs, kept, arrived, rows=half)
+    message = packed(body, "keep_half", *inputs, arrived, away, kept, rows=half)
     norm_factor = 1.0 / math.sqrt(3.0 * cells_x * shares * cells_y * groups * cells_z)
     step = 2
     while step < shares:
@@ -633,7 +644,10 @@
         vmem_spec(),
     )(message, arrived)
     kept = [finished] + [from_step(finished, "ta", t) for t in range(1, times)]
-    other = [from_partner(block, "gx", 1) for block in kept]
+    other = [from_partner(finished, "gx", 1)]
+    for t in range(1, times):
+        source = lambda row, x: ((row + t) % times, x ^ 1)
+        other.append(from_diagonal(finished, ("ta", "gx"), source))
     split = own_ops % 2 == 0
     now_ops = own_ops // 2 if split else own_ops
     sums_shape = (2 * now_ops, 32, vectors)
@@ -641,13 +655,6 @@
         pltpu.VMEM((2 * now_ops * vectors, 2 * vectors), bf16),
         pltpu.VMEM((2 * vectors, 2 * now_ops * vectors), bf16),
     ]
-    margins = local_call(
-        margins_kernel,
-        "margins_out",
-        jax.ShapeDtypeStruct((1, own_rows, vectors), f32),
-        [vmem_spec()] * 2,
-        vmem_spec(),
-    )(kept[0], other[0])
     live, sums = local_call(
         functools.partial(first_contract_kernel, times, split),
         "first_contraction",
@@ -656,6 +663,13 @@
         (vmem_spec(),) * 2,
         scratch,
     )(slot_counts, weights, perams[0], *kept)
+    margins = local_call(
+        margins_kernel,
+        "margins_out",
+        jax.ShapeDtypeStruct((1, own_rows, vectors), f32),
+        [vmem_spec()] * 2,
+        vmem_spec(),
+    )(*lax.optimization_barrier((kept[0], other[0], sums))[:2])
     correlators = local_call(
         functools.partial(second_contract_kernel, times, split),
         "second_contraction",
@@ -663,7 +677,7 @@
         [vmem_spec()] * (4 + 2 * times),
         vmem_spec(),
         [pltpu.VMEM(sums_shape, f32)] + scratch,
-    )(weights, perams[0], *kept, *other, live, sums)
+    )(weights, perams[0], *other, *kept, live, sums)
     return (margins.reshape(1, own_ops, 2, vectors, vectors), correlators)
 
 

time: 37.8 us -> 35.2 us (0.931)
  waiting for transfers between devices: 17.3 us -> 10.6 us
  starting transfers between devices: 11.8 us -> 16 us
    ppermute x8 -> x6, waiting for transfers between devices: 14.5 us -> 8.59 us  [from_partner(): return lax.ppermute(block, axis, [(i ^ step, i) for i in range(count)])]
    ppermute x0 -> x2, starting transfers between devices: none -> 4.46 us  [from_diagonal(): return lax.ppermute(block, axes, perm)]
    ppermute x3, waiting for transfers between devices: 2.78 us -> 0.16 us  [from_step(): lax.ppermute(block, axis, [((i + step) % count, i) for i in range(count)])]
    ppermute x0 -> x2, waiting for transfers between devices: none -> 1.88 us  [from_diagonal(): return lax.ppermute(block, axes, perm)]
    ppermute x8 -> x6, starting transfers between devices: 4.41 us -> 4.16 us  [from_partner(): return lax.ppermute(block, axis, [(i ^ step, i) for i in range(count)])]
  transfers between devices with their start and end apart: 11 -> 11, of which waited for: 8 -> 9; matrix products, arithmetic and copies ran while one was open for 0% -> 0% of each run, Pallas kernels for 12% -> 11%
where the time goes in v12:
time: 35.2 us; the launch traced here: 35.1 us
  starting transfers between devices  16 us (45%)
  waiting for transfers between devices  10.6 us (30%)
  Pallas kernels  7.12 us (20%)
  between operations  1.36 us (4%)
    ppermute x6, waiting for transfers between devices, from_partner(): return lax.ppermute(block, axis, [(i ^ step, i) for i in range(count)])  8.59 us
    ppermute x3, starting transfers between devices, from_step(): lax.ppermute(block, axis, [((i + step) % count, i) for i in range(count)])  7.34 us
    ppermute x2, starting transfers between devices, from_diagonal(): return lax.ppermute(block, axes, perm)  4.46 us
    ppermute x6, starting transfers between devices, from_partner(): return lax.ppermute(block, axis, [(i ^ step, i) for i in range(count)])  4.16 us
    pallas_call x1, Pallas kernels, per_device(): local_call(functools.partial(prepare_kernel, cells_x, cells_y), 'prepare_...  2.25 us
    ppermute x2, waiting for transfers between devices, from_diagonal(): return lax.ppermute(block, axes, perm)  1.88 us
    pallas_call x1, Pallas kernels, per_device(): local_call(functools.partial(second_contract_kernel, times, split), 'seco...  1.51 us
    pallas_call x1, Pallas kernels, per_device(): local_call(functools.partial(first_margin_kernel, cells_x, cells_y, group...  1.15 us
  transfers between devices with their start and end apart: 11, of which 9 were waited for; matrix products, arithmetic and copies ran while one was open for 0% of the time, Pallas kernels for 11%

profile of v12, /device:TPU:0, one launch (start us, length us, event | category | flops | bytes accessed | tf_op | source)
XLA Modules:
  0.0 35.1 jit_solution(9121593800405394293)
XLA Ops:
  0.6 5.1 %collective-permute-start = (bf16[1,2,144,128]{3,2,1,0:T(8,128)(2,1)}, bf16[1,2,144,128]{3,2,1,0:T(8,128)(2,1)S(1)}, u32[]{:S(2)}, u32[]{:S(2)}) collective-permute-start(bf16[1,2,144,128]{3,2,1,0:T(8,128)(2,1)} %bitcast.11), channel_id=1, source_target_pairs={{4,0},{8,4},{12,8},{0,12},{5,1},{9,5},{13,9},{1,13},{6,2},{10,6},{... | collective-permute-start | bytes 221192 | tf_op jit(solution)/shard_map/ppermute | solution.py:514
  5.7 0.7 %collective-permute-start.1 = (bf16[1,2,144,128]{3,2,1,0:T(8,128)(2,1)}, bf16[1,2,144,128]{3,2,1,0:T(8,128)(2,1)S(1)}, u32[]{:S(2)}, u32[]{:S(2)}) collective-permute-start(bf16[1,2,144,128]{3,2,1,0:T(8,128)(2,1)} %bitcast.12), channel_id=1, source_target_pairs={{1,0},{2,1},{3,2},{0,3},{5,4},{6,5},{7,6},{4,7},{9,8},{10,9},{11,1... | collective-permute-start | bytes 221192 | tf_op jit(solution)/shard_map/ppermute | solution.py:514
  6.4 2.3 %prepare_lines.1 = (bf16[3,144,128]{2,1,0:T(8,128)(2,1)S(1)}, f32[11,144,128]{2,1,0:T(8,128)S(1)}, bf16[2,128,288]{2,1,0:T(8,128)(2,1)S(1)}, f32[8,72,256]{2,1,0:T(8,128)S(1)}, f32[2,2,8,128]{3,2,1,0:T(8,128)S(1)}) custom-call(bf16[1,2,144,128]{3,2,1,0:T(8,128)(2,1)} %bitcast.13, bf16[2,27,2,24]{3,2,1,0:T(2,128)(2,1)} %bitcast.14, s32[8]{0:T(128)} %refs_6_.1, ...), custom_call_target="tpu_custom_call" | custom-call | tf_op jit(solution)/shard_map/prepare_lines/pallas_call | solution.py:553
  8.7 0.0 collective-permute-done.refs_4_
  8.7 0.0 collective-permute-done.1.refs_5_
  8.7 1.1 %first_margins.1 = (f32[1,512,128]{2,1,0:T(8,128)S(1)}, f32[1,512,128]{2,1,0:T(8,128)S(1)}, bf16[4,128,288]{2,1,0:T(8,128)(2,1)S(1)}, bf16[4,288,256]{2,1,0:T(8,128)(2,1)S(1)}) custom-call(bf16[3,144,128]{2,1,0:T(8,128)(2,1)S(1)} %get-tuple-element.19.refs_0_, f32[11,144,128]{2,1,0:T(8,128)S(1)} %get-tuple-element.20.refs_1_, ...), custom_call_target="tpu_custom_call" | custom-call | tf_op jit(solution)/shard_map/first_margins/pallas_call | solution.py:573
  9.9 0.3 second_margins.1
  10.2 1.0 %collective-permute-start.2 = (f32[1,512,128]{2,1,0:T(8,128)S(1)}, f32[1,512,128]{2,1,0:T(8,128)S(1)}, u32[]{:S(2)}, u32[]{:S(2)}) collective-permute-start(f32[1,512,128]{2,1,0:T(8,128)S(1)} %get-tuple-element.26), channel_id=1, source_target_pairs={{1,0},{0,1},{3,2},{2,3},{5,4},{4,5},{7,6},{6,7},{9,8},{8,9},{11,10... | collective-permute-start | bytes 786440 | tf_op jit(solution)/shard_map/ppermute | solution.py:519
  11.2 0.1 collective-permute-start.4
  11.2 1.1 %collective-permute-done.2.swapped_ref = f32[1,512,128]{2,1,0:T(8,128)S(1)} collective-permute-done((f32[1,512,128]{2,1,0:T(8,128)S(1)}, f32[1,512,128]{2,1,0:T(8,128)S(1)}, u32[]{:S(2)}, u32[]{:S(2)}) %collective-permute-start.2) | collective-permute-done | bytes 262176 | tf_op jit(solution)/shard_map/ppermute | solution.py:519
  12.3 0.0 copy-start
  12.3 0.1 send_half.1
  12.4 0.1 collective-permute-start.3
  12.5 0.2 collective-permute-done.4.swapped_ref
  12.7 0.1 fold_halves.1
  12.8 2.5 %collective-permute-start.5 = (s16[272,128]{1,0:T(8,128)(2,1)S(1)}, s16[272,128]{1,0:T(8,128)(2,1)S(1)}, u32[]{:S(2)}, u32[]{:S(2)}) collective-permute-start(s16[272,128]{1,0:T(8,128)(2,1)S(1)} %get-tuple-element.29), channel_id=1, source_target_pairs={{6,0},{7,1},{4,2},{5,3},{2,4},{3,5},{0,6},{1,7},{14,8},{15,9},{12,... | collective-permute-start | bytes 208904 | tf_op jit(solution)/shard_map/ppermute | solution.py:529
  15.3 0.9 %collective-permute-start.6 = (s16[272,128]{1,0:T(8,128)(2,1)S(1)}, s16[272,128]{1,0:T(8,128)(2,1)S(1)}, u32[]{:S(2)}, u32[]{:S(2)}) collective-permute-start(s16[272,128]{1,0:T(8,128)(2,1)S(1)} %get-tuple-element.30), channel_id=1, source_target_pairs={{2,0},{3,1},{0,2},{1,3},{6,4},{7,5},{4,6},{5,7},{10,8},{11,9},{8,1... | collective-permute-start | bytes 208904 | tf_op jit(solution)/shard_map/ppermute | solution.py:519
  16.2 1.3 %collective-permute-done.3.refs_0_ = s16[272,128]{1,0:T(8,128)(2,1)S(1)} collective-permute-done((s16[272,128]{1,0:T(8,128)(2,1)S(1)}, s16[272,128]{1,0:T(8,128)(2,1)S(1)}, u32[]{:S(2)}, u32[]{:S(2)}) %collective-permute-start.3) | collective-permute-done | bytes 69664 | tf_op jit(solution)/shard_map/ppermute | solution.py:519
  17.4 1.7 %collective-permute-done.5.refs_1_ = s16[272,128]{1,0:T(8,128)(2,1)S(1)} collective-permute-done((s16[272,128]{1,0:T(8,128)(2,1)S(1)}, s16[272,128]{1,0:T(8,128)(2,1)S(1)}, u32[]{:S(2)}, u32[]{:S(2)}) %collective-permute-start.5) | collective-permute-done | bytes 69664 | tf_op jit(solution)/shard_map/ppermute | solution.py:529
  19.1 1.2 %collective-permute-done.6.refs_2_ = s16[272,128]{1,0:T(8,128)(2,1)S(1)} collective-permute-done((s16[272,128]{1,0:T(8,128)(2,1)S(1)}, s16[272,128]{1,0:T(8,128)(2,1)S(1)}, u32[]{:S(2)}, u32[]{:S(2)}) %collective-permute-start.6) | collective-permute-done | bytes 69664 | tf_op jit(solution)/shard_map/ppermute | solution.py:519
  20.3 0.1 keep_half.1.own_ref
  20.4 2.1 %collective-permute-start.7 = (s16[272,128]{1,0:T(8,128)(2,1)S(1)}, s16[272,128]{1,0:T(8,128)(2,1)S(1)}, u32[]{:S(2)}, u32[]{:S(2)}) collective-permute-start(s16[272,128]{1,0:T(8,128)(2,1)S(1)} %keep_half.1.own_ref), channel_id=1, source_target_pairs={{8,0},{12,4},{0,8},{4,12},{9,1},{13,5},{1,9},{5,13},{10,2},{14,6},... | collective-permute-start | bytes 208904 | tf_op jit(solution)/shard_map/ppermute | solution.py:519
  22.6 4.2 %collective-permute-done.7.arrived_ref = s16[272,128]{1,0:T(8,128)(2,1)S(1)} collective-permute-done((s16[272,128]{1,0:T(8,128)(2,1)S(1)}, s16[272,128]{1,0:T(8,128)(2,1)S(1)}, u32[]{:S(2)}, u32[]{:S(2)}) %collective-permute-start.7) | collective-permute-done | bytes 69664 | tf_op jit(solution)/shard_map/ppermute | solution.py:519
  26.8 1.6 %collective-permute-start.9 = (bf16[256,128]{1,0:T(8,128)(2,1)S(1)}, bf16[256,128]{1,0:T(8,128)(2,1)S(1)}, u32[]{:S(2)}, u32[]{:S(2)}) collective-permute-start(bf16[256,128]{1,0:T(8,128)(2,1)S(1)} %finish_half.1.refs_0_.kept_ref.refs_2_), channel_id=1, source_target_pairs={{16,0},{0,16},{17,1},{1,17},{18,2},{2,18},{19,3},{3,19},{20,4},{4,... | collective-permute-start | bytes 196616 | tf_op jit(solution)/shard_map/ppermute | solution.py:514
  28.4 0.0 collective-permute-start.8
  28.4 2.0 %collective-permute-start.10 = (bf16[256,128]{1,0:T(8,128)(2,1)S(1)}, bf16[256,128]{1,0:T(8,128)(2,1)S(1)}, u32[]{:S(2)}, u32[]{:S(2)}) collective-permute-start(bf16[256,128]{1,0:T(8,128)(2,1)S(1)} %finish_half.1.refs_0_.kept_ref.refs_2_), channel_id=1, source_target_pairs={{20,0},{16,4},{28,8},{24,12},{4,16},{0,20},{12,24},{8,28},{21,1},{... | collective-permute-start | bytes 196616 | tf_op jit(solution)/shard_map/ppermute | solution.py:529
  31.0 0.1 collective-permute-done.9.refs_1_.refs_3_
  31.2 0.0 copy-done
  31.2 0.9 %first_contraction.1 = (f32[8,128]{1,0:T(8,128)S(1)}, f32[2,32,128]{2,1,0:T(8,128)S(1)}) custom-call(s32[1]{0:T(128)S(6)} %copy.10.live_ref, f32[2,2,8,128]{3,2,1,0:T(8,128)S(1)} %get-tuple-element.31.weight_ref, bf16[2,512,512]{2,1,0:T(8,128)(2,1)S(1)} %bitcast.8, bf16[256,128]{1,0:T(8,128)(2,1)S(1)} %finish_half.1.refs_0_.kept_ref.refs_2_, ...), custom_call_target="tpu_custom_call" | custom-call | tf_op jit(solution)/shard_map/first_contraction/pallas_call | solution.py:658
  32.0 0.6 %collective-permute-done.8.other_ref.refs_0_ = bf16[256,128]{1,0:T(8,128)(2,1)S(1)} collective-permute-done((bf16[256,128]{1,0:T(8,128)(2,1)S(1)}, bf16[256,128]{1,0:T(8,128)(2,1)S(1)}, u32[]{:S(2)}, u32[]{:S(2)}) %collective-permute-start.8) | collective-permute-done | bytes 65568 | tf_op jit(solution)/shard_map/ppermute | solution.py:519
  32.7 0.7 %margins_out.1 = f32[1,512,128]{2,1,0:T(8,128)} custom-call(bf16[256,128]{1,0:T(8,128)(2,1)S(1)} %finish_half.1.refs_0_.kept_ref.refs_2_, bf16[256,128]{1,0:T(8,128)(2,1)S(1)} %collective-permute-done.8.other_ref.refs_0_), custom_call_target="tpu_custom_call" | custom-call | tf_op jit(solution)/shard_map/margins_out/pallas_call | solution.py:666
  33.4 0.2 collective-permute-done.10.refs_1_
  33.6 1.5 %second_contraction.1 = f32[1,2,2]{2,1,0:T(2,128)} custom-call(f32[2,2,8,128]{3,2,1,0:T(8,128)S(1)} %get-tuple-element.31.weight_ref, bf16[2,512,512]{2,1,0:T(8,128)(2,1)S(1)} %bitcast.9, bf16[256,128]{1,0:T(8,128)(2,1)S(1)} %collective-permute-done.8.other_ref.refs_0_, bf16[256,128]{1,0:T(8,128)(2,1)S(1)} %collective-permute-done.10.refs_1_, ...), custom_call_target="tpu_custom_call" | custom-call | tf_op jit(solution)/shard_map/second_contraction/pallas_call | solution.py:673
  (1 shorter events, 0.0 us)
Async XLA Ops:
  0.6 8.0 %collective-permute-start = (bf16[1,2,144,128]{3,2,1,0:T(8,128)(2,1)}, bf16[1,2,144,128]{3,2,1,0:T(8,128)(2,1)S(1)}, u32[]{:S(2)}, u32[]{:S(2)}) collective-permute-start(bf16[1,2,144,128]{3,2,1,0:T(8,128)(2,1)} %bitcast.11), channel_id=1, source_target_pairs={{4,0},{8,4},{12,8},{0,12},{5,1},{9,5},{13,9},{1,13},{6,2},{10,6},{... | collective-permute-start | bytes 221192 | tf_op jit(solution)/shard_map/ppermute | solution.py:514
  5.7 3.0 %collective-permute-start.1 = (bf16[1,2,144,128]{3,2,1,0:T(8,128)(2,1)}, bf16[1,2,144,128]{3,2,1,0:T(8,128)(2,1)S(1)}, u32[]{:S(2)}, u32[]{:S(2)}) collective-permute-start(bf16[1,2,144,128]{3,2,1,0:T(8,128)(2,1)} %bitcast.12), channel_id=1, source_target_pairs={{1,0},{2,1},{3,2},{0,3},{5,4},{6,5},{7,6},{4,7},{9,8},{10,9},{11,1... | collective-permute-start | bytes 221192 | tf_op jit(solution)/shard_map/ppermute | solution.py:514
  10.2 2.2 %collective-permute-start.2 = (f32[1,512,128]{2,1,0:T(8,128)S(1)}, f32[1,512,128]{2,1,0:T(8,128)S(1)}, u32[]{:S(2)}, u32[]{:S(2)}) collective-permute-start(f32[1,512,128]{2,1,0:T(8,128)S(1)} %get-tuple-element.26), channel_id=1, source_target_pairs={{1,0},{0,1},{3,2},{2,3},{5,4},{4,5},{7,6},{6,7},{9,8},{8,9},{11,10... | collective-permute-start | bytes 786440 | tf_op jit(solution)/shard_map/ppermute | solution.py:519
  11.2 1.5 %collective-permute-start.4 = (f32[1,512,128]{2,1,0:T(8,128)S(1)}, f32[1,512,128]{2,1,0:T(8,128)S(1)}, u32[]{:S(2)}, u32[]{:S(2)}) collective-permute-start(f32[1,512,128]{2,1,0:T(8,128)S(1)} %get-tuple-element.28), channel_id=1, source_target_pairs={{1,0},{0,1},{3,2},{2,3},{5,4},{4,5},{7,6},{6,7},{9,8},{8,9},{11,10... | collective-permute-start | bytes 786440 | tf_op jit(solution)/shard_map/ppermute | solution.py:519
  12.3 18.8 %copy-start = (bf16[1,2,512,512]{3,2,1,0:T(8,128)(2,1)S(1)}, bf16[1,2,512,512]{3,2,1,0:T(8,128)(2,1)}, u32[]{:S(2)}) copy-start(bf16[1,2,512,512]{3,2,1,0:T(8,128)(2,1)} %param.12) | copy-start | bytes 3145732
  12.4 5.0 %collective-permute-start.3 = (s16[272,128]{1,0:T(8,128)(2,1)S(1)}, s16[272,128]{1,0:T(8,128)(2,1)S(1)}, u32[]{:S(2)}, u32[]{:S(2)}) collective-permute-start(s16[272,128]{1,0:T(8,128)(2,1)S(1)} %send_half.1), channel_id=1, source_target_pairs={{4,0},{0,4},{12,8},{8,12},{5,1},{1,5},{13,9},{9,13},{6,2},{2,6},{1... | collective-permute-start | bytes 208904 | tf_op jit(solution)/shard_map/ppermute | solution.py:519
  12.8 6.3 %collective-permute-start.5 = (s16[272,128]{1,0:T(8,128)(2,1)S(1)}, s16[272,128]{1,0:T(8,128)(2,1)S(1)}, u32[]{:S(2)}, u32[]{:S(2)}) collective-permute-start(s16[272,128]{1,0:T(8,128)(2,1)S(1)} %get-tuple-element.29), channel_id=1, source_target_pairs={{6,0},{7,1},{4,2},{5,3},{2,4},{3,5},{0,6},{1,7},{14,8},{15,9},{12,... | collective-permute-start | bytes 208904 | tf_op jit(solution)/shard_map/ppermute | solution.py:529
  15.3 5.0 %collective-permute-start.6 = (s16[272,128]{1,0:T(8,128)(2,1)S(1)}, s16[272,128]{1,0:T(8,128)(2,1)S(1)}, u32[]{:S(2)}, u32[]{:S(2)}) collective-permute-start(s16[272,128]{1,0:T(8,128)(2,1)S(1)} %get-tuple-element.30), channel_id=1, source_target_pairs={{2,0},{3,1},{0,2},{1,3},{6,4},{7,5},{4,6},{5,7},{10,8},{11,9},{8,1... | collective-permute-start | bytes 208904 | tf_op jit(solution)/shard_map/ppermute | solution.py:519
  20.4 6.4 %collective-permute-start.7 = (s16[272,128]{1,0:T(8,128)(2,1)S(1)}, s16[272,128]{1,0:T(8,128)(2,1)S(1)}, u32[]{:S(2)}, u32[]{:S(2)}) collective-permute-start(s16[272,128]{1,0:T(8,128)(2,1)S(1)} %keep_half.1.own_ref), channel_id=1, source_target_pairs={{8,0},{12,4},{0,8},{4,12},{9,1},{13,5},{1,9},{5,13},{10,2},{14,6},... | collective-permute-start | bytes 208904 | tf_op jit(solution)/shard_map/ppermute | solution.py:519
  26.8 4.3 %collective-permute-start.9 = (bf16[256,128]{1,0:T(8,128)(2,1)S(1)}, bf16[256,128]{1,0:T(8,128)(2,1)S(1)}, u32[]{:S(2)}, u32[]{:S(2)}) collective-permute-start(bf16[256,128]{1,0:T(8,128)(2,1)S(1)} %finish_half.1.refs_0_.kept_ref.refs_2_), channel_id=1, source_target_pairs={{16,0},{0,16},{17,1},{1,17},{18,2},{2,18},{19,3},{3,19},{20,4},{4,... | collective-permute-start | bytes 196616 | tf_op jit(solution)/shard_map/ppermute | solution.py:514
  28.4 4.3 %collective-permute-start.8 = (bf16[256,128]{1,0:T(8,128)(2,1)S(1)}, bf16[256,128]{1,0:T(8,128)(2,1)S(1)}, u32[]{:S(2)}, u32[]{:S(2)}) collective-permute-start(bf16[256,128]{1,0:T(8,128)(2,1)S(1)} %finish_half.1.refs_0_.kept_ref.refs_2_), channel_id=1, source_target_pairs={{4,0},{0,4},{12,8},{8,12},{5,1},{1,5},{13,9},{9,13},{6,2},{2,6},{1... | collective-permute-start | bytes 196616 | tf_op jit(solution)/shard_map/ppermute | solution.py:519
  28.4 5.2 %collective-permute-start.10 = (bf16[256,128]{1,0:T(8,128)(2,1)S(1)}, bf16[256,128]{1,0:T(8,128)(2,1)S(1)}, u32[]{:S(2)}, u32[]{:S(2)}) collective-permute-start(bf16[256,128]{1,0:T(8,128)(2,1)S(1)} %finish_half.1.refs_0_.kept_ref.refs_2_), channel_id=1, source_target_pairs={{20,0},{16,4},{28,8},{24,12},{4,16},{0,20},{12,24},{8,28},{21,1},{... | collective-permute-start | bytes 196616 | tf_op jit(solution)/shard_map/ppermute | solution.py:529

commit v13 on v12

--- a/solution.py
+++ b/solution.py
@@ -183,34 +183,10 @@
         )
 
 
-def low_bit(j):
-    return (j & -j).bit_length() - 1
-
-
-def parts_of_product(side, pair):
-    vectors = pair.shape[1] // 2
-    product = jnp.dot(side, pair, preferred_element_type=jnp.float32)
-    return [product[:, :vectors], product[:, vectors:]]
-
-
-def put_product(out_ref, place, i, side, pair):
-    for k, block in enumerate(parts_of_product(side, pair)):
-        rows = block.shape[0]
-        out_ref[place, (2 * i + k) * rows : (2 * i + k + 1) * rows] = block
-
-
-def first_groups(groups):
-    return sorted((j for j in range(groups) if j & 2), key=lambda j: -(j & 1))
-
-
-def second_groups(groups):
-    return sorted((j for j in range(groups) if not j & 2), key=lambda j: -(j & 1))
-
-
-def first_margin_kernel(cells_x, cells_y, groups, own_ops, *refs):
+def margin_kernel(cells_x, cells_y, groups, own_ops, *refs):
     matrix_ref, local_ref, left_ref, phase_ref, halo_x_ref, halo_y_ref, dirs_hbm = refs[:7]
-    swap_ref, hold_ref, later_side_ref, later_pair_ref = refs[7:11]
-    field_ref, side_ref, dirs_ref, sem = refs[11:]
+    swap_ref, hold_ref = refs[7:9]
+    field_ref, side_ref, dirs_ref, sem = refs[9:]
     f32, bf16 = jnp.float32, jnp.bfloat16
     copy = pltpu.make_async_copy(dirs_hbm, dirs_ref, sem)
     copy.start()
@@ -238,8 +214,8 @@
         field_ref[code, line] = local_ref[k]
     copy.wait()
     me = lax.axis_index("gy")
-    later = 0
-    for j in first_groups(groups) + second_groups(groups):
+    for j in sorted(range(groups), key=lambda j: -(j & 1)):
+        blocks = []
         for i in range(own_ops):
             o = (me ^ j) * own_ops + i
             code = dirs_ref[o]
@@ -253,22 +229,13 @@
                 pairs.append(jnp.concatenate([turned_r, turned_i], axis=1))
                 pairs.append(jnp.concatenate([turned_i, -turned_r], axis=1))
             pair = jnp.concatenate(pairs, axis=0).astype(bf16)
-            if j & 2:
-                put_product(swap_ref if j & 1 else hold_ref, j >> 2, i, side_ref[side], pair)
-            else:
-                later_side_ref[later] = side_ref[side]
-                later_pair_ref[later] = pair
-                later += 1
-
-
-def second_margin_kernel(groups, own_ops, side_ref, pair_ref, swap_ref, *hold_refs):
-    later = 0
-    for j in second_groups(groups):
-        level = low_bit(j) if j else groups.bit_length() - 1
-        for i in range(own_ops):
-            out_ref, place = (swap_ref, j >> 2) if j & 1 else (hold_refs[level - 2], j >> (level + 1))
-            put_product(out_ref, place, i, side_ref[later], pair_ref[later])
-            later += 1
+            product = jnp.dot(side_ref[side], pair, preferred_element_type=f32)
+            blocks += [product[:, :vectors], product[:, vectors:]]
+        if j & 1:
+            put_fixed(swap_ref.at[j >> 1], blocks)
+            continue
+        for k, block in enumerate(blocks):
+            hold_ref[j >> 1, k * vectors : (k + 1) * vectors] = block
 
 
 def scale_of(block):
@@ -294,10 +261,9 @@
     return block * jnp.exp2(scales[k : k + 1] - FIXED_BITS)
 
 
-def group_block(held_ref, swapped_ref, messages, k, j, start, rows):
-    span = pl.ds(start, rows)
-    total = held_ref[k, span] + swapped_ref[j >> 2, span]
-    for b, ref in enumerate(messages, 1):
+def group_block(held_ref, messages, j, start, rows):
+    total = held_ref[j >> 1, pl.ds(start, rows)]
+    for b, ref in enumerate(messages):
         total = total + fixed_at(ref.at[j >> (b + 1)], start, rows)
     return total
 
@@ -311,42 +277,37 @@
     return block * jnp.exp2(scale - FIXED_BITS)
 
 
-def fold_kernel(level, vectors, held_ref, swapped_ref, *refs):
+def fold_kernel(level, vectors, held_ref, *refs):
     messages, out_ref = refs[:-1], refs[-1]
-    for k in range(held_ref.shape[0]):
+    for k in range(out_ref.shape[0]):
         blocks = [
-            group_block(held_ref, swapped_ref, messages, k, (2 * k + 1) << level, start, vectors)
+            group_block(held_ref, messages, (2 * k + 1) << level, start, vectors)
             for start in range(0, held_ref.shape[1], vectors)
         ]
         put_fixed(out_ref.at[k], blocks)
 
 
-def half_rows(rows, vectors, kept):
+def half_blocks(held_ref, messages, j, kept, vectors):
     me = lax.axis_index("gx") & 1
-    half = rows // 2
+    half = held_ref.shape[1] // 2
     base = pl.multiple_of((me if kept else 1 - me) * half, half)
-    return [base + step for step in range(0, half, vectors)]
-
-
-def fold_halves_kernel(level, vectors, held_ref, swapped_ref, *refs):
-    messages, outs = refs[:-2], refs[-2:]
-    group = 1 << level
-    for kept, out_ref in enumerate(outs):
-        starts = half_rows(held_ref.shape[1], vectors, kept)
-        put_fixed(
-            out_ref,
-            [group_block(held_ref, swapped_ref, messages, 0, group, s, vectors) for s in starts],
-        )
-
-
-def half_kernel(levels, vectors, kept, own_ref, swapped_ref, *refs):
-    messages, came, out_ref = refs[: levels - 2], refs[levels - 2 : -1], refs[-1]
-    blocks = []
-    for p, start in enumerate(half_rows(own_ref.shape[1], vectors, kept)):
-        total = group_block(own_ref, swapped_ref, messages, 0, 0, start, vectors)
+    steps = range(0, half, vectors)
+    return [group_block(held_ref, messages, j, base + step, vectors) for step in steps]
+
+
+def spread_kernel(level, vectors, held_ref, *refs):
+    messages, (y_ref, diagonal_ref, x_ref) = refs[:-3], refs[-3:]
+    put_fixed(y_ref, half_blocks(held_ref, messages, 1 << level, True, vectors))
+    put_fixed(diagonal_ref, half_blocks(held_ref, messages, 1 << level, False, vectors))
+    put_fixed(x_ref, half_blocks(held_ref, messages, 0, False, vectors))
+
+
+def keep_kernel(vectors, held_ref, *refs):
+    messages, came, out_ref = refs[:-4], refs[-4:-1], refs[-1]
+    blocks = half_blocks(held_ref, messages, 0, True, vectors)
+    for p in range(len(blocks)):
         for ref in came:
-            total = total + from_fixed(ref, vectors, p)
-        blocks.append(total)
+            blocks[p] = blocks[p] + from_fixed(ref, vectors, p)
     put_fixed(out_ref, blocks)
 
 
@@ -568,19 +529,16 @@
             pltpu.SemaphoreType.DMA((len(inputs),)),
         ],
     )(*inputs)
-    part = lambda count: jax.ShapeDtypeStruct((count, own_rows, vectors), f32)
-    later = count_ops // 2
-    swap_a, hold_a, later_sides, later_pairs = local_call(
-        functools.partial(first_margin_kernel, cells_x, cells_y, groups, own_ops),
-        "first_margins",
+    message = lambda rows, *lead: jax.ShapeDtypeStruct((*lead, rows + TAIL, vectors), jnp.int16)
+    swap, held = local_call(
+        functools.partial(margin_kernel, cells_x, cells_y, groups, own_ops),
+        "partial_margins",
         (
-            part(groups // 4),
-            part(groups // 4),
-            jax.ShapeDtypeStruct((later, vectors, lines * order), bf16),
-            jax.ShapeDtypeStruct((later, lines * order, 2 * vectors), bf16),
+            message(own_rows, groups // 2),
+            jax.ShapeDtypeStruct((groups // 2, own_rows, vectors), f32),
         ),
         [vmem_spec()] * 6 + [hbm_spec()],
-        (vmem_spec(),) * 4,
+        (vmem_spec(),) * 2,
         [
             pltpu.VMEM((7, lines, order, vectors), f32),
             pltpu.VMEM((4, vectors, lines * order), bf16),
@@ -588,61 +546,39 @@
             pltpu.SemaphoreType.DMA,
         ],
     )(matrices, local, left, phases, halo_x, halo_y, in_hbm(op_dirs))
-    swapped_a = from_partner(swap_a, "gy", 1)
-    held_shapes = [part(groups >> (b + 1)) for b in range(2, levels)] + [part(1)]
-    swap_b, *held = local_call(
-        functools.partial(second_margin_kernel, groups, own_ops),
-        "second_margins",
-        (part(groups // 4), *held_shapes),
-        [vmem_spec()] * 2,
-        (vmem_spec(),) * (1 + len(held_shapes)),
-        cost=pl.CostEstimate(
-            flops=later * 4 * lines * order * vectors * vectors,
-            bytes_accessed=later * 6 * lines * order * vectors + later * 8 * vectors * vectors,
-            transcendentals=0,
-        ),
-    )(later_sides, later_pairs)
-    swapped_b = from_partner(swap_b, "gy", 1)
-
-    def packed(body, name, *inputs, rows=own_rows, lead=(), count=1):
-        shape = jax.ShapeDtypeStruct((*lead, rows + TAIL, vectors), jnp.int16)
-        outs = shape if count == 1 else (shape,) * count
-        specs = vmem_spec() if count == 1 else (vmem_spec(),) * count
+
+    def in_vmem(body, name, outs, *inputs):
+        outs = outs if isinstance(outs, tuple) else (outs,)
+        specs = (vmem_spec(),) * len(outs)
         return local_call(body, name, outs, [vmem_spec()] * len(inputs), specs)(*inputs)
 
     half = own_rows // 2
-    messages = []
-    for b in range(1, levels):
-        inputs = (hold_a, swapped_a) if b == 1 else (held[b - 2], swapped_b, *messages)
-        if b < levels - 1:
-            body = functools.partial(fold_kernel, b, vectors)
-            sent = packed(body, "fold_groups", *inputs, lead=inputs[0].shape[:1])
-            messages.append(from_partner(sent, "gy", 1 << b))
-            continue
-        body = functools.partial(fold_halves_kernel, b, vectors)
-        away, kept = packed(body, "fold_halves", *inputs, rows=half, count=2)
-        away = from_diagonal(away, ("gx", "gy"), lambda x, y: (x ^ 1, y ^ (1 << b)))
-        kept = from_partner(kept, "gy", 1 << b)
-    inputs = (held[-1], swapped_b, *messages)
-    body = functools.partial(half_kernel, levels, vectors, False)
-    arrived = from_partner(packed(body, "send_half", *inputs, rows=half), "gx", 1)
-    body = functools.partial(half_kernel, levels, vectors, True)
-    message = packed(body, "keep_half", *inputs, arrived, away, kept, rows=half)
+    messages = [from_partner(swap, "gy", 1)]
+    last = levels - 1
+    for b in range(1, last):
+        body = functools.partial(fold_kernel, b, vectors)
+        shape = message(own_rows, groups >> (b + 1))
+        (sent,) = in_vmem(body, "fold_groups", shape, held, *messages)
+        messages.append(from_partner(sent, "gy", 1 << b))
+    body = functools.partial(spread_kernel, last, vectors)
+    for_y, for_both, for_x = in_vmem(body, "spread_halves", (message(half),) * 3, held, *messages)
+    came = [
+        from_partner(for_y, "gy", 1 << last),
+        from_diagonal(for_both, ("gx", "gy"), lambda x, y: (x ^ 1, y ^ (1 << last))),
+        from_partner(for_x, "gx", 1),
+    ]
+    body = functools.partial(keep_kernel, vectors)
+    (packed,) = in_vmem(body, "keep_half", message(half), held, *messages, *came)
     norm_factor = 1.0 / math.sqrt(3.0 * cells_x * shares * cells_y * groups * cells_z)
     step = 2
     while step < shares:
-        arrived = from_partner(message, "gx", step)
+        arrived = from_partner(packed, "gx", step)
         step *= 2
-        if step < shares:
-            body = functools.partial(both_kernel, vectors, None)
-            message = packed(body, "sum_both", message, arrived, rows=half)
-    finished = local_call(
-        functools.partial(both_kernel, vectors, norm_factor),
-        "finish_half",
-        jax.ShapeDtypeStruct((half, vectors), bf16),
-        [vmem_spec()] * 2,
-        vmem_spec(),
-    )(message, arrived)
+        last_one = step >= shares
+        body = functools.partial(both_kernel, vectors, norm_factor if last_one else None)
+        shape = jax.ShapeDtypeStruct((half, vectors), bf16) if last_one else message(half)
+        (packed,) = in_vmem(body, "finish_half" if last_one else "sum_both", shape, packed, arrived)
+    finished = packed
     kept = [finished] + [from_step(finished, "ta", t) for t in range(1, times)]
     other = [from_partner(finished, "gx", 1)]
     for t in range(1, times):

time: 35.2 us -> 34.1 us (0.969)
  waiting for transfers between devices: 10.6 us -> 9.71 us
    ppermute x6 -> x5, starting transfers between devices: 4.16 us -> 6.69 us  [from_partner(): return lax.ppermute(block, axis, [(i ^ step, i) for i in range(count)])]
    ppermute x2, starting transfers between devices: 4.46 us -> 1.97 us  [from_diagonal(): return lax.ppermute(block, axes, perm)]
    ppermute x6 -> x5, waiting for transfers between devices: 8.59 us -> 6.83 us  [from_partner(): return lax.ppermute(block, axis, [(i ^ step, i) for i in range(count)])]
    ppermute x2, waiting for transfers between devices: 1.88 us -> 2.72 us  [from_diagonal(): return lax.ppermute(block, axes, perm)]
    pallas_call x6 -> x4, Pallas kernels: 1.78 us -> 1.54 us  [the longest x1 1.18 us: per_device(): local_call(functools.partial(margin_kernel, cells_x, cells_y, groups, own...]
  transfers between devices with their start and end apart: 11 -> 10, of which waited for: 9 -> 8; matrix products, arithmetic and copies ran while one was open for 0% -> 0% of each run, Pallas kernels for 11% -> 11%
where the time goes in v13:
time: 34.1 us; the launch traced here: 33.9 us
  starting transfers between devices  16 us (47%)
  waiting for transfers between devices  9.71 us (28%)
  Pallas kernels  6.88 us (20%)
  between operations  1.34 us (4%)
    ppermute x3, starting transfers between devices, from_step(): lax.ppermute(block, axis, [((i + step) % count, i) for i in range(count)])  7.33 us
    ppermute x5, waiting for transfers between devices, from_partner(): return lax.ppermute(block, axis, [(i ^ step, i) for i in range(count)])  6.83 us
    ppermute x5, starting transfers between devices, from_partner(): return lax.ppermute(block, axis, [(i ^ step, i) for i in range(count)])  6.69 us
    ppermute x2, waiting for transfers between devices, from_diagonal(): return lax.ppermute(block, axes, perm)  2.72 us
    pallas_call x1, Pallas kernels, per_device(): local_call(functools.partial(prepare_kernel, cells_x, cells_y), 'prepare_...  2.25 us
    ppermute x2, starting transfers between devices, from_diagonal(): return lax.ppermute(block, axes, perm)  1.97 us
    pallas_call x1, Pallas kernels, per_device(): local_call(functools.partial(second_contract_kernel, times, split), 'seco...  1.51 us
    pallas_call x1, Pallas kernels, per_device(): local_call(functools.partial(margin_kernel, cells_x, cells_y, groups, own...  1.18 us
  transfers between devices with their start and end apart: 10, of which 8 were waited for; matrix products, arithmetic and copies ran while one was open for 0% of the time, Pallas kernels for 11%

profile of v13, /device:TPU:0, one launch (start us, length us, event | category | flops | bytes accessed | tf_op | source)
XLA Modules:
  0.0 33.9 jit_solution(6626580314422004155)
XLA Ops:
  0.6 5.1 %collective-permute-start = (bf16[1,2,144,128]{3,2,1,0:T(8,128)(2,1)}, bf16[1,2,144,128]{3,2,1,0:T(8,128)(2,1)S(1)}, u32[]{:S(2)}, u32[]{:S(2)}) collective-permute-start(bf16[1,2,144,128]{3,2,1,0:T(8,128)(2,1)} %bitcast.11), channel_id=1, source_target_pairs={{4,0},{8,4},{12,8},{0,12},{5,1},{9,5},{13,9},{1,13},{6,2},{10,6},{... | collective-permute-start | bytes 221192 | tf_op jit(solution)/shard_map/ppermute | solution.py:475
  5.7 0.7 %collective-permute-start.1 = (bf16[1,2,144,128]{3,2,1,0:T(8,128)(2,1)}, bf16[1,2,144,128]{3,2,1,0:T(8,128)(2,1)S(1)}, u32[]{:S(2)}, u32[]{:S(2)}) collective-permute-start(bf16[1,2,144,128]{3,2,1,0:T(8,128)(2,1)} %bitcast.12), channel_id=1, source_target_pairs={{1,0},{2,1},{3,2},{0,3},{5,4},{6,5},{7,6},{4,7},{9,8},{10,9},{11,1... | collective-permute-start | bytes 221192 | tf_op jit(solution)/shard_map/ppermute | solution.py:475
  6.4 2.3 %prepare_lines.1 = (bf16[3,144,128]{2,1,0:T(8,128)(2,1)S(1)}, f32[11,144,128]{2,1,0:T(8,128)S(1)}, bf16[2,128,288]{2,1,0:T(8,128)(2,1)S(1)}, f32[8,72,256]{2,1,0:T(8,128)S(1)}, f32[2,2,8,128]{3,2,1,0:T(8,128)S(1)}) custom-call(bf16[1,2,144,128]{3,2,1,0:T(8,128)(2,1)} %bitcast.13, bf16[2,27,2,24]{3,2,1,0:T(2,128)(2,1)} %bitcast.14, s32[8]{0:T(128)} %refs_6_.1, ...), custom_call_target="tpu_custom_call" | custom-call | tf_op jit(solution)/shard_map/prepare_lines/pallas_call | solution.py:514
  8.7 0.0 collective-permute-done.refs_4_
  8.7 0.0 collective-permute-done.1.refs_5_
  8.7 1.2 %partial_margins.1 = (s16[2,528,128]{2,1,0:T(8,128)(2,1)S(1)}, f32[2,512,128]{2,1,0:T(8,128)S(1)}) custom-call(bf16[3,144,128]{2,1,0:T(8,128)(2,1)S(1)} %get-tuple-element.16.refs_0_, f32[11,144,128]{2,1,0:T(8,128)S(1)} %get-tuple-element.17.refs_1_, bf16[2,128,288]{2,1,0:T(8,128)(2,1)S(1)} %get-tuple-element.18.refs_2_, ...), custom_call_target="tpu_custom_call" | custom-call | tf_op jit(solution)/shard_map/partial_margins/pallas_call | solution.py:533
  9.9 0.0 copy-start
  9.9 1.0 %collective-permute-start.2 = (s16[2,528,128]{2,1,0:T(8,128)(2,1)S(1)}, s16[2,528,128]{2,1,0:T(8,128)(2,1)S(1)}, u32[]{:S(2)}, u32[]{:S(2)}) collective-permute-start(s16[2,528,128]{2,1,0:T(8,128)(2,1)S(1)} %get-tuple-element.21), channel_id=1, source_target_pairs={{1,0},{0,1},{3,2},{2,3},{5,4},{4,5},{7,6},{6,7},{9,8},{8,9},{11,10... | collective-permute-start | bytes 811016 | tf_op jit(solution)/shard_map/ppermute | solution.py:480
  10.9 1.2 %collective-permute-done.2.refs_0_ = s16[2,528,128]{2,1,0:T(8,128)(2,1)S(1)} collective-permute-done((s16[2,528,128]{2,1,0:T(8,128)(2,1)S(1)}, s16[2,528,128]{2,1,0:T(8,128)(2,1)S(1)}, u32[]{:S(2)}, u32[]{:S(2)}) %collective-permute-start.2) | collective-permute-done | bytes 270368 | tf_op jit(solution)/shard_map/ppermute | solution.py:480
  12.1 0.2 spread_halves.1
  12.3 1.2 %collective-permute-start.3 = (s16[272,128]{1,0:T(8,128)(2,1)S(1)}, s16[272,128]{1,0:T(8,128)(2,1)S(1)}, u32[]{:S(2)}, u32[]{:S(2)}) collective-permute-start(s16[272,128]{1,0:T(8,128)(2,1)S(1)} %get-tuple-element.22), channel_id=1, source_target_pairs={{2,0},{3,1},{0,2},{1,3},{6,4},{7,5},{4,6},{5,7},{10,8},{11,9},{8,1... | collective-permute-start | bytes 208904 | tf_op jit(solution)/shard_map/ppermute | solution.py:480
  13.5 0.0 collective-permute-start.4
  13.5 2.3 %collective-permute-start.5 = (s16[272,128]{1,0:T(8,128)(2,1)S(1)}, s16[272,128]{1,0:T(8,128)(2,1)S(1)}, u32[]{:S(2)}, u32[]{:S(2)}) collective-permute-start(s16[272,128]{1,0:T(8,128)(2,1)S(1)} %get-tuple-element.24), channel_id=1, source_target_pairs={{4,0},{0,4},{12,8},{8,12},{5,1},{1,5},{13,9},{9,13},{6,2},{2,6},{1... | collective-permute-start | bytes 208904 | tf_op jit(solution)/shard_map/ppermute | solution.py:480
  15.8 1.0 %collective-permute-done.3.refs_1_ = s16[272,128]{1,0:T(8,128)(2,1)S(1)} collective-permute-done((s16[272,128]{1,0:T(8,128)(2,1)S(1)}, s16[272,128]{1,0:T(8,128)(2,1)S(1)}, u32[]{:S(2)}, u32[]{:S(2)}) %collective-permute-start.3) | collective-permute-done | bytes 69664 | tf_op jit(solution)/shard_map/ppermute | solution.py:480
  16.8 2.5 %collective-permute-done.4.refs_2_ = s16[272,128]{1,0:T(8,128)(2,1)S(1)} collective-permute-done((s16[272,128]{1,0:T(8,128)(2,1)S(1)}, s16[272,128]{1,0:T(8,128)(2,1)S(1)}, u32[]{:S(2)}, u32[]{:S(2)}) %collective-permute-start.4) | collective-permute-done | bytes 69664 | tf_op jit(solution)/shard_map/ppermute | solution.py:490
  19.3 0.2 collective-permute-done.5.refs_3_
  19.5 0.1 keep_half.1.own_ref
  19.6 2.1 %collective-permute-start.6 = (s16[272,128]{1,0:T(8,128)(2,1)S(1)}, s16[272,128]{1,0:T(8,128)(2,1)S(1)}, u32[]{:S(2)}, u32[]{:S(2)}) collective-permute-start(s16[272,128]{1,0:T(8,128)(2,1)S(1)} %keep_half.1.own_ref), channel_id=1, source_target_pairs={{8,0},{12,4},{0,8},{4,12},{9,1},{13,5},{1,9},{5,13},{10,2},{14,6},... | collective-permute-start | bytes 208904 | tf_op jit(solution)/shard_map/ppermute | solution.py:480
  21.7 3.9 %collective-permute-done.6.arrived_ref = s16[272,128]{1,0:T(8,128)(2,1)S(1)} collective-permute-done((s16[272,128]{1,0:T(8,128)(2,1)S(1)}, s16[272,128]{1,0:T(8,128)(2,1)S(1)}, u32[]{:S(2)}, u32[]{:S(2)}) %collective-permute-start.6) | collective-permute-done | bytes 69664 | tf_op jit(solution)/shard_map/ppermute | solution.py:480
  25.7 1.6 %collective-permute-start.8 = (bf16[256,128]{1,0:T(8,128)(2,1)S(1)}, bf16[256,128]{1,0:T(8,128)(2,1)S(1)}, u32[]{:S(2)}, u32[]{:S(2)}) collective-permute-start(bf16[256,128]{1,0:T(8,128)(2,1)S(1)} %finish_half.1.refs_0_.kept_ref.refs_2_), channel_id=1, source_target_pairs={{16,0},{0,16},{17,1},{1,17},{18,2},{2,18},{19,3},{3,19},{20,4},{4,... | collective-permute-start | bytes 196616 | tf_op jit(solution)/shard_map/ppermute | solution.py:475
  27.2 0.0 collective-permute-start.7
  27.3 2.0 %collective-permute-start.9 = (bf16[256,128]{1,0:T(8,128)(2,1)S(1)}, bf16[256,128]{1,0:T(8,128)(2,1)S(1)}, u32[]{:S(2)}, u32[]{:S(2)}) collective-permute-start(bf16[256,128]{1,0:T(8,128)(2,1)S(1)} %finish_half.1.refs_0_.kept_ref.refs_2_), channel_id=1, source_target_pairs={{20,0},{16,4},{28,8},{24,12},{4,16},{0,20},{12,24},{8,28},{21,1},{... | collective-permute-start | bytes 196616 | tf_op jit(solution)/shard_map/ppermute | solution.py:490
  29.9 0.1 collective-permute-done.8.refs_1_.refs_3_
  30.0 0.0 copy-done
  30.0 0.9 %first_contraction.1 = (f32[8,128]{1,0:T(8,128)S(1)}, f32[2,32,128]{2,1,0:T(8,128)S(1)}) custom-call(s32[1]{0:T(128)S(6)} %copy.10.live_ref, f32[2,2,8,128]{3,2,1,0:T(8,128)S(1)} %get-tuple-element.25.weight_ref, bf16[2,512,512]{2,1,0:T(8,128)(2,1)S(1)} %bitcast.8, bf16[256,128]{1,0:T(8,128)(2,1)S(1)} %finish_half.1.refs_0_.kept_ref.refs_2_, ...), custom_call_target="tpu_custom_call" | custom-call | tf_op jit(solution)/shard_map/first_contraction/pallas_call | solution.py:594
  30.9 0.6 %collective-permute-done.7.other_ref.refs_0_ = bf16[256,128]{1,0:T(8,128)(2,1)S(1)} collective-permute-done((bf16[256,128]{1,0:T(8,128)(2,1)S(1)}, bf16[256,128]{1,0:T(8,128)(2,1)S(1)}, u32[]{:S(2)}, u32[]{:S(2)}) %collective-permute-start.7) | collective-permute-done | bytes 65568 | tf_op jit(solution)/shard_map/ppermute | solution.py:480
  31.5 0.7 %margins_out.1 = f32[1,512,128]{2,1,0:T(8,128)} custom-call(bf16[256,128]{1,0:T(8,128)(2,1)S(1)} %finish_half.1.refs_0_.kept_ref.refs_2_, bf16[256,128]{1,0:T(8,128)(2,1)S(1)} %collective-permute-done.7.other_ref.refs_0_), custom_call_target="tpu_custom_call" | custom-call | tf_op jit(solution)/shard_map/margins_out/pallas_call | solution.py:602
  32.2 0.2 collective-permute-done.9.refs_1_
  32.4 1.5 %second_contraction.1 = f32[1,2,2]{2,1,0:T(2,128)} custom-call(f32[2,2,8,128]{3,2,1,0:T(8,128)S(1)} %get-tuple-element.25.weight_ref, bf16[2,512,512]{2,1,0:T(8,128)(2,1)S(1)} %bitcast.9, bf16[256,128]{1,0:T(8,128)(2,1)S(1)} %collective-permute-done.7.other_ref.refs_0_, bf16[256,128]{1,0:T(8,128)(2,1)S(1)} %collective-permute-done.9.refs_1_, ...), custom_call_target="tpu_custom_call" | custom-call | tf_op jit(solution)/shard_map/second_contraction/pallas_call | solution.py:609
  (1 shorter events, 0.0 us)
Async XLA Ops:
  0.6 8.0 %collective-permute-start = (bf16[1,2,144,128]{3,2,1,0:T(8,128)(2,1)}, bf16[1,2,144,128]{3,2,1,0:T(8,128)(2,1)S(1)}, u32[]{:S(2)}, u32[]{:S(2)}) collective-permute-start(bf16[1,2,144,128]{3,2,1,0:T(8,128)(2,1)} %bitcast.11), channel_id=1, source_target_pairs={{4,0},{8,4},{12,8},{0,12},{5,1},{9,5},{13,9},{1,13},{6,2},{10,6},{... | collective-permute-start | bytes 221192 | tf_op jit(solution)/shard_map/ppermute | solution.py:475
  5.7 3.0 %collective-permute-start.1 = (bf16[1,2,144,128]{3,2,1,0:T(8,128)(2,1)}, bf16[1,2,144,128]{3,2,1,0:T(8,128)(2,1)S(1)}, u32[]{:S(2)}, u32[]{:S(2)}) collective-permute-start(bf16[1,2,144,128]{3,2,1,0:T(8,128)(2,1)} %bitcast.12), channel_id=1, source_target_pairs={{1,0},{2,1},{3,2},{0,3},{5,4},{6,5},{7,6},{4,7},{9,8},{10,9},{11,1... | collective-permute-start | bytes 221192 | tf_op jit(solution)/shard_map/ppermute | solution.py:475
  9.9 20.1 %copy-start = (bf16[1,2,512,512]{3,2,1,0:T(8,128)(2,1)S(1)}, bf16[1,2,512,512]{3,2,1,0:T(8,128)(2,1)}, u32[]{:S(2)}) copy-start(bf16[1,2,512,512]{3,2,1,0:T(8,128)(2,1)} %param.12) | copy-start | bytes 3145732
  9.9 2.2 %collective-permute-start.2 = (s16[2,528,128]{2,1,0:T(8,128)(2,1)S(1)}, s16[2,528,128]{2,1,0:T(8,128)(2,1)S(1)}, u32[]{:S(2)}, u32[]{:S(2)}) collective-permute-start(s16[2,528,128]{2,1,0:T(8,128)(2,1)S(1)} %get-tuple-element.21), channel_id=1, source_target_pairs={{1,0},{0,1},{3,2},{2,3},{5,4},{4,5},{7,6},{6,7},{9,8},{8,9},{11,10... | collective-permute-start | bytes 811016 | tf_op jit(solution)/shard_map/ppermute | solution.py:480
  12.3 4.5 %collective-permute-start.3 = (s16[272,128]{1,0:T(8,128)(2,1)S(1)}, s16[272,128]{1,0:T(8,128)(2,1)S(1)}, u32[]{:S(2)}, u32[]{:S(2)}) collective-permute-start(s16[272,128]{1,0:T(8,128)(2,1)S(1)} %get-tuple-element.22), channel_id=1, source_target_pairs={{2,0},{3,1},{0,2},{1,3},{6,4},{7,5},{4,6},{5,7},{10,8},{11,9},{8,1... | collective-permute-start | bytes 208904 | tf_op jit(solution)/shard_map/ppermute | solution.py:480
  13.5 5.8 %collective-permute-start.4 = (s16[272,128]{1,0:T(8,128)(2,1)S(1)}, s16[272,128]{1,0:T(8,128)(2,1)S(1)}, u32[]{:S(2)}, u32[]{:S(2)}) collective-permute-start(s16[272,128]{1,0:T(8,128)(2,1)S(1)} %get-tuple-element.23), channel_id=1, source_target_pairs={{6,0},{7,1},{4,2},{5,3},{2,4},{3,5},{0,6},{1,7},{14,8},{15,9},{12,... | collective-permute-start | bytes 208904 | tf_op jit(solution)/shard_map/ppermute | solution.py:490
  13.5 6.0 %collective-permute-start.5 = (s16[272,128]{1,0:T(8,128)(2,1)S(1)}, s16[272,128]{1,0:T(8,128)(2,1)S(1)}, u32[]{:S(2)}, u32[]{:S(2)}) collective-permute-start(s16[272,128]{1,0:T(8,128)(2,1)S(1)} %get-tuple-element.24), channel_id=1, source_target_pairs={{4,0},{0,4},{12,8},{8,12},{5,1},{1,5},{13,9},{9,13},{6,2},{2,6},{1... | collective-permute-start | bytes 208904 | tf_op jit(solution)/shard_map/ppermute | solution.py:480
  19.6 6.0 %collective-permute-start.6 = (s16[272,128]{1,0:T(8,128)(2,1)S(1)}, s16[272,128]{1,0:T(8,128)(2,1)S(1)}, u32[]{:S(2)}, u32[]{:S(2)}) collective-permute-start(s16[272,128]{1,0:T(8,128)(2,1)S(1)} %keep_half.1.own_ref), channel_id=1, source_target_pairs={{8,0},{12,4},{0,8},{4,12},{9,1},{13,5},{1,9},{5,13},{10,2},{14,6},... | collective-permute-start | bytes 208904 | tf_op jit(solution)/shard_map/ppermute | solution.py:480
  25.7 4.3 %collective-permute-start.8 = (bf16[256,128]{1,0:T(8,128)(2,1)S(1)}, bf16[256,128]{1,0:T(8,128)(2,1)S(1)}, u32[]{:S(2)}, u32[]{:S(2)}) collective-permute-start(bf16[256,128]{1,0:T(8,128)(2,1)S(1)} %finish_half.1.refs_0_.kept_ref.refs_2_), channel_id=1, source_target_pairs={{16,0},{0,16},{17,1},{1,17},{18,2},{2,18},{19,3},{3,19},{20,4},{4,... | collective-permute-start | bytes 196616 | tf_op jit(solution)/shard_map/ppermute | solution.py:475
  27.2 4.3 %collective-permute-start.7 = (bf16[256,128]{1,0:T(8,128)(2,1)S(1)}, bf16[256,128]{1,0:T(8,128)(2,1)S(1)}, u32[]{:S(2)}, u32[]{:S(2)}) collective-permute-start(bf16[256,128]{1,0:T(8,128)(2,1)S(1)} %finish_half.1.refs_0_.kept_ref.refs_2_), channel_id=1, source_target_pairs={{4,0},{0,4},{12,8},{8,12},{5,1},{1,5},{13,9},{9,13},{6,2},{2,6},{1... | collective-permute-start | bytes 196616 | tf_op jit(solution)/shard_map/ppermute | solution.py:480
  27.3 5.2 %collective-permute-start.9 = (bf16[256,128]{1,0:T(8,128)(2,1)S(1)}, bf16[256,128]{1,0:T(8,128)(2,1)S(1)}, u32[]{:S(2)}, u32[]{:S(2)}) collective-permute-start(bf16[256,128]{1,0:T(8,128)(2,1)S(1)} %finish_half.1.refs_0_.kept_ref.refs_2_), channel_id=1, source_target_pairs={{20,0},{16,4},{28,8},{24,12},{4,16},{0,20},{12,24},{8,28},{21,1},{... | collective-permute-start | bytes 196616 | tf_op jit(solution)/shard_map/ppermute | solution.py:490

commit v14 on v13

--- a/solution.py
+++ b/solution.py
@@ -385,32 +385,39 @@
     return lambda k: ref[k * vectors : (k + 1) * vectors]
 
 
+def traces(sums_ref, shape, first):
+    vectors = sums_ref.shape[2]
+    row, col = iota(shape, 0), iota(shape, 1)
+    result = jnp.zeros(shape, jnp.float32)
+    for k in range(sums_ref.shape[0]):
+        total = jnp.sum(jnp.sum(sums_ref[k], axis=0, keepdims=True), axis=1, keepdims=True)
+        here = (row == first + k // 2) & (col == k % 2)
+        result = jnp.where(here, total * (1.0 / vectors), result)
+    return result
+
+
 def first_contract_kernel(times, split, live_ref, weight_ref, tau_ref, *refs):
-    blocks, (live_out_ref, sums_ref, left_ref, right_ref) = refs[:times], refs[times:]
+    blocks, (live_out_ref, corr_ref, sums_ref, left_ref, right_ref) = refs[:times], refs[times:]
     live = jnp.where(live_ref[0] > 0, 1.0, 0.0)
     live_out_ref[...] = jnp.full(live_out_ref.shape, live, jnp.float32)
-    if split:
-        vectors = sums_ref.shape[2]
-        blocks = [part_of(ref, vectors) for ref in blocks]
-        contract(sums_ref, weight_ref, blocks, tau_ref, left_ref, right_ref)
-    else:
-        sums_ref[...] = jnp.zeros_like(sums_ref)
-
-
-def margins_kernel(kept_ref, other_ref, margin_ref):
-    half = kept_ref.shape[0]
-    me = lax.axis_index("gx") & 1
-    for place, ref in ((me, kept_ref), (1 - me, other_ref)):
-        rows = pl.ds(pl.multiple_of(place * half, half), half)
-        margin_ref[0, rows] = ref[...].astype(jnp.float32)
+    if not split:
+        corr_ref[...] = jnp.zeros_like(corr_ref)
+        return
+    blocks = [part_of(ref, sums_ref.shape[2]) for ref in blocks]
+    contract(sums_ref, weight_ref, blocks, tau_ref, left_ref, right_ref)
+    first = (lax.axis_index("gx") & 1) * (sums_ref.shape[0] // 2)
+    corr_ref[...] = traces(sums_ref, corr_ref.shape, first)
 
 
 def second_contract_kernel(times, split, weight_ref, tau_ref, *refs):
-    other, kept, refs = refs[:times], refs[times : 2 * times], refs[2 * times :]
-    live_ref, first_sums_ref, corr_ref, sums_ref, left_ref, right_ref = refs
+    other, kept, refs = refs[:times][::-1], refs[times : 2 * times], refs[2 * times :]
+    live_ref, first_corr_ref, margin_ref, corr_ref, sums_ref, left_ref, right_ref = refs
     vectors = sums_ref.shape[2]
     half = kept[0].shape[0]
     me = lax.axis_index("gx") & 1
+    for place, ref in ((me, kept[0]), (1 - me, other[0])):
+        rows = pl.ds(pl.multiple_of(place * half, half), half)
+        margin_ref[0, rows] = ref[...].astype(jnp.float32)
     parts_per_half = half // vectors
 
     def either(kept_ref, other_ref):
@@ -426,18 +433,9 @@
     if not split:
         blocks = [either(a, b) for a, b in zip(kept, other)]
     contract(sums_ref, weight_ref, blocks, tau_ref, left_ref, right_ref)
-    now_ops = sums_ref.shape[0] // 2
-    known = [(sums_ref, (1 - me) * now_ops)] if split else [(sums_ref, 0)]
-    if split:
-        known.append((first_sums_ref, me * now_ops))
     shape = corr_ref.shape[1:]
-    row, col = iota(shape, 0), iota(shape, 1)
-    result = jnp.zeros(shape, jnp.float32)
-    for ref, first in known:
-        for k in range(2 * now_ops):
-            total = jnp.sum(jnp.sum(ref[k], axis=0, keepdims=True), axis=1, keepdims=True)
-            here = (row == first + k // 2) & (col == k % 2)
-            result = jnp.where(here, total * (1.0 / vectors), result)
+    first = (1 - me) * (sums_ref.shape[0] // 2) if split else 0
+    result = traces(sums_ref, shape, first) + first_corr_ref[...]
     corr_ref[0] = result * live_ref[0 : shape[0], 0 : shape[1]]
 
 
@@ -591,29 +589,28 @@
         pltpu.VMEM((2 * now_ops * vectors, 2 * vectors), bf16),
         pltpu.VMEM((2 * vectors, 2 * now_ops * vectors), bf16),
     ]
-    live, sums = local_call(
+    live, first_corr = local_call(
         functools.partial(first_contract_kernel, times, split),
         "first_contraction",
-        (jax.ShapeDtypeStruct((8, vectors), f32), jax.ShapeDtypeStruct(sums_shape, f32)),
+        (
+            jax.ShapeDtypeStruct((8, vectors), f32),
+            jax.ShapeDtypeStruct((own_ops, 2), f32),
+        ),
         [smem_spec()] + [vmem_spec()] * (2 + times),
         (vmem_spec(),) * 2,
-        scratch,
+        [pltpu.VMEM(sums_shape, f32)] + scratch,
     )(slot_counts, weights, perams[0], *kept)
-    margins = local_call(
-        margins_kernel,
-        "margins_out",
-        jax.ShapeDtypeStruct((1, own_rows, vectors), f32),
-        [vmem_spec()] * 2,
-        vmem_spec(),
-    )(*lax.optimization_barrier((kept[0], other[0], sums))[:2])
-    correlators = local_call(
+    margins, correlators = local_call(
         functools.partial(second_contract_kernel, times, split),
         "second_contraction",
-        jax.ShapeDtypeStruct((1, own_ops, 2), f32),
+        (
+            jax.ShapeDtypeStruct((1, own_rows, vectors), f32),
+            jax.ShapeDtypeStruct((1, own_ops, 2), f32),
+        ),
         [vmem_spec()] * (4 + 2 * times),
-        vmem_spec(),
+        (vmem_spec(),) * 2,
         [pltpu.VMEM(sums_shape, f32)] + scratch,
-    )(weights, perams[0], *other, *kept, live, sums)
+    )(weights, perams[0], *other[::-1], *kept, live, first_corr)
     return (margins.reshape(1, own_ops, 2, vectors, vectors), correlators)
 
 

time: 34.1 us -> 34.1 us (level)
  waiting for transfers between devices: 9.71 us -> 10.4 us
  Pallas kernels: 6.88 us -> 6.26 us
    ppermute x5, starting transfers between devices: 6.69 us -> 8.66 us  [from_partner(): return lax.ppermute(block, axis, [(i ^ step, i) for i in range(count)])]
    ppermute x2, starting transfers between devices: 1.97 us -> 0.01 us  [from_diagonal(): return lax.ppermute(block, axes, perm)]
    ppermute x2, waiting for transfers between devices: 2.72 us -> 3.98 us  [from_diagonal(): return lax.ppermute(block, axes, perm)]
    pallas_call x1 -> x0, Pallas kernels: 0.73 us -> none  [per_device(): local_call(margins_kernel, 'margins_out', jax.ShapeDtypeStruct((1, own_ro...]
    ppermute x5, waiting for transfers between devices: 6.83 us -> 6.22 us  [from_partner(): return lax.ppermute(block, axis, [(i ^ step, i) for i in range(count)])]
  transfers between devices with their start and end apart: 10 -> 10, of which waited for: 8 -> 7; matrix products, arithmetic and copies ran while one was open for 0% -> 0% of each run, Pallas kernels for 11% -> 9%
where the time goes in v14:
time: 34.1 us; the launch traced here: 34 us
  starting transfers between devices  16 us (47%)
  waiting for transfers between devices  10.4 us (30%)
  Pallas kernels  6.26 us (18%)
  between operations  1.33 us (4%)
    ppermute x5, starting transfers between devices, from_partner(): return lax.ppermute(block, axis, [(i ^ step, i) for i in range(count)])  8.66 us
    ppermute x3, starting transfers between devices, from_step(): lax.ppermute(block, axis, [((i + step) % count, i) for i in range(count)])  7.33 us
    ppermute x5, waiting for transfers between devices, from_partner(): return lax.ppermute(block, axis, [(i ^ step, i) for i in range(count)])  6.22 us
    ppermute x2, waiting for transfers between devices, from_diagonal(): return lax.ppermute(block, axes, perm)  3.98 us
    pallas_call x1, Pallas kernels, per_device(): local_call(functools.partial(prepare_kernel, cells_x, cells_y), 'prepare_...  2.25 us
    pallas_call x1, Pallas kernels, per_device(): local_call(functools.partial(second_contract_kernel, times, split), 'seco...  1.55 us
    pallas_call x1, Pallas kernels, per_device(): local_call(functools.partial(margin_kernel, cells_x, cells_y, groups, own...  1.18 us
    pallas_call x1, Pallas kernels, per_device(): local_call(functools.partial(first_contract_kernel, times, split), 'first...  0.92 us
  transfers between devices with their start and end apart: 10, of which 7 were waited for; matrix products, arithmetic and copies ran while one was open for 0% of the time, Pallas kernels for 9%

profile of v14, /device:TPU:0, one launch (start us, length us, event | category | flops | bytes accessed | tf_op | source)
XLA Modules:
  0.0 34.0 jit_solution(12548311569324238625)
XLA Ops:
  0.6 5.1 %collective-permute-start = (bf16[1,2,144,128]{3,2,1,0:T(8,128)(2,1)}, bf16[1,2,144,128]{3,2,1,0:T(8,128)(2,1)S(1)}, u32[]{:S(2)}, u32[]{:S(2)}) collective-permute-start(bf16[1,2,144,128]{3,2,1,0:T(8,128)(2,1)} %bitcast.10), channel_id=1, source_target_pairs={{4,0},{8,4},{12,8},{0,12},{5,1},{9,5},{13,9},{1,13},{6,2},{10,6},{... | collective-permute-start | bytes 221192 | tf_op jit(solution)/shard_map/ppermute | solution.py:473
  5.7 0.7 %collective-permute-start.1 = (bf16[1,2,144,128]{3,2,1,0:T(8,128)(2,1)}, bf16[1,2,144,128]{3,2,1,0:T(8,128)(2,1)S(1)}, u32[]{:S(2)}, u32[]{:S(2)}) collective-permute-start(bf16[1,2,144,128]{3,2,1,0:T(8,128)(2,1)} %bitcast.11), channel_id=1, source_target_pairs={{1,0},{2,1},{3,2},{0,3},{5,4},{6,5},{7,6},{4,7},{9,8},{10,9},{11,1... | collective-permute-start | bytes 221192 | tf_op jit(solution)/shard_map/ppermute | solution.py:473
  6.4 2.3 %prepare_lines.1 = (bf16[3,144,128]{2,1,0:T(8,128)(2,1)S(1)}, f32[11,144,128]{2,1,0:T(8,128)S(1)}, bf16[2,128,288]{2,1,0:T(8,128)(2,1)S(1)}, f32[8,72,256]{2,1,0:T(8,128)S(1)}, f32[2,2,8,128]{3,2,1,0:T(8,128)S(1)}) custom-call(bf16[1,2,144,128]{3,2,1,0:T(8,128)(2,1)} %bitcast.12, bf16[2,27,2,24]{3,2,1,0:T(2,128)(2,1)} %bitcast.13, s32[8]{0:T(128)} %refs_6_.1, ...), custom_call_target="tpu_custom_call" | custom-call | tf_op jit(solution)/shard_map/prepare_lines/pallas_call | solution.py:512
  8.7 0.0 collective-permute-done.refs_4_
  8.7 0.0 collective-permute-done.1.refs_5_
  8.7 1.2 %partial_margins.1 = (s16[2,528,128]{2,1,0:T(8,128)(2,1)S(1)}, f32[2,512,128]{2,1,0:T(8,128)S(1)}) custom-call(bf16[3,144,128]{2,1,0:T(8,128)(2,1)S(1)} %get-tuple-element.17.refs_0_, f32[11,144,128]{2,1,0:T(8,128)S(1)} %get-tuple-element.18.refs_1_, bf16[2,128,288]{2,1,0:T(8,128)(2,1)S(1)} %get-tuple-element.19.refs_2_, ...), custom_call_target="tpu_custom_call" | custom-call | tf_op jit(solution)/shard_map/partial_margins/pallas_call | solution.py:531
  9.9 0.0 copy-start
  9.9 1.0 %collective-permute-start.2 = (s16[2,528,128]{2,1,0:T(8,128)(2,1)S(1)}, s16[2,528,128]{2,1,0:T(8,128)(2,1)S(1)}, u32[]{:S(2)}, u32[]{:S(2)}) collective-permute-start(s16[2,528,128]{2,1,0:T(8,128)(2,1)S(1)} %get-tuple-element.22), channel_id=1, source_target_pairs={{1,0},{0,1},{3,2},{2,3},{5,4},{4,5},{7,6},{6,7},{9,8},{8,9},{11,10... | collective-permute-start | bytes 811016 | tf_op jit(solution)/shard_map/ppermute | solution.py:478
  10.9 1.2 %collective-permute-done.2.refs_0_ = s16[2,528,128]{2,1,0:T(8,128)(2,1)S(1)} collective-permute-done((s16[2,528,128]{2,1,0:T(8,128)(2,1)S(1)}, s16[2,528,128]{2,1,0:T(8,128)(2,1)S(1)}, u32[]{:S(2)}, u32[]{:S(2)}) %collective-permute-start.2) | collective-permute-done | bytes 270368 | tf_op jit(solution)/shard_map/ppermute | solution.py:478
  12.1 0.2 spread_halves.1
  12.3 1.2 %collective-permute-start.3 = (s16[272,128]{1,0:T(8,128)(2,1)S(1)}, s16[272,128]{1,0:T(8,128)(2,1)S(1)}, u32[]{:S(2)}, u32[]{:S(2)}) collective-permute-start(s16[272,128]{1,0:T(8,128)(2,1)S(1)} %get-tuple-element.23), channel_id=1, source_target_pairs={{2,0},{3,1},{0,2},{1,3},{6,4},{7,5},{4,6},{5,7},{10,8},{11,9},{8,1... | collective-permute-start | bytes 208904 | tf_op jit(solution)/shard_map/ppermute | solution.py:478
  13.5 0.0 collective-permute-start.4
  13.5 2.3 %collective-permute-start.5 = (s16[272,128]{1,0:T(8,128)(2,1)S(1)}, s16[272,128]{1,0:T(8,128)(2,1)S(1)}, u32[]{:S(2)}, u32[]{:S(2)}) collective-permute-start(s16[272,128]{1,0:T(8,128)(2,1)S(1)} %get-tuple-element.25), channel_id=1, source_target_pairs={{4,0},{0,4},{12,8},{8,12},{5,1},{1,5},{13,9},{9,13},{6,2},{2,6},{1... | collective-permute-start | bytes 208904 | tf_op jit(solution)/shard_map/ppermute | solution.py:478
  15.8 1.0 %collective-permute-done.3.refs_1_ = s16[272,128]{1,0:T(8,128)(2,1)S(1)} collective-permute-done((s16[272,128]{1,0:T(8,128)(2,1)S(1)}, s16[272,128]{1,0:T(8,128)(2,1)S(1)}, u32[]{:S(2)}, u32[]{:S(2)}) %collective-permute-start.3) | collective-permute-done | bytes 69664 | tf_op jit(solution)/shard_map/ppermute | solution.py:478
  16.8 2.5 %collective-permute-done.4.refs_2_ = s16[272,128]{1,0:T(8,128)(2,1)S(1)} collective-permute-done((s16[272,128]{1,0:T(8,128)(2,1)S(1)}, s16[272,128]{1,0:T(8,128)(2,1)S(1)}, u32[]{:S(2)}, u32[]{:S(2)}) %collective-permute-start.4) | collective-permute-done | bytes 69664 | tf_op jit(solution)/shard_map/ppermute | solution.py:488
  19.3 0.2 collective-permute-done.5.refs_3_
  19.5 0.1 keep_half.1.own_ref
  19.6 2.1 %collective-permute-start.6 = (s16[272,128]{1,0:T(8,128)(2,1)S(1)}, s16[272,128]{1,0:T(8,128)(2,1)S(1)}, u32[]{:S(2)}, u32[]{:S(2)}) collective-permute-start(s16[272,128]{1,0:T(8,128)(2,1)S(1)} %keep_half.1.own_ref), channel_id=1, source_target_pairs={{8,0},{12,4},{0,8},{4,12},{9,1},{13,5},{1,9},{5,13},{10,2},{14,6},... | collective-permute-start | bytes 208904 | tf_op jit(solution)/shard_map/ppermute | solution.py:478
  21.7 3.9 %collective-permute-done.6.arrived_ref = s16[272,128]{1,0:T(8,128)(2,1)S(1)} collective-permute-done((s16[272,128]{1,0:T(8,128)(2,1)S(1)}, s16[272,128]{1,0:T(8,128)(2,1)S(1)}, u32[]{:S(2)}, u32[]{:S(2)}) %collective-permute-start.6) | collective-permute-done | bytes 69664 | tf_op jit(solution)/shard_map/ppermute | solution.py:478
  25.7 1.6 %collective-permute-start.9 = (bf16[256,128]{1,0:T(8,128)(2,1)S(1)}, bf16[256,128]{1,0:T(8,128)(2,1)S(1)}, u32[]{:S(2)}, u32[]{:S(2)}) collective-permute-start(bf16[256,128]{1,0:T(8,128)(2,1)S(1)} %finish_half.1.refs_0_.refs_2_), channel_id=1, source_target_pairs={{16,0},{0,16},{17,1},{1,17},{18,2},{2,18},{19,3},{3,19},{20,4},{4,... | collective-permute-start | bytes 196616 | tf_op jit(solution)/shard_map/ppermute | solution.py:473
  27.2 0.0 collective-permute-start.7
  27.2 2.0 %collective-permute-start.8 = (bf16[256,128]{1,0:T(8,128)(2,1)S(1)}, bf16[256,128]{1,0:T(8,128)(2,1)S(1)}, u32[]{:S(2)}, u32[]{:S(2)}) collective-permute-start(bf16[256,128]{1,0:T(8,128)(2,1)S(1)} %finish_half.1.refs_0_.refs_2_), channel_id=1, source_target_pairs={{4,0},{0,4},{12,8},{8,12},{5,1},{1,5},{13,9},{9,13},{6,2},{2,6},{1... | collective-permute-start | bytes 196616 | tf_op jit(solution)/shard_map/ppermute | solution.py:478
  29.9 0.1 collective-permute-done.9.refs_1_.refs_3_
  30.0 0.0 copy-done
  30.0 0.9 %first_contraction.1 = (f32[8,128]{1,0:T(8,128)S(1)}, f32[2,2]{1,0:T(2,128)S(1)}) custom-call(s32[1]{0:T(128)S(6)} %copy.10.live_ref, f32[2,2,8,128]{3,2,1,0:T(8,128)S(1)} %get-tuple-element.16.weight_ref, bf16[2,512,512]{2,1,0:T(8,128)(2,1)S(1)} %bitcast.8, bf16[256,128]{1,0:T(8,128)(2,1)S(1)} %finish_half.1.refs_0_.refs_2_, ...), custom_call_target="tpu_custom_call" | custom-call | tf_op jit(solution)/shard_map/first_contraction/pallas_call | solution.py:592
  30.9 1.5 %collective-permute-done.7.refs_0_ = bf16[256,128]{1,0:T(8,128)(2,1)S(1)} collective-permute-done((bf16[256,128]{1,0:T(8,128)(2,1)S(1)}, bf16[256,128]{1,0:T(8,128)(2,1)S(1)}, u32[]{:S(2)}, u32[]{:S(2)}) %collective-permute-start.7) | collective-permute-done | bytes 65568 | tf_op jit(solution)/shard_map/ppermute | solution.py:488
  32.4 0.0 collective-permute-done.8.refs_1_
  32.4 1.6 %second_contraction.1 = (f32[1,512,128]{2,1,0:T(8,128)}, f32[1,2,2]{2,1,0:T(2,128)}) custom-call(f32[2,2,8,128]{3,2,1,0:T(8,128)S(1)} %get-tuple-element.16.weight_ref, bf16[2,512,512]{2,1,0:T(8,128)(2,1)S(1)} %bitcast.9, bf16[256,128]{1,0:T(8,128)(2,1)S(1)} %collective-permute-done.7.refs_0_, bf16[256,128]{1,0:T(8,128)(2,1)S(1)} %collective-permute-done.8.refs_1_, ...), custom_call_target="tpu_custom_call" | custom-call | tf_op jit(solution)/shard_map/second_contraction/pallas_call | solution.py:603
  (1 shorter events, 0.0 us)
Async XLA Ops:
  0.6 8.0 %collective-permute-start = (bf16[1,2,144,128]{3,2,1,0:T(8,128)(2,1)}, bf16[1,2,144,128]{3,2,1,0:T(8,128)(2,1)S(1)}, u32[]{:S(2)}, u32[]{:S(2)}) collective-permute-start(bf16[1,2,144,128]{3,2,1,0:T(8,128)(2,1)} %bitcast.10), channel_id=1, source_target_pairs={{4,0},{8,4},{12,8},{0,12},{5,1},{9,5},{13,9},{1,13},{6,2},{10,6},{... | collective-permute-start | bytes 221192 | tf_op jit(solution)/shard_map/ppermute | solution.py:473
  5.7 3.0 %collective-permute-start.1 = (bf16[1,2,144,128]{3,2,1,0:T(8,128)(2,1)}, bf16[1,2,144,128]{3,2,1,0:T(8,128)(2,1)S(1)}, u32[]{:S(2)}, u32[]{:S(2)}) collective-permute-start(bf16[1,2,144,128]{3,2,1,0:T(8,128)(2,1)} %bitcast.11), channel_id=1, source_target_pairs={{1,0},{2,1},{3,2},{0,3},{5,4},{6,5},{7,6},{4,7},{9,8},{10,9},{11,1... | collective-permute-start | bytes 221192 | tf_op jit(solution)/shard_map/ppermute | solution.py:473
  9.9 20.1 %copy-start = (bf16[1,2,512,512]{3,2,1,0:T(8,128)(2,1)S(1)}, bf16[1,2,512,512]{3,2,1,0:T(8,128)(2,1)}, u32[]{:S(2)}) copy-start(bf16[1,2,512,512]{3,2,1,0:T(8,128)(2,1)} %param.12) | copy-start | bytes 3145732
  9.9 2.2 %collective-permute-start.2 = (s16[2,528,128]{2,1,0:T(8,128)(2,1)S(1)}, s16[2,528,128]{2,1,0:T(8,128)(2,1)S(1)}, u32[]{:S(2)}, u32[]{:S(2)}) collective-permute-start(s16[2,528,128]{2,1,0:T(8,128)(2,1)S(1)} %get-tuple-element.22), channel_id=1, source_target_pairs={{1,0},{0,1},{3,2},{2,3},{5,4},{4,5},{7,6},{6,7},{9,8},{8,9},{11,10... | collective-permute-start | bytes 811016 | tf_op jit(solution)/shard_map/ppermute | solution.py:478
  12.3 4.5 %collective-permute-start.3 = (s16[272,128]{1,0:T(8,128)(2,1)S(1)}, s16[272,128]{1,0:T(8,128)(2,1)S(1)}, u32[]{:S(2)}, u32[]{:S(2)}) collective-permute-start(s16[272,128]{1,0:T(8,128)(2,1)S(1)} %get-tuple-element.23), channel_id=1, source_target_pairs={{2,0},{3,1},{0,2},{1,3},{6,4},{7,5},{4,6},{5,7},{10,8},{11,9},{8,1... | collective-permute-start | bytes 208904 | tf_op jit(solution)/shard_map/ppermute | solution.py:478
  13.5 5.8 %collective-permute-start.4 = (s16[272,128]{1,0:T(8,128)(2,1)S(1)}, s16[272,128]{1,0:T(8,128)(2,1)S(1)}, u32[]{:S(2)}, u32[]{:S(2)}) collective-permute-start(s16[272,128]{1,0:T(8,128)(2,1)S(1)} %get-tuple-element.24), channel_id=1, source_target_pairs={{6,0},{7,1},{4,2},{5,3},{2,4},{3,5},{0,6},{1,7},{14,8},{15,9},{12,... | collective-permute-start | bytes 208904 | tf_op jit(solution)/shard_map/ppermute | solution.py:488
  13.5 6.0 %collective-permute-start.5 = (s16[272,128]{1,0:T(8,128)(2,1)S(1)}, s16[272,128]{1,0:T(8,128)(2,1)S(1)}, u32[]{:S(2)}, u32[]{:S(2)}) collective-permute-start(s16[272,128]{1,0:T(8,128)(2,1)S(1)} %get-tuple-element.25), channel_id=1, source_target_pairs={{4,0},{0,4},{12,8},{8,12},{5,1},{1,5},{13,9},{9,13},{6,2},{2,6},{1... | collective-permute-start | bytes 208904 | tf_op jit(solution)/shard_map/ppermute | solution.py:478
  19.6 6.0 %collective-permute-start.6 = (s16[272,128]{1,0:T(8,128)(2,1)S(1)}, s16[272,128]{1,0:T(8,128)(2,1)S(1)}, u32[]{:S(2)}, u32[]{:S(2)}) collective-permute-start(s16[272,128]{1,0:T(8,128)(2,1)S(1)} %keep_half.1.own_ref), channel_id=1, source_target_pairs={{8,0},{12,4},{0,8},{4,12},{9,1},{13,5},{1,9},{5,13},{10,2},{14,6},... | collective-permute-start | bytes 208904 | tf_op jit(solution)/shard_map/ppermute | solution.py:478
  25.7 4.3 %collective-permute-start.9 = (bf16[256,128]{1,0:T(8,128)(2,1)S(1)}, bf16[256,128]{1,0:T(8,128)(2,1)S(1)}, u32[]{:S(2)}, u32[]{:S(2)}) collective-permute-start(bf16[256,128]{1,0:T(8,128)(2,1)S(1)} %finish_half.1.refs_0_.refs_2_), channel_id=1, source_target_pairs={{16,0},{0,16},{17,1},{1,17},{18,2},{2,18},{19,3},{3,19},{20,4},{4,... | collective-permute-start | bytes 196616 | tf_op jit(solution)/shard_map/ppermute | solution.py:473
  27.2 5.2 %collective-permute-start.7 = (bf16[256,128]{1,0:T(8,128)(2,1)S(1)}, bf16[256,128]{1,0:T(8,128)(2,1)S(1)}, u32[]{:S(2)}, u32[]{:S(2)}) collective-permute-start(bf16[256,128]{1,0:T(8,128)(2,1)S(1)} %finish_half.1.refs_0_.refs_2_), channel_id=1, source_target_pairs={{20,0},{16,4},{28,8},{24,12},{4,16},{0,20},{12,24},{8,28},{21,1},{... | collective-permute-start | bytes 196616 | tf_op jit(solution)/shard_map/ppermute | solution.py:488
  27.2 5.2 %collective-permute-start.8 = (bf16[256,128]{1,0:T(8,128)(2,1)S(1)}, bf16[256,128]{1,0:T(8,128)(2,1)S(1)}, u32[]{:S(2)}, u32[]{:S(2)}) collective-permute-start(bf16[256,128]{1,0:T(8,128)(2,1)S(1)} %finish_half.1.refs_0_.refs_2_), channel_id=1, source_target_pairs={{4,0},{0,4},{12,8},{8,12},{5,1},{1,5},{13,9},{9,13},{6,2},{2,6},{1... | collective-permute-start | bytes 196616 | tf_op jit(solution)/shard_map/ppermute | solution.py:478

commit v15 on v13

--- a/solution.py
+++ b/solution.py
@@ -70,16 +70,58 @@
     )
 
 
-def halo_fields(cells_x, cells_y):
-    pairs = [(0, (cells_x - 1) * cells_y + y) for y in range(cells_y)]
-    return pairs + [(1, x * cells_y + cells_y - 1) for x in range(cells_x)]
+def leaves(cells_x, cells_y, code, line):
+    if code in (0, 3):
+        return line // cells_y == 0
+    return code == 1 and line % cells_y == cells_y - 1
 
 
 def local_fields(cells_x, cells_y):
-    lines = cells_x * cells_y
-    outside = halo_fields(cells_x, cells_y)
-    every = [(code, line) for code in range(7) for line in range(lines)]
-    return [pair for pair in every if pair not in outside]
+    every = [(code, line) for code in range(7) for line in range(cells_x * cells_y)]
+    return [pair for pair in every if not leaves(cells_x, cells_y, *pair)]
+
+
+class LinkForms:
+    def __init__(self, half):
+        cells_z = half // 3
+        self.half = half
+        self.spread = one_hot(third(iota((half, cells_z), 0)) == iota((half, cells_z), 1))
+        row, col = iota((half, LINK_COLS), 0), iota((half, LINK_COLS), 1)
+        row_color = row - 3 * third(row)
+        pair_at = third(col >> 1)
+        col_in, col_out = (col >> 1) - 3 * pair_at, pair_at - 3 * third(pair_at)
+        self.pick = [(row_color == c).astype(jnp.float32) for c in (col_out, col_in)]
+        row, col = iota((LINK_COLS, 6 * 128), 0), iota((LINK_COLS, 6 * 128), 1)
+        block, place = col >> 7, col & 127
+        color = place - 3 * third(place)
+        pair_at = third(row >> 1)
+        row_in, row_out = (row >> 1) - 3 * pair_at, pair_at - 3 * third(pair_at)
+        fits = 2 * third(pair_at) + (row & 1) == block
+        self.expand = [one_hot(fits & (c == color)) for c in (row_in, row_out)]
+        row, col = iota((half, 128), 0), iota((half, 128), 1)
+        self.near = ((third(row) == third(col)) & (col < half)).astype(jnp.float32)
+
+    def seen(self, link_ref, rows_ref):
+        for k in range(LINK_COLS // 2):
+            rows_ref[2 * k : 2 * k + 2] = link_ref[k].astype(jnp.float32)
+        return lax.dot_general(
+            self.spread,
+            rows_ref[...].astype(jnp.bfloat16),
+            (((1,), (1,)), ((), ())),
+            preferred_element_type=jnp.float32,
+        )
+
+    def matrices(self, seen, way, directions):
+        blocks = jnp.dot(
+            (seen * self.pick[way]).astype(jnp.bfloat16),
+            self.expand[way][:, : 256 * directions],
+            preferred_element_type=jnp.float32,
+        )
+        cut = lambda k: blocks[:, 128 * k : 128 * k + 128] * self.near
+        return [
+            jnp.concatenate([cut(2 * d), cut(2 * d + 1)], axis=0).astype(jnp.bfloat16)
+            for d in range(directions)
+        ]
 
 
 def prepare_kernel(cells_x, cells_y, *refs):
@@ -95,25 +137,10 @@
     v_ref, link_ref, dirs_ref, moms_ref, waves_ref, pair_ref = held
     f32, bf16 = jnp.float32, jnp.bfloat16
     order, vectors = v_ref.shape[2], v_ref.shape[3]
-    half, cells_z = order // 2, order // 6
+    half = order // 2
     lines = cells_x * cells_y
     times = weight_ref.shape[1]
-    spread = one_hot(third(iota((half, cells_z), 0)) == iota((half, cells_z), 1))
-    row, col = iota((half, LINK_COLS), 0), iota((half, LINK_COLS), 1)
-    row_color = row - 3 * third(row)
-    pair_at = third(col >> 1)
-    col_in, col_out = (col >> 1) - 3 * pair_at, pair_at - 3 * third(pair_at)
-    pick = [(row_color == col_out).astype(f32), (row_color == col_in).astype(f32)]
-    wide = (LINK_COLS, 6 * 128)
-    row, col = iota(wide, 0), iota(wide, 1)
-    block, place = col >> 7, col & 127
-    color = place - 3 * third(place)
-    pair_at = third(row >> 1)
-    row_in, row_out = (row >> 1) - 3 * pair_at, pair_at - 3 * third(pair_at)
-    fits = 2 * third(pair_at) + (row & 1) == block
-    expand = [one_hot(fits & (row_in == color)), one_hot(fits & (row_out == color))]
-    row, col = iota((half, 128), 0), iota((half, 128), 1)
-    near = ((third(row) == third(col)) & (col < half)).astype(f32)
+    forms = LinkForms(half)
     planar = planar_order(order)
     for copy in copies:
         copy.wait()
@@ -122,10 +149,6 @@
         source = pair_ref[0, 1] == t
         weight_ref[0, t] = jnp.full(weight_ref.shape[2:], jnp.where(sink, 1.0, 0.0), f32)
         weight_ref[1, t] = jnp.full(weight_ref.shape[2:], jnp.where(source, 1.0, 0.0), f32)
-    for line in range(lines):
-        for k in range(LINK_COLS // 2):
-            link_rows_ref[line, 2 * k : 2 * k + 2] = link_ref[line, k].astype(f32)
-    outside = halo_fields(cells_x, cells_y)
     inside = local_fields(cells_x, cells_y)
     ordered = []
     for line in range(lines):
@@ -142,35 +165,24 @@
         columns = slice(line * order, (line + 1) * order)
         left_ref[0, :, columns] = here.T.astype(bf16)
         left_ref[1, :, columns] = ahead_z.T.astype(bf16)
-        seen = lax.dot_general(
-            spread,
-            link_rows_ref[line].astype(bf16),
-            (((1,), (1,)), ((), ())),
-            preferred_element_type=f32,
-        )
+        seen = forms.seen(link_ref.at[line], link_rows_ref.at[line])
         pair = side_by_side(here)
-        for way in range(2):
-            blocks = jnp.dot(
-                (seen * pick[way]).astype(bf16), expand[way], preferred_element_type=f32
+        on_x = line + cells_y if line + cells_y < lines else None
+        for d, matrix in enumerate(forms.matrices(seen, 0, 3)):
+            if d == 0 and on_x is None:
+                continue
+            if d == 1 and leaves(cells_x, cells_y, 1, line):
+                matrix_ref[line // cells_y] = matrix
+                continue
+            ahead = (ordered[on_x] if d == 0 else ordered[line + 1]) if d < 2 else ahead_z
+            local_ref[inside.index((d, on_x if d == 0 else line))] = transport(
+                matrix[:, :half], side_by_side(ahead), 1
             )
-            for d in range(3):
-                matrix = jnp.concatenate(
-                    [
-                        blocks[:, 256 * d : 256 * d + 128] * near,
-                        blocks[:, 256 * d + 128 : 256 * d + 256] * near,
-                    ],
-                    axis=0,
-                ).astype(bf16)
-                if way == 1:
-                    carried = transport(matrix[:, :half], pair, -1)
-                    local_ref[inside.index((3 + d, line))] = carried.astype(bf16).astype(f32)
-                elif (d, line) in outside:
-                    matrix_ref[outside.index((d, line))] = matrix
-                else:
-                    ahead = ahead_z if d == 2 else ordered[line + (cells_y if d == 0 else 1)]
-                    local_ref[inside.index((d, line))] = transport(
-                        matrix[:, :half], side_by_side(ahead), 1
-                    )
+        for d, matrix in enumerate(forms.matrices(seen, 1, 3)):
+            if d == 0 and on_x is None:
+                continue
+            carried = transport(matrix[:, :half], pair, -1).astype(bf16).astype(f32)
+            local_ref[inside.index((3 + d, on_x if d == 0 else line))] = carried
     wave_cols = waves_ref.shape[1]
     per_term = wave_cols // 3
     row, col = iota((wave_cols, 2 * vectors), 0), iota((wave_cols, 2 * vectors), 1)
@@ -184,9 +196,10 @@
 
 
 def margin_kernel(cells_x, cells_y, groups, own_ops, *refs):
-    matrix_ref, local_ref, left_ref, phase_ref, halo_x_ref, halo_y_ref, dirs_hbm = refs[:7]
-    swap_ref, hold_ref = refs[7:9]
-    field_ref, side_ref, dirs_ref, sem = refs[9:]
+    matrix_ref, local_ref, left_ref, phase_ref = refs[:4]
+    links_x_ref, halo_x_ref, halo_y_ref, dirs_hbm = refs[4:8]
+    swap_ref, hold_ref = refs[8:10]
+    field_ref, side_ref, rows_ref, dirs_ref, sem = refs[10:]
     f32, bf16 = jnp.float32, jnp.bfloat16
     copy = pltpu.make_async_copy(dirs_hbm, dirs_ref, sem)
     copy.start()
@@ -194,23 +207,32 @@
     order, vectors = halo_x_ref.shape[2], halo_x_ref.shape[3]
     half = order // 2
     planar = planar_order(order)
+    forms = LinkForms(half)
+    inside = local_fields(cells_x, cells_y)
     side_ref[0] = left_ref[0]
     side_ref[3] = left_ref[1]
-    outside = halo_fields(cells_x, cells_y)
-    for d in range(2):
-        for line in range(lines):
-            x, y = line // cells_y, line % cells_y
-            columns = slice(line * order, (line + 1) * order)
-            if (d, line) not in outside:
-                ahead = line + (cells_y if d == 0 else 1)
-                side_ref[1 + d, :, columns] = left_ref[0, :, ahead * order : (ahead + 1) * order]
-                continue
-            halo = halo_x_ref[0, y] if d == 0 else halo_y_ref[x, 0]
-            ahead = jnp.dot(planar, halo, preferred_element_type=f32)
-            side_ref[1 + d, :, columns] = ahead.T.astype(bf16)
-            matrix = matrix_ref[outside.index((d, line))]
-            field_ref[d, line] = transport(matrix[:, :half], side_by_side(ahead), 1)
-    for k, (code, line) in enumerate(local_fields(cells_x, cells_y)):
+    for line in range(lines):
+        x, y = line // cells_y, line % cells_y
+        columns = slice(line * order, (line + 1) * order)
+        if x:
+            back = line - cells_y
+            side_ref[1, :, columns] = left_ref[0, :, back * order : (back + 1) * order]
+        else:
+            seen = forms.seen(links_x_ref.at[y], rows_ref.at[y])
+            here = side_by_side(local_ref[inside.index((6, line))])
+            field_ref[0, line] = transport(forms.matrices(seen, 0, 1)[0][:, :half], here, 1)
+            back = jnp.dot(planar, halo_x_ref[0, y], preferred_element_type=f32)
+            side_ref[1, :, columns] = back.T.astype(bf16)
+            adjoint = forms.matrices(seen, 1, 1)[0][:, :half]
+            carried = transport(adjoint, side_by_side(back), -1)
+            field_ref[3, line] = carried.astype(bf16).astype(f32)
+        if y + 1 < cells_y:
+            side_ref[2, :, columns] = left_ref[0, :, (line + 1) * order : (line + 2) * order]
+        else:
+            ahead = jnp.dot(planar, halo_y_ref[x, 0], preferred_element_type=f32)
+            side_ref[2, :, columns] = ahead.T.astype(bf16)
+            field_ref[1, line] = transport(matrix_ref[x, :, :half], side_by_side(ahead), 1)
+    for k, (code, line) in enumerate(inside):
         field_ref[code, line] = local_ref[k]
     copy.wait()
     me = lax.axis_index("gy")
@@ -219,7 +241,7 @@
         for i in range(own_ops):
             o = (me ^ j) * own_ops + i
             code = dirs_ref[o]
-            side = jnp.where((code >= 3) & (code < 6), code - 2, 0)
+            side = jnp.where(code == 0, 1, jnp.where((code == 4) | (code == 5), code - 2, 0))
             cosine = phase_ref[o, :, 0:vectors]
             sine = phase_ref[o, :, vectors : 2 * vectors]
             pairs = []
@@ -362,13 +384,16 @@
             jnp.concatenate([tau_ref[0, rows], tau_ref[1, rows]], axis=0),
             preferred_element_type=f32,
         )
-        for c in range(spins):
-            cols = slice(c * vectors, (c + 1) * vectors)
-            y = jnp.dot(
-                jnp.concatenate([tau_ref[0, rows, cols], tau_ref[1, rows, cols]], axis=1),
-                right_ref[...],
-                preferred_element_type=f32,
-            )
+        columns = [slice(c * vectors, (c + 1) * vectors) for c in range(spins)]
+        side = [
+            jnp.concatenate([tau_ref[0, rows, cols], tau_ref[1, rows, cols]], axis=1)
+            for cols in columns
+        ]
+        whole_y = jnp.dot(
+            jnp.concatenate(side, axis=0), right_ref[...], preferred_element_type=f32
+        )
+        for c, cols in enumerate(columns):
+            y = whole_y[c * vectors : (c + 1) * vectors]
             for o in range(count_ops):
                 first = 2 * o * vectors
                 x_r = x[first : first + vectors, cols]
@@ -501,10 +526,11 @@
     own_ops = count_ops // groups
     own_rows = own_ops * 2 * vectors
     field = eigvecs.reshape(cells_x, cells_y, order, vectors)
-    halo_x = from_step(field[0:1], "gx", 1)
+    link_field = links[0].transpose(0, 1, 3, 5, 6, 4, 2).reshape(lines, 27, 2, cells_z)
+    links_x = from_step(link_field[lines - cells_y :], "gx", -1)
+    halo_x = from_step(field[cells_x - 1 :], "gx", -1)
     halo_y = from_step(field, "gy", 1)
-    link_field = links[0].transpose(0, 1, 3, 5, 6, 4, 2).reshape(lines, 27, 2, cells_z)
-    outside, inside = halo_fields(cells_x, cells_y), local_fields(cells_x, cells_y)
+    inside = local_fields(cells_x, cells_y)
     inputs = [field, link_field, op_dirs, op_moms, wave_constants(cells_z), pair_times]
     inputs = [in_hbm(x) for x in inputs]
     held = [
@@ -515,7 +541,7 @@
         functools.partial(prepare_kernel, cells_x, cells_y),
         "prepare_lines",
         (
-            jax.ShapeDtypeStruct((len(outside), order, 128), bf16),
+            jax.ShapeDtypeStruct((cells_x, order, 128), bf16),
             jax.ShapeDtypeStruct((len(inside), order, vectors), f32),
             jax.ShapeDtypeStruct((2, vectors, lines * order), bf16),
             jax.ShapeDtypeStruct((count_ops, order // 2, 2 * vectors), f32),
@@ -537,15 +563,16 @@
             message(own_rows, groups // 2),
             jax.ShapeDtypeStruct((groups // 2, own_rows, vectors), f32),
         ),
-        [vmem_spec()] * 6 + [hbm_spec()],
+        [vmem_spec()] * 7 + [hbm_spec()],
         (vmem_spec(),) * 2,
         [
             pltpu.VMEM((7, lines, order, vectors), f32),
             pltpu.VMEM((4, vectors, lines * order), bf16),
+            pltpu.VMEM((cells_y, LINK_COLS, cells_z), f32),
             pltpu.SMEM((count_ops,), jnp.int32),
             pltpu.SemaphoreType.DMA,
         ],
-    )(matrices, local, left, phases, halo_x, halo_y, in_hbm(op_dirs))
+    )(matrices, local, left, phases, links_x, halo_x, halo_y, in_hbm(op_dirs))
 
     def in_vmem(body, name, outs, *inputs):
         outs = outs if isinstance(outs, tuple) else (outs,)

time: 34.1 us -> 35.4 us (1.038)
  waiting for transfers between devices: 9.71 us -> 13.5 us
  starting transfers between devices: 16 us -> 13.4 us
    ppermute x5, waiting for transfers between devices: 6.83 us -> 9.35 us  [from_partner(): return lax.ppermute(block, axis, [(i ^ step, i) for i in range(count)])]
    ppermute x5, starting transfers between devices: 6.69 us -> 4.34 us  [from_partner(): return lax.ppermute(block, axis, [(i ^ step, i) for i in range(count)])]
    ppermute x3 -> x4, waiting for transfers between devices: 0.16 us -> 2.38 us  [from_step(): lax.ppermute(block, axis, [((i + step) % count, i) for i in range(count)])]
    ppermute x2, waiting for transfers between devices: 2.72 us -> 1.8 us  [from_diagonal(): return lax.ppermute(block, axes, perm)]
    ppermute x3 -> x4, starting transfers between devices: 7.33 us -> 6.89 us  [from_step(): lax.ppermute(block, axis, [((i + step) % count, i) for i in range(count)])]
  transfers between devices with their start and end apart: 10 -> 11, of which waited for: 8 -> 9; matrix products, arithmetic and copies ran while one was open for 0% -> 0% of each run, Pallas kernels for 11% -> 10%
where the time goes in v15:
time: 35.4 us; the launch traced here: 35.2 us
  waiting for transfers between devices  13.5 us (38%)
  starting transfers between devices  13.4 us (38%)
  Pallas kernels  6.99 us (20%)
  between operations  1.34 us (4%)
    ppermute x5, waiting for transfers between devices, from_partner(): return lax.ppermute(block, axis, [(i ^ step, i) for i in range(count)])  9.35 us
    ppermute x4, starting transfers between devices, from_step(): lax.ppermute(block, axis, [((i + step) % count, i) for i in range(count)])  6.89 us
    ppermute x5, starting transfers between devices, from_partner(): return lax.ppermute(block, axis, [(i ^ step, i) for i in range(count)])  4.34 us
    ppermute x4, waiting for transfers between devices, from_step(): lax.ppermute(block, axis, [((i + step) % count, i) for i in range(count)])  2.38 us
    ppermute x2, starting transfers between devices, from_diagonal(): return lax.ppermute(block, axes, perm)  2.14 us
    pallas_call x1, Pallas kernels, per_device(): local_call(functools.partial(prepare_kernel, cells_x, cells_y), 'prepare_...  2.03 us
    ppermute x2, waiting for transfers between devices, from_diagonal(): return lax.ppermute(block, axes, perm)  1.8 us
    pallas_call x1, Pallas kernels, per_device(): local_call(functools.partial(margin_kernel, cells_x, cells_y, groups, own...  1.51 us
  transfers between devices with their start and end apart: 11, of which 9 were waited for; matrix products, arithmetic and copies ran while one was open for 0% of the time, Pallas kernels for 10%

profile of v15, /device:TPU:0, one launch (start us, length us, event | category | flops | bytes accessed | tf_op | source)
XLA Modules:
  0.0 35.2 jit_solution(8452116925128399887)
XLA Ops:
  0.6 3.1 %collective-permute-start.1 = (bf16[1,2,144,128]{3,2,1,0:T(8,128)(2,1)}, bf16[1,2,144,128]{3,2,1,0:T(8,128)(2,1)S(1)}, u32[]{:S(2)}, u32[]{:S(2)}) collective-permute-start(bf16[1,2,144,128]{3,2,1,0:T(8,128)(2,1)} %bitcast.11), channel_id=1, source_target_pairs={{12,0},{0,4},{4,8},{8,12},{13,1},{1,5},{5,9},{9,13},{14,2},{2,6},{... | collective-permute-start | bytes 221192 | tf_op jit(solution)/shard_map/ppermute | solution.py:500
  3.7 0.7 %collective-permute-start.2 = (bf16[1,2,144,128]{3,2,1,0:T(8,128)(2,1)}, bf16[1,2,144,128]{3,2,1,0:T(8,128)(2,1)S(1)}, u32[]{:S(2)}, u32[]{:S(2)}) collective-permute-start(bf16[1,2,144,128]{3,2,1,0:T(8,128)(2,1)} %bitcast.12), channel_id=1, source_target_pairs={{1,0},{2,1},{3,2},{0,3},{5,4},{6,5},{7,6},{4,7},{9,8},{10,9},{11,1... | collective-permute-start | bytes 221192 | tf_op jit(solution)/shard_map/ppermute | solution.py:500
  4.4 1.6 %collective-permute-start = (bf16[2,27,2,24]{3,2,1,0:T(2,128)(2,1)}, bf16[2,27,2,24]{3,2,1,0:T(2,128)(2,1)S(1)}, u32[]{:S(2)}, u32[]{:S(2)}) collective-permute-start(bf16[2,27,2,24]{3,2,1,0:T(2,128)(2,1)} %bitcast.14), channel_id=1, source_target_pairs={{12,0},{0,4},{4,8},{8,12},{13,1},{1,5},{5,9},{9,13},{14,2},{2,6},{... | collective-permute-start | bytes 15560 | tf_op jit(solution)/shard_map/ppermute | solution.py:500
  6.0 2.0 %prepare_lines.1 = (bf16[1,144,128]{2,1,0:T(8,128)(2,1)S(1)}, f32[9,144,128]{2,1,0:T(8,128)S(1)}, bf16[2,128,288]{2,1,0:T(8,128)(2,1)S(1)}, f32[8,72,256]{2,1,0:T(8,128)S(1)}, f32[2,2,8,128]{3,2,1,0:T(8,128)S(1)}) custom-call(bf16[1,2,144,128]{3,2,1,0:T(8,128)(2,1)} %bitcast.13, bf16[2,27,2,24]{3,2,1,0:T(2,128)(2,1)} %bitcast.15, s32[8]{0:T(128)} %refs_7_.1, ...), custom_call_target="tpu_custom_call" | custom-call | tf_op jit(solution)/shard_map/prepare_lines/pallas_call | solution.py:540
  8.0 2.3 %collective-permute-done.refs_4_ = bf16[2,27,2,24]{3,2,1,0:T(2,128)(2,1)S(1)} collective-permute-done((bf16[2,27,2,24]{3,2,1,0:T(2,128)(2,1)}, bf16[2,27,2,24]{3,2,1,0:T(2,128)(2,1)S(1)}, u32[]{:S(2)}, u32[]{:S(2)}) %collective-permute-start) | collective-permute-done | bytes 5216 | tf_op jit(solution)/shard_map/ppermute | solution.py:500
  10.3 0.0 collective-permute-done.1.refs_5_
  10.3 0.0 collective-permute-done.2.refs_6_
  10.3 1.5 %partial_margins.1 = (s16[2,528,128]{2,1,0:T(8,128)(2,1)S(1)}, f32[2,512,128]{2,1,0:T(8,128)S(1)}) custom-call(bf16[1,144,128]{2,1,0:T(8,128)(2,1)S(1)} %get-tuple-element.16.refs_0_, f32[9,144,128]{2,1,0:T(8,128)S(1)} %get-tuple-element.17.refs_1_, bf16[2,128,288]{2,1,0:T(8,128)(2,1)S(1)} %get-tuple-element.18.refs_2_, ...), custom_call_target="tpu_custom_call" | custom-call | tf_op jit(solution)/shard_map/partial_margins/pallas_call | solution.py:559
  11.8 0.0 copy-start
  11.8 0.1 collective-permute-start.3
  11.9 1.5 %collective-permute-done.3.refs_0_ = s16[2,528,128]{2,1,0:T(8,128)(2,1)S(1)} collective-permute-done((s16[2,528,128]{2,1,0:T(8,128)(2,1)S(1)}, s16[2,528,128]{2,1,0:T(8,128)(2,1)S(1)}, u32[]{:S(2)}, u32[]{:S(2)}) %collective-permute-start.3) | collective-permute-done | bytes 270368 | tf_op jit(solution)/shard_map/ppermute | solution.py:505
  13.4 0.2 spread_halves.1
  13.6 0.9 %collective-permute-start.4 = (s16[272,128]{1,0:T(8,128)(2,1)S(1)}, s16[272,128]{1,0:T(8,128)(2,1)S(1)}, u32[]{:S(2)}, u32[]{:S(2)}) collective-permute-start(s16[272,128]{1,0:T(8,128)(2,1)S(1)} %get-tuple-element.22), channel_id=1, source_target_pairs={{2,0},{3,1},{0,2},{1,3},{6,4},{7,5},{4,6},{5,7},{10,8},{11,9},{8,1... | collective-permute-start | bytes 208904 | tf_op jit(solution)/shard_map/ppermute | solution.py:505
  14.5 0.4 %collective-permute-start.5 = (s16[272,128]{1,0:T(8,128)(2,1)S(1)}, s16[272,128]{1,0:T(8,128)(2,1)S(1)}, u32[]{:S(2)}, u32[]{:S(2)}) collective-permute-start(s16[272,128]{1,0:T(8,128)(2,1)S(1)} %get-tuple-element.23), channel_id=1, source_target_pairs={{6,0},{7,1},{4,2},{5,3},{2,4},{3,5},{0,6},{1,7},{14,8},{15,9},{12,... | collective-permute-start | bytes 208904 | tf_op jit(solution)/shard_map/ppermute | solution.py:515
  14.9 2.2 %collective-permute-start.6 = (s16[272,128]{1,0:T(8,128)(2,1)S(1)}, s16[272,128]{1,0:T(8,128)(2,1)S(1)}, u32[]{:S(2)}, u32[]{:S(2)}) collective-permute-start(s16[272,128]{1,0:T(8,128)(2,1)S(1)} %get-tuple-element.24), channel_id=1, source_target_pairs={{4,0},{0,4},{12,8},{8,12},{5,1},{1,5},{13,9},{9,13},{6,2},{2,6},{1... | collective-permute-start | bytes 208904 | tf_op jit(solution)/shard_map/ppermute | solution.py:505
  17.1 1.6 %collective-permute-done.4.refs_1_ = s16[272,128]{1,0:T(8,128)(2,1)S(1)} collective-permute-done((s16[272,128]{1,0:T(8,128)(2,1)S(1)}, s16[272,128]{1,0:T(8,128)(2,1)S(1)}, u32[]{:S(2)}, u32[]{:S(2)}) %collective-permute-start.4) | collective-permute-done | bytes 69664 | tf_op jit(solution)/shard_map/ppermute | solution.py:505
  18.7 1.4 %collective-permute-done.5.refs_2_ = s16[272,128]{1,0:T(8,128)(2,1)S(1)} collective-permute-done((s16[272,128]{1,0:T(8,128)(2,1)S(1)}, s16[272,128]{1,0:T(8,128)(2,1)S(1)}, u32[]{:S(2)}, u32[]{:S(2)}) %collective-permute-start.5) | collective-permute-done | bytes 69664 | tf_op jit(solution)/shard_map/ppermute | solution.py:515
  20.1 0.5 %collective-permute-done.6.refs_3_ = s16[272,128]{1,0:T(8,128)(2,1)S(1)} collective-permute-done((s16[272,128]{1,0:T(8,128)(2,1)S(1)}, s16[272,128]{1,0:T(8,128)(2,1)S(1)}, u32[]{:S(2)}, u32[]{:S(2)}) %collective-permute-start.6) | collective-permute-done | bytes 69664 | tf_op jit(solution)/shard_map/ppermute | solution.py:505
  20.6 0.1 keep_half.1.own_ref
  20.7 0.9 %collective-permute-start.7 = (s16[272,128]{1,0:T(8,128)(2,1)S(1)}, s16[272,128]{1,0:T(8,128)(2,1)S(1)}, u32[]{:S(2)}, u32[]{:S(2)}) collective-permute-start(s16[272,128]{1,0:T(8,128)(2,1)S(1)} %keep_half.1.own_ref), channel_id=1, source_target_pairs={{8,0},{12,4},{0,8},{4,12},{9,1},{13,5},{1,9},{5,13},{10,2},{14,6},... | collective-permute-start | bytes 208904 | tf_op jit(solution)/shard_map/ppermute | solution.py:505
  21.5 5.2 %collective-permute-done.7.arrived_ref = s16[272,128]{1,0:T(8,128)(2,1)S(1)} collective-permute-done((s16[272,128]{1,0:T(8,128)(2,1)S(1)}, s16[272,128]{1,0:T(8,128)(2,1)S(1)}, u32[]{:S(2)}, u32[]{:S(2)}) %collective-permute-start.7) | collective-permute-done | bytes 69664 | tf_op jit(solution)/shard_map/ppermute | solution.py:505
  26.8 1.6 %collective-permute-start.9 = (bf16[256,128]{1,0:T(8,128)(2,1)S(1)}, bf16[256,128]{1,0:T(8,128)(2,1)S(1)}, u32[]{:S(2)}, u32[]{:S(2)}) collective-permute-start(bf16[256,128]{1,0:T(8,128)(2,1)S(1)} %finish_half.1.refs_0_.kept_ref.refs_2_), channel_id=1, source_target_pairs={{16,0},{0,16},{17,1},{1,17},{18,2},{2,18},{19,3},{3,19},{20,4},{4,... | collective-permute-start | bytes 196616 | tf_op jit(solution)/shard_map/ppermute | solution.py:500
  28.3 0.3 collective-permute-start.8
  28.6 1.7 %collective-permute-start.10 = (bf16[256,128]{1,0:T(8,128)(2,1)S(1)}, bf16[256,128]{1,0:T(8,128)(2,1)S(1)}, u32[]{:S(2)}, u32[]{:S(2)}) collective-permute-start(bf16[256,128]{1,0:T(8,128)(2,1)S(1)} %finish_half.1.refs_0_.kept_ref.refs_2_), channel_id=1, source_target_pairs={{20,0},{16,4},{28,8},{24,12},{4,16},{0,20},{12,24},{8,28},{21,1},{... | collective-permute-start | bytes 196616 | tf_op jit(solution)/shard_map/ppermute | solution.py:515
  31.0 0.1 collective-permute-done.9.refs_1_.refs_3_
  31.1 0.0 copy-done
  31.1 0.9 %first_contraction.1 = (f32[8,128]{1,0:T(8,128)S(1)}, f32[2,32,128]{2,1,0:T(8,128)S(1)}) custom-call(s32[1]{0:T(128)S(6)} %copy.10.live_ref, f32[2,2,8,128]{3,2,1,0:T(8,128)S(1)} %get-tuple-element.25.weight_ref, bf16[2,512,512]{2,1,0:T(8,128)(2,1)S(1)} %bitcast.8, bf16[256,128]{1,0:T(8,128)(2,1)S(1)} %finish_half.1.refs_0_.kept_ref.refs_2_, ...), custom_call_target="tpu_custom_call" | custom-call | tf_op jit(solution)/shard_map/first_contraction/pallas_call | solution.py:621
  32.0 0.6 %collective-permute-done.8.other_ref.refs_0_ = bf16[256,128]{1,0:T(8,128)(2,1)S(1)} collective-permute-done((bf16[256,128]{1,0:T(8,128)(2,1)S(1)}, bf16[256,128]{1,0:T(8,128)(2,1)S(1)}, u32[]{:S(2)}, u32[]{:S(2)}) %collective-permute-start.8) | collective-permute-done | bytes 65568 | tf_op jit(solution)/shard_map/ppermute | solution.py:505
  32.6 0.7 %margins_out.1 = f32[1,512,128]{2,1,0:T(8,128)} custom-call(bf16[256,128]{1,0:T(8,128)(2,1)S(1)} %finish_half.1.refs_0_.kept_ref.refs_2_, bf16[256,128]{1,0:T(8,128)(2,1)S(1)} %collective-permute-done.8.other_ref.refs_0_), custom_call_target="tpu_custom_call" | custom-call | tf_op jit(solution)/shard_map/margins_out/pallas_call | solution.py:629
  33.3 0.4 %collective-permute-done.10.refs_1_ = bf16[256,128]{1,0:T(8,128)(2,1)S(1)} collective-permute-done((bf16[256,128]{1,0:T(8,128)(2,1)S(1)}, bf16[256,128]{1,0:T(8,128)(2,1)S(1)}, u32[]{:S(2)}, u32[]{:S(2)}) %collective-permute-start.10) | collective-permute-done | bytes 65568 | tf_op jit(solution)/shard_map/ppermute | solution.py:515
  33.7 1.5 %second_contraction.1 = f32[1,2,2]{2,1,0:T(2,128)} custom-call(f32[2,2,8,128]{3,2,1,0:T(8,128)S(1)} %get-tuple-element.25.weight_ref, bf16[2,512,512]{2,1,0:T(8,128)(2,1)S(1)} %bitcast.9, bf16[256,128]{1,0:T(8,128)(2,1)S(1)} %collective-permute-done.8.other_ref.refs_0_, bf16[256,128]{1,0:T(8,128)(2,1)S(1)} %collective-permute-done.10.refs_1_, ...), custom_call_target="tpu_custom_call" | custom-call | tf_op jit(solution)/shard_map/second_contraction/pallas_call | solution.py:636
  (1 shorter events, 0.0 us)
Async XLA Ops:
  0.6 9.6 %collective-permute-start.1 = (bf16[1,2,144,128]{3,2,1,0:T(8,128)(2,1)}, bf16[1,2,144,128]{3,2,1,0:T(8,128)(2,1)S(1)}, u32[]{:S(2)}, u32[]{:S(2)}) collective-permute-start(bf16[1,2,144,128]{3,2,1,0:T(8,128)(2,1)} %bitcast.11), channel_id=1, source_target_pairs={{12,0},{0,4},{4,8},{8,12},{13,1},{1,5},{5,9},{9,13},{14,2},{2,6},{... | collective-permute-start | bytes 221192 | tf_op jit(solution)/shard_map/ppermute | solution.py:500
  3.7 6.6 %collective-permute-start.2 = (bf16[1,2,144,128]{3,2,1,0:T(8,128)(2,1)}, bf16[1,2,144,128]{3,2,1,0:T(8,128)(2,1)S(1)}, u32[]{:S(2)}, u32[]{:S(2)}) collective-permute-start(bf16[1,2,144,128]{3,2,1,0:T(8,128)(2,1)} %bitcast.12), channel_id=1, source_target_pairs={{1,0},{2,1},{3,2},{0,3},{5,4},{6,5},{7,6},{4,7},{9,8},{10,9},{11,1... | collective-permute-start | bytes 221192 | tf_op jit(solution)/shard_map/ppermute | solution.py:500
  4.4 5.9 %collective-permute-start = (bf16[2,27,2,24]{3,2,1,0:T(2,128)(2,1)}, bf16[2,27,2,24]{3,2,1,0:T(2,128)(2,1)S(1)}, u32[]{:S(2)}, u32[]{:S(2)}) collective-permute-start(bf16[2,27,2,24]{3,2,1,0:T(2,128)(2,1)} %bitcast.14), channel_id=1, source_target_pairs={{12,0},{0,4},{4,8},{8,12},{13,1},{1,5},{5,9},{9,13},{14,2},{2,6},{... | collective-permute-start | bytes 15560 | tf_op jit(solution)/shard_map/ppermute | solution.py:500
  11.8 19.3 %copy-start = (bf16[1,2,512,512]{3,2,1,0:T(8,128)(2,1)S(1)}, bf16[1,2,512,512]{3,2,1,0:T(8,128)(2,1)}, u32[]{:S(2)}) copy-start(bf16[1,2,512,512]{3,2,1,0:T(8,128)(2,1)} %param.12) | copy-start | bytes 3145732
  11.8 1.6 %collective-permute-start.3 = (s16[2,528,128]{2,1,0:T(8,128)(2,1)S(1)}, s16[2,528,128]{2,1,0:T(8,128)(2,1)S(1)}, u32[]{:S(2)}, u32[]{:S(2)}) collective-permute-start(s16[2,528,128]{2,1,0:T(8,128)(2,1)S(1)} %get-tuple-element.21), channel_id=1, source_target_pairs={{1,0},{0,1},{3,2},{2,3},{5,4},{4,5},{7,6},{6,7},{9,8},{8,9},{11,10... | collective-permute-start | bytes 811016 | tf_op jit(solution)/shard_map/ppermute | solution.py:505
  13.6 5.1 %collective-permute-start.4 = (s16[272,128]{1,0:T(8,128)(2,1)S(1)}, s16[272,128]{1,0:T(8,128)(2,1)S(1)}, u32[]{:S(2)}, u32[]{:S(2)}) collective-permute-start(s16[272,128]{1,0:T(8,128)(2,1)S(1)} %get-tuple-element.22), channel_id=1, source_target_pairs={{2,0},{3,1},{0,2},{1,3},{6,4},{7,5},{4,6},{5,7},{10,8},{11,9},{8,1... | collective-permute-start | bytes 208904 | tf_op jit(solution)/shard_map/ppermute | solution.py:505
  14.5 5.6 %collective-permute-start.5 = (s16[272,128]{1,0:T(8,128)(2,1)S(1)}, s16[272,128]{1,0:T(8,128)(2,1)S(1)}, u32[]{:S(2)}, u32[]{:S(2)}) collective-permute-start(s16[272,128]{1,0:T(8,128)(2,1)S(1)} %get-tuple-element.23), channel_id=1, source_target_pairs={{6,0},{7,1},{4,2},{5,3},{2,4},{3,5},{0,6},{1,7},{14,8},{15,9},{12,... | collective-permute-start | bytes 208904 | tf_op jit(solution)/shard_map/ppermute | solution.py:515
  14.9 5.7 %collective-permute-start.6 = (s16[272,128]{1,0:T(8,128)(2,1)S(1)}, s16[272,128]{1,0:T(8,128)(2,1)S(1)}, u32[]{:S(2)}, u32[]{:S(2)}) collective-permute-start(s16[272,128]{1,0:T(8,128)(2,1)S(1)} %get-tuple-element.24), channel_id=1, source_target_pairs={{4,0},{0,4},{12,8},{8,12},{5,1},{1,5},{13,9},{9,13},{6,2},{2,6},{1... | collective-permute-start | bytes 208904 | tf_op jit(solution)/shard_map/ppermute | solution.py:505
  20.7 6.0 %collective-permute-start.7 = (s16[272,128]{1,0:T(8,128)(2,1)S(1)}, s16[272,128]{1,0:T(8,128)(2,1)S(1)}, u32[]{:S(2)}, u32[]{:S(2)}) collective-permute-start(s16[272,128]{1,0:T(8,128)(2,1)S(1)} %keep_half.1.own_ref), channel_id=1, source_target_pairs={{8,0},{12,4},{0,8},{4,12},{9,1},{13,5},{1,9},{5,13},{10,2},{14,6},... | collective-permute-start | bytes 208904 | tf_op jit(solution)/shard_map/ppermute | solution.py:505
  26.8 4.3 %collective-permute-start.9 = (bf16[256,128]{1,0:T(8,128)(2,1)S(1)}, bf16[256,128]{1,0:T(8,128)(2,1)S(1)}, u32[]{:S(2)}, u32[]{:S(2)}) collective-permute-start(bf16[256,128]{1,0:T(8,128)(2,1)S(1)} %finish_half.1.refs_0_.kept_ref.refs_2_), channel_id=1, source_target_pairs={{16,0},{0,16},{17,1},{1,17},{18,2},{2,18},{19,3},{3,19},{20,4},{4,... | collective-permute-start | bytes 196616 | tf_op jit(solution)/shard_map/ppermute | solution.py:500
  28.3 4.3 %collective-permute-start.8 = (bf16[256,128]{1,0:T(8,128)(2,1)S(1)}, bf16[256,128]{1,0:T(8,128)(2,1)S(1)}, u32[]{:S(2)}, u32[]{:S(2)}) collective-permute-start(bf16[256,128]{1,0:T(8,128)(2,1)S(1)} %finish_half.1.refs_0_.kept_ref.refs_2_), channel_id=1, source_target_pairs={{4,0},{0,4},{12,8},{8,12},{5,1},{1,5},{13,9},{9,13},{6,2},{2,6},{1... | collective-permute-start | bytes 196616 | tf_op jit(solution)/shard_map/ppermute | solution.py:505
  28.6 5.2 %collective-permute-start.10 = (bf16[256,128]{1,0:T(8,128)(2,1)S(1)}, bf16[256,128]{1,0:T(8,128)(2,1)S(1)}, u32[]{:S(2)}, u32[]{:S(2)}) collective-permute-start(bf16[256,128]{1,0:T(8,128)(2,1)S(1)} %finish_half.1.refs_0_.kept_ref.refs_2_), channel_id=1, source_target_pairs={{20,0},{16,4},{28,8},{24,12},{4,16},{0,20},{12,24},{8,28},{21,1},{... | collective-permute-start | bytes 196616 | tf_op jit(solution)/shard_map/ppermute | solution.py:515

commit v16 on v14

--- a/solution.py
+++ b/solution.py
@@ -582,6 +582,8 @@
     for t in range(1, times):
         source = lambda row, x: ((row + t) % times, x ^ 1)
         other.append(from_diagonal(finished, ("ta", "gx"), source))
+    arrivals = lax.optimization_barrier((*other[1:], *kept[1:]))
+    other[1:], kept[1:] = arrivals[: times - 1], arrivals[times - 1 :]
     split = own_ops % 2 == 0
     now_ops = own_ops // 2 if split else own_ops
     sums_shape = (2 * now_ops, 32, vectors)

time: 34.1 us -> 34.3 us (level)
    ppermute x2, starting transfers between devices: 0.01 us -> 1.02 us  [from_diagonal(): return lax.ppermute(block, axes, perm)]
    ppermute x3, starting transfers between devices: 7.33 us -> 6.39 us  [from_step(): lax.ppermute(block, axis, [((i + step) % count, i) for i in range(count)])]
    ppermute x3, waiting for transfers between devices: 0.16 us -> 0.67 us  [from_step(): lax.ppermute(block, axis, [((i + step) % count, i) for i in range(count)])]
    ppermute x2, waiting for transfers between devices: 3.98 us -> 3.6 us  [from_diagonal(): return lax.ppermute(block, axes, perm)]
where the time goes in v16:
time: 34.3 us; the launch traced here: 34.1 us
  starting transfers between devices  16 us (47%)
  waiting for transfers between devices  10.5 us (31%)
  Pallas kernels  6.27 us (18%)
  between operations  1.33 us (4%)
    ppermute x5, starting transfers between devices, from_partner(): return lax.ppermute(block, axis, [(i ^ step, i) for i in range(count)])  8.58 us
    ppermute x3, starting transfers between devices, from_step(): lax.ppermute(block, axis, [((i + step) % count, i) for i in range(count)])  6.39 us
    ppermute x5, waiting for transfers between devices, from_partner(): return lax.ppermute(block, axis, [(i ^ step, i) for i in range(count)])  6.22 us
    ppermute x2, waiting for transfers between devices, from_diagonal(): return lax.ppermute(block, axes, perm)  3.6 us
    pallas_call x1, Pallas kernels, per_device(): local_call(functools.partial(prepare_kernel, cells_x, cells_y), 'prepare_...  2.25 us
    pallas_call x1, Pallas kernels, per_device(): local_call(functools.partial(second_contract_kernel, times, split), 'seco...  1.57 us
    pallas_call x1, Pallas kernels, per_device(): local_call(functools.partial(margin_kernel, cells_x, cells_y, groups, own...  1.18 us
    ppermute x2, starting transfers between devices, from_diagonal(): return lax.ppermute(block, axes, perm)  1.02 us
  transfers between devices with their start and end apart: 10, of which 7 were waited for; matrix products, arithmetic and copies ran while one was open for 0% of the time, Pallas kernels for 9%

profile of v16, /device:TPU:0, one launch (start us, length us, event | category | flops | bytes accessed | tf_op | source)
XLA Modules:
  0.0 34.1 jit_solution(5655260223142276502)
XLA Ops:
  0.6 5.1 %collective-permute-start = (bf16[1,2,144,128]{3,2,1,0:T(8,128)(2,1)}, bf16[1,2,144,128]{3,2,1,0:T(8,128)(2,1)S(1)}, u32[]{:S(2)}, u32[]{:S(2)}) collective-permute-start(bf16[1,2,144,128]{3,2,1,0:T(8,128)(2,1)} %bitcast.10), channel_id=1, source_target_pairs={{4,0},{8,4},{12,8},{0,12},{5,1},{9,5},{13,9},{1,13},{6,2},{10,6},{... | collective-permute-start | bytes 221192 | tf_op jit(solution)/shard_map/ppermute | solution.py:473
  5.7 0.7 %collective-permute-start.1 = (bf16[1,2,144,128]{3,2,1,0:T(8,128)(2,1)}, bf16[1,2,144,128]{3,2,1,0:T(8,128)(2,1)S(1)}, u32[]{:S(2)}, u32[]{:S(2)}) collective-permute-start(bf16[1,2,144,128]{3,2,1,0:T(8,128)(2,1)} %bitcast.11), channel_id=1, source_target_pairs={{1,0},{2,1},{3,2},{0,3},{5,4},{6,5},{7,6},{4,7},{9,8},{10,9},{11,1... | collective-permute-start | bytes 221192 | tf_op jit(solution)/shard_map/ppermute | solution.py:473
  6.4 2.3 %prepare_lines.1 = (bf16[3,144,128]{2,1,0:T(8,128)(2,1)S(1)}, f32[11,144,128]{2,1,0:T(8,128)S(1)}, bf16[2,128,288]{2,1,0:T(8,128)(2,1)S(1)}, f32[8,72,256]{2,1,0:T(8,128)S(1)}, f32[2,2,8,128]{3,2,1,0:T(8,128)S(1)}) custom-call(bf16[1,2,144,128]{3,2,1,0:T(8,128)(2,1)} %bitcast.12, bf16[2,27,2,24]{3,2,1,0:T(2,128)(2,1)} %bitcast.13, s32[8]{0:T(128)} %refs_6_.1, ...), custom_call_target="tpu_custom_call" | custom-call | tf_op jit(solution)/shard_map/prepare_lines/pallas_call | solution.py:512
  8.7 0.0 collective-permute-done.refs_4_
  8.7 0.0 collective-permute-done.1.refs_5_
  8.7 1.2 %partial_margins.1 = (s16[2,528,128]{2,1,0:T(8,128)(2,1)S(1)}, f32[2,512,128]{2,1,0:T(8,128)S(1)}) custom-call(bf16[3,144,128]{2,1,0:T(8,128)(2,1)S(1)} %get-tuple-element.19.refs_0_, f32[11,144,128]{2,1,0:T(8,128)S(1)} %get-tuple-element.20.refs_1_, bf16[2,128,288]{2,1,0:T(8,128)(2,1)S(1)} %get-tuple-element.21.refs_2_, ...), custom_call_target="tpu_custom_call" | custom-call | tf_op jit(solution)/shard_map/partial_margins/pallas_call | solution.py:531
  9.9 0.0 copy-start
  9.9 1.0 %collective-permute-start.2 = (s16[2,528,128]{2,1,0:T(8,128)(2,1)S(1)}, s16[2,528,128]{2,1,0:T(8,128)(2,1)S(1)}, u32[]{:S(2)}, u32[]{:S(2)}) collective-permute-start(s16[2,528,128]{2,1,0:T(8,128)(2,1)S(1)} %get-tuple-element.24), channel_id=1, source_target_pairs={{1,0},{0,1},{3,2},{2,3},{5,4},{4,5},{7,6},{6,7},{9,8},{8,9},{11,10... | collective-permute-start | bytes 811016 | tf_op jit(solution)/shard_map/ppermute | solution.py:478
  10.9 1.2 %collective-permute-done.2.refs_0_ = s16[2,528,128]{2,1,0:T(8,128)(2,1)S(1)} collective-permute-done((s16[2,528,128]{2,1,0:T(8,128)(2,1)S(1)}, s16[2,528,128]{2,1,0:T(8,128)(2,1)S(1)}, u32[]{:S(2)}, u32[]{:S(2)}) %collective-permute-start.2) | collective-permute-done | bytes 270368 | tf_op jit(solution)/shard_map/ppermute | solution.py:478
  12.1 0.2 spread_halves.1
  12.3 1.2 %collective-permute-start.3 = (s16[272,128]{1,0:T(8,128)(2,1)S(1)}, s16[272,128]{1,0:T(8,128)(2,1)S(1)}, u32[]{:S(2)}, u32[]{:S(2)}) collective-permute-start(s16[272,128]{1,0:T(8,128)(2,1)S(1)} %get-tuple-element.25), channel_id=1, source_target_pairs={{2,0},{3,1},{0,2},{1,3},{6,4},{7,5},{4,6},{5,7},{10,8},{11,9},{8,1... | collective-permute-start | bytes 208904 | tf_op jit(solution)/shard_map/ppermute | solution.py:478
  13.5 0.0 collective-permute-start.4
  13.5 2.3 %collective-permute-start.5 = (s16[272,128]{1,0:T(8,128)(2,1)S(1)}, s16[272,128]{1,0:T(8,128)(2,1)S(1)}, u32[]{:S(2)}, u32[]{:S(2)}) collective-permute-start(s16[272,128]{1,0:T(8,128)(2,1)S(1)} %get-tuple-element.27), channel_id=1, source_target_pairs={{4,0},{0,4},{12,8},{8,12},{5,1},{1,5},{13,9},{9,13},{6,2},{2,6},{1... | collective-permute-start | bytes 208904 | tf_op jit(solution)/shard_map/ppermute | solution.py:478
  15.8 1.0 %collective-permute-done.3.refs_1_ = s16[272,128]{1,0:T(8,128)(2,1)S(1)} collective-permute-done((s16[272,128]{1,0:T(8,128)(2,1)S(1)}, s16[272,128]{1,0:T(8,128)(2,1)S(1)}, u32[]{:S(2)}, u32[]{:S(2)}) %collective-permute-start.3) | collective-permute-done | bytes 69664 | tf_op jit(solution)/shard_map/ppermute | solution.py:478
  16.8 2.5 %collective-permute-done.4.refs_2_ = s16[272,128]{1,0:T(8,128)(2,1)S(1)} collective-permute-done((s16[272,128]{1,0:T(8,128)(2,1)S(1)}, s16[272,128]{1,0:T(8,128)(2,1)S(1)}, u32[]{:S(2)}, u32[]{:S(2)}) %collective-permute-start.4) | collective-permute-done | bytes 69664 | tf_op jit(solution)/shard_map/ppermute | solution.py:488
  19.3 0.2 collective-permute-done.5.refs_3_
  19.5 0.1 keep_half.1.own_ref
  19.6 2.1 %collective-permute-start.6 = (s16[272,128]{1,0:T(8,128)(2,1)S(1)}, s16[272,128]{1,0:T(8,128)(2,1)S(1)}, u32[]{:S(2)}, u32[]{:S(2)}) collective-permute-start(s16[272,128]{1,0:T(8,128)(2,1)S(1)} %keep_half.1.own_ref), channel_id=1, source_target_pairs={{8,0},{12,4},{0,8},{4,12},{9,1},{13,5},{1,9},{5,13},{10,2},{14,6},... | collective-permute-start | bytes 208904 | tf_op jit(solution)/shard_map/ppermute | solution.py:478
  21.7 3.9 %collective-permute-done.6.arrived_ref = s16[272,128]{1,0:T(8,128)(2,1)S(1)} collective-permute-done((s16[272,128]{1,0:T(8,128)(2,1)S(1)}, s16[272,128]{1,0:T(8,128)(2,1)S(1)}, u32[]{:S(2)}, u32[]{:S(2)}) %collective-permute-start.6) | collective-permute-done | bytes 69664 | tf_op jit(solution)/shard_map/ppermute | solution.py:478
  25.7 1.0 %collective-permute-start.7 = (bf16[256,128]{1,0:T(8,128)(2,1)S(1)}, bf16[256,128]{1,0:T(8,128)(2,1)S(1)}, u32[]{:S(2)}, u32[]{:S(2)}) collective-permute-start(bf16[256,128]{1,0:T(8,128)(2,1)S(1)} %finish_half.1.refs_0_.refs_2_), channel_id=1, source_target_pairs={{20,0},{16,4},{28,8},{24,12},{4,16},{0,20},{12,24},{8,28},{21,1},{... | collective-permute-start | bytes 196616 | tf_op jit(solution)/shard_map/ppermute | solution.py:488
  26.7 0.6 %collective-permute-start.8 = (bf16[256,128]{1,0:T(8,128)(2,1)S(1)}, bf16[256,128]{1,0:T(8,128)(2,1)S(1)}, u32[]{:S(2)}, u32[]{:S(2)}) collective-permute-start(bf16[256,128]{1,0:T(8,128)(2,1)S(1)} %finish_half.1.refs_0_.refs_2_), channel_id=1, source_target_pairs={{16,0},{0,16},{17,1},{1,17},{18,2},{2,18},{19,3},{3,19},{20,4},{4,... | collective-permute-start | bytes 196616 | tf_op jit(solution)/shard_map/ppermute | solution.py:473
  27.3 1.9 %collective-permute-start.9 = (bf16[256,128]{1,0:T(8,128)(2,1)S(1)}, bf16[256,128]{1,0:T(8,128)(2,1)S(1)}, u32[]{:S(2)}, u32[]{:S(2)}) collective-permute-start(bf16[256,128]{1,0:T(8,128)(2,1)S(1)} %finish_half.1.refs_0_.refs_2_), channel_id=1, source_target_pairs={{4,0},{0,4},{12,8},{8,12},{5,1},{1,5},{13,9},{9,13},{6,2},{2,6},{1... | collective-permute-start | bytes 196616 | tf_op jit(solution)/shard_map/ppermute | solution.py:478
  29.9 1.1 %collective-permute-done.7.refs_0_ = bf16[256,128]{1,0:T(8,128)(2,1)S(1)} collective-permute-done((bf16[256,128]{1,0:T(8,128)(2,1)S(1)}, bf16[256,128]{1,0:T(8,128)(2,1)S(1)}, u32[]{:S(2)}, u32[]{:S(2)}) %collective-permute-start.7) | collective-permute-done | bytes 65568 | tf_op jit(solution)/shard_map/ppermute | solution.py:488
  31.0 0.6 %collective-permute-done.8.refs_1_.refs_3_ = bf16[256,128]{1,0:T(8,128)(2,1)S(1)} collective-permute-done((bf16[256,128]{1,0:T(8,128)(2,1)S(1)}, bf16[256,128]{1,0:T(8,128)(2,1)S(1)}, u32[]{:S(2)}, u32[]{:S(2)}) %collective-permute-start.8) | collective-permute-done | bytes 65568 | tf_op jit(solution)/shard_map/ppermute | solution.py:473
  31.6 0.0 copy-done
  31.6 0.9 %first_contraction.1 = (f32[8,128]{1,0:T(8,128)S(1)}, f32[2,2]{1,0:T(2,128)S(1)}) custom-call(s32[1]{0:T(128)S(6)} %copy.10.live_ref, f32[2,2,8,128]{3,2,1,0:T(8,128)S(1)} %get-tuple-element.18.weight_ref, bf16[2,512,512]{2,1,0:T(8,128)(2,1)S(1)} %bitcast.8, bf16[256,128]{1,0:T(8,128)(2,1)S(1)} %finish_half.1.refs_0_.refs_2_, ...), custom_call_target="tpu_custom_call" | custom-call | tf_op jit(solution)/shard_map/first_contraction/pallas_call | solution.py:594
  32.5 0.0 collective-permute-done.9.refs_1_
  32.5 1.6 %second_contraction.1 = (f32[1,512,128]{2,1,0:T(8,128)}, f32[1,2,2]{2,1,0:T(2,128)}) custom-call(f32[2,2,8,128]{3,2,1,0:T(8,128)S(1)} %get-tuple-element.18.weight_ref, bf16[2,512,512]{2,1,0:T(8,128)(2,1)S(1)} %bitcast.9, bf16[256,128]{1,0:T(8,128)(2,1)S(1)} %collective-permute-done.7.refs_0_, bf16[256,128]{1,0:T(8,128)(2,1)S(1)} %collective-permute-done.9.refs_1_, ...), custom_call_target="tpu_custom_call" | custom-call | tf_op jit(solution)/shard_map/second_contraction/pallas_call | solution.py:605
  (1 shorter events, 0.0 us)
Async XLA Ops:
  0.6 8.0 %collective-permute-start = (bf16[1,2,144,128]{3,2,1,0:T(8,128)(2,1)}, bf16[1,2,144,128]{3,2,1,0:T(8,128)(2,1)S(1)}, u32[]{:S(2)}, u32[]{:S(2)}) collective-permute-start(bf16[1,2,144,128]{3,2,1,0:T(8,128)(2,1)} %bitcast.10), channel_id=1, source_target_pairs={{4,0},{8,4},{12,8},{0,12},{5,1},{9,5},{13,9},{1,13},{6,2},{10,6},{... | collective-permute-start | bytes 221192 | tf_op jit(solution)/shard_map/ppermute | solution.py:473
  5.7 3.0 %collective-permute-start.1 = (bf16[1,2,144,128]{3,2,1,0:T(8,128)(2,1)}, bf16[1,2,144,128]{3,2,1,0:T(8,128)(2,1)S(1)}, u32[]{:S(2)}, u32[]{:S(2)}) collective-permute-start(bf16[1,2,144,128]{3,2,1,0:T(8,128)(2,1)} %bitcast.11), channel_id=1, source_target_pairs={{1,0},{2,1},{3,2},{0,3},{5,4},{6,5},{7,6},{4,7},{9,8},{10,9},{11,1... | collective-permute-start | bytes 221192 | tf_op jit(solution)/shard_map/ppermute | solution.py:473
  9.9 21.7 %copy-start = (bf16[1,2,512,512]{3,2,1,0:T(8,128)(2,1)S(1)}, bf16[1,2,512,512]{3,2,1,0:T(8,128)(2,1)}, u32[]{:S(2)}) copy-start(bf16[1,2,512,512]{3,2,1,0:T(8,128)(2,1)} %param.12) | copy-start | bytes 3145732
  9.9 2.2 %collective-permute-start.2 = (s16[2,528,128]{2,1,0:T(8,128)(2,1)S(1)}, s16[2,528,128]{2,1,0:T(8,128)(2,1)S(1)}, u32[]{:S(2)}, u32[]{:S(2)}) collective-permute-start(s16[2,528,128]{2,1,0:T(8,128)(2,1)S(1)} %get-tuple-element.24), channel_id=1, source_target_pairs={{1,0},{0,1},{3,2},{2,3},{5,4},{4,5},{7,6},{6,7},{9,8},{8,9},{11,10... | collective-permute-start | bytes 811016 | tf_op jit(solution)/shard_map/ppermute | solution.py:478
  12.3 4.5 %collective-permute-start.3 = (s16[272,128]{1,0:T(8,128)(2,1)S(1)}, s16[272,128]{1,0:T(8,128)(2,1)S(1)}, u32[]{:S(2)}, u32[]{:S(2)}) collective-permute-start(s16[272,128]{1,0:T(8,128)(2,1)S(1)} %get-tuple-element.25), channel_id=1, source_target_pairs={{2,0},{3,1},{0,2},{1,3},{6,4},{7,5},{4,6},{5,7},{10,8},{11,9},{8,1... | collective-permute-start | bytes 208904 | tf_op jit(solution)/shard_map/ppermute | solution.py:478
  13.5 5.8 %collective-permute-start.4 = (s16[272,128]{1,0:T(8,128)(2,1)S(1)}, s16[272,128]{1,0:T(8,128)(2,1)S(1)}, u32[]{:S(2)}, u32[]{:S(2)}) collective-permute-start(s16[272,128]{1,0:T(8,128)(2,1)S(1)} %get-tuple-element.26), channel_id=1, source_target_pairs={{6,0},{7,1},{4,2},{5,3},{2,4},{3,5},{0,6},{1,7},{14,8},{15,9},{12,... | collective-permute-start | bytes 208904 | tf_op jit(solution)/shard_map/ppermute | solution.py:488
  13.5 6.0 %collective-permute-start.5 = (s16[272,128]{1,0:T(8,128)(2,1)S(1)}, s16[272,128]{1,0:T(8,128)(2,1)S(1)}, u32[]{:S(2)}, u32[]{:S(2)}) collective-permute-start(s16[272,128]{1,0:T(8,128)(2,1)S(1)} %get-tuple-element.27), channel_id=1, source_target_pairs={{4,0},{0,4},{12,8},{8,12},{5,1},{1,5},{13,9},{9,13},{6,2},{2,6},{1... | collective-permute-start | bytes 208904 | tf_op jit(solution)/shard_map/ppermute | solution.py:478
  19.6 6.0 %collective-permute-start.6 = (s16[272,128]{1,0:T(8,128)(2,1)S(1)}, s16[272,128]{1,0:T(8,128)(2,1)S(1)}, u32[]{:S(2)}, u32[]{:S(2)}) collective-permute-start(s16[272,128]{1,0:T(8,128)(2,1)S(1)} %keep_half.1.own_ref), channel_id=1, source_target_pairs={{8,0},{12,4},{0,8},{4,12},{9,1},{13,5},{1,9},{5,13},{10,2},{14,6},... | collective-permute-start | bytes 208904 | tf_op jit(solution)/shard_map/ppermute | solution.py:478
  25.7 5.3 %collective-permute-start.7 = (bf16[256,128]{1,0:T(8,128)(2,1)S(1)}, bf16[256,128]{1,0:T(8,128)(2,1)S(1)}, u32[]{:S(2)}, u32[]{:S(2)}) collective-permute-start(bf16[256,128]{1,0:T(8,128)(2,1)S(1)} %finish_half.1.refs_0_.refs_2_), channel_id=1, source_target_pairs={{20,0},{16,4},{28,8},{24,12},{4,16},{0,20},{12,24},{8,28},{21,1},{... | collective-permute-start | bytes 196616 | tf_op jit(solution)/shard_map/ppermute | solution.py:488
  26.7 4.9 %collective-permute-start.8 = (bf16[256,128]{1,0:T(8,128)(2,1)S(1)}, bf16[256,128]{1,0:T(8,128)(2,1)S(1)}, u32[]{:S(2)}, u32[]{:S(2)}) collective-permute-start(bf16[256,128]{1,0:T(8,128)(2,1)S(1)} %finish_half.1.refs_0_.refs_2_), channel_id=1, source_target_pairs={{16,0},{0,16},{17,1},{1,17},{18,2},{2,18},{19,3},{3,19},{20,4},{4,... | collective-permute-start | bytes 196616 | tf_op jit(solution)/shard_map/ppermute | solution.py:473
  27.3 5.2 %collective-permute-start.9 = (bf16[256,128]{1,0:T(8,128)(2,1)S(1)}, bf16[256,128]{1,0:T(8,128)(2,1)S(1)}, u32[]{:S(2)}, u32[]{:S(2)}) collective-permute-start(bf16[256,128]{1,0:T(8,128)(2,1)S(1)} %finish_half.1.refs_0_.refs_2_), channel_id=1, source_target_pairs={{4,0},{0,4},{12,8},{8,12},{5,1},{1,5},{13,9},{9,13},{6,2},{2,6},{1... | collective-permute-start | bytes 196616 | tf_op jit(solution)/shard_map/ppermute | solution.py:478

commit v17 on v13

--- a/solution.py
+++ b/solution.py
@@ -564,8 +564,8 @@
     for_y, for_both, for_x = in_vmem(body, "spread_halves", (message(half),) * 3, held, *messages)
     came = [
         from_partner(for_y, "gy", 1 << last),
+        from_partner(for_x, "gx", 1),
         from_diagonal(for_both, ("gx", "gy"), lambda x, y: (x ^ 1, y ^ (1 << last))),
-        from_partner(for_x, "gx", 1),
     ]
     body = functools.partial(keep_kernel, vectors)
     (packed,) = in_vmem(body, "keep_half", message(half), held, *messages, *came)

time: 34.1 us -> 34.7 us (1.018)
  starting transfers between devices: 16 us -> 17 us
  waiting for transfers between devices: 9.71 us -> 9.34 us
    ppermute x2, starting transfers between devices: 1.97 us -> 3.78 us  [from_diagonal(): return lax.ppermute(block, axes, perm)]
    ppermute x2, waiting for transfers between devices: 2.72 us -> 1.79 us  [from_diagonal(): return lax.ppermute(block, axes, perm)]
    ppermute x5, starting transfers between devices: 6.69 us -> 5.83 us  [from_partner(): return lax.ppermute(block, axis, [(i ^ step, i) for i in range(count)])]
    ppermute x5, waiting for transfers between devices: 6.83 us -> 7.4 us  [from_partner(): return lax.ppermute(block, axis, [(i ^ step, i) for i in range(count)])]
where the time goes in v17:
time: 34.7 us; the launch traced here: 34.5 us
  starting transfers between devices  17 us (49%)
  waiting for transfers between devices  9.34 us (27%)
  Pallas kernels  6.88 us (20%)
  between operations  1.34 us (4%)
    ppermute x5, waiting for transfers between devices, from_partner(): return lax.ppermute(block, axis, [(i ^ step, i) for i in range(count)])  7.4 us
    ppermute x3, starting transfers between devices, from_step(): lax.ppermute(block, axis, [((i + step) % count, i) for i in range(count)])  7.34 us
    ppermute x5, starting transfers between devices, from_partner(): return lax.ppermute(block, axis, [(i ^ step, i) for i in range(count)])  5.83 us
    ppermute x2, starting transfers between devices, from_diagonal(): return lax.ppermute(block, axes, perm)  3.78 us
    pallas_call x1, Pallas kernels, per_device(): local_call(functools.partial(prepare_kernel, cells_x, cells_y), 'prepare_...  2.25 us
    ppermute x2, waiting for transfers between devices, from_diagonal(): return lax.ppermute(block, axes, perm)  1.79 us
    pallas_call x1, Pallas kernels, per_device(): local_call(functools.partial(second_contract_kernel, times, split), 'seco...  1.51 us
    pallas_call x1, Pallas kernels, per_device(): local_call(functools.partial(margin_kernel, cells_x, cells_y, groups, own...  1.18 us
  transfers between devices with their start and end apart: 10, of which 8 were waited for; matrix products, arithmetic and copies ran while one was open for 0% of the time, Pallas kernels for 11%

profile of v17, /device:TPU:0, one launch (start us, length us, event | category | flops | bytes accessed | tf_op | source)
XLA Modules:
  0.0 34.5 jit_solution(16584819509390667396)
XLA Ops:
  0.6 5.1 %collective-permute-start = (bf16[1,2,144,128]{3,2,1,0:T(8,128)(2,1)}, bf16[1,2,144,128]{3,2,1,0:T(8,128)(2,1)S(1)}, u32[]{:S(2)}, u32[]{:S(2)}) collective-permute-start(bf16[1,2,144,128]{3,2,1,0:T(8,128)(2,1)} %bitcast.11), channel_id=1, source_target_pairs={{4,0},{8,4},{12,8},{0,12},{5,1},{9,5},{13,9},{1,13},{6,2},{10,6},{... | collective-permute-start | bytes 221192 | tf_op jit(solution)/shard_map/ppermute | solution.py:475
  5.7 0.7 %collective-permute-start.1 = (bf16[1,2,144,128]{3,2,1,0:T(8,128)(2,1)}, bf16[1,2,144,128]{3,2,1,0:T(8,128)(2,1)S(1)}, u32[]{:S(2)}, u32[]{:S(2)}) collective-permute-start(bf16[1,2,144,128]{3,2,1,0:T(8,128)(2,1)} %bitcast.12), channel_id=1, source_target_pairs={{1,0},{2,1},{3,2},{0,3},{5,4},{6,5},{7,6},{4,7},{9,8},{10,9},{11,1... | collective-permute-start | bytes 221192 | tf_op jit(solution)/shard_map/ppermute | solution.py:475
  6.4 2.3 %prepare_lines.1 = (bf16[3,144,128]{2,1,0:T(8,128)(2,1)S(1)}, f32[11,144,128]{2,1,0:T(8,128)S(1)}, bf16[2,128,288]{2,1,0:T(8,128)(2,1)S(1)}, f32[8,72,256]{2,1,0:T(8,128)S(1)}, f32[2,2,8,128]{3,2,1,0:T(8,128)S(1)}) custom-call(bf16[1,2,144,128]{3,2,1,0:T(8,128)(2,1)} %bitcast.13, bf16[2,27,2,24]{3,2,1,0:T(2,128)(2,1)} %bitcast.14, s32[8]{0:T(128)} %refs_6_.1, ...), custom_call_target="tpu_custom_call" | custom-call | tf_op jit(solution)/shard_map/prepare_lines/pallas_call | solution.py:514
  8.7 0.0 collective-permute-done.refs_4_
  8.7 0.0 collective-permute-done.1.refs_5_
  8.7 1.2 %partial_margins.1 = (s16[2,528,128]{2,1,0:T(8,128)(2,1)S(1)}, f32[2,512,128]{2,1,0:T(8,128)S(1)}) custom-call(bf16[3,144,128]{2,1,0:T(8,128)(2,1)S(1)} %get-tuple-element.16.refs_0_, f32[11,144,128]{2,1,0:T(8,128)S(1)} %get-tuple-element.17.refs_1_, bf16[2,128,288]{2,1,0:T(8,128)(2,1)S(1)} %get-tuple-element.18.refs_2_, ...), custom_call_target="tpu_custom_call" | custom-call | tf_op jit(solution)/shard_map/partial_margins/pallas_call | solution.py:533
  9.9 0.0 copy-start
  9.9 1.0 %collective-permute-start.2 = (s16[2,528,128]{2,1,0:T(8,128)(2,1)S(1)}, s16[2,528,128]{2,1,0:T(8,128)(2,1)S(1)}, u32[]{:S(2)}, u32[]{:S(2)}) collective-permute-start(s16[2,528,128]{2,1,0:T(8,128)(2,1)S(1)} %get-tuple-element.21), channel_id=1, source_target_pairs={{1,0},{0,1},{3,2},{2,3},{5,4},{4,5},{7,6},{6,7},{9,8},{8,9},{11,10... | collective-permute-start | bytes 811016 | tf_op jit(solution)/shard_map/ppermute | solution.py:480
  10.9 1.2 %collective-permute-done.2.refs_0_ = s16[2,528,128]{2,1,0:T(8,128)(2,1)S(1)} collective-permute-done((s16[2,528,128]{2,1,0:T(8,128)(2,1)S(1)}, s16[2,528,128]{2,1,0:T(8,128)(2,1)S(1)}, u32[]{:S(2)}, u32[]{:S(2)}) %collective-permute-start.2) | collective-permute-done | bytes 270368 | tf_op jit(solution)/shard_map/ppermute | solution.py:480
  12.1 0.2 spread_halves.1
  12.3 1.2 %collective-permute-start.3 = (s16[272,128]{1,0:T(8,128)(2,1)S(1)}, s16[272,128]{1,0:T(8,128)(2,1)S(1)}, u32[]{:S(2)}, u32[]{:S(2)}) collective-permute-start(s16[272,128]{1,0:T(8,128)(2,1)S(1)} %get-tuple-element.22), channel_id=1, source_target_pairs={{2,0},{3,1},{0,2},{1,3},{6,4},{7,5},{4,6},{5,7},{10,8},{11,9},{8,1... | collective-permute-start | bytes 208904 | tf_op jit(solution)/shard_map/ppermute | solution.py:480
  13.5 0.0 collective-permute-start.4
  13.5 2.3 %collective-permute-start.5 = (s16[272,128]{1,0:T(8,128)(2,1)S(1)}, s16[272,128]{1,0:T(8,128)(2,1)S(1)}, u32[]{:S(2)}, u32[]{:S(2)}) collective-permute-start(s16[272,128]{1,0:T(8,128)(2,1)S(1)} %get-tuple-element.24), channel_id=1, source_target_pairs={{6,0},{7,1},{4,2},{5,3},{2,4},{3,5},{0,6},{1,7},{14,8},{15,9},{12,... | collective-permute-start | bytes 208904 | tf_op jit(solution)/shard_map/ppermute | solution.py:490
  15.8 1.0 %collective-permute-done.3.refs_1_ = s16[272,128]{1,0:T(8,128)(2,1)S(1)} collective-permute-done((s16[272,128]{1,0:T(8,128)(2,1)S(1)}, s16[272,128]{1,0:T(8,128)(2,1)S(1)}, u32[]{:S(2)}, u32[]{:S(2)}) %collective-permute-start.3) | collective-permute-done | bytes 69664 | tf_op jit(solution)/shard_map/ppermute | solution.py:480
  16.8 1.6 %collective-permute-done.4.refs_2_ = s16[272,128]{1,0:T(8,128)(2,1)S(1)} collective-permute-done((s16[272,128]{1,0:T(8,128)(2,1)S(1)}, s16[272,128]{1,0:T(8,128)(2,1)S(1)}, u32[]{:S(2)}, u32[]{:S(2)}) %collective-permute-start.4) | collective-permute-done | bytes 69664 | tf_op jit(solution)/shard_map/ppermute | solution.py:480
  18.4 1.1 %collective-permute-done.5.refs_3_ = s16[272,128]{1,0:T(8,128)(2,1)S(1)} collective-permute-done((s16[272,128]{1,0:T(8,128)(2,1)S(1)}, s16[272,128]{1,0:T(8,128)(2,1)S(1)}, u32[]{:S(2)}, u32[]{:S(2)}) %collective-permute-start.5) | collective-permute-done | bytes 69664 | tf_op jit(solution)/shard_map/ppermute | solution.py:490
  19.5 0.1 keep_half.1.own_ref
  19.6 3.0 %collective-permute-start.6 = (s16[272,128]{1,0:T(8,128)(2,1)S(1)}, s16[272,128]{1,0:T(8,128)(2,1)S(1)}, u32[]{:S(2)}, u32[]{:S(2)}) collective-permute-start(s16[272,128]{1,0:T(8,128)(2,1)S(1)} %keep_half.1.own_ref), channel_id=1, source_target_pairs={{8,0},{12,4},{0,8},{4,12},{9,1},{13,5},{1,9},{5,13},{10,2},{14,6},... | collective-permute-start | bytes 208904 | tf_op jit(solution)/shard_map/ppermute | solution.py:480
  22.7 3.0 %collective-permute-done.6.arrived_ref = s16[272,128]{1,0:T(8,128)(2,1)S(1)} collective-permute-done((s16[272,128]{1,0:T(8,128)(2,1)S(1)}, s16[272,128]{1,0:T(8,128)(2,1)S(1)}, u32[]{:S(2)}, u32[]{:S(2)}) %collective-permute-start.6) | collective-permute-done | bytes 69664 | tf_op jit(solution)/shard_map/ppermute | solution.py:480
  25.7 1.6 %collective-permute-start.8 = (bf16[256,128]{1,0:T(8,128)(2,1)S(1)}, bf16[256,128]{1,0:T(8,128)(2,1)S(1)}, u32[]{:S(2)}, u32[]{:S(2)}) collective-permute-start(bf16[256,128]{1,0:T(8,128)(2,1)S(1)} %finish_half.1.refs_0_.kept_ref.refs_2_), channel_id=1, source_target_pairs={{16,0},{0,16},{17,1},{1,17},{18,2},{2,18},{19,3},{3,19},{20,4},{4,... | collective-permute-start | bytes 196616 | tf_op jit(solution)/shard_map/ppermute | solution.py:475
  27.3 0.6 %collective-permute-start.7 = (bf16[256,128]{1,0:T(8,128)(2,1)S(1)}, bf16[256,128]{1,0:T(8,128)(2,1)S(1)}, u32[]{:S(2)}, u32[]{:S(2)}) collective-permute-start(bf16[256,128]{1,0:T(8,128)(2,1)S(1)} %finish_half.1.refs_0_.kept_ref.refs_2_), channel_id=1, source_target_pairs={{4,0},{0,4},{12,8},{8,12},{5,1},{1,5},{13,9},{9,13},{6,2},{2,6},{1... | collective-permute-start | bytes 196616 | tf_op jit(solution)/shard_map/ppermute | solution.py:480
  27.9 1.4 %collective-permute-start.9 = (bf16[256,128]{1,0:T(8,128)(2,1)S(1)}, bf16[256,128]{1,0:T(8,128)(2,1)S(1)}, u32[]{:S(2)}, u32[]{:S(2)}) collective-permute-start(bf16[256,128]{1,0:T(8,128)(2,1)S(1)} %finish_half.1.refs_0_.kept_ref.refs_2_), channel_id=1, source_target_pairs={{20,0},{16,4},{28,8},{24,12},{4,16},{0,20},{12,24},{8,28},{21,1},{... | collective-permute-start | bytes 196616 | tf_op jit(solution)/shard_map/ppermute | solution.py:490
  29.9 0.1 collective-permute-done.8.refs_1_.refs_3_
  30.1 0.0 copy-done
  30.1 0.9 %first_contraction.1 = (f32[8,128]{1,0:T(8,128)S(1)}, f32[2,32,128]{2,1,0:T(8,128)S(1)}) custom-call(s32[1]{0:T(128)S(6)} %copy.10.live_ref, f32[2,2,8,128]{3,2,1,0:T(8,128)S(1)} %get-tuple-element.25.weight_ref, bf16[2,512,512]{2,1,0:T(8,128)(2,1)S(1)} %bitcast.8, bf16[256,128]{1,0:T(8,128)(2,1)S(1)} %finish_half.1.refs_0_.kept_ref.refs_2_, ...), custom_call_target="tpu_custom_call" | custom-call | tf_op jit(solution)/shard_map/first_contraction/pallas_call | solution.py:594
  30.9 0.6 %collective-permute-done.7.other_ref.refs_0_ = bf16[256,128]{1,0:T(8,128)(2,1)S(1)} collective-permute-done((bf16[256,128]{1,0:T(8,128)(2,1)S(1)}, bf16[256,128]{1,0:T(8,128)(2,1)S(1)}, u32[]{:S(2)}, u32[]{:S(2)}) %collective-permute-start.7) | collective-permute-done | bytes 65568 | tf_op jit(solution)/shard_map/ppermute | solution.py:480
  31.6 0.7 %margins_out.1 = f32[1,512,128]{2,1,0:T(8,128)} custom-call(bf16[256,128]{1,0:T(8,128)(2,1)S(1)} %finish_half.1.refs_0_.kept_ref.refs_2_, bf16[256,128]{1,0:T(8,128)(2,1)S(1)} %collective-permute-done.7.other_ref.refs_0_), custom_call_target="tpu_custom_call" | custom-call | tf_op jit(solution)/shard_map/margins_out/pallas_call | solution.py:602
  32.3 0.7 %collective-permute-done.9.refs_1_ = bf16[256,128]{1,0:T(8,128)(2,1)S(1)} collective-permute-done((bf16[256,128]{1,0:T(8,128)(2,1)S(1)}, bf16[256,128]{1,0:T(8,128)(2,1)S(1)}, u32[]{:S(2)}, u32[]{:S(2)}) %collective-permute-start.9) | collective-permute-done | bytes 65568 | tf_op jit(solution)/shard_map/ppermute | solution.py:490
  33.0 1.5 %second_contraction.1 = f32[1,2,2]{2,1,0:T(2,128)} custom-call(f32[2,2,8,128]{3,2,1,0:T(8,128)S(1)} %get-tuple-element.25.weight_ref, bf16[2,512,512]{2,1,0:T(8,128)(2,1)S(1)} %bitcast.9, bf16[256,128]{1,0:T(8,128)(2,1)S(1)} %collective-permute-done.7.other_ref.refs_0_, bf16[256,128]{1,0:T(8,128)(2,1)S(1)} %collective-permute-done.9.refs_1_, ...), custom_call_target="tpu_custom_call" | custom-call | tf_op jit(solution)/shard_map/second_contraction/pallas_call | solution.py:609
  (1 shorter events, 0.0 us)
Async XLA Ops:
  0.6 8.0 %collective-permute-start = (bf16[1,2,144,128]{3,2,1,0:T(8,128)(2,1)}, bf16[1,2,144,128]{3,2,1,0:T(8,128)(2,1)S(1)}, u32[]{:S(2)}, u32[]{:S(2)}) collective-permute-start(bf16[1,2,144,128]{3,2,1,0:T(8,128)(2,1)} %bitcast.11), channel_id=1, source_target_pairs={{4,0},{8,4},{12,8},{0,12},{5,1},{9,5},{13,9},{1,13},{6,2},{10,6},{... | collective-permute-start | bytes 221192 | tf_op jit(solution)/shard_map/ppermute | solution.py:475
  5.7 3.0 %collective-permute-start.1 = (bf16[1,2,144,128]{3,2,1,0:T(8,128)(2,1)}, bf16[1,2,144,128]{3,2,1,0:T(8,128)(2,1)S(1)}, u32[]{:S(2)}, u32[]{:S(2)}) collective-permute-start(bf16[1,2,144,128]{3,2,1,0:T(8,128)(2,1)} %bitcast.12), channel_id=1, source_target_pairs={{1,0},{2,1},{3,2},{0,3},{5,4},{6,5},{7,6},{4,7},{9,8},{10,9},{11,1... | collective-permute-start | bytes 221192 | tf_op jit(solution)/shard_map/ppermute | solution.py:475
  9.9 20.2 %copy-start = (bf16[1,2,512,512]{3,2,1,0:T(8,128)(2,1)S(1)}, bf16[1,2,512,512]{3,2,1,0:T(8,128)(2,1)}, u32[]{:S(2)}) copy-start(bf16[1,2,512,512]{3,2,1,0:T(8,128)(2,1)} %param.12) | copy-start | bytes 3145732
  9.9 2.2 %collective-permute-start.2 = (s16[2,528,128]{2,1,0:T(8,128)(2,1)S(1)}, s16[2,528,128]{2,1,0:T(8,128)(2,1)S(1)}, u32[]{:S(2)}, u32[]{:S(2)}) collective-permute-start(s16[2,528,128]{2,1,0:T(8,128)(2,1)S(1)} %get-tuple-element.21), channel_id=1, source_target_pairs={{1,0},{0,1},{3,2},{2,3},{5,4},{4,5},{7,6},{6,7},{9,8},{8,9},{11,10... | collective-permute-start | bytes 811016 | tf_op jit(solution)/shard_map/ppermute | solution.py:480
  12.3 4.5 %collective-permute-start.3 = (s16[272,128]{1,0:T(8,128)(2,1)S(1)}, s16[272,128]{1,0:T(8,128)(2,1)S(1)}, u32[]{:S(2)}, u32[]{:S(2)}) collective-permute-start(s16[272,128]{1,0:T(8,128)(2,1)S(1)} %get-tuple-element.22), channel_id=1, source_target_pairs={{2,0},{3,1},{0,2},{1,3},{6,4},{7,5},{4,6},{5,7},{10,8},{11,9},{8,1... | collective-permute-start | bytes 208904 | tf_op jit(solution)/shard_map/ppermute | solution.py:480
  13.5 4.9 %collective-permute-start.4 = (s16[272,128]{1,0:T(8,128)(2,1)S(1)}, s16[272,128]{1,0:T(8,128)(2,1)S(1)}, u32[]{:S(2)}, u32[]{:S(2)}) collective-permute-start(s16[272,128]{1,0:T(8,128)(2,1)S(1)} %get-tuple-element.23), channel_id=1, source_target_pairs={{4,0},{0,4},{12,8},{8,12},{5,1},{1,5},{13,9},{9,13},{6,2},{2,6},{1... | collective-permute-start | bytes 208904 | tf_op jit(solution)/shard_map/ppermute | solution.py:480
  13.5 6.0 %collective-permute-start.5 = (s16[272,128]{1,0:T(8,128)(2,1)S(1)}, s16[272,128]{1,0:T(8,128)(2,1)S(1)}, u32[]{:S(2)}, u32[]{:S(2)}) collective-permute-start(s16[272,128]{1,0:T(8,128)(2,1)S(1)} %get-tuple-element.24), channel_id=1, source_target_pairs={{6,0},{7,1},{4,2},{5,3},{2,4},{3,5},{0,6},{1,7},{14,8},{15,9},{12,... | collective-permute-start | bytes 208904 | tf_op jit(solution)/shard_map/ppermute | solution.py:490
  19.6 6.1 %collective-permute-start.6 = (s16[272,128]{1,0:T(8,128)(2,1)S(1)}, s16[272,128]{1,0:T(8,128)(2,1)S(1)}, u32[]{:S(2)}, u32[]{:S(2)}) collective-permute-start(s16[272,128]{1,0:T(8,128)(2,1)S(1)} %keep_half.1.own_ref), channel_id=1, source_target_pairs={{8,0},{12,4},{0,8},{4,12},{9,1},{13,5},{1,9},{5,13},{10,2},{14,6},... | collective-permute-start | bytes 208904 | tf_op jit(solution)/shard_map/ppermute | solution.py:480
  25.7 4.3 %collective-permute-start.8 = (bf16[256,128]{1,0:T(8,128)(2,1)S(1)}, bf16[256,128]{1,0:T(8,128)(2,1)S(1)}, u32[]{:S(2)}, u32[]{:S(2)}) collective-permute-start(bf16[256,128]{1,0:T(8,128)(2,1)S(1)} %finish_half.1.refs_0_.kept_ref.refs_2_), channel_id=1, source_target_pairs={{16,0},{0,16},{17,1},{1,17},{18,2},{2,18},{19,3},{3,19},{20,4},{4,... | collective-permute-start | bytes 196616 | tf_op jit(solution)/shard_map/ppermute | solution.py:475
  27.3 4.3 %collective-permute-start.7 = (bf16[256,128]{1,0:T(8,128)(2,1)S(1)}, bf16[256,128]{1,0:T(8,128)(2,1)S(1)}, u32[]{:S(2)}, u32[]{:S(2)}) collective-permute-start(bf16[256,128]{1,0:T(8,128)(2,1)S(1)} %finish_half.1.refs_0_.kept_ref.refs_2_), channel_id=1, source_target_pairs={{4,0},{0,4},{12,8},{8,12},{5,1},{1,5},{13,9},{9,13},{6,2},{2,6},{1... | collective-permute-start | bytes 196616 | tf_op jit(solution)/shard_map/ppermute | solution.py:480
  27.9 5.2 %collective-permute-start.9 = (bf16[256,128]{1,0:T(8,128)(2,1)S(1)}, bf16[256,128]{1,0:T(8,128)(2,1)S(1)}, u32[]{:S(2)}, u32[]{:S(2)}) collective-permute-start(bf16[256,128]{1,0:T(8,128)(2,1)S(1)} %finish_half.1.refs_0_.kept_ref.refs_2_), channel_id=1, source_target_pairs={{20,0},{16,4},{28,8},{24,12},{4,16},{0,20},{12,24},{8,28},{21,1},{... | collective-permute-start | bytes 196616 | tf_op jit(solution)/shard_map/ppermute | solution.py:490

commit v18 on v13

--- a/solution.py
+++ b/solution.py
@@ -183,10 +183,34 @@
         )
 
 
-def margin_kernel(cells_x, cells_y, groups, own_ops, *refs):
+def put_margins(slots, own_ops, field_ref, side_ref, phase_ref, dirs_ref):
+    f32, bf16 = jnp.float32, jnp.bfloat16
+    lines, order, vectors = field_ref.shape[1:]
+    half = order // 2
+    me = lax.axis_index("gy")
+    for j, out_ref in slots:
+        for i in range(own_ops):
+            o = (me ^ j) * own_ops + i
+            code = dirs_ref[o]
+            side = jnp.where((code >= 3) & (code < 6), code - 2, 0)
+            cosine = phase_ref[o, :, 0:vectors]
+            sine = phase_ref[o, :, vectors : 2 * vectors]
+            pairs = []
+            for line in range(lines):
+                real, imag = field_ref[code, line, 0:half], field_ref[code, line, half:order]
+                turned_r, turned_i = cosine * real - sine * imag, sine * real + cosine * imag
+                pairs.append(jnp.concatenate([turned_r, turned_i], axis=1))
+                pairs.append(jnp.concatenate([turned_i, -turned_r], axis=1))
+            pair = jnp.concatenate(pairs, axis=0).astype(bf16)
+            product = jnp.dot(side_ref[side], pair, preferred_element_type=f32)
+            first = 2 * i * vectors
+            out_ref[j >> 2, first : first + vectors] = product[:, :vectors]
+            out_ref[j >> 2, first + vectors : first + 2 * vectors] = product[:, vectors:]
+
+
+def first_margin_kernel(cells_x, cells_y, groups, own_ops, *refs):
     matrix_ref, local_ref, left_ref, phase_ref, halo_x_ref, halo_y_ref, dirs_hbm = refs[:7]
-    swap_ref, hold_ref = refs[7:9]
-    field_ref, side_ref, dirs_ref, sem = refs[9:]
+    swap_ref, field_ref, side_ref, dirs_ref, sem = refs[7:]
     f32, bf16 = jnp.float32, jnp.bfloat16
     copy = pltpu.make_async_copy(dirs_hbm, dirs_ref, sem)
     copy.start()
@@ -213,29 +237,19 @@
     for k, (code, line) in enumerate(local_fields(cells_x, cells_y)):
         field_ref[code, line] = local_ref[k]
     copy.wait()
-    me = lax.axis_index("gy")
-    for j in sorted(range(groups), key=lambda j: -(j & 1)):
-        blocks = []
-        for i in range(own_ops):
-            o = (me ^ j) * own_ops + i
-            code = dirs_ref[o]
-            side = jnp.where((code >= 3) & (code < 6), code - 2, 0)
-            cosine = phase_ref[o, :, 0:vectors]
-            sine = phase_ref[o, :, vectors : 2 * vectors]
-            pairs = []
-            for line in range(lines):
-                real, imag = field_ref[code, line, 0:half], field_ref[code, line, half:order]
-                turned_r, turned_i = cosine * real - sine * imag, sine * real + cosine * imag
-                pairs.append(jnp.concatenate([turned_r, turned_i], axis=1))
-                pairs.append(jnp.concatenate([turned_i, -turned_r], axis=1))
-            pair = jnp.concatenate(pairs, axis=0).astype(bf16)
-            product = jnp.dot(side_ref[side], pair, preferred_element_type=f32)
-            blocks += [product[:, :vectors], product[:, vectors:]]
-        if j & 1:
-            put_fixed(swap_ref.at[j >> 1], blocks)
-            continue
-        for k, block in enumerate(blocks):
-            hold_ref[j >> 1, k * vectors : (k + 1) * vectors] = block
+    slots = [(j, swap_ref) for j in range(groups) if j & 3 == 3]
+    put_margins(slots, own_ops, field_ref, side_ref, phase_ref, dirs_ref)
+
+
+def second_margin_kernel(groups, own_ops, *refs):
+    field_ref, side_ref, phase_ref, dirs_hbm = refs[:4]
+    hold_a_ref, swap_b_ref, hold_b_ref, dirs_ref, sem = refs[4:]
+    copy = pltpu.make_async_copy(dirs_hbm, dirs_ref, sem)
+    copy.start()
+    copy.wait()
+    for kind, out_ref in ((2, hold_a_ref), (1, swap_b_ref), (0, hold_b_ref)):
+        slots = [(j, out_ref) for j in range(groups) if j & 3 == kind]
+        put_margins(slots, own_ops, field_ref, side_ref, phase_ref, dirs_ref)
 
 
 def scale_of(block):
@@ -261,9 +275,10 @@
     return block * jnp.exp2(scales[k : k + 1] - FIXED_BITS)
 
 
-def group_block(held_ref, messages, j, start, rows):
-    total = held_ref[j >> 1, pl.ds(start, rows)]
-    for b, ref in enumerate(messages):
+def group_block(held_ref, swapped_ref, messages, j, start, rows):
+    span = pl.ds(start, rows)
+    total = held_ref[j >> 2, span] + swapped_ref[j >> 2, span]
+    for b, ref in enumerate(messages, 1):
         total = total + fixed_at(ref.at[j >> (b + 1)], start, rows)
     return total
 
@@ -277,34 +292,42 @@
     return block * jnp.exp2(scale - FIXED_BITS)
 
 
-def fold_kernel(level, vectors, held_ref, *refs):
+def fold_kernel(level, vectors, held_ref, swapped_ref, *refs):
     messages, out_ref = refs[:-1], refs[-1]
     for k in range(out_ref.shape[0]):
+        j = (2 * k + 1) << level
         blocks = [
-            group_block(held_ref, messages, (2 * k + 1) << level, start, vectors)
+            group_block(held_ref, swapped_ref, messages, j, start, vectors)
             for start in range(0, held_ref.shape[1], vectors)
         ]
         put_fixed(out_ref.at[k], blocks)
 
 
-def half_blocks(held_ref, messages, j, kept, vectors):
+def half_blocks(held_ref, swapped_ref, messages, j, kept, vectors):
     me = lax.axis_index("gx") & 1
     half = held_ref.shape[1] // 2
     base = pl.multiple_of((me if kept else 1 - me) * half, half)
     steps = range(0, half, vectors)
-    return [group_block(held_ref, messages, j, base + step, vectors) for step in steps]
-
-
-def spread_kernel(level, vectors, held_ref, *refs):
-    messages, (y_ref, diagonal_ref, x_ref) = refs[:-3], refs[-3:]
-    put_fixed(y_ref, half_blocks(held_ref, messages, 1 << level, True, vectors))
-    put_fixed(diagonal_ref, half_blocks(held_ref, messages, 1 << level, False, vectors))
-    put_fixed(x_ref, half_blocks(held_ref, messages, 0, False, vectors))
-
-
-def keep_kernel(vectors, held_ref, *refs):
+    return [
+        group_block(held_ref, swapped_ref, messages, j, base + step, vectors) for step in steps
+    ]
+
+
+def spread_kernel(level, vectors, held_ref, swapped_ref, *refs):
+    messages, (y_ref, diagonal_ref) = refs[:-2], refs[-2:]
+    for kept, out_ref in ((True, y_ref), (False, diagonal_ref)):
+        blocks = half_blocks(held_ref, swapped_ref, messages, 1 << level, kept, vectors)
+        put_fixed(out_ref, blocks)
+
+
+def send_kernel(vectors, held_ref, swapped_ref, *refs):
+    messages, out_ref = refs[:-1], refs[-1]
+    put_fixed(out_ref, half_blocks(held_ref, swapped_ref, messages, 0, False, vectors))
+
+
+def keep_kernel(vectors, held_ref, swapped_ref, *refs):
     messages, came, out_ref = refs[:-4], refs[-4:-1], refs[-1]
-    blocks = half_blocks(held_ref, messages, 0, True, vectors)
+    blocks = half_blocks(held_ref, swapped_ref, messages, 0, True, vectors)
     for p in range(len(blocks)):
         for ref in came:
             blocks[p] = blocks[p] + from_fixed(ref, vectors, p)
@@ -530,45 +553,61 @@
         ],
     )(*inputs)
     message = lambda rows, *lead: jax.ShapeDtypeStruct((*lead, rows + TAIL, vectors), jnp.int16)
-    swap, held = local_call(
-        functools.partial(margin_kernel, cells_x, cells_y, groups, own_ops),
-        "partial_margins",
+    part = jax.ShapeDtypeStruct((groups // 4, own_rows, vectors), f32)
+    dirs = in_hbm(op_dirs)
+    dirs_scratch = [pltpu.SMEM((count_ops,), jnp.int32), pltpu.SemaphoreType.DMA]
+    swap_a, fields, sides = local_call(
+        functools.partial(first_margin_kernel, cells_x, cells_y, groups, own_ops),
+        "first_margins",
         (
-            message(own_rows, groups // 2),
-            jax.ShapeDtypeStruct((groups // 2, own_rows, vectors), f32),
+            part,
+            jax.ShapeDtypeStruct((7, lines, order, vectors), f32),
+            jax.ShapeDtypeStruct((4, vectors, lines * order), bf16),
         ),
         [vmem_spec()] * 6 + [hbm_spec()],
-        (vmem_spec(),) * 2,
-        [
-            pltpu.VMEM((7, lines, order, vectors), f32),
-            pltpu.VMEM((4, vectors, lines * order), bf16),
-            pltpu.SMEM((count_ops,), jnp.int32),
-            pltpu.SemaphoreType.DMA,
-        ],
-    )(matrices, local, left, phases, halo_x, halo_y, in_hbm(op_dirs))
-
+        (vmem_spec(),) * 3,
+        dirs_scratch,
+    )(matrices, local, left, phases, halo_x, halo_y, dirs)
+    swapped_a = from_partner(swap_a, "gy", 1)
+    hold_a, swap_b, hold_b = local_call(
+        functools.partial(second_margin_kernel, groups, own_ops),
+        "second_margins",
+        (part,) * 3,
+        [vmem_spec()] * 3 + [hbm_spec()],
+        (vmem_spec(),) * 3,
+        dirs_scratch,
+    )(fields, sides, phases, dirs)
     def in_vmem(body, name, outs, *inputs):
         outs = outs if isinstance(outs, tuple) else (outs,)
         specs = (vmem_spec(),) * len(outs)
         return local_call(body, name, outs, [vmem_spec()] * len(inputs), specs)(*inputs)
 
     half = own_rows // 2
-    messages = [from_partner(swap, "gy", 1)]
+    messages = []
     last = levels - 1
+    if last > 1:
+        swapped_b = from_partner(swap_b, "gy", 1)
     for b in range(1, last):
         body = functools.partial(fold_kernel, b, vectors)
-        shape = message(own_rows, groups >> (b + 1))
-        (sent,) = in_vmem(body, "fold_groups", shape, held, *messages)
+        inputs = (hold_a, swapped_a) if b == 1 else (hold_b, swapped_b)
+        (sent,) = in_vmem(body, "fold_groups", message(own_rows, groups >> (b + 1)), *inputs, *messages)
         messages.append(from_partner(sent, "gy", 1 << b))
     body = functools.partial(spread_kernel, last, vectors)
-    for_y, for_both, for_x = in_vmem(body, "spread_halves", (message(half),) * 3, held, *messages)
+    inputs = (hold_a, swapped_a) if last == 1 else (hold_b, swapped_b)
+    for_y, for_both = in_vmem(body, "spread_halves", (message(half),) * 2, *inputs, *messages)
+    if last == 1:
+        for_y, for_both, swap_b = lax.optimization_barrier((for_y, for_both, swap_b))
+        swapped_b = from_partner(swap_b, "gy", 1)
+    own = (hold_b, swapped_b, *messages)
+    body = functools.partial(send_kernel, vectors)
+    (for_x,) = in_vmem(body, "send_half", message(half), *own)
     came = [
         from_partner(for_y, "gy", 1 << last),
         from_diagonal(for_both, ("gx", "gy"), lambda x, y: (x ^ 1, y ^ (1 << last))),
         from_partner(for_x, "gx", 1),
     ]
     body = functools.partial(keep_kernel, vectors)
-    (packed,) = in_vmem(body, "keep_half", message(half), held, *messages, *came)
+    (packed,) = in_vmem(body, "keep_half", message(half), *own, *came)
     norm_factor = 1.0 / math.sqrt(3.0 * cells_x * shares * cells_y * groups * cells_z)
     step = 2
     while step < shares:

time: 34.1 us -> 34.7 us (1.018)
  waiting for transfers between devices: 9.71 us -> 8.45 us
  Pallas kernels: 6.88 us -> 8.09 us
  starting transfers between devices: 16 us -> 16.6 us
    ppermute x5 -> x6, waiting for transfers between devices: 6.83 us -> 5.3 us  [from_partner(): return lax.ppermute(block, axis, [(i ^ step, i) for i in range(count)])]
    pallas_call x1 -> x2, Pallas kernels: 1.18 us -> 2.42 us  [the longest x1 1.33 us: per_device(): local_call(functools.partial(first_margin_kernel, cells_x, cells_y, group...]
    ppermute x5 -> x6, starting transfers between devices: 6.69 us -> 7.64 us  [from_partner(): return lax.ppermute(block, axis, [(i ^ step, i) for i in range(count)])]
    ppermute x2, starting transfers between devices: 1.97 us -> 1.6 us  [from_diagonal(): return lax.ppermute(block, axes, perm)]
  transfers between devices with their start and end apart: 10 -> 11, of which waited for: 8 -> 8; matrix products, arithmetic and copies ran while one was open for 0% -> 0% of each run, Pallas kernels for 11% -> 14%
where the time goes in v18:
time: 34.7 us; the launch traced here: 34.5 us
  starting transfers between devices  16.6 us (48%)
  waiting for transfers between devices  8.45 us (24%)
  Pallas kernels  8.09 us (23%)
  between operations  1.35 us (4%)
    ppermute x6, starting transfers between devices, from_partner(): return lax.ppermute(block, axis, [(i ^ step, i) for i in range(count)])  7.64 us
    ppermute x3, starting transfers between devices, from_step(): lax.ppermute(block, axis, [((i + step) % count, i) for i in range(count)])  7.34 us
    ppermute x6, waiting for transfers between devices, from_partner(): return lax.ppermute(block, axis, [(i ^ step, i) for i in range(count)])  5.3 us
    ppermute x2, waiting for transfers between devices, from_diagonal(): return lax.ppermute(block, axes, perm)  3 us
    pallas_call x1, Pallas kernels, per_device(): local_call(functools.partial(prepare_kernel, cells_x, cells_y), 'prepare_...  2.25 us
    ppermute x2, starting transfers between devices, from_diagonal(): return lax.ppermute(block, axes, perm)  1.6 us
    pallas_call x1, Pallas kernels, per_device(): local_call(functools.partial(second_contract_kernel, times, split), 'seco...  1.5 us
    pallas_call x1, Pallas kernels, per_device(): local_call(functools.partial(first_margin_kernel, cells_x, cells_y, group...  1.33 us
  transfers between devices with their start and end apart: 11, of which 8 were waited for; matrix products, arithmetic and copies ran while one was open for 0% of the time, Pallas kernels for 14%

profile of v18, /device:TPU:0, one launch (start us, length us, event | category | flops | bytes accessed | tf_op | source)
XLA Modules:
  0.0 34.5 jit_solution(4071138876679969326)
XLA Ops:
  0.6 5.1 %collective-permute-start = (bf16[1,2,144,128]{3,2,1,0:T(8,128)(2,1)}, bf16[1,2,144,128]{3,2,1,0:T(8,128)(2,1)S(1)}, u32[]{:S(2)}, u32[]{:S(2)}) collective-permute-start(bf16[1,2,144,128]{3,2,1,0:T(8,128)(2,1)} %bitcast.11), channel_id=1, source_target_pairs={{4,0},{8,4},{12,8},{0,12},{5,1},{9,5},{13,9},{1,13},{6,2},{10,6},{... | collective-permute-start | bytes 221192 | tf_op jit(solution)/shard_map/ppermute | solution.py:498
  5.7 0.7 %collective-permute-start.1 = (bf16[1,2,144,128]{3,2,1,0:T(8,128)(2,1)}, bf16[1,2,144,128]{3,2,1,0:T(8,128)(2,1)S(1)}, u32[]{:S(2)}, u32[]{:S(2)}) collective-permute-start(bf16[1,2,144,128]{3,2,1,0:T(8,128)(2,1)} %bitcast.12), channel_id=1, source_target_pairs={{1,0},{2,1},{3,2},{0,3},{5,4},{6,5},{7,6},{4,7},{9,8},{10,9},{11,1... | collective-permute-start | bytes 221192 | tf_op jit(solution)/shard_map/ppermute | solution.py:498
  6.4 2.3 %prepare_lines.1 = (bf16[3,144,128]{2,1,0:T(8,128)(2,1)S(1)}, f32[11,144,128]{2,1,0:T(8,128)S(1)}, bf16[2,128,288]{2,1,0:T(8,128)(2,1)S(1)}, f32[8,72,256]{2,1,0:T(8,128)S(1)}, f32[2,2,8,128]{3,2,1,0:T(8,128)S(1)}) custom-call(bf16[1,2,144,128]{3,2,1,0:T(8,128)(2,1)} %bitcast.13, bf16[2,27,2,24]{3,2,1,0:T(2,128)(2,1)} %bitcast.14, s32[8]{0:T(128)} %refs_3_.3, ...), custom_call_target="tpu_custom_call" | custom-call | tf_op jit(solution)/shard_map/prepare_lines/pallas_call | solution.py:537
  8.7 0.0 collective-permute-done.refs_4_
  8.7 0.0 collective-permute-done.1.refs_5_
  8.7 1.3 %first_margins.1 = (f32[1,512,128]{2,1,0:T(8,128)S(1)}, f32[7,2,144,128]{3,2,1,0:T(8,128)S(1)}, bf16[4,128,288]{2,1,0:T(8,128)(2,1)S(1)}) custom-call(bf16[3,144,128]{2,1,0:T(8,128)(2,1)S(1)} %get-tuple-element.22.refs_0_, f32[11,144,128]{2,1,0:T(8,128)S(1)} %get-tuple-element.23.refs_1_, bf16[2,128,288]{2,1,0:T(8,128)(2,1)S(1)} %get-tuple-element.24.refs_2_, ...), custom_call_target="tpu_custom_call" | custom-call | tf_op jit(solution)/shard_map/first_margins/pallas_call | solution.py:559
  10.0 1.0 %collective-permute-start.2 = (f32[1,512,128]{2,1,0:T(8,128)S(1)}, f32[1,512,128]{2,1,0:T(8,128)S(1)}, u32[]{:S(2)}, u32[]{:S(2)}) collective-permute-start(f32[1,512,128]{2,1,0:T(8,128)S(1)} %get-tuple-element.30), channel_id=1, source_target_pairs={{1,0},{0,1},{3,2},{2,3},{5,4},{4,5},{7,6},{6,7},{9,8},{8,9},{11,10... | collective-permute-start | bytes 786440 | tf_op jit(solution)/shard_map/ppermute | solution.py:503
  11.1 1.1 %second_margins.1 = (f32[1,512,128]{2,1,0:T(8,128)S(1)}, f32[1,512,128]{2,1,0:T(8,128)S(1)}, f32[1,512,128]{2,1,0:T(8,128)S(1)}) custom-call(f32[7,2,144,128]{3,2,1,0:T(8,128)S(1)} %get-tuple-element.26.refs_0_, bf16[4,128,288]{2,1,0:T(8,128)(2,1)S(1)} %get-tuple-element.27.refs_1_, f32[8,72,256]{2,1,0:T(8,128)S(1)} %get-tuple-element.25.refs_3_.refs_2_, ...), custom_call_target="tpu_custom_call" | custom-call | tf_op jit(solution)/shard_map/second_margins/pallas_call | solution.py:572
  12.2 0.1 collective-permute-done.2.swapped_ref
  12.2 0.0 copy-start
  12.2 0.1 spread_halves.1
  12.3 0.4 %collective-permute-start.3 = (f32[1,512,128]{2,1,0:T(8,128)S(1)}, f32[1,512,128]{2,1,0:T(8,128)S(1)}, u32[]{:S(2)}, u32[]{:S(2)}) collective-permute-start(f32[1,512,128]{2,1,0:T(8,128)S(1)} %get-tuple-element.34), channel_id=1, source_target_pairs={{1,0},{0,1},{3,2},{2,3},{5,4},{4,5},{7,6},{6,7},{9,8},{8,9},{11,10... | collective-permute-start | bytes 786440 | tf_op jit(solution)/shard_map/ppermute | solution.py:503
  12.8 1.1 %collective-permute-start.4 = (s16[272,128]{1,0:T(8,128)(2,1)S(1)}, s16[272,128]{1,0:T(8,128)(2,1)S(1)}, u32[]{:S(2)}, u32[]{:S(2)}) collective-permute-start(s16[272,128]{1,0:T(8,128)(2,1)S(1)} %get-tuple-element.35), channel_id=1, source_target_pairs={{2,0},{3,1},{0,2},{1,3},{6,4},{7,5},{4,6},{5,7},{10,8},{11,9},{8,1... | collective-permute-start | bytes 208904 | tf_op jit(solution)/shard_map/ppermute | solution.py:503
  13.9 0.0 collective-permute-start.5
  13.9 0.0 collective-permute-done.3.swapped_ref
  13.9 0.1 send_half.1
  14.0 2.4 %collective-permute-start.6 = (s16[272,128]{1,0:T(8,128)(2,1)S(1)}, s16[272,128]{1,0:T(8,128)(2,1)S(1)}, u32[]{:S(2)}, u32[]{:S(2)}) collective-permute-start(s16[272,128]{1,0:T(8,128)(2,1)S(1)} %send_half.1), channel_id=1, source_target_pairs={{4,0},{0,4},{12,8},{8,12},{5,1},{1,5},{13,9},{9,13},{6,2},{2,6},{1... | collective-permute-start | bytes 208904 | tf_op jit(solution)/shard_map/ppermute | solution.py:503
  16.4 0.7 %collective-permute-done.4.refs_0_ = s16[272,128]{1,0:T(8,128)(2,1)S(1)} collective-permute-done((s16[272,128]{1,0:T(8,128)(2,1)S(1)}, s16[272,128]{1,0:T(8,128)(2,1)S(1)}, u32[]{:S(2)}, u32[]{:S(2)}) %collective-permute-start.4) | collective-permute-done | bytes 69664 | tf_op jit(solution)/shard_map/ppermute | solution.py:503
  17.1 2.4 %collective-permute-done.5.refs_1_ = s16[272,128]{1,0:T(8,128)(2,1)S(1)} collective-permute-done((s16[272,128]{1,0:T(8,128)(2,1)S(1)}, s16[272,128]{1,0:T(8,128)(2,1)S(1)}, u32[]{:S(2)}, u32[]{:S(2)}) %collective-permute-start.5) | collective-permute-done | bytes 69664 | tf_op jit(solution)/shard_map/ppermute | solution.py:513
  19.5 0.2 collective-permute-done.6.refs_2_
  19.7 0.1 keep_half.1.own_ref
  19.8 2.2 %collective-permute-start.7 = (s16[272,128]{1,0:T(8,128)(2,1)S(1)}, s16[272,128]{1,0:T(8,128)(2,1)S(1)}, u32[]{:S(2)}, u32[]{:S(2)}) collective-permute-start(s16[272,128]{1,0:T(8,128)(2,1)S(1)} %keep_half.1.own_ref), channel_id=1, source_target_pairs={{8,0},{12,4},{0,8},{4,12},{9,1},{13,5},{1,9},{5,13},{10,2},{14,6},... | collective-permute-start | bytes 208904 | tf_op jit(solution)/shard_map/ppermute | solution.py:503
  22.0 3.8 %collective-permute-done.7.arrived_ref = s16[272,128]{1,0:T(8,128)(2,1)S(1)} collective-permute-done((s16[272,128]{1,0:T(8,128)(2,1)S(1)}, s16[272,128]{1,0:T(8,128)(2,1)S(1)}, u32[]{:S(2)}, u32[]{:S(2)}) %collective-permute-start.7) | collective-permute-done | bytes 69664 | tf_op jit(solution)/shard_map/ppermute | solution.py:503
  25.9 1.6 %collective-permute-start.9 = (bf16[256,128]{1,0:T(8,128)(2,1)S(1)}, bf16[256,128]{1,0:T(8,128)(2,1)S(1)}, u32[]{:S(2)}, u32[]{:S(2)}) collective-permute-start(bf16[256,128]{1,0:T(8,128)(2,1)S(1)} %finish_half.1.refs_0_.kept_ref.refs_2_), channel_id=1, source_target_pairs={{16,0},{0,16},{17,1},{1,17},{18,2},{2,18},{19,3},{3,19},{20,4},{4,... | collective-permute-start | bytes 196616 | tf_op jit(solution)/shard_map/ppermute | solution.py:498
  27.4 0.4 %collective-permute-start.8 = (bf16[256,128]{1,0:T(8,128)(2,1)S(1)}, bf16[256,128]{1,0:T(8,128)(2,1)S(1)}, u32[]{:S(2)}, u32[]{:S(2)}) collective-permute-start(bf16[256,128]{1,0:T(8,128)(2,1)S(1)} %finish_half.1.refs_0_.kept_ref.refs_2_), channel_id=1, source_target_pairs={{4,0},{0,4},{12,8},{8,12},{5,1},{1,5},{13,9},{9,13},{6,2},{2,6},{1... | collective-permute-start | bytes 196616 | tf_op jit(solution)/shard_map/ppermute | solution.py:503
  27.8 1.6 %collective-permute-start.10 = (bf16[256,128]{1,0:T(8,128)(2,1)S(1)}, bf16[256,128]{1,0:T(8,128)(2,1)S(1)}, u32[]{:S(2)}, u32[]{:S(2)}) collective-permute-start(bf16[256,128]{1,0:T(8,128)(2,1)S(1)} %finish_half.1.refs_0_.kept_ref.refs_2_), channel_id=1, source_target_pairs={{20,0},{16,4},{28,8},{24,12},{4,16},{0,20},{12,24},{8,28},{21,1},{... | collective-permute-start | bytes 196616 | tf_op jit(solution)/shard_map/ppermute | solution.py:513
  30.1 0.1 collective-permute-done.9.refs_1_.refs_3_
  30.2 0.0 copy-done
  30.2 0.9 %first_contraction.1 = (f32[8,128]{1,0:T(8,128)S(1)}, f32[2,32,128]{2,1,0:T(8,128)S(1)}) custom-call(s32[1]{0:T(128)S(6)} %copy.10.live_ref, f32[2,2,8,128]{3,2,1,0:T(8,128)S(1)} %get-tuple-element.37.weight_ref, bf16[2,512,512]{2,1,0:T(8,128)(2,1)S(1)} %bitcast.8, bf16[256,128]{1,0:T(8,128)(2,1)S(1)} %finish_half.1.refs_0_.kept_ref.refs_2_, ...), custom_call_target="tpu_custom_call" | custom-call | tf_op jit(solution)/shard_map/first_contraction/pallas_call | solution.py:633
  31.1 0.6 %collective-permute-done.8.other_ref.refs_0_ = bf16[256,128]{1,0:T(8,128)(2,1)S(1)} collective-permute-done((bf16[256,128]{1,0:T(8,128)(2,1)S(1)}, bf16[256,128]{1,0:T(8,128)(2,1)S(1)}, u32[]{:S(2)}, u32[]{:S(2)}) %collective-permute-start.8) | collective-permute-done | bytes 65568 | tf_op jit(solution)/shard_map/ppermute | solution.py:503
  31.7 0.7 %margins_out.1 = f32[1,512,128]{2,1,0:T(8,128)} custom-call(bf16[256,128]{1,0:T(8,128)(2,1)S(1)} %finish_half.1.refs_0_.kept_ref.refs_2_, bf16[256,128]{1,0:T(8,128)(2,1)S(1)} %collective-permute-done.8.other_ref.refs_0_), custom_call_target="tpu_custom_call" | custom-call | tf_op jit(solution)/shard_map/margins_out/pallas_call | solution.py:641
  32.4 0.6 %collective-permute-done.10.refs_1_ = bf16[256,128]{1,0:T(8,128)(2,1)S(1)} collective-permute-done((bf16[256,128]{1,0:T(8,128)(2,1)S(1)}, bf16[256,128]{1,0:T(8,128)(2,1)S(1)}, u32[]{:S(2)}, u32[]{:S(2)}) %collective-permute-start.10) | collective-permute-done | bytes 65568 | tf_op jit(solution)/shard_map/ppermute | solution.py:513
  33.0 1.5 %second_contraction.1 = f32[1,2,2]{2,1,0:T(2,128)} custom-call(f32[2,2,8,128]{3,2,1,0:T(8,128)S(1)} %get-tuple-element.37.weight_ref, bf16[2,512,512]{2,1,0:T(8,128)(2,1)S(1)} %bitcast.9, bf16[256,128]{1,0:T(8,128)(2,1)S(1)} %collective-permute-done.8.other_ref.refs_0_, bf16[256,128]{1,0:T(8,128)(2,1)S(1)} %collective-permute-done.10.refs_1_, ...), custom_call_target="tpu_custom_call" | custom-call | tf_op jit(solution)/shard_map/second_contraction/pallas_call | solution.py:648
  (1 shorter events, 0.0 us)
Async XLA Ops:
  0.6 8.0 %collective-permute-start = (bf16[1,2,144,128]{3,2,1,0:T(8,128)(2,1)}, bf16[1,2,144,128]{3,2,1,0:T(8,128)(2,1)S(1)}, u32[]{:S(2)}, u32[]{:S(2)}) collective-permute-start(bf16[1,2,144,128]{3,2,1,0:T(8,128)(2,1)} %bitcast.11), channel_id=1, source_target_pairs={{4,0},{8,4},{12,8},{0,12},{5,1},{9,5},{13,9},{1,13},{6,2},{10,6},{... | collective-permute-start | bytes 221192 | tf_op jit(solution)/shard_map/ppermute | solution.py:498
  5.7 3.0 %collective-permute-start.1 = (bf16[1,2,144,128]{3,2,1,0:T(8,128)(2,1)}, bf16[1,2,144,128]{3,2,1,0:T(8,128)(2,1)S(1)}, u32[]{:S(2)}, u32[]{:S(2)}) collective-permute-start(bf16[1,2,144,128]{3,2,1,0:T(8,128)(2,1)} %bitcast.12), channel_id=1, source_target_pairs={{1,0},{2,1},{3,2},{0,3},{5,4},{6,5},{7,6},{4,7},{9,8},{10,9},{11,1... | collective-permute-start | bytes 221192 | tf_op jit(solution)/shard_map/ppermute | solution.py:498
  10.0 2.2 %collective-permute-start.2 = (f32[1,512,128]{2,1,0:T(8,128)S(1)}, f32[1,512,128]{2,1,0:T(8,128)S(1)}, u32[]{:S(2)}, u32[]{:S(2)}) collective-permute-start(f32[1,512,128]{2,1,0:T(8,128)S(1)} %get-tuple-element.30), channel_id=1, source_target_pairs={{1,0},{0,1},{3,2},{2,3},{5,4},{4,5},{7,6},{6,7},{9,8},{8,9},{11,10... | collective-permute-start | bytes 786440 | tf_op jit(solution)/shard_map/ppermute | solution.py:503
  12.2 18.0 %copy-start = (bf16[1,2,512,512]{3,2,1,0:T(8,128)(2,1)S(1)}, bf16[1,2,512,512]{3,2,1,0:T(8,128)(2,1)}, u32[]{:S(2)}) copy-start(bf16[1,2,512,512]{3,2,1,0:T(8,128)(2,1)} %param.12) | copy-start | bytes 3145732
  12.3 1.6 %collective-permute-start.3 = (f32[1,512,128]{2,1,0:T(8,128)S(1)}, f32[1,512,128]{2,1,0:T(8,128)S(1)}, u32[]{:S(2)}, u32[]{:S(2)}) collective-permute-start(f32[1,512,128]{2,1,0:T(8,128)S(1)} %get-tuple-element.34), channel_id=1, source_target_pairs={{1,0},{0,1},{3,2},{2,3},{5,4},{4,5},{7,6},{6,7},{9,8},{8,9},{11,10... | collective-permute-start | bytes 786440 | tf_op jit(solution)/shard_map/ppermute | solution.py:503
  12.8 4.3 %collective-permute-start.4 = (s16[272,128]{1,0:T(8,128)(2,1)S(1)}, s16[272,128]{1,0:T(8,128)(2,1)S(1)}, u32[]{:S(2)}, u32[]{:S(2)}) collective-permute-start(s16[272,128]{1,0:T(8,128)(2,1)S(1)} %get-tuple-element.35), channel_id=1, source_target_pairs={{2,0},{3,1},{0,2},{1,3},{6,4},{7,5},{4,6},{5,7},{10,8},{11,9},{8,1... | collective-permute-start | bytes 208904 | tf_op jit(solution)/shard_map/ppermute | solution.py:503
  13.9 5.6 %collective-permute-start.5 = (s16[272,128]{1,0:T(8,128)(2,1)S(1)}, s16[272,128]{1,0:T(8,128)(2,1)S(1)}, u32[]{:S(2)}, u32[]{:S(2)}) collective-permute-start(s16[272,128]{1,0:T(8,128)(2,1)S(1)} %get-tuple-element.36), channel_id=1, source_target_pairs={{6,0},{7,1},{4,2},{5,3},{2,4},{3,5},{0,6},{1,7},{14,8},{15,9},{12,... | collective-permute-start | bytes 208904 | tf_op jit(solution)/shard_map/ppermute | solution.py:513
  14.0 5.7 %collective-permute-start.6 = (s16[272,128]{1,0:T(8,128)(2,1)S(1)}, s16[272,128]{1,0:T(8,128)(2,1)S(1)}, u32[]{:S(2)}, u32[]{:S(2)}) collective-permute-start(s16[272,128]{1,0:T(8,128)(2,1)S(1)} %send_half.1), channel_id=1, source_target_pairs={{4,0},{0,4},{12,8},{8,12},{5,1},{1,5},{13,9},{9,13},{6,2},{2,6},{1... | collective-permute-start | bytes 208904 | tf_op jit(solution)/shard_map/ppermute | solution.py:503
  19.8 6.0 %collective-permute-start.7 = (s16[272,128]{1,0:T(8,128)(2,1)S(1)}, s16[272,128]{1,0:T(8,128)(2,1)S(1)}, u32[]{:S(2)}, u32[]{:S(2)}) collective-permute-start(s16[272,128]{1,0:T(8,128)(2,1)S(1)} %keep_half.1.own_ref), channel_id=1, source_target_pairs={{8,0},{12,4},{0,8},{4,12},{9,1},{13,5},{1,9},{5,13},{10,2},{14,6},... | collective-permute-start | bytes 208904 | tf_op jit(solution)/shard_map/ppermute | solution.py:503
  25.9 4.3 %collective-permute-start.9 = (bf16[256,128]{1,0:T(8,128)(2,1)S(1)}, bf16[256,128]{1,0:T(8,128)(2,1)S(1)}, u32[]{:S(2)}, u32[]{:S(2)}) collective-permute-start(bf16[256,128]{1,0:T(8,128)(2,1)S(1)} %finish_half.1.refs_0_.kept_ref.refs_2_), channel_id=1, source_target_pairs={{16,0},{0,16},{17,1},{1,17},{18,2},{2,18},{19,3},{3,19},{20,4},{4,... | collective-permute-start | bytes 196616 | tf_op jit(solution)/shard_map/ppermute | solution.py:498
  27.4 4.3 %collective-permute-start.8 = (bf16[256,128]{1,0:T(8,128)(2,1)S(1)}, bf16[256,128]{1,0:T(8,128)(2,1)S(1)}, u32[]{:S(2)}, u32[]{:S(2)}) collective-permute-start(bf16[256,128]{1,0:T(8,128)(2,1)S(1)} %finish_half.1.refs_0_.kept_ref.refs_2_), channel_id=1, source_target_pairs={{4,0},{0,4},{12,8},{8,12},{5,1},{1,5},{13,9},{9,13},{6,2},{2,6},{1... | collective-permute-start | bytes 196616 | tf_op jit(solution)/shard_map/ppermute | solution.py:503
  27.8 5.2 %collective-permute-start.10 = (bf16[256,128]{1,0:T(8,128)(2,1)S(1)}, bf16[256,128]{1,0:T(8,128)(2,1)S(1)}, u32[]{:S(2)}, u32[]{:S(2)}) collective-permute-start(bf16[256,128]{1,0:T(8,128)(2,1)S(1)} %finish_half.1.refs_0_.kept_ref.refs_2_), channel_id=1, source_target_pairs={{20,0},{16,4},{28,8},{24,12},{4,16},{0,20},{12,24},{8,28},{21,1},{... | collective-permute-start | bytes 196616 | tf_op jit(solution)/shard_map/ppermute | solution.py:513

commit v19 on v13

--- a/solution.py
+++ b/solution.py
@@ -84,8 +84,8 @@
 
 def prepare_kernel(cells_x, cells_y, *refs):
     inputs, refs = refs[:6], refs[6:]
-    matrix_ref, local_ref, left_ref, phase_ref, weight_ref = refs[:5]
-    held, link_rows_ref, sems = refs[5:11], refs[11], refs[12]
+    matrix_ref, local_ref, left_ref, phase_ref, weight_ref, code_ref = refs[:6]
+    held, link_rows_ref, sems = refs[6:12], refs[12], refs[13]
     copies = [
         pltpu.make_async_copy(src, dst, sems.at[k])
         for k, (src, dst) in enumerate(zip(inputs, held))
@@ -177,6 +177,7 @@
     term = (row >= per_term).astype(jnp.int32) + (row >= 2 * per_term).astype(jnp.int32)
     wave_at = row - per_term * term - (col >= vectors).astype(jnp.int32)
     for o in range(phase_ref.shape[0]):
+        code_ref[o] = jnp.full(code_ref.shape[1:], dirs_ref[o], jnp.int32).astype(f32)
         column = 2 * (jnp.where(dirs_ref[o] == 5, MOMENTA, 0) + moms_ref[o])
         phase_ref[o] = jnp.dot(
             waves_ref[...], one_hot(wave_at == column), preferred_element_type=f32
@@ -184,12 +185,14 @@
 
 
 def margin_kernel(cells_x, cells_y, groups, own_ops, *refs):
-    matrix_ref, local_ref, left_ref, phase_ref, halo_x_ref, halo_y_ref, dirs_hbm = refs[:7]
-    swap_ref, hold_ref = refs[7:9]
-    field_ref, side_ref, dirs_ref, sem = refs[9:]
+    matrix_ref, local_ref, left_ref, phase_ref, code_ref, halo_x_ref, halo_y_ref = refs[:7]
+    swap_ref, hold_ref, field_ref, side_ref = refs[7:]
     f32, bf16 = jnp.float32, jnp.bfloat16
-    copy = pltpu.make_async_copy(dirs_hbm, dirs_ref, sem)
-    copy.start()
+    me = lax.axis_index("gy")
+    codes = {}
+    for j in range(groups):
+        for i in range(own_ops):
+            codes[j, i] = jnp.max(code_ref[(me ^ j) * own_ops + i]).astype(jnp.int32)
     lines = cells_x * cells_y
     order, vectors = halo_x_ref.shape[2], halo_x_ref.shape[3]
     half = order // 2
@@ -212,13 +215,11 @@
             field_ref[d, line] = transport(matrix[:, :half], side_by_side(ahead), 1)
     for k, (code, line) in enumerate(local_fields(cells_x, cells_y)):
         field_ref[code, line] = local_ref[k]
-    copy.wait()
-    me = lax.axis_index("gy")
     for j in sorted(range(groups), key=lambda j: -(j & 1)):
         blocks = []
         for i in range(own_ops):
             o = (me ^ j) * own_ops + i
-            code = dirs_ref[o]
+            code = codes[j, i]
             side = jnp.where((code >= 3) & (code < 6), code - 2, 0)
             cosine = phase_ref[o, :, 0:vectors]
             sine = phase_ref[o, :, vectors : 2 * vectors]
@@ -511,7 +512,7 @@
         pltpu.SMEM(x.shape, x.dtype) if x.dtype == jnp.int32 else pltpu.VMEM(x.shape, x.dtype)
         for x in inputs
     ]
-    matrices, local, left, phases, weights = local_call(
+    matrices, local, left, phases, weights, codes = local_call(
         functools.partial(prepare_kernel, cells_x, cells_y),
         "prepare_lines",
         (
@@ -520,9 +521,10 @@
             jax.ShapeDtypeStruct((2, vectors, lines * order), bf16),
             jax.ShapeDtypeStruct((count_ops, order // 2, 2 * vectors), f32),
             jax.ShapeDtypeStruct((2, times, 8, vectors), f32),
+            jax.ShapeDtypeStruct((count_ops, 8, vectors), f32),
         ),
         [hbm_spec()] * len(inputs),
-        (vmem_spec(),) * 5,
+        (vmem_spec(),) * 6,
         held
         + [
             pltpu.VMEM((lines, LINK_COLS, cells_z), f32),
@@ -537,15 +539,13 @@
             message(own_rows, groups // 2),
             jax.ShapeDtypeStruct((groups // 2, own_rows, vectors), f32),
         ),
-        [vmem_spec()] * 6 + [hbm_spec()],
+        [vmem_spec()] * 7,
         (vmem_spec(),) * 2,
         [
             pltpu.VMEM((7, lines, order, vectors), f32),
             pltpu.VMEM((4, vectors, lines * order), bf16),
-            pltpu.SMEM((count_ops,), jnp.int32),
-            pltpu.SemaphoreType.DMA,
         ],
-    )(matrices, local, left, phases, halo_x, halo_y, in_hbm(op_dirs))
+    )(matrices, local, left, phases, codes, halo_x, halo_y)
 
     def in_vmem(body, name, outs, *inputs):
         outs = outs if isinstance(outs, tuple) else (outs,)

time: 34.1 us -> 34 us (level)
  no operation moved by 1% of the time
where the time goes in v19:
time: 34 us; the launch traced here: 33.8 us
  starting transfers between devices  16 us (47%)
  waiting for transfers between devices  9.71 us (29%)
  Pallas kernels  6.78 us (20%)
  between operations  1.34 us (4%)
    ppermute x3, starting transfers between devices, from_step(): lax.ppermute(block, axis, [((i + step) % count, i) for i in range(count)])  7.34 us
    ppermute x5, waiting for transfers between devices, from_partner(): return lax.ppermute(block, axis, [(i ^ step, i) for i in range(count)])  6.83 us
    ppermute x5, starting transfers between devices, from_partner(): return lax.ppermute(block, axis, [(i ^ step, i) for i in range(count)])  6.69 us
    ppermute x2, waiting for transfers between devices, from_diagonal(): return lax.ppermute(block, axes, perm)  2.72 us
    pallas_call x1, Pallas kernels, per_device(): local_call(functools.partial(prepare_kernel, cells_x, cells_y), 'prepare_...  2.25 us
    ppermute x2, starting transfers between devices, from_diagonal(): return lax.ppermute(block, axes, perm)  1.97 us
    pallas_call x1, Pallas kernels, per_device(): local_call(functools.partial(second_contract_kernel, times, split), 'seco...  1.5 us
    pallas_call x1, Pallas kernels, per_device(): local_call(functools.partial(margin_kernel, cells_x, cells_y, groups, own...  1.08 us
  transfers between devices with their start and end apart: 10, of which 8 were waited for; matrix products, arithmetic and copies ran while one was open for 0% of the time, Pallas kernels for 11%

profile of v19, /device:TPU:0, one launch (start us, length us, event | category | flops | bytes accessed | tf_op | source)
XLA Modules:
  0.0 33.8 jit_solution(4670824673598710996)
XLA Ops:
  0.6 5.1 %collective-permute-start = (bf16[1,2,144,128]{3,2,1,0:T(8,128)(2,1)}, bf16[1,2,144,128]{3,2,1,0:T(8,128)(2,1)S(1)}, u32[]{:S(2)}, u32[]{:S(2)}) collective-permute-start(bf16[1,2,144,128]{3,2,1,0:T(8,128)(2,1)} %bitcast.11), channel_id=1, source_target_pairs={{4,0},{8,4},{12,8},{0,12},{5,1},{9,5},{13,9},{1,13},{6,2},{10,6},{... | collective-permute-start | bytes 221192 | tf_op jit(solution)/shard_map/ppermute | solution.py:476
  5.7 0.7 %collective-permute-start.1 = (bf16[1,2,144,128]{3,2,1,0:T(8,128)(2,1)}, bf16[1,2,144,128]{3,2,1,0:T(8,128)(2,1)S(1)}, u32[]{:S(2)}, u32[]{:S(2)}) collective-permute-start(bf16[1,2,144,128]{3,2,1,0:T(8,128)(2,1)} %bitcast.12), channel_id=1, source_target_pairs={{1,0},{2,1},{3,2},{0,3},{5,4},{6,5},{7,6},{4,7},{9,8},{10,9},{11,1... | collective-permute-start | bytes 221192 | tf_op jit(solution)/shard_map/ppermute | solution.py:476
  6.4 2.3 %prepare_lines.1 = (bf16[3,144,128]{2,1,0:T(8,128)(2,1)S(1)}, f32[11,144,128]{2,1,0:T(8,128)S(1)}, bf16[2,128,288]{2,1,0:T(8,128)(2,1)S(1)}, f32[8,72,256]{2,1,0...) custom-call(bf16[1,2,144,128]{3,2,1,0:T(8,128)(2,1)} %bitcast.13, bf16[2,27,2,24]{3,2,1,0:T(2,128)(2,1)} %bitcast.14, ...), custom_call_target="tpu_custom_call" | custom-call | tf_op jit(solution)/shard_map/prepare_lines/pallas_call | solution.py:515
  8.7 0.0 collective-permute-done.refs_5_
  8.7 0.0 collective-permute-done.1.refs_6_
  8.7 1.1 %partial_margins.1 = (s16[2,528,128]{2,1,0:T(8,128)(2,1)S(1)}, f32[2,512,128]{2,1,0:T(8,128)S(1)}) custom-call(bf16[3,144,128]{2,1,0:T(8,128)(2,1)S(1)} %get-tuple-element.17.refs_0_, f32[11,144,128]{2,1,0:T(8,128)S(1)} %get-tuple-element.18.refs_1_, bf16[2,128,288]{2,1,0:T(8,128)(2,1)S(1)} %get-tuple-element.19.refs_2_, ...), custom_call_target="tpu_custom_call" | custom-call | tf_op jit(solution)/shard_map/partial_margins/pallas_call | solution.py:535
  9.8 0.0 copy-start
  9.8 1.0 %collective-permute-start.2 = (s16[2,528,128]{2,1,0:T(8,128)(2,1)S(1)}, s16[2,528,128]{2,1,0:T(8,128)(2,1)S(1)}, u32[]{:S(2)}, u32[]{:S(2)}) collective-permute-start(s16[2,528,128]{2,1,0:T(8,128)(2,1)S(1)} %get-tuple-element.23), channel_id=1, source_target_pairs={{1,0},{0,1},{3,2},{2,3},{5,4},{4,5},{7,6},{6,7},{9,8},{8,9},{11,10... | collective-permute-start | bytes 811016 | tf_op jit(solution)/shard_map/ppermute | solution.py:481
  10.8 1.2 %collective-permute-done.2.refs_0_ = s16[2,528,128]{2,1,0:T(8,128)(2,1)S(1)} collective-permute-done((s16[2,528,128]{2,1,0:T(8,128)(2,1)S(1)}, s16[2,528,128]{2,1,0:T(8,128)(2,1)S(1)}, u32[]{:S(2)}, u32[]{:S(2)}) %collective-permute-start.2) | collective-permute-done | bytes 270368 | tf_op jit(solution)/shard_map/ppermute | solution.py:481
  12.0 0.2 spread_halves.1
  12.2 1.2 %collective-permute-start.3 = (s16[272,128]{1,0:T(8,128)(2,1)S(1)}, s16[272,128]{1,0:T(8,128)(2,1)S(1)}, u32[]{:S(2)}, u32[]{:S(2)}) collective-permute-start(s16[272,128]{1,0:T(8,128)(2,1)S(1)} %get-tuple-element.24), channel_id=1, source_target_pairs={{2,0},{3,1},{0,2},{1,3},{6,4},{7,5},{4,6},{5,7},{10,8},{11,9},{8,1... | collective-permute-start | bytes 208904 | tf_op jit(solution)/shard_map/ppermute | solution.py:481
  13.4 0.0 collective-permute-start.4
  13.4 2.3 %collective-permute-start.5 = (s16[272,128]{1,0:T(8,128)(2,1)S(1)}, s16[272,128]{1,0:T(8,128)(2,1)S(1)}, u32[]{:S(2)}, u32[]{:S(2)}) collective-permute-start(s16[272,128]{1,0:T(8,128)(2,1)S(1)} %get-tuple-element.26), channel_id=1, source_target_pairs={{4,0},{0,4},{12,8},{8,12},{5,1},{1,5},{13,9},{9,13},{6,2},{2,6},{1... | collective-permute-start | bytes 208904 | tf_op jit(solution)/shard_map/ppermute | solution.py:481
  15.7 1.0 %collective-permute-done.3.refs_1_ = s16[272,128]{1,0:T(8,128)(2,1)S(1)} collective-permute-done((s16[272,128]{1,0:T(8,128)(2,1)S(1)}, s16[272,128]{1,0:T(8,128)(2,1)S(1)}, u32[]{:S(2)}, u32[]{:S(2)}) %collective-permute-start.3) | collective-permute-done | bytes 69664 | tf_op jit(solution)/shard_map/ppermute | solution.py:481
  16.7 2.5 %collective-permute-done.4.refs_2_ = s16[272,128]{1,0:T(8,128)(2,1)S(1)} collective-permute-done((s16[272,128]{1,0:T(8,128)(2,1)S(1)}, s16[272,128]{1,0:T(8,128)(2,1)S(1)}, u32[]{:S(2)}, u32[]{:S(2)}) %collective-permute-start.4) | collective-permute-done | bytes 69664 | tf_op jit(solution)/shard_map/ppermute | solution.py:491
  19.2 0.2 collective-permute-done.5.refs_3_
  19.4 0.1 keep_half.1.own_ref
  19.5 2.1 %collective-permute-start.6 = (s16[272,128]{1,0:T(8,128)(2,1)S(1)}, s16[272,128]{1,0:T(8,128)(2,1)S(1)}, u32[]{:S(2)}, u32[]{:S(2)}) collective-permute-start(s16[272,128]{1,0:T(8,128)(2,1)S(1)} %keep_half.1.own_ref), channel_id=1, source_target_pairs={{8,0},{12,4},{0,8},{4,12},{9,1},{13,5},{1,9},{5,13},{10,2},{14,6},... | collective-permute-start | bytes 208904 | tf_op jit(solution)/shard_map/ppermute | solution.py:481
  21.6 3.9 %collective-permute-done.6.arrived_ref = s16[272,128]{1,0:T(8,128)(2,1)S(1)} collective-permute-done((s16[272,128]{1,0:T(8,128)(2,1)S(1)}, s16[272,128]{1,0:T(8,128)(2,1)S(1)}, u32[]{:S(2)}, u32[]{:S(2)}) %collective-permute-start.6) | collective-permute-done | bytes 69664 | tf_op jit(solution)/shard_map/ppermute | solution.py:481
  25.6 1.6 %collective-permute-start.8 = (bf16[256,128]{1,0:T(8,128)(2,1)S(1)}, bf16[256,128]{1,0:T(8,128)(2,1)S(1)}, u32[]{:S(2)}, u32[]{:S(2)}) collective-permute-start(bf16[256,128]{1,0:T(8,128)(2,1)S(1)} %finish_half.1.refs_0_.kept_ref.refs_2_), channel_id=1, source_target_pairs={{16,0},{0,16},{17,1},{1,17},{18,2},{2,18},{19,3},{3,19},{20,4},{4,... | collective-permute-start | bytes 196616 | tf_op jit(solution)/shard_map/ppermute | solution.py:476
  27.1 0.0 collective-permute-start.7
  27.2 2.0 %collective-permute-start.9 = (bf16[256,128]{1,0:T(8,128)(2,1)S(1)}, bf16[256,128]{1,0:T(8,128)(2,1)S(1)}, u32[]{:S(2)}, u32[]{:S(2)}) collective-permute-start(bf16[256,128]{1,0:T(8,128)(2,1)S(1)} %finish_half.1.refs_0_.kept_ref.refs_2_), channel_id=1, source_target_pairs={{20,0},{16,4},{28,8},{24,12},{4,16},{0,20},{12,24},{8,28},{21,1},{... | collective-permute-start | bytes 196616 | tf_op jit(solution)/shard_map/ppermute | solution.py:491
  29.8 0.1 collective-permute-done.8.refs_1_.refs_3_
  29.9 0.0 copy-done
  29.9 0.9 %first_contraction.1 = (f32[8,128]{1,0:T(8,128)S(1)}, f32[2,32,128]{2,1,0:T(8,128)S(1)}) custom-call(s32[1]{0:T(128)S(6)} %copy.10.live_ref, f32[2,2,8,128]{3,2,1,0:T(8,128)S(1)} %get-tuple-element.27.weight_ref, bf16[2,512,512]{2,1,0:T(8,128)(2,1)S(1)} %bitcast.8, bf16[256,128]{1,0:T(8,128)(2,1)S(1)} %finish_half.1.refs_0_.kept_ref.refs_2_, ...), custom_call_target="tpu_custom_call" | custom-call | tf_op jit(solution)/shard_map/first_contraction/pallas_call | solution.py:594
  30.8 0.6 %collective-permute-done.7.other_ref.refs_0_ = bf16[256,128]{1,0:T(8,128)(2,1)S(1)} collective-permute-done((bf16[256,128]{1,0:T(8,128)(2,1)S(1)}, bf16[256,128]{1,0:T(8,128)(2,1)S(1)}, u32[]{:S(2)}, u32[]{:S(2)}) %collective-permute-start.7) | collective-permute-done | bytes 65568 | tf_op jit(solution)/shard_map/ppermute | solution.py:481
  31.4 0.7 %margins_out.1 = f32[1,512,128]{2,1,0:T(8,128)} custom-call(bf16[256,128]{1,0:T(8,128)(2,1)S(1)} %finish_half.1.refs_0_.kept_ref.refs_2_, bf16[256,128]{1,0:T(8,128)(2,1)S(1)} %collective-permute-done.7.other_ref.refs_0_), custom_call_target="tpu_custom_call" | custom-call | tf_op jit(solution)/shard_map/margins_out/pallas_call | solution.py:602
  32.1 0.2 collective-permute-done.9.refs_1_
  32.3 1.5 %second_contraction.1 = f32[1,2,2]{2,1,0:T(2,128)} custom-call(f32[2,2,8,128]{3,2,1,0:T(8,128)S(1)} %get-tuple-element.27.weight_ref, bf16[2,512,512]{2,1,0:T(8,128)(2,1)S(1)} %bitcast.9, bf16[256,128]{1,0:T(8,128)(2,1)S(1)} %collective-permute-done.7.other_ref.refs_0_, bf16[256,128]{1,0:T(8,128)(2,1)S(1)} %collective-permute-done.9.refs_1_, ...), custom_call_target="tpu_custom_call" | custom-call | tf_op jit(solution)/shard_map/second_contraction/pallas_call | solution.py:609
  (1 shorter events, 0.0 us)
Async XLA Ops:
  0.6 8.0 %collective-permute-start = (bf16[1,2,144,128]{3,2,1,0:T(8,128)(2,1)}, bf16[1,2,144,128]{3,2,1,0:T(8,128)(2,1)S(1)}, u32[]{:S(2)}, u32[]{:S(2)}) collective-permute-start(bf16[1,2,144,128]{3,2,1,0:T(8,128)(2,1)} %bitcast.11), channel_id=1, source_target_pairs={{4,0},{8,4},{12,8},{0,12},{5,1},{9,5},{13,9},{1,13},{6,2},{10,6},{... | collective-permute-start | bytes 221192 | tf_op jit(solution)/shard_map/ppermute | solution.py:476
  5.7 3.0 %collective-permute-start.1 = (bf16[1,2,144,128]{3,2,1,0:T(8,128)(2,1)}, bf16[1,2,144,128]{3,2,1,0:T(8,128)(2,1)S(1)}, u32[]{:S(2)}, u32[]{:S(2)}) collective-permute-start(bf16[1,2,144,128]{3,2,1,0:T(8,128)(2,1)} %bitcast.12), channel_id=1, source_target_pairs={{1,0},{2,1},{3,2},{0,3},{5,4},{6,5},{7,6},{4,7},{9,8},{10,9},{11,1... | collective-permute-start | bytes 221192 | tf_op jit(solution)/shard_map/ppermute | solution.py:476
  9.8 20.1 %copy-start = (bf16[1,2,512,512]{3,2,1,0:T(8,128)(2,1)S(1)}, bf16[1,2,512,512]{3,2,1,0:T(8,128)(2,1)}, u32[]{:S(2)}) copy-start(bf16[1,2,512,512]{3,2,1,0:T(8,128)(2,1)} %param.12) | copy-start | bytes 3145732
  9.8 2.2 %collective-permute-start.2 = (s16[2,528,128]{2,1,0:T(8,128)(2,1)S(1)}, s16[2,528,128]{2,1,0:T(8,128)(2,1)S(1)}, u32[]{:S(2)}, u32[]{:S(2)}) collective-permute-start(s16[2,528,128]{2,1,0:T(8,128)(2,1)S(1)} %get-tuple-element.23), channel_id=1, source_target_pairs={{1,0},{0,1},{3,2},{2,3},{5,4},{4,5},{7,6},{6,7},{9,8},{8,9},{11,10... | collective-permute-start | bytes 811016 | tf_op jit(solution)/shard_map/ppermute | solution.py:481
  12.2 4.5 %collective-permute-start.3 = (s16[272,128]{1,0:T(8,128)(2,1)S(1)}, s16[272,128]{1,0:T(8,128)(2,1)S(1)}, u32[]{:S(2)}, u32[]{:S(2)}) collective-permute-start(s16[272,128]{1,0:T(8,128)(2,1)S(1)} %get-tuple-element.24), channel_id=1, source_target_pairs={{2,0},{3,1},{0,2},{1,3},{6,4},{7,5},{4,6},{5,7},{10,8},{11,9},{8,1... | collective-permute-start | bytes 208904 | tf_op jit(solution)/shard_map/ppermute | solution.py:481
  13.4 5.8 %collective-permute-start.4 = (s16[272,128]{1,0:T(8,128)(2,1)S(1)}, s16[272,128]{1,0:T(8,128)(2,1)S(1)}, u32[]{:S(2)}, u32[]{:S(2)}) collective-permute-start(s16[272,128]{1,0:T(8,128)(2,1)S(1)} %get-tuple-element.25), channel_id=1, source_target_pairs={{6,0},{7,1},{4,2},{5,3},{2,4},{3,5},{0,6},{1,7},{14,8},{15,9},{12,... | collective-permute-start | bytes 208904 | tf_op jit(solution)/shard_map/ppermute | solution.py:491
  13.4 6.0 %collective-permute-start.5 = (s16[272,128]{1,0:T(8,128)(2,1)S(1)}, s16[272,128]{1,0:T(8,128)(2,1)S(1)}, u32[]{:S(2)}, u32[]{:S(2)}) collective-permute-start(s16[272,128]{1,0:T(8,128)(2,1)S(1)} %get-tuple-element.26), channel_id=1, source_target_pairs={{4,0},{0,4},{12,8},{8,12},{5,1},{1,5},{13,9},{9,13},{6,2},{2,6},{1... | collective-permute-start | bytes 208904 | tf_op jit(solution)/shard_map/ppermute | solution.py:481
  19.5 6.0 %collective-permute-start.6 = (s16[272,128]{1,0:T(8,128)(2,1)S(1)}, s16[272,128]{1,0:T(8,128)(2,1)S(1)}, u32[]{:S(2)}, u32[]{:S(2)}) collective-permute-start(s16[272,128]{1,0:T(8,128)(2,1)S(1)} %keep_half.1.own_ref), channel_id=1, source_target_pairs={{8,0},{12,4},{0,8},{4,12},{9,1},{13,5},{1,9},{5,13},{10,2},{14,6},... | collective-permute-start | bytes 208904 | tf_op jit(solution)/shard_map/ppermute | solution.py:481
  25.6 4.3 %collective-permute-start.8 = (bf16[256,128]{1,0:T(8,128)(2,1)S(1)}, bf16[256,128]{1,0:T(8,128)(2,1)S(1)}, u32[]{:S(2)}, u32[]{:S(2)}) collective-permute-start(bf16[256,128]{1,0:T(8,128)(2,1)S(1)} %finish_half.1.refs_0_.kept_ref.refs_2_), channel_id=1, source_target_pairs={{16,0},{0,16},{17,1},{1,17},{18,2},{2,18},{19,3},{3,19},{20,4},{4,... | collective-permute-start | bytes 196616 | tf_op jit(solution)/shard_map/ppermute | solution.py:476
  27.1 4.3 %collective-permute-start.7 = (bf16[256,128]{1,0:T(8,128)(2,1)S(1)}, bf16[256,128]{1,0:T(8,128)(2,1)S(1)}, u32[]{:S(2)}, u32[]{:S(2)}) collective-permute-start(bf16[256,128]{1,0:T(8,128)(2,1)S(1)} %finish_half.1.refs_0_.kept_ref.refs_2_), channel_id=1, source_target_pairs={{4,0},{0,4},{12,8},{8,12},{5,1},{1,5},{13,9},{9,13},{6,2},{2,6},{1... | collective-permute-start | bytes 196616 | tf_op jit(solution)/shard_map/ppermute | solution.py:481
  27.2 5.2 %collective-permute-start.9 = (bf16[256,128]{1,0:T(8,128)(2,1)S(1)}, bf16[256,128]{1,0:T(8,128)(2,1)S(1)}, u32[]{:S(2)}, u32[]{:S(2)}) collective-permute-start(bf16[256,128]{1,0:T(8,128)(2,1)S(1)} %finish_half.1.refs_0_.kept_ref.refs_2_), channel_id=1, source_target_pairs={{20,0},{16,4},{28,8},{24,12},{4,16},{0,20},{12,24},{8,28},{21,1},{... | collective-permute-start | bytes 196616 | tf_op jit(solution)/shard_map/ppermute | solution.py:491

commit v20 on v19

--- a/solution.py
+++ b/solution.py
@@ -68,6 +68,15 @@
     return jnp.concatenate(
         [real[:, :vectors] + imag[:, vectors:], real[:, vectors:] - imag[:, :vectors]], axis=0
     )
+
+
+def natural_form(matrix, planar):
+    half = matrix.shape[0] // 2
+    turned = jnp.concatenate([-matrix[half:].astype(jnp.float32), matrix[:half].astype(jnp.float32)])
+    whole = jnp.dot(matrix, planar[:half], preferred_element_type=jnp.float32) + jnp.dot(
+        turned.astype(jnp.bfloat16), planar[half:], preferred_element_type=jnp.float32
+    )
+    return whole.astype(jnp.bfloat16)
 
 
 def halo_fields(cells_x, cells_y):
@@ -165,7 +174,7 @@
                     carried = transport(matrix[:, :half], pair, -1)
                     local_ref[inside.index((3 + d, line))] = carried.astype(bf16).astype(f32)
                 elif (d, line) in outside:
-                    matrix_ref[outside.index((d, line))] = matrix
+                    matrix_ref[outside.index((d, line))] = natural_form(matrix[:, :half], planar)
                 else:
                     ahead = ahead_z if d == 2 else ordered[line + (cells_y if d == 0 else 1)]
                     local_ref[inside.index((d, line))] = transport(
@@ -212,7 +221,7 @@
             ahead = jnp.dot(planar, halo, preferred_element_type=f32)
             side_ref[1 + d, :, columns] = ahead.T.astype(bf16)
             matrix = matrix_ref[outside.index((d, line))]
-            field_ref[d, line] = transport(matrix[:, :half], side_by_side(ahead), 1)
+            field_ref[d, line] = jnp.dot(matrix, halo, preferred_element_type=f32)
     for k, (code, line) in enumerate(local_fields(cells_x, cells_y)):
         field_ref[code, line] = local_ref[k]
     for j in sorted(range(groups), key=lambda j: -(j & 1)):
@@ -516,7 +525,7 @@
         functools.partial(prepare_kernel, cells_x, cells_y),
         "prepare_lines",
         (
-            jax.ShapeDtypeStruct((len(outside), order, 128), bf16),
+            jax.ShapeDtypeStruct((len(outside), order, order), bf16),
             jax.ShapeDtypeStruct((len(inside), order, vectors), f32),
             jax.ShapeDtypeStruct((2, vectors, lines * order), bf16),
             jax.ShapeDtypeStruct((count_ops, order // 2, 2 * vectors), f32),

time: 34 us -> 33.8 us (level)
  transfers between devices with their start and end apart: 10 -> 10, of which waited for: 8 -> 8; matrix products, arithmetic and copies ran while one was open for 0% -> 0% of each run, Pallas kernels for 11% -> 12%
where the time goes in v20:
time: 33.8 us; the launch traced here: 33.6 us
  starting transfers between devices  15.9 us (47%)
  waiting for transfers between devices  9.69 us (29%)
  Pallas kernels  6.68 us (20%)
  between operations  1.35 us (4%)
    ppermute x3, starting transfers between devices, from_step(): lax.ppermute(block, axis, [((i + step) % count, i) for i in range(count)])  7.33 us
    ppermute x5, waiting for transfers between devices, from_partner(): return lax.ppermute(block, axis, [(i ^ step, i) for i in range(count)])  6.84 us
    ppermute x5, starting transfers between devices, from_partner(): return lax.ppermute(block, axis, [(i ^ step, i) for i in range(count)])  6.6 us
    ppermute x2, waiting for transfers between devices, from_diagonal(): return lax.ppermute(block, axes, perm)  2.71 us
    pallas_call x1, Pallas kernels, per_device(): local_call(functools.partial(prepare_kernel, cells_x, cells_y), 'prepare_...  2.36 us
    ppermute x2, starting transfers between devices, from_diagonal(): return lax.ppermute(block, axes, perm)  1.97 us
    pallas_call x1, Pallas kernels, per_device(): local_call(functools.partial(second_contract_kernel, times, split), 'seco...  1.51 us
    pallas_call x1, Pallas kernels, per_device(): local_call(functools.partial(margin_kernel, cells_x, cells_y, groups, own...  0.87 us
  transfers between devices with their start and end apart: 10, of which 8 were waited for; matrix products, arithmetic and copies ran while one was open for 0% of the time, Pallas kernels for 12%

profile of v20, /device:TPU:0, one launch (start us, length us, event | category | flops | bytes accessed | tf_op | source)
XLA Modules:
  0.0 33.6 jit_solution(17997899982597206665)
XLA Ops:
  0.6 5.1 %collective-permute-start = (bf16[1,2,144,128]{3,2,1,0:T(8,128)(2,1)}, bf16[1,2,144,128]{3,2,1,0:T(8,128)(2,1)S(1)}, u32[]{:S(2)}, u32[]{:S(2)}) collective-permute-start(bf16[1,2,144,128]{3,2,1,0:T(8,128)(2,1)} %bitcast.11), channel_id=1, source_target_pairs={{4,0},{8,4},{12,8},{0,12},{5,1},{9,5},{13,9},{1,13},{6,2},{10,6},{... | collective-permute-start | bytes 221192 | tf_op jit(solution)/shard_map/ppermute | solution.py:485
  5.7 0.7 %collective-permute-start.1 = (bf16[1,2,144,128]{3,2,1,0:T(8,128)(2,1)}, bf16[1,2,144,128]{3,2,1,0:T(8,128)(2,1)S(1)}, u32[]{:S(2)}, u32[]{:S(2)}) collective-permute-start(bf16[1,2,144,128]{3,2,1,0:T(8,128)(2,1)} %bitcast.12), channel_id=1, source_target_pairs={{1,0},{2,1},{3,2},{0,3},{5,4},{6,5},{7,6},{4,7},{9,8},{10,9},{11,1... | collective-permute-start | bytes 221192 | tf_op jit(solution)/shard_map/ppermute | solution.py:485
  6.4 2.4 %prepare_lines.1 = (bf16[3,144,144]{2,1,0:T(8,128)(2,1)S(1)}, f32[11,144,128]{2,1,0:T(8,128)S(1)}, bf16[2,128,288]{2,1,0:T(8,128)(2,1)S(1)}, f32[8,72,256]{2,1,0...) custom-call(bf16[1,2,144,128]{3,2,1,0:T(8,128)(2,1)} %bitcast.13, bf16[2,27,2,24]{3,2,1,0:T(2,128)(2,1)} %bitcast.14, ...), custom_call_target="tpu_custom_call" | custom-call | tf_op jit(solution)/shard_map/prepare_lines/pallas_call | solution.py:524
  8.8 0.0 collective-permute-done.refs_5_
  8.8 0.0 collective-permute-done.1.refs_6_
  8.8 0.9 %partial_margins.1 = (s16[2,528,128]{2,1,0:T(8,128)(2,1)S(1)}, f32[2,512,128]{2,1,0:T(8,128)S(1)}) custom-call(bf16[3,144,144]{2,1,0:T(8,128)(2,1)S(1)} %get-tuple-element.17.refs_0_, f32[11,144,128]{2,1,0:T(8,128)S(1)} %get-tuple-element.18.refs_1_, bf16[2,128,288]{2,1,0:T(8,128)(2,1)S(1)} %get-tuple-element.19.refs_2_, ...), custom_call_target="tpu_custom_call" | custom-call | tf_op jit(solution)/shard_map/partial_margins/pallas_call | solution.py:544
  9.7 0.0 copy-start
  9.7 0.9 %collective-permute-start.2 = (s16[2,528,128]{2,1,0:T(8,128)(2,1)S(1)}, s16[2,528,128]{2,1,0:T(8,128)(2,1)S(1)}, u32[]{:S(2)}, u32[]{:S(2)}) collective-permute-start(s16[2,528,128]{2,1,0:T(8,128)(2,1)S(1)} %get-tuple-element.23), channel_id=1, source_target_pairs={{1,0},{0,1},{3,2},{2,3},{5,4},{4,5},{7,6},{6,7},{9,8},{8,9},{11,10... | collective-permute-start | bytes 811016 | tf_op jit(solution)/shard_map/ppermute | solution.py:490
  10.6 1.2 %collective-permute-done.2.refs_0_ = s16[2,528,128]{2,1,0:T(8,128)(2,1)S(1)} collective-permute-done((s16[2,528,128]{2,1,0:T(8,128)(2,1)S(1)}, s16[2,528,128]{2,1,0:T(8,128)(2,1)S(1)}, u32[]{:S(2)}, u32[]{:S(2)}) %collective-permute-start.2) | collective-permute-done | bytes 270368 | tf_op jit(solution)/shard_map/ppermute | solution.py:490
  11.8 0.2 spread_halves.1
  12.0 1.2 %collective-permute-start.3 = (s16[272,128]{1,0:T(8,128)(2,1)S(1)}, s16[272,128]{1,0:T(8,128)(2,1)S(1)}, u32[]{:S(2)}, u32[]{:S(2)}) collective-permute-start(s16[272,128]{1,0:T(8,128)(2,1)S(1)} %get-tuple-element.24), channel_id=1, source_target_pairs={{2,0},{3,1},{0,2},{1,3},{6,4},{7,5},{4,6},{5,7},{10,8},{11,9},{8,1... | collective-permute-start | bytes 208904 | tf_op jit(solution)/shard_map/ppermute | solution.py:490
  13.2 0.0 collective-permute-start.4
  13.2 2.3 %collective-permute-start.5 = (s16[272,128]{1,0:T(8,128)(2,1)S(1)}, s16[272,128]{1,0:T(8,128)(2,1)S(1)}, u32[]{:S(2)}, u32[]{:S(2)}) collective-permute-start(s16[272,128]{1,0:T(8,128)(2,1)S(1)} %get-tuple-element.26), channel_id=1, source_target_pairs={{4,0},{0,4},{12,8},{8,12},{5,1},{1,5},{13,9},{9,13},{6,2},{2,6},{1... | collective-permute-start | bytes 208904 | tf_op jit(solution)/shard_map/ppermute | solution.py:490
  15.5 1.0 %collective-permute-done.3.refs_1_ = s16[272,128]{1,0:T(8,128)(2,1)S(1)} collective-permute-done((s16[272,128]{1,0:T(8,128)(2,1)S(1)}, s16[272,128]{1,0:T(8,128)(2,1)S(1)}, u32[]{:S(2)}, u32[]{:S(2)}) %collective-permute-start.3) | collective-permute-done | bytes 69664 | tf_op jit(solution)/shard_map/ppermute | solution.py:490
  16.5 2.5 %collective-permute-done.4.refs_2_ = s16[272,128]{1,0:T(8,128)(2,1)S(1)} collective-permute-done((s16[272,128]{1,0:T(8,128)(2,1)S(1)}, s16[272,128]{1,0:T(8,128)(2,1)S(1)}, u32[]{:S(2)}, u32[]{:S(2)}) %collective-permute-start.4) | collective-permute-done | bytes 69664 | tf_op jit(solution)/shard_map/ppermute | solution.py:500
  19.0 0.2 collective-permute-done.5.refs_3_
  19.2 0.1 keep_half.1.own_ref
  19.3 2.1 %collective-permute-start.6 = (s16[272,128]{1,0:T(8,128)(2,1)S(1)}, s16[272,128]{1,0:T(8,128)(2,1)S(1)}, u32[]{:S(2)}, u32[]{:S(2)}) collective-permute-start(s16[272,128]{1,0:T(8,128)(2,1)S(1)} %keep_half.1.own_ref), channel_id=1, source_target_pairs={{8,0},{12,4},{0,8},{4,12},{9,1},{13,5},{1,9},{5,13},{10,2},{14,6},... | collective-permute-start | bytes 208904 | tf_op jit(solution)/shard_map/ppermute | solution.py:490
  21.4 3.9 %collective-permute-done.6.arrived_ref = s16[272,128]{1,0:T(8,128)(2,1)S(1)} collective-permute-done((s16[272,128]{1,0:T(8,128)(2,1)S(1)}, s16[272,128]{1,0:T(8,128)(2,1)S(1)}, u32[]{:S(2)}, u32[]{:S(2)}) %collective-permute-start.6) | collective-permute-done | bytes 69664 | tf_op jit(solution)/shard_map/ppermute | solution.py:490
  25.4 1.6 %collective-permute-start.8 = (bf16[256,128]{1,0:T(8,128)(2,1)S(1)}, bf16[256,128]{1,0:T(8,128)(2,1)S(1)}, u32[]{:S(2)}, u32[]{:S(2)}) collective-permute-start(bf16[256,128]{1,0:T(8,128)(2,1)S(1)} %finish_half.1.refs_0_.kept_ref.refs_2_), channel_id=1, source_target_pairs={{16,0},{0,16},{17,1},{1,17},{18,2},{2,18},{19,3},{3,19},{20,4},{4,... | collective-permute-start | bytes 196616 | tf_op jit(solution)/shard_map/ppermute | solution.py:485
  26.9 0.0 collective-permute-start.7
  27.0 2.0 %collective-permute-start.9 = (bf16[256,128]{1,0:T(8,128)(2,1)S(1)}, bf16[256,128]{1,0:T(8,128)(2,1)S(1)}, u32[]{:S(2)}, u32[]{:S(2)}) collective-permute-start(bf16[256,128]{1,0:T(8,128)(2,1)S(1)} %finish_half.1.refs_0_.kept_ref.refs_2_), channel_id=1, source_target_pairs={{20,0},{16,4},{28,8},{24,12},{4,16},{0,20},{12,24},{8,28},{21,1},{... | collective-permute-start | bytes 196616 | tf_op jit(solution)/shard_map/ppermute | solution.py:500
  29.6 0.1 collective-permute-done.8.refs_1_.refs_3_
  29.7 0.0 copy-done
  29.7 0.9 %first_contraction.1 = (f32[8,128]{1,0:T(8,128)S(1)}, f32[2,32,128]{2,1,0:T(8,128)S(1)}) custom-call(s32[1]{0:T(128)S(6)} %copy.10.live_ref, f32[2,2,8,128]{3,2,1,0:T(8,128)S(1)} %get-tuple-element.27.weight_ref, bf16[2,512,512]{2,1,0:T(8,128)(2,1)S(1)} %bitcast.8, bf16[256,128]{1,0:T(8,128)(2,1)S(1)} %finish_half.1.refs_0_.kept_ref.refs_2_, ...), custom_call_target="tpu_custom_call" | custom-call | tf_op jit(solution)/shard_map/first_contraction/pallas_call | solution.py:603
  30.6 0.6 %collective-permute-done.7.other_ref.refs_0_ = bf16[256,128]{1,0:T(8,128)(2,1)S(1)} collective-permute-done((bf16[256,128]{1,0:T(8,128)(2,1)S(1)}, bf16[256,128]{1,0:T(8,128)(2,1)S(1)}, u32[]{:S(2)}, u32[]{:S(2)}) %collective-permute-start.7) | collective-permute-done | bytes 65568 | tf_op jit(solution)/shard_map/ppermute | solution.py:490
  31.2 0.7 %margins_out.1 = f32[1,512,128]{2,1,0:T(8,128)} custom-call(bf16[256,128]{1,0:T(8,128)(2,1)S(1)} %finish_half.1.refs_0_.kept_ref.refs_2_, bf16[256,128]{1,0:T(8,128)(2,1)S(1)} %collective-permute-done.7.other_ref.refs_0_), custom_call_target="tpu_custom_call" | custom-call | tf_op jit(solution)/shard_map/margins_out/pallas_call | solution.py:611
  31.9 0.2 collective-permute-done.9.refs_1_
  32.1 1.5 %second_contraction.1 = f32[1,2,2]{2,1,0:T(2,128)} custom-call(f32[2,2,8,128]{3,2,1,0:T(8,128)S(1)} %get-tuple-element.27.weight_ref, bf16[2,512,512]{2,1,0:T(8,128)(2,1)S(1)} %bitcast.9, bf16[256,128]{1,0:T(8,128)(2,1)S(1)} %collective-permute-done.7.other_ref.refs_0_, bf16[256,128]{1,0:T(8,128)(2,1)S(1)} %collective-permute-done.9.refs_1_, ...), custom_call_target="tpu_custom_call" | custom-call | tf_op jit(solution)/shard_map/second_contraction/pallas_call | solution.py:618
  (1 shorter events, 0.0 us)
Async XLA Ops:
  0.6 8.1 %collective-permute-start = (bf16[1,2,144,128]{3,2,1,0:T(8,128)(2,1)}, bf16[1,2,144,128]{3,2,1,0:T(8,128)(2,1)S(1)}, u32[]{:S(2)}, u32[]{:S(2)}) collective-permute-start(bf16[1,2,144,128]{3,2,1,0:T(8,128)(2,1)} %bitcast.11), channel_id=1, source_target_pairs={{4,0},{8,4},{12,8},{0,12},{5,1},{9,5},{13,9},{1,13},{6,2},{10,6},{... | collective-permute-start | bytes 221192 | tf_op jit(solution)/shard_map/ppermute | solution.py:485
  5.7 3.1 %collective-permute-start.1 = (bf16[1,2,144,128]{3,2,1,0:T(8,128)(2,1)}, bf16[1,2,144,128]{3,2,1,0:T(8,128)(2,1)S(1)}, u32[]{:S(2)}, u32[]{:S(2)}) collective-permute-start(bf16[1,2,144,128]{3,2,1,0:T(8,128)(2,1)} %bitcast.12), channel_id=1, source_target_pairs={{1,0},{2,1},{3,2},{0,3},{5,4},{6,5},{7,6},{4,7},{9,8},{10,9},{11,1... | collective-permute-start | bytes 221192 | tf_op jit(solution)/shard_map/ppermute | solution.py:485
  9.7 20.0 %copy-start = (bf16[1,2,512,512]{3,2,1,0:T(8,128)(2,1)S(1)}, bf16[1,2,512,512]{3,2,1,0:T(8,128)(2,1)}, u32[]{:S(2)}) copy-start(bf16[1,2,512,512]{3,2,1,0:T(8,128)(2,1)} %param.12) | copy-start | bytes 3145732
  9.7 2.1 %collective-permute-start.2 = (s16[2,528,128]{2,1,0:T(8,128)(2,1)S(1)}, s16[2,528,128]{2,1,0:T(8,128)(2,1)S(1)}, u32[]{:S(2)}, u32[]{:S(2)}) collective-permute-start(s16[2,528,128]{2,1,0:T(8,128)(2,1)S(1)} %get-tuple-element.23), channel_id=1, source_target_pairs={{1,0},{0,1},{3,2},{2,3},{5,4},{4,5},{7,6},{6,7},{9,8},{8,9},{11,10... | collective-permute-start | bytes 811016 | tf_op jit(solution)/shard_map/ppermute | solution.py:490
  12.0 4.5 %collective-permute-start.3 = (s16[272,128]{1,0:T(8,128)(2,1)S(1)}, s16[272,128]{1,0:T(8,128)(2,1)S(1)}, u32[]{:S(2)}, u32[]{:S(2)}) collective-permute-start(s16[272,128]{1,0:T(8,128)(2,1)S(1)} %get-tuple-element.24), channel_id=1, source_target_pairs={{2,0},{3,1},{0,2},{1,3},{6,4},{7,5},{4,6},{5,7},{10,8},{11,9},{8,1... | collective-permute-start | bytes 208904 | tf_op jit(solution)/shard_map/ppermute | solution.py:490
  13.2 5.8 %collective-permute-start.4 = (s16[272,128]{1,0:T(8,128)(2,1)S(1)}, s16[272,128]{1,0:T(8,128)(2,1)S(1)}, u32[]{:S(2)}, u32[]{:S(2)}) collective-permute-start(s16[272,128]{1,0:T(8,128)(2,1)S(1)} %get-tuple-element.25), channel_id=1, source_target_pairs={{6,0},{7,1},{4,2},{5,3},{2,4},{3,5},{0,6},{1,7},{14,8},{15,9},{12,... | collective-permute-start | bytes 208904 | tf_op jit(solution)/shard_map/ppermute | solution.py:500
  13.2 6.0 %collective-permute-start.5 = (s16[272,128]{1,0:T(8,128)(2,1)S(1)}, s16[272,128]{1,0:T(8,128)(2,1)S(1)}, u32[]{:S(2)}, u32[]{:S(2)}) collective-permute-start(s16[272,128]{1,0:T(8,128)(2,1)S(1)} %get-tuple-element.26), channel_id=1, source_target_pairs={{4,0},{0,4},{12,8},{8,12},{5,1},{1,5},{13,9},{9,13},{6,2},{2,6},{1... | collective-permute-start | bytes 208904 | tf_op jit(solution)/shard_map/ppermute | solution.py:490
  19.3 6.0 %collective-permute-start.6 = (s16[272,128]{1,0:T(8,128)(2,1)S(1)}, s16[272,128]{1,0:T(8,128)(2,1)S(1)}, u32[]{:S(2)}, u32[]{:S(2)}) collective-permute-start(s16[272,128]{1,0:T(8,128)(2,1)S(1)} %keep_half.1.own_ref), channel_id=1, source_target_pairs={{8,0},{12,4},{0,8},{4,12},{9,1},{13,5},{1,9},{5,13},{10,2},{14,6},... | collective-permute-start | bytes 208904 | tf_op jit(solution)/shard_map/ppermute | solution.py:490
  25.4 4.3 %collective-permute-start.8 = (bf16[256,128]{1,0:T(8,128)(2,1)S(1)}, bf16[256,128]{1,0:T(8,128)(2,1)S(1)}, u32[]{:S(2)}, u32[]{:S(2)}) collective-permute-start(bf16[256,128]{1,0:T(8,128)(2,1)S(1)} %finish_half.1.refs_0_.kept_ref.refs_2_), channel_id=1, source_target_pairs={{16,0},{0,16},{17,1},{1,17},{18,2},{2,18},{19,3},{3,19},{20,4},{4,... | collective-permute-start | bytes 196616 | tf_op jit(solution)/shard_map/ppermute | solution.py:485
  26.9 4.3 %collective-permute-start.7 = (bf16[256,128]{1,0:T(8,128)(2,1)S(1)}, bf16[256,128]{1,0:T(8,128)(2,1)S(1)}, u32[]{:S(2)}, u32[]{:S(2)}) collective-permute-start(bf16[256,128]{1,0:T(8,128)(2,1)S(1)} %finish_half.1.refs_0_.kept_ref.refs_2_), channel_id=1, source_target_pairs={{4,0},{0,4},{12,8},{8,12},{5,1},{1,5},{13,9},{9,13},{6,2},{2,6},{1... | collective-permute-start | bytes 196616 | tf_op jit(solution)/shard_map/ppermute | solution.py:490
  27.0 5.2 %collective-permute-start.9 = (bf16[256,128]{1,0:T(8,128)(2,1)S(1)}, bf16[256,128]{1,0:T(8,128)(2,1)S(1)}, u32[]{:S(2)}, u32[]{:S(2)}) collective-permute-start(bf16[256,128]{1,0:T(8,128)(2,1)S(1)} %finish_half.1.refs_0_.kept_ref.refs_2_), channel_id=1, source_target_pairs={{20,0},{16,4},{28,8},{24,12},{4,16},{0,20},{12,24},{8,28},{21,1},{... | collective-permute-start | bytes 196616 | tf_op jit(solution)/shard_map/ppermute | solution.py:500

commit v21 on v20

--- a/solution.py
+++ b/solution.py
@@ -218,8 +218,9 @@
                 side_ref[1 + d, :, columns] = left_ref[0, :, ahead * order : (ahead + 1) * order]
                 continue
             halo = halo_x_ref[0, y] if d == 0 else halo_y_ref[x, 0]
-            ahead = jnp.dot(planar, halo, preferred_element_type=f32)
-            side_ref[1 + d, :, columns] = ahead.T.astype(bf16)
+            side_ref[1 + d, :, columns] = lax.dot_general(
+                halo, planar, (((0,), (1,)), ((), ())), preferred_element_type=f32
+            ).astype(bf16)
             matrix = matrix_ref[outside.index((d, line))]
             field_ref[d, line] = jnp.dot(matrix, halo, preferred_element_type=f32)
     for k, (code, line) in enumerate(local_fields(cells_x, cells_y)):

time: 33.8 us -> 33.7 us (level)
  no operation moved by 1% of the time
where the time goes in v21:
time: 33.7 us; the launch traced here: 33.6 us
  starting transfers between devices  15.9 us (47%)
  waiting for transfers between devices  9.68 us (29%)
  Pallas kernels  6.61 us (20%)
  between operations  1.35 us (4%)
    ppermute x3, starting transfers between devices, from_step(): lax.ppermute(block, axis, [((i + step) % count, i) for i in range(count)])  7.34 us
    ppermute x5, waiting for transfers between devices, from_partner(): return lax.ppermute(block, axis, [(i ^ step, i) for i in range(count)])  6.83 us
    ppermute x5, starting transfers between devices, from_partner(): return lax.ppermute(block, axis, [(i ^ step, i) for i in range(count)])  6.6 us
    ppermute x2, waiting for transfers between devices, from_diagonal(): return lax.ppermute(block, axes, perm)  2.72 us
    pallas_call x1, Pallas kernels, per_device(): local_call(functools.partial(prepare_kernel, cells_x, cells_y), 'prepare_...  2.36 us
    ppermute x2, starting transfers between devices, from_diagonal(): return lax.ppermute(block, axes, perm)  1.96 us
    pallas_call x1, Pallas kernels, per_device(): local_call(functools.partial(second_contract_kernel, times, split), 'seco...  1.5 us
    pallas_call x1, Pallas kernels, per_device(): local_call(functools.partial(first_contract_kernel, times, split), 'first...  0.86 us
  transfers between devices with their start and end apart: 10, of which 8 were waited for; matrix products, arithmetic and copies ran while one was open for 0% of the time, Pallas kernels for 12%

profile of v21, /device:TPU:0, one launch (start us, length us, event | category | flops | bytes accessed | tf_op | source)
XLA Modules:
  0.0 33.6 jit_solution(16896640875165264893)
XLA Ops:
  0.6 5.1 %collective-permute-start = (bf16[1,2,144,128]{3,2,1,0:T(8,128)(2,1)}, bf16[1,2,144,128]{3,2,1,0:T(8,128)(2,1)S(1)}, u32[]{:S(2)}, u32[]{:S(2)}) collective-permute-start(bf16[1,2,144,128]{3,2,1,0:T(8,128)(2,1)} %bitcast.11), channel_id=1, source_target_pairs={{4,0},{8,4},{12,8},{0,12},{5,1},{9,5},{13,9},{1,13},{6,2},{10,6},{... | collective-permute-start | bytes 221192 | tf_op jit(solution)/shard_map/ppermute | solution.py:486
  5.7 0.7 %collective-permute-start.1 = (bf16[1,2,144,128]{3,2,1,0:T(8,128)(2,1)}, bf16[1,2,144,128]{3,2,1,0:T(8,128)(2,1)S(1)}, u32[]{:S(2)}, u32[]{:S(2)}) collective-permute-start(bf16[1,2,144,128]{3,2,1,0:T(8,128)(2,1)} %bitcast.12), channel_id=1, source_target_pairs={{1,0},{2,1},{3,2},{0,3},{5,4},{6,5},{7,6},{4,7},{9,8},{10,9},{11,1... | collective-permute-start | bytes 221192 | tf_op jit(solution)/shard_map/ppermute | solution.py:486
  6.4 2.4 %prepare_lines.1 = (bf16[3,144,144]{2,1,0:T(8,128)(2,1)S(1)}, f32[11,144,128]{2,1,0:T(8,128)S(1)}, bf16[2,128,288]{2,1,0:T(8,128)(2,1)S(1)}, f32[8,72,256]{2,1,0...) custom-call(bf16[1,2,144,128]{3,2,1,0:T(8,128)(2,1)} %bitcast.13, bf16[2,27,2,24]{3,2,1,0:T(2,128)(2,1)} %bitcast.14, ...), custom_call_target="tpu_custom_call" | custom-call | tf_op jit(solution)/shard_map/prepare_lines/pallas_call | solution.py:525
  8.8 0.0 collective-permute-done.refs_5_
  8.8 0.0 collective-permute-done.1.refs_6_
  8.8 0.8 %partial_margins.1 = (s16[2,528,128]{2,1,0:T(8,128)(2,1)S(1)}, f32[2,512,128]{2,1,0:T(8,128)S(1)}) custom-call(bf16[3,144,144]{2,1,0:T(8,128)(2,1)S(1)} %get-tuple-element.17.refs_0_, f32[11,144,128]{2,1,0:T(8,128)S(1)} %get-tuple-element.18.refs_1_, bf16[2,128,288]{2,1,0:T(8,128)(2,1)S(1)} %get-tuple-element.19.refs_2_, ...), custom_call_target="tpu_custom_call" | custom-call | tf_op jit(solution)/shard_map/partial_margins/pallas_call | solution.py:545
  9.6 0.0 copy-start
  9.6 0.9 %collective-permute-start.2 = (s16[2,528,128]{2,1,0:T(8,128)(2,1)S(1)}, s16[2,528,128]{2,1,0:T(8,128)(2,1)S(1)}, u32[]{:S(2)}, u32[]{:S(2)}) collective-permute-start(s16[2,528,128]{2,1,0:T(8,128)(2,1)S(1)} %get-tuple-element.23), channel_id=1, source_target_pairs={{1,0},{0,1},{3,2},{2,3},{5,4},{4,5},{7,6},{6,7},{9,8},{8,9},{11,10... | collective-permute-start | bytes 811016 | tf_op jit(solution)/shard_map/ppermute | solution.py:491
  10.5 1.2 %collective-permute-done.2.refs_0_ = s16[2,528,128]{2,1,0:T(8,128)(2,1)S(1)} collective-permute-done((s16[2,528,128]{2,1,0:T(8,128)(2,1)S(1)}, s16[2,528,128]{2,1,0:T(8,128)(2,1)S(1)}, u32[]{:S(2)}, u32[]{:S(2)}) %collective-permute-start.2) | collective-permute-done | bytes 270368 | tf_op jit(solution)/shard_map/ppermute | solution.py:491
  11.7 0.2 spread_halves.1
  11.9 1.2 %collective-permute-start.3 = (s16[272,128]{1,0:T(8,128)(2,1)S(1)}, s16[272,128]{1,0:T(8,128)(2,1)S(1)}, u32[]{:S(2)}, u32[]{:S(2)}) collective-permute-start(s16[272,128]{1,0:T(8,128)(2,1)S(1)} %get-tuple-element.24), channel_id=1, source_target_pairs={{2,0},{3,1},{0,2},{1,3},{6,4},{7,5},{4,6},{5,7},{10,8},{11,9},{8,1... | collective-permute-start | bytes 208904 | tf_op jit(solution)/shard_map/ppermute | solution.py:491
  13.1 0.0 collective-permute-start.4
  13.1 2.3 %collective-permute-start.5 = (s16[272,128]{1,0:T(8,128)(2,1)S(1)}, s16[272,128]{1,0:T(8,128)(2,1)S(1)}, u32[]{:S(2)}, u32[]{:S(2)}) collective-permute-start(s16[272,128]{1,0:T(8,128)(2,1)S(1)} %get-tuple-element.26), channel_id=1, source_target_pairs={{4,0},{0,4},{12,8},{8,12},{5,1},{1,5},{13,9},{9,13},{6,2},{2,6},{1... | collective-permute-start | bytes 208904 | tf_op jit(solution)/shard_map/ppermute | solution.py:491
  15.5 1.0 %collective-permute-done.3.refs_1_ = s16[272,128]{1,0:T(8,128)(2,1)S(1)} collective-permute-done((s16[272,128]{1,0:T(8,128)(2,1)S(1)}, s16[272,128]{1,0:T(8,128)(2,1)S(1)}, u32[]{:S(2)}, u32[]{:S(2)}) %collective-permute-start.3) | collective-permute-done | bytes 69664 | tf_op jit(solution)/shard_map/ppermute | solution.py:491
  16.4 2.5 %collective-permute-done.4.refs_2_ = s16[272,128]{1,0:T(8,128)(2,1)S(1)} collective-permute-done((s16[272,128]{1,0:T(8,128)(2,1)S(1)}, s16[272,128]{1,0:T(8,128)(2,1)S(1)}, u32[]{:S(2)}, u32[]{:S(2)}) %collective-permute-start.4) | collective-permute-done | bytes 69664 | tf_op jit(solution)/shard_map/ppermute | solution.py:501
  18.9 0.2 collective-permute-done.5.refs_3_
  19.1 0.1 keep_half.1.own_ref
  19.2 2.1 %collective-permute-start.6 = (s16[272,128]{1,0:T(8,128)(2,1)S(1)}, s16[272,128]{1,0:T(8,128)(2,1)S(1)}, u32[]{:S(2)}, u32[]{:S(2)}) collective-permute-start(s16[272,128]{1,0:T(8,128)(2,1)S(1)} %keep_half.1.own_ref), channel_id=1, source_target_pairs={{8,0},{12,4},{0,8},{4,12},{9,1},{13,5},{1,9},{5,13},{10,2},{14,6},... | collective-permute-start | bytes 208904 | tf_op jit(solution)/shard_map/ppermute | solution.py:491
  21.3 3.9 %collective-permute-done.6.arrived_ref = s16[272,128]{1,0:T(8,128)(2,1)S(1)} collective-permute-done((s16[272,128]{1,0:T(8,128)(2,1)S(1)}, s16[272,128]{1,0:T(8,128)(2,1)S(1)}, u32[]{:S(2)}, u32[]{:S(2)}) %collective-permute-start.6) | collective-permute-done | bytes 69664 | tf_op jit(solution)/shard_map/ppermute | solution.py:491
  25.3 1.6 %collective-permute-start.8 = (bf16[256,128]{1,0:T(8,128)(2,1)S(1)}, bf16[256,128]{1,0:T(8,128)(2,1)S(1)}, u32[]{:S(2)}, u32[]{:S(2)}) collective-permute-start(bf16[256,128]{1,0:T(8,128)(2,1)S(1)} %finish_half.1.refs_0_.kept_ref.refs_2_), channel_id=1, source_target_pairs={{16,0},{0,16},{17,1},{1,17},{18,2},{2,18},{19,3},{3,19},{20,4},{4,... | collective-permute-start | bytes 196616 | tf_op jit(solution)/shard_map/ppermute | solution.py:486
  26.9 0.0 collective-permute-start.7
  26.9 2.0 %collective-permute-start.9 = (bf16[256,128]{1,0:T(8,128)(2,1)S(1)}, bf16[256,128]{1,0:T(8,128)(2,1)S(1)}, u32[]{:S(2)}, u32[]{:S(2)}) collective-permute-start(bf16[256,128]{1,0:T(8,128)(2,1)S(1)} %finish_half.1.refs_0_.kept_ref.refs_2_), channel_id=1, source_target_pairs={{20,0},{16,4},{28,8},{24,12},{4,16},{0,20},{12,24},{8,28},{21,1},{... | collective-permute-start | bytes 196616 | tf_op jit(solution)/shard_map/ppermute | solution.py:501
  29.5 0.1 collective-permute-done.8.refs_1_.refs_3_
  29.6 0.0 copy-done
  29.6 0.9 %first_contraction.1 = (f32[8,128]{1,0:T(8,128)S(1)}, f32[2,32,128]{2,1,0:T(8,128)S(1)}) custom-call(s32[1]{0:T(128)S(6)} %copy.10.live_ref, f32[2,2,8,128]{3,2,1,0:T(8,128)S(1)} %get-tuple-element.27.weight_ref, bf16[2,512,512]{2,1,0:T(8,128)(2,1)S(1)} %bitcast.8, bf16[256,128]{1,0:T(8,128)(2,1)S(1)} %finish_half.1.refs_0_.kept_ref.refs_2_, ...), custom_call_target="tpu_custom_call" | custom-call | tf_op jit(solution)/shard_map/first_contraction/pallas_call | solution.py:604
  30.5 0.6 %collective-permute-done.7.other_ref.refs_0_ = bf16[256,128]{1,0:T(8,128)(2,1)S(1)} collective-permute-done((bf16[256,128]{1,0:T(8,128)(2,1)S(1)}, bf16[256,128]{1,0:T(8,128)(2,1)S(1)}, u32[]{:S(2)}, u32[]{:S(2)}) %collective-permute-start.7) | collective-permute-done | bytes 65568 | tf_op jit(solution)/shard_map/ppermute | solution.py:491
  31.1 0.7 %margins_out.1 = f32[1,512,128]{2,1,0:T(8,128)} custom-call(bf16[256,128]{1,0:T(8,128)(2,1)S(1)} %finish_half.1.refs_0_.kept_ref.refs_2_, bf16[256,128]{1,0:T(8,128)(2,1)S(1)} %collective-permute-done.7.other_ref.refs_0_), custom_call_target="tpu_custom_call" | custom-call | tf_op jit(solution)/shard_map/margins_out/pallas_call | solution.py:612
  31.8 0.2 collective-permute-done.9.refs_1_
  32.0 1.5 %second_contraction.1 = f32[1,2,2]{2,1,0:T(2,128)} custom-call(f32[2,2,8,128]{3,2,1,0:T(8,128)S(1)} %get-tuple-element.27.weight_ref, bf16[2,512,512]{2,1,0:T(8,128)(2,1)S(1)} %bitcast.9, bf16[256,128]{1,0:T(8,128)(2,1)S(1)} %collective-permute-done.7.other_ref.refs_0_, bf16[256,128]{1,0:T(8,128)(2,1)S(1)} %collective-permute-done.9.refs_1_, ...), custom_call_target="tpu_custom_call" | custom-call | tf_op jit(solution)/shard_map/second_contraction/pallas_call | solution.py:619
  (1 shorter events, 0.0 us)
Async XLA Ops:
  0.6 8.1 %collective-permute-start = (bf16[1,2,144,128]{3,2,1,0:T(8,128)(2,1)}, bf16[1,2,144,128]{3,2,1,0:T(8,128)(2,1)S(1)}, u32[]{:S(2)}, u32[]{:S(2)}) collective-permute-start(bf16[1,2,144,128]{3,2,1,0:T(8,128)(2,1)} %bitcast.11), channel_id=1, source_target_pairs={{4,0},{8,4},{12,8},{0,12},{5,1},{9,5},{13,9},{1,13},{6,2},{10,6},{... | collective-permute-start | bytes 221192 | tf_op jit(solution)/shard_map/ppermute | solution.py:486
  5.7 3.1 %collective-permute-start.1 = (bf16[1,2,144,128]{3,2,1,0:T(8,128)(2,1)}, bf16[1,2,144,128]{3,2,1,0:T(8,128)(2,1)S(1)}, u32[]{:S(2)}, u32[]{:S(2)}) collective-permute-start(bf16[1,2,144,128]{3,2,1,0:T(8,128)(2,1)} %bitcast.12), channel_id=1, source_target_pairs={{1,0},{2,1},{3,2},{0,3},{5,4},{6,5},{7,6},{4,7},{9,8},{10,9},{11,1... | collective-permute-start | bytes 221192 | tf_op jit(solution)/shard_map/ppermute | solution.py:486
  9.6 20.0 %copy-start = (bf16[1,2,512,512]{3,2,1,0:T(8,128)(2,1)S(1)}, bf16[1,2,512,512]{3,2,1,0:T(8,128)(2,1)}, u32[]{:S(2)}) copy-start(bf16[1,2,512,512]{3,2,1,0:T(8,128)(2,1)} %param.12) | copy-start | bytes 3145732
  9.6 2.1 %collective-permute-start.2 = (s16[2,528,128]{2,1,0:T(8,128)(2,1)S(1)}, s16[2,528,128]{2,1,0:T(8,128)(2,1)S(1)}, u32[]{:S(2)}, u32[]{:S(2)}) collective-permute-start(s16[2,528,128]{2,1,0:T(8,128)(2,1)S(1)} %get-tuple-element.23), channel_id=1, source_target_pairs={{1,0},{0,1},{3,2},{2,3},{5,4},{4,5},{7,6},{6,7},{9,8},{8,9},{11,10... | collective-permute-start | bytes 811016 | tf_op jit(solution)/shard_map/ppermute | solution.py:491
  11.9 4.5 %collective-permute-start.3 = (s16[272,128]{1,0:T(8,128)(2,1)S(1)}, s16[272,128]{1,0:T(8,128)(2,1)S(1)}, u32[]{:S(2)}, u32[]{:S(2)}) collective-permute-start(s16[272,128]{1,0:T(8,128)(2,1)S(1)} %get-tuple-element.24), channel_id=1, source_target_pairs={{2,0},{3,1},{0,2},{1,3},{6,4},{7,5},{4,6},{5,7},{10,8},{11,9},{8,1... | collective-permute-start | bytes 208904 | tf_op jit(solution)/shard_map/ppermute | solution.py:491
  13.1 5.8 %collective-permute-start.4 = (s16[272,128]{1,0:T(8,128)(2,1)S(1)}, s16[272,128]{1,0:T(8,128)(2,1)S(1)}, u32[]{:S(2)}, u32[]{:S(2)}) collective-permute-start(s16[272,128]{1,0:T(8,128)(2,1)S(1)} %get-tuple-element.25), channel_id=1, source_target_pairs={{6,0},{7,1},{4,2},{5,3},{2,4},{3,5},{0,6},{1,7},{14,8},{15,9},{12,... | collective-permute-start | bytes 208904 | tf_op jit(solution)/shard_map/ppermute | solution.py:501
  13.1 6.0 %collective-permute-start.5 = (s16[272,128]{1,0:T(8,128)(2,1)S(1)}, s16[272,128]{1,0:T(8,128)(2,1)S(1)}, u32[]{:S(2)}, u32[]{:S(2)}) collective-permute-start(s16[272,128]{1,0:T(8,128)(2,1)S(1)} %get-tuple-element.26), channel_id=1, source_target_pairs={{4,0},{0,4},{12,8},{8,12},{5,1},{1,5},{13,9},{9,13},{6,2},{2,6},{1... | collective-permute-start | bytes 208904 | tf_op jit(solution)/shard_map/ppermute | solution.py:491
  19.2 6.0 %collective-permute-start.6 = (s16[272,128]{1,0:T(8,128)(2,1)S(1)}, s16[272,128]{1,0:T(8,128)(2,1)S(1)}, u32[]{:S(2)}, u32[]{:S(2)}) collective-permute-start(s16[272,128]{1,0:T(8,128)(2,1)S(1)} %keep_half.1.own_ref), channel_id=1, source_target_pairs={{8,0},{12,4},{0,8},{4,12},{9,1},{13,5},{1,9},{5,13},{10,2},{14,6},... | collective-permute-start | bytes 208904 | tf_op jit(solution)/shard_map/ppermute | solution.py:491
  25.3 4.3 %collective-permute-start.8 = (bf16[256,128]{1,0:T(8,128)(2,1)S(1)}, bf16[256,128]{1,0:T(8,128)(2,1)S(1)}, u32[]{:S(2)}, u32[]{:S(2)}) collective-permute-start(bf16[256,128]{1,0:T(8,128)(2,1)S(1)} %finish_half.1.refs_0_.kept_ref.refs_2_), channel_id=1, source_target_pairs={{16,0},{0,16},{17,1},{1,17},{18,2},{2,18},{19,3},{3,19},{20,4},{4,... | collective-permute-start | bytes 196616 | tf_op jit(solution)/shard_map/ppermute | solution.py:486
  26.9 4.3 %collective-permute-start.7 = (bf16[256,128]{1,0:T(8,128)(2,1)S(1)}, bf16[256,128]{1,0:T(8,128)(2,1)S(1)}, u32[]{:S(2)}, u32[]{:S(2)}) collective-permute-start(bf16[256,128]{1,0:T(8,128)(2,1)S(1)} %finish_half.1.refs_0_.kept_ref.refs_2_), channel_id=1, source_target_pairs={{4,0},{0,4},{12,8},{8,12},{5,1},{1,5},{13,9},{9,13},{6,2},{2,6},{1... | collective-permute-start | bytes 196616 | tf_op jit(solution)/shard_map/ppermute | solution.py:491
  26.9 5.2 %collective-permute-start.9 = (bf16[256,128]{1,0:T(8,128)(2,1)S(1)}, bf16[256,128]{1,0:T(8,128)(2,1)S(1)}, u32[]{:S(2)}, u32[]{:S(2)}) collective-permute-start(bf16[256,128]{1,0:T(8,128)(2,1)S(1)} %finish_half.1.refs_0_.kept_ref.refs_2_), channel_id=1, source_target_pairs={{20,0},{16,4},{28,8},{24,12},{4,16},{0,20},{12,24},{8,28},{21,1},{... | collective-permute-start | bytes 196616 | tf_op jit(solution)/shard_map/ppermute | solution.py:501

commit v22 on v21

--- a/solution.py
+++ b/solution.py
@@ -45,10 +45,12 @@
     return condition.astype(jnp.float32).astype(jnp.bfloat16)
 
 
-def planar_order(order):
+def planar_order(order, ahead=0):
     row, col = iota((order, order), 0), iota((order, order), 1)
     half = order // 2
-    source = jnp.where(row < half, 2 * row, 2 * (row - half) + 1)
+    part = (row >= half).astype(jnp.int32)
+    site = row - part * half + ahead
+    source = 2 * jnp.where(site >= half, site - half, site) + part
     return one_hot(col == source)
 
 
@@ -124,6 +126,7 @@
     row, col = iota((half, 128), 0), iota((half, 128), 1)
     near = ((third(row) == third(col)) & (col < half)).astype(f32)
     planar = planar_order(order)
+    planar_ahead = planar_order(order, 3)
     for copy in copies:
         copy.wait()
     for t in range(times):
@@ -149,8 +152,13 @@
             [here[3:half], here[:3], here[half + 3 :], here[half : half + 3]], axis=0
         )
         columns = slice(line * order, (line + 1) * order)
-        left_ref[0, :, columns] = here.T.astype(bf16)
-        left_ref[1, :, columns] = ahead_z.T.astype(bf16)
+        for k, reordering in enumerate((planar, planar_ahead)):
+            left_ref[k, :, columns] = lax.dot_general(
+                v_ref[line // cells_y, line % cells_y],
+                reordering,
+                (((0,), (1,)), ((), ())),
+                preferred_element_type=f32,
+            ).astype(bf16)
         seen = lax.dot_general(
             spread,
             link_rows_ref[line].astype(bf16),

time: 33.7 us -> 33.7 us (level)
  no operation moved by 1% of the time
where the time goes in v22:
time: 33.7 us; the launch traced here: 33.6 us
  starting transfers between devices  15.8 us (47%)
  waiting for transfers between devices  9.68 us (29%)
  Pallas kernels  6.69 us (20%)
  between operations  1.35 us (4%)
    ppermute x3, starting transfers between devices, from_step(): lax.ppermute(block, axis, [((i + step) % count, i) for i in range(count)])  7.34 us
    ppermute x5, waiting for transfers between devices, from_partner(): return lax.ppermute(block, axis, [(i ^ step, i) for i in range(count)])  6.83 us
    ppermute x5, starting transfers between devices, from_partner(): return lax.ppermute(block, axis, [(i ^ step, i) for i in range(count)])  6.52 us
    ppermute x2, waiting for transfers between devices, from_diagonal(): return lax.ppermute(block, axes, perm)  2.72 us
    pallas_call x1, Pallas kernels, per_device(): local_call(functools.partial(prepare_kernel, cells_x, cells_y), 'prepare_...  2.44 us
    ppermute x2, starting transfers between devices, from_diagonal(): return lax.ppermute(block, axes, perm)  1.96 us
    pallas_call x1, Pallas kernels, per_device(): local_call(functools.partial(second_contract_kernel, times, split), 'seco...  1.5 us
    pallas_call x1, Pallas kernels, per_device(): local_call(functools.partial(first_contract_kernel, times, split), 'first...  0.86 us
  transfers between devices with their start and end apart: 10, of which 8 were waited for; matrix products, arithmetic and copies ran while one was open for 0% of the time, Pallas kernels for 12%

profile of v22, /device:TPU:0, one launch (start us, length us, event | category | flops | bytes accessed | tf_op | source)
XLA Modules:
  0.0 33.6 jit_solution(18408025566888630786)
XLA Ops:
  0.6 5.1 %collective-permute-start = (bf16[1,2,144,128]{3,2,1,0:T(8,128)(2,1)}, bf16[1,2,144,128]{3,2,1,0:T(8,128)(2,1)S(1)}, u32[]{:S(2)}, u32[]{:S(2)}) collective-permute-start(bf16[1,2,144,128]{3,2,1,0:T(8,128)(2,1)} %bitcast.11), channel_id=1, source_target_pairs={{4,0},{8,4},{12,8},{0,12},{5,1},{9,5},{13,9},{1,13},{6,2},{10,6},{... | collective-permute-start | bytes 221192 | tf_op jit(solution)/shard_map/ppermute | solution.py:494
  5.7 0.7 %collective-permute-start.1 = (bf16[1,2,144,128]{3,2,1,0:T(8,128)(2,1)}, bf16[1,2,144,128]{3,2,1,0:T(8,128)(2,1)S(1)}, u32[]{:S(2)}, u32[]{:S(2)}) collective-permute-start(bf16[1,2,144,128]{3,2,1,0:T(8,128)(2,1)} %bitcast.12), channel_id=1, source_target_pairs={{1,0},{2,1},{3,2},{0,3},{5,4},{6,5},{7,6},{4,7},{9,8},{10,9},{11,1... | collective-permute-start | bytes 221192 | tf_op jit(solution)/shard_map/ppermute | solution.py:494
  6.4 2.4 %prepare_lines.1 = (bf16[3,144,144]{2,1,0:T(8,128)(2,1)S(1)}, f32[11,144,128]{2,1,0:T(8,128)S(1)}, bf16[2,128,288]{2,1,0:T(8,128)(2,1)S(1)}, f32[8,72,256]{2,1,0...) custom-call(bf16[1,2,144,128]{3,2,1,0:T(8,128)(2,1)} %bitcast.13, bf16[2,27,2,24]{3,2,1,0:T(2,128)(2,1)} %bitcast.14, ...), custom_call_target="tpu_custom_call" | custom-call | tf_op jit(solution)/shard_map/prepare_lines/pallas_call | solution.py:533
  8.9 0.0 collective-permute-done.refs_5_
  8.9 0.0 collective-permute-done.1.refs_6_
  8.9 0.8 %partial_margins.1 = (s16[2,528,128]{2,1,0:T(8,128)(2,1)S(1)}, f32[2,512,128]{2,1,0:T(8,128)S(1)}) custom-call(bf16[3,144,144]{2,1,0:T(8,128)(2,1)S(1)} %get-tuple-element.17.refs_0_, f32[11,144,128]{2,1,0:T(8,128)S(1)} %get-tuple-element.18.refs_1_, bf16[2,128,288]{2,1,0:T(8,128)(2,1)S(1)} %get-tuple-element.19.refs_2_, ...), custom_call_target="tpu_custom_call" | custom-call | tf_op jit(solution)/shard_map/partial_margins/pallas_call | solution.py:553
  9.7 0.0 copy-start
  9.7 0.8 %collective-permute-start.2 = (s16[2,528,128]{2,1,0:T(8,128)(2,1)S(1)}, s16[2,528,128]{2,1,0:T(8,128)(2,1)S(1)}, u32[]{:S(2)}, u32[]{:S(2)}) collective-permute-start(s16[2,528,128]{2,1,0:T(8,128)(2,1)S(1)} %get-tuple-element.23), channel_id=1, source_target_pairs={{1,0},{0,1},{3,2},{2,3},{5,4},{4,5},{7,6},{6,7},{9,8},{8,9},{11,10... | collective-permute-start | bytes 811016 | tf_op jit(solution)/shard_map/ppermute | solution.py:499
  10.5 1.2 %collective-permute-done.2.refs_0_ = s16[2,528,128]{2,1,0:T(8,128)(2,1)S(1)} collective-permute-done((s16[2,528,128]{2,1,0:T(8,128)(2,1)S(1)}, s16[2,528,128]{2,1,0:T(8,128)(2,1)S(1)}, u32[]{:S(2)}, u32[]{:S(2)}) %collective-permute-start.2) | collective-permute-done | bytes 270368 | tf_op jit(solution)/shard_map/ppermute | solution.py:499
  11.7 0.2 spread_halves.1
  11.9 1.2 %collective-permute-start.3 = (s16[272,128]{1,0:T(8,128)(2,1)S(1)}, s16[272,128]{1,0:T(8,128)(2,1)S(1)}, u32[]{:S(2)}, u32[]{:S(2)}) collective-permute-start(s16[272,128]{1,0:T(8,128)(2,1)S(1)} %get-tuple-element.24), channel_id=1, source_target_pairs={{2,0},{3,1},{0,2},{1,3},{6,4},{7,5},{4,6},{5,7},{10,8},{11,9},{8,1... | collective-permute-start | bytes 208904 | tf_op jit(solution)/shard_map/ppermute | solution.py:499
  13.1 0.0 collective-permute-start.4
  13.1 2.3 %collective-permute-start.5 = (s16[272,128]{1,0:T(8,128)(2,1)S(1)}, s16[272,128]{1,0:T(8,128)(2,1)S(1)}, u32[]{:S(2)}, u32[]{:S(2)}) collective-permute-start(s16[272,128]{1,0:T(8,128)(2,1)S(1)} %get-tuple-element.26), channel_id=1, source_target_pairs={{4,0},{0,4},{12,8},{8,12},{5,1},{1,5},{13,9},{9,13},{6,2},{2,6},{1... | collective-permute-start | bytes 208904 | tf_op jit(solution)/shard_map/ppermute | solution.py:499
  15.5 1.0 %collective-permute-done.3.refs_1_ = s16[272,128]{1,0:T(8,128)(2,1)S(1)} collective-permute-done((s16[272,128]{1,0:T(8,128)(2,1)S(1)}, s16[272,128]{1,0:T(8,128)(2,1)S(1)}, u32[]{:S(2)}, u32[]{:S(2)}) %collective-permute-start.3) | collective-permute-done | bytes 69664 | tf_op jit(solution)/shard_map/ppermute | solution.py:499
  16.4 2.5 %collective-permute-done.4.refs_2_ = s16[272,128]{1,0:T(8,128)(2,1)S(1)} collective-permute-done((s16[272,128]{1,0:T(8,128)(2,1)S(1)}, s16[272,128]{1,0:T(8,128)(2,1)S(1)}, u32[]{:S(2)}, u32[]{:S(2)}) %collective-permute-start.4) | collective-permute-done | bytes 69664 | tf_op jit(solution)/shard_map/ppermute | solution.py:509
  18.9 0.2 collective-permute-done.5.refs_3_
  19.1 0.1 keep_half.1.own_ref
  19.2 2.1 %collective-permute-start.6 = (s16[272,128]{1,0:T(8,128)(2,1)S(1)}, s16[272,128]{1,0:T(8,128)(2,1)S(1)}, u32[]{:S(2)}, u32[]{:S(2)}) collective-permute-start(s16[272,128]{1,0:T(8,128)(2,1)S(1)} %keep_half.1.own_ref), channel_id=1, source_target_pairs={{8,0},{12,4},{0,8},{4,12},{9,1},{13,5},{1,9},{5,13},{10,2},{14,6},... | collective-permute-start | bytes 208904 | tf_op jit(solution)/shard_map/ppermute | solution.py:499
  21.3 3.9 %collective-permute-done.6.arrived_ref = s16[272,128]{1,0:T(8,128)(2,1)S(1)} collective-permute-done((s16[272,128]{1,0:T(8,128)(2,1)S(1)}, s16[272,128]{1,0:T(8,128)(2,1)S(1)}, u32[]{:S(2)}, u32[]{:S(2)}) %collective-permute-start.6) | collective-permute-done | bytes 69664 | tf_op jit(solution)/shard_map/ppermute | solution.py:499
  25.3 1.6 %collective-permute-start.8 = (bf16[256,128]{1,0:T(8,128)(2,1)S(1)}, bf16[256,128]{1,0:T(8,128)(2,1)S(1)}, u32[]{:S(2)}, u32[]{:S(2)}) collective-permute-start(bf16[256,128]{1,0:T(8,128)(2,1)S(1)} %finish_half.1.refs_0_.kept_ref.refs_2_), channel_id=1, source_target_pairs={{16,0},{0,16},{17,1},{1,17},{18,2},{2,18},{19,3},{3,19},{20,4},{4,... | collective-permute-start | bytes 196616 | tf_op jit(solution)/shard_map/ppermute | solution.py:494
  26.9 0.0 collective-permute-start.7
  26.9 2.0 %collective-permute-start.9 = (bf16[256,128]{1,0:T(8,128)(2,1)S(1)}, bf16[256,128]{1,0:T(8,128)(2,1)S(1)}, u32[]{:S(2)}, u32[]{:S(2)}) collective-permute-start(bf16[256,128]{1,0:T(8,128)(2,1)S(1)} %finish_half.1.refs_0_.kept_ref.refs_2_), channel_id=1, source_target_pairs={{20,0},{16,4},{28,8},{24,12},{4,16},{0,20},{12,24},{8,28},{21,1},{... | collective-permute-start | bytes 196616 | tf_op jit(solution)/shard_map/ppermute | solution.py:509
  29.5 0.1 collective-permute-done.8.refs_1_.refs_3_
  29.6 0.0 copy-done
  29.6 0.9 %first_contraction.1 = (f32[8,128]{1,0:T(8,128)S(1)}, f32[2,32,128]{2,1,0:T(8,128)S(1)}) custom-call(s32[1]{0:T(128)S(6)} %copy.10.live_ref, f32[2,2,8,128]{3,2,1,0:T(8,128)S(1)} %get-tuple-element.27.weight_ref, bf16[2,512,512]{2,1,0:T(8,128)(2,1)S(1)} %bitcast.8, bf16[256,128]{1,0:T(8,128)(2,1)S(1)} %finish_half.1.refs_0_.kept_ref.refs_2_, ...), custom_call_target="tpu_custom_call" | custom-call | tf_op jit(solution)/shard_map/first_contraction/pallas_call | solution.py:612
  30.5 0.6 %collective-permute-done.7.other_ref.refs_0_ = bf16[256,128]{1,0:T(8,128)(2,1)S(1)} collective-permute-done((bf16[256,128]{1,0:T(8,128)(2,1)S(1)}, bf16[256,128]{1,0:T(8,128)(2,1)S(1)}, u32[]{:S(2)}, u32[]{:S(2)}) %collective-permute-start.7) | collective-permute-done | bytes 65568 | tf_op jit(solution)/shard_map/ppermute | solution.py:499
  31.1 0.7 %margins_out.1 = f32[1,512,128]{2,1,0:T(8,128)} custom-call(bf16[256,128]{1,0:T(8,128)(2,1)S(1)} %finish_half.1.refs_0_.kept_ref.refs_2_, bf16[256,128]{1,0:T(8,128)(2,1)S(1)} %collective-permute-done.7.other_ref.refs_0_), custom_call_target="tpu_custom_call" | custom-call | tf_op jit(solution)/shard_map/margins_out/pallas_call | solution.py:620
  31.8 0.2 collective-permute-done.9.refs_1_
  32.0 1.5 %second_contraction.1 = f32[1,2,2]{2,1,0:T(2,128)} custom-call(f32[2,2,8,128]{3,2,1,0:T(8,128)S(1)} %get-tuple-element.27.weight_ref, bf16[2,512,512]{2,1,0:T(8,128)(2,1)S(1)} %bitcast.9, bf16[256,128]{1,0:T(8,128)(2,1)S(1)} %collective-permute-done.7.other_ref.refs_0_, bf16[256,128]{1,0:T(8,128)(2,1)S(1)} %collective-permute-done.9.refs_1_, ...), custom_call_target="tpu_custom_call" | custom-call | tf_op jit(solution)/shard_map/second_contraction/pallas_call | solution.py:627
  (1 shorter events, 0.0 us)
Async XLA Ops:
  0.6 8.2 %collective-permute-start = (bf16[1,2,144,128]{3,2,1,0:T(8,128)(2,1)}, bf16[1,2,144,128]{3,2,1,0:T(8,128)(2,1)S(1)}, u32[]{:S(2)}, u32[]{:S(2)}) collective-permute-start(bf16[1,2,144,128]{3,2,1,0:T(8,128)(2,1)} %bitcast.11), channel_id=1, source_target_pairs={{4,0},{8,4},{12,8},{0,12},{5,1},{9,5},{13,9},{1,13},{6,2},{10,6},{... | collective-permute-start | bytes 221192 | tf_op jit(solution)/shard_map/ppermute | solution.py:494
  5.7 3.1 %collective-permute-start.1 = (bf16[1,2,144,128]{3,2,1,0:T(8,128)(2,1)}, bf16[1,2,144,128]{3,2,1,0:T(8,128)(2,1)S(1)}, u32[]{:S(2)}, u32[]{:S(2)}) collective-permute-start(bf16[1,2,144,128]{3,2,1,0:T(8,128)(2,1)} %bitcast.12), channel_id=1, source_target_pairs={{1,0},{2,1},{3,2},{0,3},{5,4},{6,5},{7,6},{4,7},{9,8},{10,9},{11,1... | collective-permute-start | bytes 221192 | tf_op jit(solution)/shard_map/ppermute | solution.py:494
  9.7 19.9 %copy-start = (bf16[1,2,512,512]{3,2,1,0:T(8,128)(2,1)S(1)}, bf16[1,2,512,512]{3,2,1,0:T(8,128)(2,1)}, u32[]{:S(2)}) copy-start(bf16[1,2,512,512]{3,2,1,0:T(8,128)(2,1)} %param.12) | copy-start | bytes 3145732
  9.7 2.0 %collective-permute-start.2 = (s16[2,528,128]{2,1,0:T(8,128)(2,1)S(1)}, s16[2,528,128]{2,1,0:T(8,128)(2,1)S(1)}, u32[]{:S(2)}, u32[]{:S(2)}) collective-permute-start(s16[2,528,128]{2,1,0:T(8,128)(2,1)S(1)} %get-tuple-element.23), channel_id=1, source_target_pairs={{1,0},{0,1},{3,2},{2,3},{5,4},{4,5},{7,6},{6,7},{9,8},{8,9},{11,10... | collective-permute-start | bytes 811016 | tf_op jit(solution)/shard_map/ppermute | solution.py:499
  11.9 4.5 %collective-permute-start.3 = (s16[272,128]{1,0:T(8,128)(2,1)S(1)}, s16[272,128]{1,0:T(8,128)(2,1)S(1)}, u32[]{:S(2)}, u32[]{:S(2)}) collective-permute-start(s16[272,128]{1,0:T(8,128)(2,1)S(1)} %get-tuple-element.24), channel_id=1, source_target_pairs={{2,0},{3,1},{0,2},{1,3},{6,4},{7,5},{4,6},{5,7},{10,8},{11,9},{8,1... | collective-permute-start | bytes 208904 | tf_op jit(solution)/shard_map/ppermute | solution.py:499
  13.1 5.8 %collective-permute-start.4 = (s16[272,128]{1,0:T(8,128)(2,1)S(1)}, s16[272,128]{1,0:T(8,128)(2,1)S(1)}, u32[]{:S(2)}, u32[]{:S(2)}) collective-permute-start(s16[272,128]{1,0:T(8,128)(2,1)S(1)} %get-tuple-element.25), channel_id=1, source_target_pairs={{6,0},{7,1},{4,2},{5,3},{2,4},{3,5},{0,6},{1,7},{14,8},{15,9},{12,... | collective-permute-start | bytes 208904 | tf_op jit(solution)/shard_map/ppermute | solution.py:509
  13.1 6.0 %collective-permute-start.5 = (s16[272,128]{1,0:T(8,128)(2,1)S(1)}, s16[272,128]{1,0:T(8,128)(2,1)S(1)}, u32[]{:S(2)}, u32[]{:S(2)}) collective-permute-start(s16[272,128]{1,0:T(8,128)(2,1)S(1)} %get-tuple-element.26), channel_id=1, source_target_pairs={{4,0},{0,4},{12,8},{8,12},{5,1},{1,5},{13,9},{9,13},{6,2},{2,6},{1... | collective-permute-start | bytes 208904 | tf_op jit(solution)/shard_map/ppermute | solution.py:499
  19.2 6.0 %collective-permute-start.6 = (s16[272,128]{1,0:T(8,128)(2,1)S(1)}, s16[272,128]{1,0:T(8,128)(2,1)S(1)}, u32[]{:S(2)}, u32[]{:S(2)}) collective-permute-start(s16[272,128]{1,0:T(8,128)(2,1)S(1)} %keep_half.1.own_ref), channel_id=1, source_target_pairs={{8,0},{12,4},{0,8},{4,12},{9,1},{13,5},{1,9},{5,13},{10,2},{14,6},... | collective-permute-start | bytes 208904 | tf_op jit(solution)/shard_map/ppermute | solution.py:499
  25.3 4.3 %collective-permute-start.8 = (bf16[256,128]{1,0:T(8,128)(2,1)S(1)}, bf16[256,128]{1,0:T(8,128)(2,1)S(1)}, u32[]{:S(2)}, u32[]{:S(2)}) collective-permute-start(bf16[256,128]{1,0:T(8,128)(2,1)S(1)} %finish_half.1.refs_0_.kept_ref.refs_2_), channel_id=1, source_target_pairs={{16,0},{0,16},{17,1},{1,17},{18,2},{2,18},{19,3},{3,19},{20,4},{4,... | collective-permute-start | bytes 196616 | tf_op jit(solution)/shard_map/ppermute | solution.py:494
  26.9 4.3 %collective-permute-start.7 = (bf16[256,128]{1,0:T(8,128)(2,1)S(1)}, bf16[256,128]{1,0:T(8,128)(2,1)S(1)}, u32[]{:S(2)}, u32[]{:S(2)}) collective-permute-start(bf16[256,128]{1,0:T(8,128)(2,1)S(1)} %finish_half.1.refs_0_.kept_ref.refs_2_), channel_id=1, source_target_pairs={{4,0},{0,4},{12,8},{8,12},{5,1},{1,5},{13,9},{9,13},{6,2},{2,6},{1... | collective-permute-start | bytes 196616 | tf_op jit(solution)/shard_map/ppermute | solution.py:499
  26.9 5.2 %collective-permute-start.9 = (bf16[256,128]{1,0:T(8,128)(2,1)S(1)}, bf16[256,128]{1,0:T(8,128)(2,1)S(1)}, u32[]{:S(2)}, u32[]{:S(2)}) collective-permute-start(bf16[256,128]{1,0:T(8,128)(2,1)S(1)} %finish_half.1.refs_0_.kept_ref.refs_2_), channel_id=1, source_target_pairs={{20,0},{16,4},{28,8},{24,12},{4,16},{0,20},{12,24},{8,28},{21,1},{... | collective-permute-start | bytes 196616 | tf_op jit(solution)/shard_map/ppermute | solution.py:509

commit v23 on v22

--- a/solution.py
+++ b/solution.py
@@ -127,13 +127,8 @@
     near = ((third(row) == third(col)) & (col < half)).astype(f32)
     planar = planar_order(order)
     planar_ahead = planar_order(order, 3)
-    for copy in copies:
-        copy.wait()
-    for t in range(times):
-        sink = pair_ref[0, 0] == t
-        source = pair_ref[0, 1] == t
-        weight_ref[0, t] = jnp.full(weight_ref.shape[2:], jnp.where(sink, 1.0, 0.0), f32)
-        weight_ref[1, t] = jnp.full(weight_ref.shape[2:], jnp.where(source, 1.0, 0.0), f32)
+    copies[0].wait()
+    copies[1].wait()
     for line in range(lines):
         for k in range(LINK_COLS // 2):
             link_rows_ref[line, 2 * k : 2 * k + 2] = link_ref[line, k].astype(f32)
@@ -188,6 +183,13 @@
                     local_ref[inside.index((d, line))] = transport(
                         matrix[:, :half], side_by_side(ahead), 1
                     )
+    for copy in copies[2:]:
+        copy.wait()
+    for t in range(times):
+        sink = pair_ref[0, 0] == t
+        source = pair_ref[0, 1] == t
+        weight_ref[0, t] = jnp.full(weight_ref.shape[2:], jnp.where(sink, 1.0, 0.0), f32)
+        weight_ref[1, t] = jnp.full(weight_ref.shape[2:], jnp.where(source, 1.0, 0.0), f32)
     wave_cols = waves_ref.shape[1]
     per_term = wave_cols // 3
     row, col = iota((wave_cols, 2 * vectors), 0), iota((wave_cols, 2 * vectors), 1)

time: 33.7 us -> 33.7 us (level)
  no operation moved by 1% of the time
where the time goes in v23:
time: 33.7 us; the launch traced here: 33.6 us
  starting transfers between devices  15.7 us (47%)
  waiting for transfers between devices  9.68 us (29%)
  Pallas kernels  6.83 us (20%)
  between operations  1.35 us (4%)
    ppermute x3, starting transfers between devices, from_step(): lax.ppermute(block, axis, [((i + step) % count, i) for i in range(count)])  7.34 us
    ppermute x5, waiting for transfers between devices, from_partner(): return lax.ppermute(block, axis, [(i ^ step, i) for i in range(count)])  6.83 us
    ppermute x5, starting transfers between devices, from_partner(): return lax.ppermute(block, axis, [(i ^ step, i) for i in range(count)])  6.38 us
    ppermute x2, waiting for transfers between devices, from_diagonal(): return lax.ppermute(block, axes, perm)  2.72 us
    pallas_call x1, Pallas kernels, per_device(): local_call(functools.partial(prepare_kernel, cells_x, cells_y), 'prepare_...  2.58 us
    ppermute x2, starting transfers between devices, from_diagonal(): return lax.ppermute(block, axes, perm)  1.96 us
    pallas_call x1, Pallas kernels, per_device(): local_call(functools.partial(second_contract_kernel, times, split), 'seco...  1.5 us
    pallas_call x1, Pallas kernels, per_device(): local_call(functools.partial(first_contract_kernel, times, split), 'first...  0.86 us
  transfers between devices with their start and end apart: 10, of which 8 were waited for; matrix products, arithmetic and copies ran while one was open for 0% of the time, Pallas kernels for 12%

profile of v23, /device:TPU:0, one launch (start us, length us, event | category | flops | bytes accessed | tf_op | source)
XLA Modules:
  0.0 33.6 jit_solution(960812977382289802)
XLA Ops:
  0.6 5.1 %collective-permute-start = (bf16[1,2,144,128]{3,2,1,0:T(8,128)(2,1)}, bf16[1,2,144,128]{3,2,1,0:T(8,128)(2,1)S(1)}, u32[]{:S(2)}, u32[]{:S(2)}) collective-permute-start(bf16[1,2,144,128]{3,2,1,0:T(8,128)(2,1)} %bitcast.11), channel_id=1, source_target_pairs={{4,0},{8,4},{12,8},{0,12},{5,1},{9,5},{13,9},{1,13},{6,2},{10,6},{... | collective-permute-start | bytes 221192 | tf_op jit(solution)/shard_map/ppermute | solution.py:496
  5.7 0.7 %collective-permute-start.1 = (bf16[1,2,144,128]{3,2,1,0:T(8,128)(2,1)}, bf16[1,2,144,128]{3,2,1,0:T(8,128)(2,1)S(1)}, u32[]{:S(2)}, u32[]{:S(2)}) collective-permute-start(bf16[1,2,144,128]{3,2,1,0:T(8,128)(2,1)} %bitcast.12), channel_id=1, source_target_pairs={{1,0},{2,1},{3,2},{0,3},{5,4},{6,5},{7,6},{4,7},{9,8},{10,9},{11,1... | collective-permute-start | bytes 221192 | tf_op jit(solution)/shard_map/ppermute | solution.py:496
  6.4 2.6 %prepare_lines.1 = (bf16[3,144,144]{2,1,0:T(8,128)(2,1)S(1)}, f32[11,144,128]{2,1,0:T(8,128)S(1)}, bf16[2,128,288]{2,1,0:T(8,128)(2,1)S(1)}, f32[8,72,256]{2,1,0...) custom-call(bf16[1,2,144,128]{3,2,1,0:T(8,128)(2,1)} %bitcast.13, bf16[2,27,2,24]{3,2,1,0:T(2,128)(2,1)} %bitcast.14, ...), custom_call_target="tpu_custom_call" | custom-call | tf_op jit(solution)/shard_map/prepare_lines/pallas_call | solution.py:535
  9.0 0.0 collective-permute-done.refs_5_
  9.0 0.0 collective-permute-done.1.refs_6_
  9.0 0.8 %partial_margins.1 = (s16[2,528,128]{2,1,0:T(8,128)(2,1)S(1)}, f32[2,512,128]{2,1,0:T(8,128)S(1)}) custom-call(bf16[3,144,144]{2,1,0:T(8,128)(2,1)S(1)} %get-tuple-element.17.refs_0_, f32[11,144,128]{2,1,0:T(8,128)S(1)} %get-tuple-element.18.refs_1_, bf16[2,128,288]{2,1,0:T(8,128)(2,1)S(1)} %get-tuple-element.19.refs_2_, ...), custom_call_target="tpu_custom_call" | custom-call | tf_op jit(solution)/shard_map/partial_margins/pallas_call | solution.py:555
  9.8 0.0 copy-start
  9.8 0.7 %collective-permute-start.2 = (s16[2,528,128]{2,1,0:T(8,128)(2,1)S(1)}, s16[2,528,128]{2,1,0:T(8,128)(2,1)S(1)}, u32[]{:S(2)}, u32[]{:S(2)}) collective-permute-start(s16[2,528,128]{2,1,0:T(8,128)(2,1)S(1)} %get-tuple-element.23), channel_id=1, source_target_pairs={{1,0},{0,1},{3,2},{2,3},{5,4},{4,5},{7,6},{6,7},{9,8},{8,9},{11,10... | collective-permute-start | bytes 811016 | tf_op jit(solution)/shard_map/ppermute | solution.py:501
  10.5 1.2 %collective-permute-done.2.refs_0_ = s16[2,528,128]{2,1,0:T(8,128)(2,1)S(1)} collective-permute-done((s16[2,528,128]{2,1,0:T(8,128)(2,1)S(1)}, s16[2,528,128]{2,1,0:T(8,128)(2,1)S(1)}, u32[]{:S(2)}, u32[]{:S(2)}) %collective-permute-start.2) | collective-permute-done | bytes 270368 | tf_op jit(solution)/shard_map/ppermute | solution.py:501
  11.7 0.2 spread_halves.1
  11.9 1.2 %collective-permute-start.3 = (s16[272,128]{1,0:T(8,128)(2,1)S(1)}, s16[272,128]{1,0:T(8,128)(2,1)S(1)}, u32[]{:S(2)}, u32[]{:S(2)}) collective-permute-start(s16[272,128]{1,0:T(8,128)(2,1)S(1)} %get-tuple-element.24), channel_id=1, source_target_pairs={{2,0},{3,1},{0,2},{1,3},{6,4},{7,5},{4,6},{5,7},{10,8},{11,9},{8,1... | collective-permute-start | bytes 208904 | tf_op jit(solution)/shard_map/ppermute | solution.py:501
  13.1 0.0 collective-permute-start.4
  13.1 2.3 %collective-permute-start.5 = (s16[272,128]{1,0:T(8,128)(2,1)S(1)}, s16[272,128]{1,0:T(8,128)(2,1)S(1)}, u32[]{:S(2)}, u32[]{:S(2)}) collective-permute-start(s16[272,128]{1,0:T(8,128)(2,1)S(1)} %get-tuple-element.26), channel_id=1, source_target_pairs={{4,0},{0,4},{12,8},{8,12},{5,1},{1,5},{13,9},{9,13},{6,2},{2,6},{1... | collective-permute-start | bytes 208904 | tf_op jit(solution)/shard_map/ppermute | solution.py:501
  15.5 1.0 %collective-permute-done.3.refs_1_ = s16[272,128]{1,0:T(8,128)(2,1)S(1)} collective-permute-done((s16[272,128]{1,0:T(8,128)(2,1)S(1)}, s16[272,128]{1,0:T(8,128)(2,1)S(1)}, u32[]{:S(2)}, u32[]{:S(2)}) %collective-permute-start.3) | collective-permute-done | bytes 69664 | tf_op jit(solution)/shard_map/ppermute | solution.py:501
  16.4 2.5 %collective-permute-done.4.refs_2_ = s16[272,128]{1,0:T(8,128)(2,1)S(1)} collective-permute-done((s16[272,128]{1,0:T(8,128)(2,1)S(1)}, s16[272,128]{1,0:T(8,128)(2,1)S(1)}, u32[]{:S(2)}, u32[]{:S(2)}) %collective-permute-start.4) | collective-permute-done | bytes 69664 | tf_op jit(solution)/shard_map/ppermute | solution.py:511
  18.9 0.2 collective-permute-done.5.refs_3_
  19.1 0.1 keep_half.1.own_ref
  19.2 2.1 %collective-permute-start.6 = (s16[272,128]{1,0:T(8,128)(2,1)S(1)}, s16[272,128]{1,0:T(8,128)(2,1)S(1)}, u32[]{:S(2)}, u32[]{:S(2)}) collective-permute-start(s16[272,128]{1,0:T(8,128)(2,1)S(1)} %keep_half.1.own_ref), channel_id=1, source_target_pairs={{8,0},{12,4},{0,8},{4,12},{9,1},{13,5},{1,9},{5,13},{10,2},{14,6},... | collective-permute-start | bytes 208904 | tf_op jit(solution)/shard_map/ppermute | solution.py:501
  21.3 3.9 %collective-permute-done.6.arrived_ref = s16[272,128]{1,0:T(8,128)(2,1)S(1)} collective-permute-done((s16[272,128]{1,0:T(8,128)(2,1)S(1)}, s16[272,128]{1,0:T(8,128)(2,1)S(1)}, u32[]{:S(2)}, u32[]{:S(2)}) %collective-permute-start.6) | collective-permute-done | bytes 69664 | tf_op jit(solution)/shard_map/ppermute | solution.py:501
  25.3 1.6 %collective-permute-start.8 = (bf16[256,128]{1,0:T(8,128)(2,1)S(1)}, bf16[256,128]{1,0:T(8,128)(2,1)S(1)}, u32[]{:S(2)}, u32[]{:S(2)}) collective-permute-start(bf16[256,128]{1,0:T(8,128)(2,1)S(1)} %finish_half.1.refs_0_.kept_ref.refs_2_), channel_id=1, source_target_pairs={{16,0},{0,16},{17,1},{1,17},{18,2},{2,18},{19,3},{3,19},{20,4},{4,... | collective-permute-start | bytes 196616 | tf_op jit(solution)/shard_map/ppermute | solution.py:496
  26.9 0.0 collective-permute-start.7
  26.9 2.0 %collective-permute-start.9 = (bf16[256,128]{1,0:T(8,128)(2,1)S(1)}, bf16[256,128]{1,0:T(8,128)(2,1)S(1)}, u32[]{:S(2)}, u32[]{:S(2)}) collective-permute-start(bf16[256,128]{1,0:T(8,128)(2,1)S(1)} %finish_half.1.refs_0_.kept_ref.refs_2_), channel_id=1, source_target_pairs={{20,0},{16,4},{28,8},{24,12},{4,16},{0,20},{12,24},{8,28},{21,1},{... | collective-permute-start | bytes 196616 | tf_op jit(solution)/shard_map/ppermute | solution.py:511
  29.5 0.1 collective-permute-done.8.refs_1_.refs_3_
  29.6 0.0 copy-done
  29.6 0.9 %first_contraction.1 = (f32[8,128]{1,0:T(8,128)S(1)}, f32[2,32,128]{2,1,0:T(8,128)S(1)}) custom-call(s32[1]{0:T(128)S(6)} %copy.10.live_ref, f32[2,2,8,128]{3,2,1,0:T(8,128)S(1)} %get-tuple-element.27.weight_ref, bf16[2,512,512]{2,1,0:T(8,128)(2,1)S(1)} %bitcast.8, bf16[256,128]{1,0:T(8,128)(2,1)S(1)} %finish_half.1.refs_0_.kept_ref.refs_2_, ...), custom_call_target="tpu_custom_call" | custom-call | tf_op jit(solution)/shard_map/first_contraction/pallas_call | solution.py:614
  30.5 0.6 %collective-permute-done.7.other_ref.refs_0_ = bf16[256,128]{1,0:T(8,128)(2,1)S(1)} collective-permute-done((bf16[256,128]{1,0:T(8,128)(2,1)S(1)}, bf16[256,128]{1,0:T(8,128)(2,1)S(1)}, u32[]{:S(2)}, u32[]{:S(2)}) %collective-permute-start.7) | collective-permute-done | bytes 65568 | tf_op jit(solution)/shard_map/ppermute | solution.py:501
  31.1 0.7 %margins_out.1 = f32[1,512,128]{2,1,0:T(8,128)} custom-call(bf16[256,128]{1,0:T(8,128)(2,1)S(1)} %finish_half.1.refs_0_.kept_ref.refs_2_, bf16[256,128]{1,0:T(8,128)(2,1)S(1)} %collective-permute-done.7.other_ref.refs_0_), custom_call_target="tpu_custom_call" | custom-call | tf_op jit(solution)/shard_map/margins_out/pallas_call | solution.py:622
  31.8 0.2 collective-permute-done.9.refs_1_
  32.0 1.5 %second_contraction.1 = f32[1,2,2]{2,1,0:T(2,128)} custom-call(f32[2,2,8,128]{3,2,1,0:T(8,128)S(1)} %get-tuple-element.27.weight_ref, bf16[2,512,512]{2,1,0:T(8,128)(2,1)S(1)} %bitcast.9, bf16[256,128]{1,0:T(8,128)(2,1)S(1)} %collective-permute-done.7.other_ref.refs_0_, bf16[256,128]{1,0:T(8,128)(2,1)S(1)} %collective-permute-done.9.refs_1_, ...), custom_call_target="tpu_custom_call" | custom-call | tf_op jit(solution)/shard_map/second_contraction/pallas_call | solution.py:629
  (1 shorter events, 0.0 us)
Async XLA Ops:
  0.6 8.4 %collective-permute-start = (bf16[1,2,144,128]{3,2,1,0:T(8,128)(2,1)}, bf16[1,2,144,128]{3,2,1,0:T(8,128)(2,1)S(1)}, u32[]{:S(2)}, u32[]{:S(2)}) collective-permute-start(bf16[1,2,144,128]{3,2,1,0:T(8,128)(2,1)} %bitcast.11), channel_id=1, source_target_pairs={{4,0},{8,4},{12,8},{0,12},{5,1},{9,5},{13,9},{1,13},{6,2},{10,6},{... | collective-permute-start | bytes 221192 | tf_op jit(solution)/shard_map/ppermute | solution.py:496
  5.7 3.3 %collective-permute-start.1 = (bf16[1,2,144,128]{3,2,1,0:T(8,128)(2,1)}, bf16[1,2,144,128]{3,2,1,0:T(8,128)(2,1)S(1)}, u32[]{:S(2)}, u32[]{:S(2)}) collective-permute-start(bf16[1,2,144,128]{3,2,1,0:T(8,128)(2,1)} %bitcast.12), channel_id=1, source_target_pairs={{1,0},{2,1},{3,2},{0,3},{5,4},{6,5},{7,6},{4,7},{9,8},{10,9},{11,1... | collective-permute-start | bytes 221192 | tf_op jit(solution)/shard_map/ppermute | solution.py:496
  9.8 19.8 %copy-start = (bf16[1,2,512,512]{3,2,1,0:T(8,128)(2,1)S(1)}, bf16[1,2,512,512]{3,2,1,0:T(8,128)(2,1)}, u32[]{:S(2)}) copy-start(bf16[1,2,512,512]{3,2,1,0:T(8,128)(2,1)} %param.12) | copy-start | bytes 3145732
  9.8 1.9 %collective-permute-start.2 = (s16[2,528,128]{2,1,0:T(8,128)(2,1)S(1)}, s16[2,528,128]{2,1,0:T(8,128)(2,1)S(1)}, u32[]{:S(2)}, u32[]{:S(2)}) collective-permute-start(s16[2,528,128]{2,1,0:T(8,128)(2,1)S(1)} %get-tuple-element.23), channel_id=1, source_target_pairs={{1,0},{0,1},{3,2},{2,3},{5,4},{4,5},{7,6},{6,7},{9,8},{8,9},{11,10... | collective-permute-start | bytes 811016 | tf_op jit(solution)/shard_map/ppermute | solution.py:501
  11.9 4.5 %collective-permute-start.3 = (s16[272,128]{1,0:T(8,128)(2,1)S(1)}, s16[272,128]{1,0:T(8,128)(2,1)S(1)}, u32[]{:S(2)}, u32[]{:S(2)}) collective-permute-start(s16[272,128]{1,0:T(8,128)(2,1)S(1)} %get-tuple-element.24), channel_id=1, source_target_pairs={{2,0},{3,1},{0,2},{1,3},{6,4},{7,5},{4,6},{5,7},{10,8},{11,9},{8,1... | collective-permute-start | bytes 208904 | tf_op jit(solution)/shard_map/ppermute | solution.py:501
  13.1 5.8 %collective-permute-start.4 = (s16[272,128]{1,0:T(8,128)(2,1)S(1)}, s16[272,128]{1,0:T(8,128)(2,1)S(1)}, u32[]{:S(2)}, u32[]{:S(2)}) collective-permute-start(s16[272,128]{1,0:T(8,128)(2,1)S(1)} %get-tuple-element.25), channel_id=1, source_target_pairs={{6,0},{7,1},{4,2},{5,3},{2,4},{3,5},{0,6},{1,7},{14,8},{15,9},{12,... | collective-permute-start | bytes 208904 | tf_op jit(solution)/shard_map/ppermute | solution.py:511
  13.1 6.0 %collective-permute-start.5 = (s16[272,128]{1,0:T(8,128)(2,1)S(1)}, s16[272,128]{1,0:T(8,128)(2,1)S(1)}, u32[]{:S(2)}, u32[]{:S(2)}) collective-permute-start(s16[272,128]{1,0:T(8,128)(2,1)S(1)} %get-tuple-element.26), channel_id=1, source_target_pairs={{4,0},{0,4},{12,8},{8,12},{5,1},{1,5},{13,9},{9,13},{6,2},{2,6},{1... | collective-permute-start | bytes 208904 | tf_op jit(solution)/shard_map/ppermute | solution.py:501
  19.2 6.0 %collective-permute-start.6 = (s16[272,128]{1,0:T(8,128)(2,1)S(1)}, s16[272,128]{1,0:T(8,128)(2,1)S(1)}, u32[]{:S(2)}, u32[]{:S(2)}) collective-permute-start(s16[272,128]{1,0:T(8,128)(2,1)S(1)} %keep_half.1.own_ref), channel_id=1, source_target_pairs={{8,0},{12,4},{0,8},{4,12},{9,1},{13,5},{1,9},{5,13},{10,2},{14,6},... | collective-permute-start | bytes 208904 | tf_op jit(solution)/shard_map/ppermute | solution.py:501
  25.3 4.3 %collective-permute-start.8 = (bf16[256,128]{1,0:T(8,128)(2,1)S(1)}, bf16[256,128]{1,0:T(8,128)(2,1)S(1)}, u32[]{:S(2)}, u32[]{:S(2)}) collective-permute-start(bf16[256,128]{1,0:T(8,128)(2,1)S(1)} %finish_half.1.refs_0_.kept_ref.refs_2_), channel_id=1, source_target_pairs={{16,0},{0,16},{17,1},{1,17},{18,2},{2,18},{19,3},{3,19},{20,4},{4,... | collective-permute-start | bytes 196616 | tf_op jit(solution)/shard_map/ppermute | solution.py:496
  26.9 4.3 %collective-permute-start.7 = (bf16[256,128]{1,0:T(8,128)(2,1)S(1)}, bf16[256,128]{1,0:T(8,128)(2,1)S(1)}, u32[]{:S(2)}, u32[]{:S(2)}) collective-permute-start(bf16[256,128]{1,0:T(8,128)(2,1)S(1)} %finish_half.1.refs_0_.kept_ref.refs_2_), channel_id=1, source_target_pairs={{4,0},{0,4},{12,8},{8,12},{5,1},{1,5},{13,9},{9,13},{6,2},{2,6},{1... | collective-permute-start | bytes 196616 | tf_op jit(solution)/shard_map/ppermute | solution.py:501
  26.9 5.2 %collective-permute-start.9 = (bf16[256,128]{1,0:T(8,128)(2,1)S(1)}, bf16[256,128]{1,0:T(8,128)(2,1)S(1)}, u32[]{:S(2)}, u32[]{:S(2)}) collective-permute-start(bf16[256,128]{1,0:T(8,128)(2,1)S(1)} %finish_half.1.refs_0_.kept_ref.refs_2_), channel_id=1, source_target_pairs={{20,0},{16,4},{28,8},{24,12},{4,16},{0,20},{12,24},{8,28},{21,1},{... | collective-permute-start | bytes 196616 | tf_op jit(solution)/shard_map/ppermute | solution.py:511
